TPU v7x, 256 devices: a whole 4x4x8 slice. The times are simulated.
256 devices in a mesh: group: 4 (over x), sub: 8 (over y, core), leaf: 8 (over z).
Axes of the slice: x: 4, y: 4, z: 8, core: 2. Of those that a mesh axis runs over, the one named last changes fastest.
Arguments:
- points: bfloat16 [524288, 256], P(('group', 'sub', 'leaf')), may hold values from -17 to 17
- right_side: float32 [64, 524288], P(None, ('group', 'sub', 'leaf')), may hold values from -26 to 26
- skel_sub: bfloat16 [8192, 256], P(('group', 'sub')), may hold values from -14 to 14
- skel_group: bfloat16 [1024, 256], P('group'), may hold values from -11 to 11
- skel_top: bfloat16 [256, 256], replicated, may hold values from -9 to 9
- neighbors: int32 [512, 2], P(('group', 'sub', 'leaf')), may hold values from 0 to 511, as said below
- counts: int32 [512], P(('group', 'sub', 'leaf')), may hold values from 0 to 2, as said below
Outputs:
- solution: float32 [64, 524288], P(None, ('group', 'sub', 'leaf'))
- residual: float32 [64, 524288], P(None, ('group', 'sub', 'leaf'))
Inputs may be any that keep to these rules, and one draw needn't show every extreme that they name: `neighbors`: row i lists, in its first counts[i] entries, only leaves i - 1 and i + 1, i - 1 first; leaf i lists i + 1 exactly when leaf i + 1 lists i; entries from counts[i] on equal i. `counts`: the number of live entries in the leaf's list; 2 is reached.
All inputs are finite; a program needn't handle non-finite values.
Results may differ from a plain program's by a relative error of at most 0.0045.
Values may be sent and summed in bfloat16 or wider, within the bound.
No kernel may reach another device: no remote copies, remote signals or barrier semaphores. Data moves between devices by JAX's collectives and lax.ppermute only.
A program may use at most 64 MiB of HBM per device.

v0:
```python
import jax
import jax.numpy as jnp
from jax import lax
from jax.sharding import PartitionSpec as P

LEAF = 1024
SKEL = 256
ITERS = 2


ridge_term = 3.0
level_one = 0.5
level_two = 0.25
level_top = 0.3


def extended(value, sides, width):
    for axis, dim in sides:
        devices, length = (lax.axis_size(axis), value.shape[dim])
        up = [(i, (i + 1) % devices) for i in range(devices - 1)]
        down = [(j, i) for i, j in up]
        last = lax.slice_in_dim(value, length - width, length, axis=dim)
        initial = lax.slice_in_dim(value, 0, width, axis=dim)
        before = lax.ppermute(last, axis, up)
        after = lax.ppermute(initial, axis, down)
        value = jnp.concatenate([before, value, after], axis=dim)
    return value


def gauss_block(left_rows, right_rows):
    cross = lax.dot_general(
        left_rows, right_rows, (((1,), (1,)), ((), ())), preferred_element_type=jnp.float32
    )
    left_sq = jnp.sum(jnp.square(left_rows.astype(jnp.float32)), axis=1)
    right_sq = jnp.sum(jnp.square(right_rows.astype(jnp.float32)), axis=1)
    return jnp.exp(
        (2.0 * cross - left_sq[:, None] - right_sq[None, :]) * (0.25 / left_rows.shape[1])
    )


def dot_plain(values, table):
    return jnp.dot(
        values, table, precision=lax.Precision.HIGHEST, preferred_element_type=jnp.float32
    )


def dot_last(values, table):
    return lax.dot_general(
        values,
        table,
        (((1,), (1,)), ((), ())),
        precision=lax.Precision.HIGHEST,
        preferred_element_type=jnp.float32,
    )


def shards(points, right_side, skel_sub, skel_group, skel_top, neighbors, counts):
    leaf_count = points.shape[0] // LEAF
    slot_count = neighbors.shape[1]
    halo_width = points.shape[0]
    halo_leaves = halo_width // LEAF
    first_leaf = lax.axis_index(("group", "sub", "leaf")) * leaf_count
    local_index = neighbors - first_leaf + halo_leaves
    padded_points = extended(points, ((("group", "sub", "leaf"), 0),), halo_width)
    self_tables = []
    neighbor_tables = []
    for position in range(leaf_count):
        own_points = points[position * LEAF : (position + 1) * LEAF]
        self_tables.append(gauss_block(own_points, own_points).astype(jnp.bfloat16))
        row_tables = []
        for column in range(slot_count):
            start = local_index[position, column] * LEAF
            other_points = lax.dynamic_slice_in_dim(padded_points, start, LEAF, 0)
            weight = (column < counts[position]).astype(jnp.float32)
            row_tables.append((gauss_block(other_points, own_points) * weight).astype(jnp.bfloat16))
        neighbor_tables.append(row_tables)
    point_table = gauss_block(points, skel_sub)
    low_table = gauss_block(skel_sub, skel_group)
    high_table = gauss_block(skel_group, skel_top)

    def squares(residual):
        return lax.psum(jnp.sum(residual * residual, axis=1), ("group", "sub", "leaf"))

    solution = jnp.zeros_like(right_side)
    residual = right_side
    direction = right_side
    norm_now = squares(residual)
    for iteration in range(ITERS):
        rounded = direction.astype(jnp.bfloat16)
        padded_dirs = extended(rounded, ((("group", "sub", "leaf"), 1),), halo_width)
        pieces = []
        for apply_position in range(leaf_count):
            own_dirs = rounded[:, apply_position * LEAF : (apply_position + 1) * LEAF]
            running = jnp.dot(
                own_dirs, self_tables[apply_position], preferred_element_type=jnp.float32
            )
            for apply_column in range(slot_count):
                apply_start = local_index[apply_position, apply_column] * LEAF
                other_dirs = lax.dynamic_slice_in_dim(padded_dirs, apply_start, LEAF, 1)
                running = running + jnp.dot(
                    other_dirs,
                    neighbor_tables[apply_position][apply_column],
                    preferred_element_type=jnp.float32,
                )
            pieces.append(running * (1.0 / LEAF))
        terms = dot_plain(direction, point_table) * (1.0 / LEAF)
        up_one = lax.psum(terms.astype(jnp.bfloat16), "leaf").astype(jnp.float32)
        up_two = lax.psum(
            (dot_plain(up_one, low_table) * (1.0 / SKEL)).astype(jnp.bfloat16), "sub"
        ).astype(jnp.float32)
        up_top = lax.psum(
            (dot_plain(up_two, high_table) * (1.0 / SKEL)).astype(jnp.bfloat16), "group"
        ).astype(jnp.float32)
        down_top = level_top * up_top
        down_two = level_two * up_two + dot_last(down_top, high_table) * (1.0 / SKEL)
        down_one = level_one * up_one + dot_last(down_two, low_table) * (1.0 / SKEL)
        applied = (
            ridge_term * direction
            + jnp.concatenate(pieces, axis=1)
            + dot_last(down_one, point_table) * (1.0 / LEAF)
        )
        bending = lax.psum(jnp.sum(direction * applied, axis=1), ("group", "sub", "leaf"))
        step_size = norm_now / bending
        solution = solution + step_size[:, None] * direction
        residual = residual - step_size[:, None] * applied
        if iteration + 1 < ITERS:
            norm_next = squares(residual)
            direction = residual + (norm_next / norm_now)[:, None] * direction
            norm_now = norm_next
    return (solution, residual)


def solution(mesh):
    return jax.shard_map(
        shards,
        mesh=mesh,
        in_specs=(
            P(("group", "sub", "leaf"), None),
            P(None, ("group", "sub", "leaf")),
            P(("group", "sub"), None),
            P("group", None),
            P(),
            P(("group", "sub", "leaf"), None),
            P(("group", "sub", "leaf")),
        ),
        out_specs=(P(None, ("group", "sub", "leaf")), P(None, ("group", "sub", "leaf"))),
        check_vma=False,
    )
```

profile of v0, /device:TPU:2, one launch (start us, length us, event | category | flops | bytes accessed | tf_op | source)
XLA Modules:
  0.0 445.9 jit_solution(11015714702044003163)
XLA Ops:
  0.6 3.8 collective-permute-start.2
  4.5 7.7 %collective-permute-start.3 = (bf16[2048,256]{1,0:T(8,128)(2,1)}, bf16[2048,256]{1,0:T(8,128)(2,1)}, u32[]{:S(2)}, u32[]{:S(2)}) collective-permute-start(bf16[2048,256]{1,0:T(8,128)(2,1)} %param.7), channel_id=1, source_target_pairs={{1,0},{2,1},{3,2},{4,3},{5,4},{6,5},{7,6},{8,7},{9,8},{10,9},{11,1... | collective-permute-start | bytes 3145736 | tf_op jit(solution)/shard_map/ppermute | solution.py:25
  13.3 1.9 collective-permute-start
  15.2 7.9 %collective-permute-start.1 = (bf16[64,2048]{1,0:T(8,128)(2,1)S(1)}, bf16[64,2048]{1,0:T(8,128)(2,1)}, u32[]{:S(2)}, u32[]{:S(2)}) collective-permute-start(bf16[64,2048]{1,0:T(8,128)(2,1)S(1)} %convert_element_type.127), channel_id=1, source_target_pairs={{1,0},{2,1},{3,2},{4,3},{5,4},{6,5},{7,6},{8,7},{9,8},{10,9},{11,1... | collective-permute-start | bytes 786440 | tf_op jit(solution)/shard_map/ppermute | solution.py:25
  27.0 1.5 multiply_reduce_fusion.6
  28.6 1.6 multiply_reduce_fusion
  30.1 2.4 exponential_convert_fusion.1
  32.5 1.4 convolution_bitcast_fusion.1
  33.9 2.5 exponential_convert_fusion
  37.4 1.3 fusion.30
  38.8 27.1 %psum.71 = bf16[64,256]{1,0:T(8,128)(2,1)S(1)} all-reduce(bf16[64,256]{1,0:T(8,128)(2,1)S(1)} %fusion.30), channel_id=1, replica_groups=mesh['group'=4,'sub'=8,'leaf'=8] {'leaf'}, use_global_device_ids=true, to_apply=%region_10.0 | all-reduce | flops 16384 | bytes 65536 | tf_op jit(solution)/shard_map/psum | solution.py:107
  66.5 23.6 %psum.72 = bf16[64,256]{1,0:T(8,128)(2,1)S(1)} all-reduce(bf16[64,256]{1,0:T(8,128)(2,1)S(1)} %fusion.26), channel_id=1, replica_groups=mesh['group'=4,'sub'=8,'leaf'=8] {'sub'}, use_global_device_ids=true, to_apply=%region_12.0 | all-reduce | flops 16384 | bytes 65536 | tf_op jit(solution)/shard_map/psum | solution.py:108
  92.6 14.4 %psum.73 = bf16[64,256]{1,0:T(8,128)(2,1)S(1)} all-reduce(bf16[64,256]{1,0:T(8,128)(2,1)S(1)} %fusion.27), channel_id=1, replica_groups=mesh['group'=4,'sub'=8,'leaf'=8] {'group'}, use_global_device_ids=true, to_apply=%region_14.0 | all-reduce | flops 16384 | bytes 65536 | tf_op jit(solution)/shard_map/psum | solution.py:111
  110.8 2.2 convolution_bitcast_fusion
  114.1 1.3 constant_dynamic-update-slice_fusion.2
  115.5 1.3 constant_dynamic-update-slice_fusion
  120.0 1.3 multiply_convert_fusion
  123.1 1.3 multiply_convert_fusion.1
  125.4 2.2 multiply_reduce_fusion.9
  127.6 74.2 %all-reduce = (f32[64]{0:T(128)S(1)}, f32[64]{0:T(128)S(1)}) all-reduce(f32[64]{0:T(128)S(1)} %get-tuple-element.9, f32[64]{0:T(128)S(1)} %get-tuple-element.8), channel_id=1, replica_groups=mesh['group'=4,'sub'=8,'leaf'=8] {'group','sub','leaf'}, use_global_device_ids=true, to_apply=%region_1.0 | all-reduce | flops 128 | bytes 1024 | tf_op jit(solution)/shard_map/psum | solution.py:82
  202.1 74.5 %psum.75 = f32[64]{0:T(128)S(1)} all-reduce(f32[64]{0:T(128)S(1)} %multiply_reduce_fusion.8), channel_id=1, replica_groups=mesh['group'=4,'sub'=8,'leaf'=8] {'group','sub','leaf'}, use_global_device_ids=true, to_apply=%region_18.0 | all-reduce | flops 64 | bytes 512 | tf_op jit(solution)/shard_map/psum | solution.py:82
  277.4 3.0 fusion.43
  280.5 3.1 collective-permute-start.4
  283.5 6.7 %collective-permute-start.5 = (bf16[64,2048]{1,0:T(8,128)(2,1)}, bf16[64,2048]{1,0:T(8,128)(2,1)}, u32[]{:S(2)}, u32[]{:S(2)}) collective-permute-start(bf16[64,2048]{1,0:T(8,128)(2,1)} %get-tuple-element.12), channel_id=1, source_target_pairs={{1,0},{2,1},{3,2},{4,3},{5,4},{6,5},{7,6},{8,7},{9,8},{10,9},{11,1... | collective-permute-start | bytes 786440 | tf_op jit(solution)/shard_map/ppermute | solution.py:25
  291.4 27.5 %psum.76 = bf16[64,256]{1,0:T(8,128)(2,1)S(1)} all-reduce(bf16[64,256]{1,0:T(8,128)(2,1)S(1)} %fusion.25), channel_id=1, replica_groups=mesh['group'=4,'sub'=8,'leaf'=8] {'leaf'}, use_global_device_ids=true, to_apply=%region_19.0 | all-reduce | flops 16384 | bytes 65536 | tf_op jit(solution)/shard_map/psum | solution.py:107
  320.1 23.6 %psum.77 = bf16[64,256]{1,0:T(8,128)(2,1)S(1)} all-reduce(bf16[64,256]{1,0:T(8,128)(2,1)S(1)} %fusion.28), channel_id=1, replica_groups=mesh['group'=4,'sub'=8,'leaf'=8] {'sub'}, use_global_device_ids=true, to_apply=%region_20.0 | all-reduce | flops 16384 | bytes 65536 | tf_op jit(solution)/shard_map/psum | solution.py:108
  344.0 14.1 %psum.78 = bf16[64,256]{1,0:T(8,128)(2,1)S(1)} all-reduce(bf16[64,256]{1,0:T(8,128)(2,1)S(1)} %fusion.29), channel_id=1, replica_groups=mesh['group'=4,'sub'=8,'leaf'=8] {'group'}, use_global_device_ids=true, to_apply=%region_21.0 | all-reduce | flops 16384 | bytes 65536 | tf_op jit(solution)/shard_map/psum | solution.py:111
  358.4 1.5 fusion.20
  359.9 2.3 fusion.41
  366.3 3.0 multiply_reduce_fusion.7
  369.3 74.2 %psum.79 = f32[64]{0:T(128)S(1)} all-reduce(f32[64]{0:T(128)S(1)} %get-tuple-element.23), channel_id=1, replica_groups=mesh['group'=4,'sub'=8,'leaf'=8] {'group','sub','leaf'}, use_global_device_ids=true, to_apply=%region_23.0 | all-reduce | flops 64 | bytes 512 | tf_op jit(solution)/shard_map/psum | solution.py:122
  443.5 2.4 multiply_subtract_fusion
  (83 shorter events, 23.0 us)
Async XLA Ops:
  0.6 113.4 %collective-permute-start.2 = (bf16[2048,256]{1,0:T(8,128)(2,1)}, bf16[2048,256]{1,0:T(8,128)(2,1)}, u32[]{:S(2)}, u32[]{:S(2)}) collective-permute-start(bf16[2048,256]{1,0:T(8,128)(2,1)} %param.7), channel_id=1, source_target_pairs={{0,1},{1,2},{2,3},{3,4},{4,5},{5,6},{6,7},{7,8},{8,9},{9,10},{10,1... | collective-permute-start | bytes 3145736 | tf_op jit(solution)/shard_map/ppermute | solution.py:24
  4.5 111.0 %collective-permute-start.3 = (bf16[2048,256]{1,0:T(8,128)(2,1)}, bf16[2048,256]{1,0:T(8,128)(2,1)}, u32[]{:S(2)}, u32[]{:S(2)}) collective-permute-start(bf16[2048,256]{1,0:T(8,128)(2,1)} %param.7), channel_id=1, source_target_pairs={{1,0},{2,1},{3,2},{4,3},{5,4},{6,5},{7,6},{8,7},{9,8},{10,9},{11,1... | collective-permute-start | bytes 3145736 | tf_op jit(solution)/shard_map/ppermute | solution.py:25
  13.3 99.7 %collective-permute-start = (bf16[64,2048]{1,0:T(8,128)(2,1)S(1)}, bf16[64,2048]{1,0:T(8,128)(2,1)}, u32[]{:S(2)}, u32[]{:S(2)}) collective-permute-start(bf16[64,2048]{1,0:T(8,128)(2,1)S(1)} %convert_element_type.127), channel_id=1, source_target_pairs={{0,1},{1,2},{2,3},{3,4},{4,5},{5,6},{6,7},{7,8},{8,9},{9,10},{10,1... | collective-permute-start | bytes 786440 | tf_op jit(solution)/shard_map/ppermute | solution.py:24
  15.2 97.8 %collective-permute-start.1 = (bf16[64,2048]{1,0:T(8,128)(2,1)S(1)}, bf16[64,2048]{1,0:T(8,128)(2,1)}, u32[]{:S(2)}, u32[]{:S(2)}) collective-permute-start(bf16[64,2048]{1,0:T(8,128)(2,1)S(1)} %convert_element_type.127), channel_id=1, source_target_pairs={{1,0},{2,1},{3,2},{4,3},{5,4},{6,5},{7,6},{8,7},{9,8},{10,9},{11,1... | collective-permute-start | bytes 786440 | tf_op jit(solution)/shard_map/ppermute | solution.py:25
  30.1 3.8 copy-start.1
  32.5 3.9 copy-start.3
  33.9 2.5 copy-start.17
  36.4 1.0 copy-start
  36.5 29.4 %copy-start.18 = (bf16[256,256]{1,0:T(8,128)(2,1)S(1)}, bf16[256,256]{1,0:T(8,128)(2,1)}, u32[]{:S(2)}) copy-start(bf16[256,256]{1,0:T(8,128)(2,1)} %param.10) | copy-start | bytes 393220
  37.4 70.3 %copy-start.19 = (s32[2]{0:T(128)S(1)}, s32[2]{0:T(128)}, u32[]{:S(2)}) copy-start(s32[2]{0:T(128)} %param.13) | copy-start | bytes 28
  66.3 47.8 %copy-start.14 = (f32[256,256]{1,0:T(8,128)}, f32[256,256]{1,0:T(8,128)S(1)}, u32[]{:S(2)}) copy-start(f32[256,256]{1,0:T(8,128)S(1)} %fusion.17) | copy-start | bytes 786436
  110.8 4.6 %copy-start.2 = (bf16[2048,256]{1,0:T(8,128)(2,1)S(1)}, bf16[2048,256]{1,0:T(8,128)(2,1)}, u32[]{:S(2)}) copy-start(bf16[2048,256]{1,0:T(8,128)(2,1)} %param.7) | copy-start | bytes 3145732
  118.7 1.3 copy-start.6
  121.3 1.8 copy-start.4
  123.1 1.3 copy-start.10
  123.1 1.3 copy-start.15
  124.4 3.2 copy-start.8
  277.4 12.8 %copy-start.12 = (f32[64,2048]{1,0:T(8,128)}, f32[64,2048]{1,0:T(8,128)S(1)}, u32[]{:S(2)}) copy-start(f32[64,2048]{1,0:T(8,128)S(1)} %get-tuple-element.13) | copy-start | bytes 1572868
  280.5 81.8 %collective-permute-start.4 = (bf16[64,2048]{1,0:T(8,128)(2,1)}, bf16[64,2048]{1,0:T(8,128)(2,1)}, u32[]{:S(2)}, u32[]{:S(2)}) collective-permute-start(bf16[64,2048]{1,0:T(8,128)(2,1)} %get-tuple-element.12), channel_id=1, source_target_pairs={{0,1},{1,2},{2,3},{3,4},{4,5},{5,6},{6,7},{7,8},{8,9},{9,10},{10,1... | collective-permute-start | bytes 786440 | tf_op jit(solution)/shard_map/ppermute | solution.py:24
  283.5 78.7 %collective-permute-start.5 = (bf16[64,2048]{1,0:T(8,128)(2,1)}, bf16[64,2048]{1,0:T(8,128)(2,1)}, u32[]{:S(2)}, u32[]{:S(2)}) collective-permute-start(bf16[64,2048]{1,0:T(8,128)(2,1)} %get-tuple-element.12), channel_id=1, source_target_pairs={{1,0},{2,1},{3,2},{4,3},{5,4},{6,5},{7,6},{8,7},{9,8},{10,9},{11,1... | collective-permute-start | bytes 786440 | tf_op jit(solution)/shard_map/ppermute | solution.py:25
  358.0 5.4 %copy-start.11 = (bf16[1024,1024]{1,0:T(8,128)(2,1)S(1)}, bf16[1024,1024]{1,0:T(8,128)(2,1)}, u32[]{:S(2)}) copy-start(bf16[1024,1024]{1,0:T(8,128)(2,1)} %copy-done.10) | copy-start | bytes 6291460
  358.0 5.4 %copy-start.16 = (f32[64,1024]{1,0:T(8,128)S(1)}, f32[64,1024]{1,0:T(8,128)}, u32[]{:S(2)}) copy-start(f32[64,1024]{1,0:T(8,128)} %fusion.43) | copy-start | bytes 786436
  359.9 4.0 copy-start.7
  363.4 1.6 copy-start.9
  364.0 1.8 copy-start.5
  365.0 1.2 copy-start.13
where the time goes:
time: 448 us; the launch traced here: 446 us
  blocking collectives  353 us (79%)
  matrix products  37 us (8%)
  starting transfers between devices  31.1 us (7%)
  other arithmetic  12.5 us (3%)
  between operations  6.19 us (1%)
  local copies, waits for them, and re-layouts  5.94 us (1%)
    psum x2, blocking collectives, squares(): lax.psum(jnp.sum(residual * residual, axis=1), ('group', 'sub', 'leaf'))  149 us
    psum x1, blocking collectives, shards(): lax.psum(jnp.sum(direction * applied, axis=1), ('group', 'sub', 'leaf'))  74.2 us
    psum x2, blocking collectives, shards(): up_one = lax.psum(terms.astype(jnp.bfloat16), 'leaf').astype(jnp.float32)  54.6 us
    psum x2, blocking collectives, shards(): lax.psum((dot_plain(up_one, low_table) * (1.0 / SKEL)).astype(jnp.bfloat1...  47.2 us
    psum x2, blocking collectives, shards(): lax.psum((dot_plain(up_two, high_table) * (1.0 / SKEL)).astype(jnp.bfloat...  28.4 us
    ppermute x3, starting transfers between devices, extended(): after = lax.ppermute(initial, axis, down)  22.3 us
    dot_general x9, matrix products, gauss_block(): lax.dot_general(left_rows, right_rows, (((1,), (1,)), ((), ())), preferre...  12 us
  transfers between devices with their start and end apart: 6, of which 0 were waited for; matrix products, arithmetic and copies ran while one was open for 7% of the time, Pallas kernels for 0%

commit v1 on v0

v1 whole, which is shorter than its diff:
```python
import jax
import jax.numpy as jnp
from jax import lax
from jax.sharding import PartitionSpec as P

LEAF = 1024
SKEL = 256
ALL = ("group", "sub", "leaf")

ridge_term = 3.0
level_one = 0.5
level_two = 0.25
level_top = 0.3

bf16 = jnp.bfloat16
f32 = jnp.float32


def gauss_block(left_rows, right_rows):
    cross = lax.dot_general(
        left_rows, right_rows, (((1,), (1,)), ((), ())), preferred_element_type=f32
    )
    left_sq = jnp.sum(jnp.square(left_rows.astype(f32)), axis=1)
    right_sq = jnp.sum(jnp.square(right_rows.astype(f32)), axis=1)
    return jnp.exp(
        (2.0 * cross - left_sq[:, None] - right_sq[None, :]) * (0.25 / left_rows.shape[1])
    )


def dot_plain(values, table):
    return jnp.dot(values, table, precision=lax.Precision.HIGHEST, preferred_element_type=f32)


def dot_last(values, table):
    return lax.dot_general(
        values,
        table,
        (((1,), (1,)), ((), ())),
        precision=lax.Precision.HIGHEST,
        preferred_element_type=f32,
    )


def dot_near(values, table):
    return jnp.dot(values, table, preferred_element_type=f32)


def dot_near_last(values, table):
    return lax.dot_general(
        values, table, (((1,), (1,)), ((), ())), preferred_element_type=f32
    )


def axis_sum(value, axis):
    count = lax.axis_size(axis)
    sent = jnp.broadcast_to(value[None], (count,) + value.shape)
    got = lax.all_to_all(sent, axis, 0, 0)
    return jnp.sum(got.astype(f32), axis=0)


def pieces_of(value):
    high = lax.reduce_precision(value, 8, 7)
    rest = value - high
    middle = lax.reduce_precision(rest, 8, 7)
    low = rest - middle
    return jnp.concatenate([high, middle, low], axis=1)


def with_scalars(weights, scalars):
    rows = jnp.pad(pieces_of(scalars), ((0, 4), (0, 64)))
    return jnp.concatenate([weights, rows], axis=0).astype(bf16)


def without_scalars(total):
    rows = total[64:68]
    return total[:64], rows[:, :64] + (rows[:, 64:128] + rows[:, 128:192])


def shift_up(value):
    count = lax.axis_size(ALL)
    return lax.ppermute(value, ALL, [(i, i + 1) for i in range(count - 1)])


def shift_down(value):
    count = lax.axis_size(ALL)
    return lax.ppermute(value, ALL, [(i + 1, i) for i in range(count - 1)])


def shards(points, right_side, skel_sub, skel_group, skel_top, neighbors, counts):
    first_leaf = lax.axis_index(ALL) * 2
    live = jnp.arange(2)[None, :] < counts[:, None]

    def listed(position, target):
        return jnp.sum((live[position] & (neighbors[position] == target)).astype(f32))

    with_before = listed(0, first_leaf - 1)
    with_inner = listed(0, first_leaf + 1)
    with_inner_back = listed(1, first_leaf)

    points_a, points_b = points[:LEAF], points[LEAF:]
    points_before = shift_up(points_b)
    table_a = gauss_block(points_a, points_a).astype(bf16)
    table_b = gauss_block(points_b, points_b).astype(bf16)
    table_ab = gauss_block(points_a, points_b).astype(bf16)
    table_before = gauss_block(points_before, points_a).astype(bf16)

    point_table = gauss_block(points, skel_sub)
    low_table = gauss_block(skel_sub, skel_group)
    high_table = gauss_block(skel_group, skel_top)

    def near(rounded):
        field_a, field_b = rounded[:, :LEAF], rounded[:, LEAF:]
        field_before = shift_up(field_b)
        from_before = with_before * dot_near(field_before, table_before)
        back = with_before * dot_near_last(field_a, table_before)
        own_a = dot_near(field_a, table_a) + with_inner * dot_near_last(field_b, table_ab)
        own_b = dot_near(field_b, table_b) + with_inner_back * dot_near(field_a, table_ab)
        after = shift_down(back)
        own = jnp.concatenate([own_a, own_b], axis=1) * (1.0 / LEAF)
        cross_a = from_before * (1.0 / LEAF)
        return own, cross_a, after * (1.0 / LEAF)

    def down(up_one, up_two, up_top):
        down_top = level_top * up_top
        down_two = level_two * up_two + dot_last(down_top, high_table) * (1.0 / SKEL)
        down_one = level_one * up_one + dot_last(down_two, low_table) * (1.0 / SKEL)
        return dot_last(down_one, point_table) * (1.0 / LEAF)

    first = right_side
    terms = dot_plain(first, point_table) * (1.0 / LEAF)
    up_one = axis_sum(terms.astype(bf16), "leaf")
    up_two = axis_sum((dot_plain(up_one, low_table) * (1.0 / SKEL)).astype(bf16), "sub")
    up_top = axis_sum((dot_plain(up_two, high_table) * (1.0 / SKEL)).astype(bf16), "group")
    own, cross_a, after = near(first.astype(bf16))
    far = down(up_one, up_two, up_top)
    second_a = own[:, :LEAF] + cross_a + far[:, :LEAF]
    second_b = own[:, LEAF:] + after + far[:, LEAF:]
    second = jnp.concatenate([second_a, second_b], axis=1)

    terms = dot_plain(second, point_table) * (1.0 / LEAF)
    own, cross_a, after = near(second.astype(bf16))
    scalars = jnp.stack(
        [
            jnp.sum(first * first, axis=1),
            jnp.sum(first * second, axis=1),
            jnp.sum(second * second, axis=1),
            jnp.sum(second * own, axis=1) + 2.0 * jnp.sum(second_a * cross_a, axis=1),
        ]
    )
    up_one, scalars = without_scalars(axis_sum(with_scalars(terms, scalars), "leaf"))
    scalars = scalars.at[3].add(level_one * jnp.sum(up_one * up_one, axis=1))
    terms = dot_plain(up_one, low_table) * (1.0 / SKEL)
    up_two, scalars = without_scalars(axis_sum(with_scalars(terms, scalars), "sub"))
    scalars = scalars.at[3].add(level_two * jnp.sum(up_two * up_two, axis=1))
    terms = dot_plain(up_two, high_table) * (1.0 / SKEL)
    up_top, scalars = without_scalars(axis_sum(with_scalars(terms, scalars), "group"))
    scalars = scalars.at[3].add(level_top * jnp.sum(up_top * up_top, axis=1))
    far = down(up_one, up_two, up_top)
    third_a = own[:, :LEAF] + cross_a + far[:, :LEAF]
    third_b = own[:, LEAF:] + after + far[:, LEAF:]
    third = jnp.concatenate([third_a, third_b], axis=1)

    bb, bu, uu, uv = scalars[0], scalars[1], scalars[2], scalars[3]
    step_one = bb / (ridge_term * bb + bu)
    ratio = bu / bb
    norm_one = step_one * step_one * (uu - ratio * bu)
    beta = norm_one / bb
    bend_rr = step_one * step_one * (ratio * ratio * bu - 2.0 * ratio * uu + uv)
    bend_rb = step_one * (ratio * bu - uu)
    bending = (
        ridge_term * (norm_one + beta * beta * bb)
        + bend_rr
        + 2.0 * beta * bend_rb
        + beta * beta * bu
    )
    step_two = norm_one / bending

    def column(value):
        return value[:, None]

    residual_one = column(step_one * ratio) * first - column(step_one) * second
    direction = residual_one + column(beta) * first
    applied = (
        ridge_term * direction
        + column(step_one * ratio + beta) * second
        - column(step_one) * third
    )
    solution = column(step_one) * first + column(step_two) * direction
    residual = residual_one - column(step_two) * applied
    return (solution, residual)


def solution(mesh):
    return jax.shard_map(
        shards,
        mesh=mesh,
        in_specs=(
            P(ALL, None),
            P(None, ALL),
            P(("group", "sub"), None),
            P("group", None),
            P(),
            P(ALL, None),
            P(ALL),
        ),
        out_specs=(P(None, ALL), P(None, ALL)),
        check_vma=False,
    )
```

time: 448 us -> 148 us (0.33)
  blocking collectives: 353 us -> 26.4 us
  waiting for transfers between devices: 0.02 us -> 8.76 us
  starting transfers between devices: 31.1 us -> 39.4 us
  matrix products: 37 us -> 44.8 us
  other arithmetic: 12.5 us -> 17.7 us
  between operations: 6.19 us -> 1.15 us
    psum x9 -> x0, blocking collectives: 353 us -> none  [the longest x2 149 us: squares(): lax.psum(jnp.sum(residual * residual, axis=1), ('group', 'sub', 'leaf'))]
    all_to_all x0 -> x2, blocking collectives: none -> 26.4 us  [axis_sum(): got = lax.all_to_all(sent, axis, 0, 0)]
    all_to_all x0 -> x4, starting transfers between devices: none -> 22.8 us  [axis_sum(): got = lax.all_to_all(sent, axis, 0, 0)]
    ppermute x6 -> x5, starting transfers between devices: 31.1 us -> 16.5 us  [the longest x3 11.5 us: shift_up(): return lax.ppermute(value, ALL, [(i, i + 1) for i in range(count - 1)])]
    dot_general x12, matrix products: 12.7 us -> 19.7 us  [the longest x4 10.2 us: dot_near_last(): lax.dot_general(values, table, (((1,), (1,)), ((), ())), preferred_elemen...]
    ppermute x6 -> x5, waiting for transfers between devices: 0.02 us -> 6.02 us  [the longest x2 3.09 us: shift_down(): return lax.ppermute(value, ALL, [(i + 1, i) for i in range(count - 1)])]
    reduce_sum x7 -> x17, other arithmetic: 5.23 us -> 10.7 us  [the longest x6 4.16 us: axis_sum(): return jnp.sum(got.astype(f32), axis=0)]
    dot_general x9 -> x7, matrix products: 12 us -> 13.3 us  [gauss_block(): lax.dot_general(left_rows, right_rows, (((1,), (1,)), ((), ())), preferre...]
  transfers between devices with their start and end apart: 6 -> 9, of which waited for: 0 -> 4; matrix products, arithmetic and copies ran while one was open for 7% -> 33% of each run, Pallas kernels for 0% -> 0%
where the time goes in v1:
time: 148 us; the launch traced here: 147 us
  matrix products  44.8 us (30%)
  starting transfers between devices  39.4 us (27%)
  blocking collectives  26.4 us (18%)
  other arithmetic  17.7 us (12%)
  waiting for transfers between devices  8.76 us (6%)
  local copies, waits for them, and re-layouts  8.5 us (6%)
    all_to_all x2, blocking collectives, axis_sum(): got = lax.all_to_all(sent, axis, 0, 0)  26.4 us
    all_to_all x4, starting transfers between devices, axis_sum(): got = lax.all_to_all(sent, axis, 0, 0)  22.8 us
    dot_general x7, matrix products, gauss_block(): lax.dot_general(left_rows, right_rows, (((1,), (1,)), ((), ())), preferre...  13.3 us
    ppermute x3, starting transfers between devices, shift_up(): return lax.ppermute(value, ALL, [(i, i + 1) for i in range(count - 1)])  11.5 us
    dot_general x4, matrix products, dot_near_last(): lax.dot_general(values, table, (((1,), (1,)), ((), ())), preferred_elemen...  10.2 us
    dot_general x8, matrix products, dot_near(): return jnp.dot(values, table, preferred_element_type=f32)  9.56 us
    dot_general x6, matrix products, dot_last(): lax.dot_general(values, table, (((1,), (1,)), ((), ())), precision=lax.Pr...  6.7 us
    dot_general x6, matrix products, dot_plain(): jnp.dot(values, table, precision=lax.Precision.HIGHEST, preferred_element...  5.07 us
  transfers between devices with their start and end apart: 9, of which 4 were waited for; matrix products, arithmetic and copies ran while one was open for 33% of the time, Pallas kernels for 0%

profile of v1, /device:TPU:2, one launch (start us, length us, event | category | flops | bytes accessed | tf_op | source)
XLA Modules:
  0.0 146.7 jit_solution(3886178694827040560)
XLA Ops:
  1.7 1.6 %multiply_reduce_fusion = f32[2048]{0:T(1024)S(1)} fusion(bf16[2048,256]{1,0:T(8,128)(2,1)} %param.13), kind=kLoop, calls=%fused_computation.11 | loop fusion | flops 1570816 | bytes 1056768 | tf_op jit(solution)/shard_map/reduce_sum | solution.py:23
  3.2 1.9 %fusion.3 = f32[2048,256]{1,0:T(8,128)S(1)} fusion(bf16[2048,256]{1,0:T(8,128)(2,1)} %param.13, bf16[256,256]{1,0:T(8,128)(2,1)} %param.15, f32[256]{0:T(256)S(1)} %multiply_reduce_fusion.11, f32[2048]{0:T(1024)S(1)} %multiply_reduce_fusion), kind=kOutput, calls=%fused_computation.8 | convolution fusion | flops 270532608 | bytes 3286016 | tf_op jit(solution)/shard_map/dot_general | solution.py:20
  7.2 8.5 %all-to-all-start = ((bf16[8,64,256]{2,1,0:T(8,128)(2,1)}), bf16[8,64,256]{2,1,0:T(8,128)(2,1)}, u32[]{:S(2)}, u32[]{:S(2)}) async-start(bf16[8,64,256]{2,1,0:T(8,128)(2,1)} %broadcast_in_dim.12), calls=%async_computation | async-start | bytes 524288 | tf_op jit(solution)/shard_map/all_to_all | solution.py:57
  15.7 2.0 %slice.169 = bf16[1024,256]{1,0:T(8,128)(2,1)} slice(bf16[2048,256]{1,0:T(8,128)(2,1)} %param.13), slice={[1024:2048], [0:256]} | slice | bytes 1048576 | tf_op jit(solution)/shard_map/slice | solution.py:100
  17.7 3.9 %collective-permute-start = (bf16[1024,256]{1,0:T(8,128)(2,1)}, bf16[1024,256]{1,0:T(8,128)(2,1)}, u32[]{:S(2)}, u32[]{:S(2)}) collective-permute-start(bf16[1024,256]{1,0:T(8,128)(2,1)} %slice.169), channel_id=1, source_target_pairs={{0,1},{1,2},{2,3},{3,4},{4,5},{5,6},{6,7},{7,8},{8,9},{9,10},{10,1... | collective-permute-start | bytes 1572872 | tf_op jit(solution)/shard_map/ppermute | solution.py:81
  22.3 3.4 %collective-permute-start.1 = (bf16[64,1024]{1,0:T(8,128)(2,1)}, bf16[64,1024]{1,0:T(8,128)(2,1)}, u32[]{:S(2)}, u32[]{:S(2)}) collective-permute-start(bf16[64,1024]{1,0:T(8,128)(2,1)} %slice.202), channel_id=1, source_target_pairs={{0,1},{1,2},{2,3},{3,4},{4,5},{5,6},{6,7},{7,8},{8,9},{9,10},{10,1... | collective-permute-start | bytes 393224 | tf_op jit(solution)/shard_map/ppermute | solution.py:81
  26.0 2.4 %exponential_convert_fusion.3 = bf16[1024,1024]{1,0:T(8,128)(2,1)} fusion(f32[1024]{0:T(1024)S(1)} %get-tuple-element.38, bf16[2048,256]{1,0:T(8,128)(2,1)S(1)} %copy-done.7), kind=kOutput, calls=%fused_computation.3 | convolution fusion | flops 542113792 | bytes 2629632 | tf_op jit(solution)/shard_map/dot_general | solution.py:20
  28.5 2.4 %exponential_convert_fusion.2 = bf16[1024,1024]{1,0:T(8,128)(2,1)} fusion(f32[1024]{0:T(1024)S(1)} %get-tuple-element.39, f32[1024]{0:T(1024)S(1)} %get-tuple-element.38, bf16[2048,256]{1,0:T(8,128)(2,1)S(1)} %copy-done.7), kind=kOutput, calls=%fused_computation.2 | convolution fusion | flops 542113792 | bytes 3153920 | tf_op jit(solution)/shard_map/dot_general | solution.py:20
  30.9 2.4 %exponential_convert_fusion.1 = bf16[1024,1024]{1,0:T(8,128)(2,1)} fusion(f32[1024]{0:T(1024)S(1)} %get-tuple-element.39, bf16[2048,256]{1,0:T(8,128)(2,1)S(1)} %copy-done.7), kind=kOutput, calls=%fused_computation.1 | convolution fusion | flops 542113792 | bytes 2629632 | tf_op jit(solution)/shard_map/dot_general | solution.py:20
  33.4 2.2 %fusion.108 = f32[1024,64]{0,1:T(8,128)S(1)} fusion(bf16[1024,1024]{1,0:T(8,128)(2,1)} %exponential_convert_fusion.1, bf16[64,2048]{1,0:T(8,128)(2,1)S(1)} %convert_element_type.109), kind=kOutput, calls=%fused_computation.209 | convolution fusion | flops 134217728 | bytes 2490368 | tf_op jit(solution)/shard_map/dot_general | solution.py:45
  36.9 1.4 convolution_multiply_fusion.12
  43.0 4.5 %all-to-all-start.1 = ((bf16[8,64,256]{2,1,0:T(8,128)(2,1)}), bf16[8,64,256]{2,1,0:T(8,128)(2,1)}, u32[]{:S(2)}, u32[]{:S(2)}) async-start(bf16[8,64,256]{2,1,0:T(8,128)(2,1)} %broadcast_in_dim.13), calls=%async_computation.1 | async-start | bytes 524288 | tf_op jit(solution)/shard_map/all_to_all | solution.py:57
  48.8 3.6 %exponential_convert_fusion = bf16[1024,1024]{1,0:T(8,128)(2,1)} fusion(f32[1024]{0:T(1024)S(1)} %multiply_reduce_fusion.1, f32[1024]{0:T(1024)S(1)} %get-tuple-element.38, bf16[1024,256]{1,0:T(8,128)(2,1)} %collective-permute-done, bf16[2048,256]{1,0:T(8,128)(2,1)} %param.13), kind=kOutput, calls=%fused_computation | convolution fusion | flops 542113792 | bytes 3153920 | tf_op jit(solution)/shard_map/dot_general | solution.py:20
  52.4 2.7 %all-to-all-done.1 = bf16[8,64,256]{2,1,0:T(8,128)(2,1)} async-done(((bf16[8,64,256]{2,1,0:T(8,128)(2,1)}), bf16[8,64,256]{2,1,0:T(8,128)(2,1)}, u32[]{:S(2)}, u32[]{:S(2)}) %all-to-all-start.1) | async-done | bytes 262176 | tf_op jit(solution)/shard_map/all_to_all | solution.py:57
  57.0 4.8 %all-to-all-start.2 = ((bf16[4,64,256]{2,1,0:T(8,128)(2,1)}), bf16[4,64,256]{2,1,0:T(8,128)(2,1)}, u32[]{:S(2)}, u32[]{:S(2)}) async-start(bf16[4,64,256]{2,1,0:T(8,128)(2,1)} %broadcast_in_dim.14), calls=%async_computation.2 | async-start | bytes 262144 | tf_op jit(solution)/shard_map/all_to_all | solution.py:57
  61.9 3.6 %fusion.13 = f32[64,1024]{1,0:T(8,128)} fusion(bf16[1024,1024]{1,0:T(8,128)(2,1)} %exponential_convert_fusion, f32[]{:T(128)} %get-tuple-element.44, bf16[64,2048]{1,0:T(8,128)(2,1)S(1)} %convert_element_type.109), kind=kOutput, calls=%fused_computation.29 | convolution fusion | flops 134283264 | bytes 2490372 | tf_op jit(solution)/shard_map/dot_general | solution.py:49
  65.5 3.1 %collective-permute-start.2 = (f32[64,1024]{1,0:T(8,128)}, f32[64,1024]{1,0:T(8,128)}, u32[]{:S(2)}, u32[]{:S(2)}) collective-permute-start(f32[64,1024]{1,0:T(8,128)} %fusion.13), channel_id=1, source_target_pairs={{1,0},{2,1},{3,2},{4,3},{5,4},{6,5},{7,6},{8,7},{9,8},{10,9},{11,1... | collective-permute-start | bytes 786440 | tf_op jit(solution)/shard_map/ppermute | solution.py:86
  70.5 2.1 %convolution_multiply_fusion.2 = f32[64,2048]{1,0:T(8,128)S(1)} fusion(f32[64,256]{1,0:T(8,128)S(1)} %fusion.25, f32[2048,256]{1,0:T(8,128)S(1)} %fusion.3), kind=kOutput, calls=%fused_computation.10 | convolution fusion | flops 402784256 | bytes 2686976 | tf_op jit(solution)/shard_map/dot_general | solution.py:35
  72.6 2.0 %fusion.22 = f32[64,1024]{1,0:T(8,128)S(1)} fusion(bf16[64,1024]{1,0:T(8,128)(2,1)} %collective-permute-done.1, bf16[1024,1024]{1,0:T(8,128)(2,1)S(1)} %copy-done, f32[64,2048]{1,0:T(8,128)S(1)} %convolution_multiply_fusion.2, f32[64,2048]{1,0:T(8,128)S(1)} %copy-done.11, f32[]{:T(128)} %get-tuple-element.44), kind=kOutput, calls=%fused_computation.41 | convolution fusion | flops 134479872 | bytes 3014660 | tf_op jit(solution)/shard_map/dot_general | solution.py:45
  79.4 4.2 %collective-permute-start.3 = (bf16[64,1024]{1,0:T(8,128)(2,1)S(1)}, bf16[64,1024]{1,0:T(8,128)(2,1)S(1)}, u32[]{:S(2)}, u32[]{:S(2)}) collective-permute-start(bf16[64,1024]{1,0:T(8,128)(2,1)S(1)} %slice.208), channel_id=1, source_target_pairs={{0,1},{1,2},{2,3},{3,4},{4,5},{5,6},{6,7},{7,8},{8,9},{9,10},{10,1... | collective-permute-start | bytes 393224 | tf_op jit(solution)/shard_map/ppermute | solution.py:81
  83.6 1.5 fusion.12
  87.2 2.9 %collective-permute-done.3 = bf16[64,1024]{1,0:T(8,128)(2,1)S(1)} collective-permute-done((bf16[64,1024]{1,0:T(8,128)(2,1)S(1)}, bf16[64,1024]{1,0:T(8,128)(2,1)S(1)}, u32[]{:S(2)}, u32[]{:S(2)}) %collective-permute-start.3) | collective-permute-done | bytes 131104 | tf_op jit(solution)/shard_map/ppermute | solution.py:81
  90.1 1.8 %multiply_reduce_fusion.8 = (f32[64]{0:T(128)S(1)}, f32[64,1024]{1,0:T(8,128)}) fusion(f32[64,1024]{1,0:T(8,128)S(1)} %fusion.22, bf16[64,1024]{1,0:T(8,128)(2,1)S(1)} %collective-permute-done.3, bf16[1024,1024]{1,0:T(8,128)(2,1)S(1)} %copy-done, f32[]{:T(128)} %get-tuple-element.44), kind=kOutput, calls=%fused_computation.95 | convolution fusion | flops 134479808 | bytes 2752772 | tf_op jit(solution)/shard_map/dot_general | solution.py:45
  92.1 14.9 %all_to_all.30 = bf16[8,72,256]{2,1,0:T(8,128)(2,1)S(1)} all-to-all(bf16[8,72,256]{2,1,0:T(8,128)(2,1)S(1)} %broadcast_in_dim.15), channel_id=1, replica_groups=mesh['group'=4,'sub'=8,'leaf'=8] {'leaf'}, dimensions={0} | all-to-all | bytes 589824 | tf_op jit(solution)/shard_map/all_to_all | solution.py:57
  107.7 11.5 %all_to_all.31 = bf16[8,72,256]{2,1,0:T(8,128)(2,1)S(1)} all-to-all(bf16[8,72,256]{2,1,0:T(8,128)(2,1)S(1)} %broadcast_in_dim.16), channel_id=1, replica_groups=mesh['group'=4,'sub'=8,'leaf'=8] {'sub'}, dimensions={0} | all-to-all | bytes 589824 | tf_op jit(solution)/shard_map/all_to_all | solution.py:57
  119.2 1.8 %fusion.32 = bf16[64,256]{1,0:T(8,128)(2,1)} fusion(f32[256,256]{1,0:T(8,128)} %copy-done.8, f32[72,256]{1,0:T(8,128)S(1)} %convert_reduce_fusion), kind=kOutput, calls=%fused_computation.61 | convolution fusion | flops 50364416 | bytes 360448 | tf_op jit(solution)/shard_map/dot_general | solution.py:31
  125.6 5.1 %all-to-all-start.5 = ((bf16[4,72,256]{2,1,0:T(8,128)(2,1)}), bf16[4,72,256]{2,1,0:T(8,128)(2,1)}, u32[]{:S(2)}, u32[]{:S(2)}) async-start(bf16[4,72,256]{2,1,0:T(8,128)(2,1)} %broadcast_in_dim.17), calls=%async_computation.5 | async-start | bytes 294912 | tf_op jit(solution)/shard_map/all_to_all | solution.py:57
  130.6 3.7 %convolution_multiply_fusion.5 = f32[64,1024]{1,0:T(8,128)} fusion(bf16[1024,1024]{1,0:T(8,128)(2,1)} %exponential_convert_fusion, f32[]{:T(128)} %get-tuple-element.44, bf16[64,2048]{1,0:T(8,128)(2,1)} %copy-done.9), kind=kOutput, calls=%fused_computation.21 | convolution fusion | flops 134283264 | bytes 2490880 | tf_op jit(solution)/shard_map/dot_general | solution.py:49
  134.3 1.9 %collective-permute-start.4 = (f32[64,1024]{1,0:T(8,128)}, f32[64,1024]{1,0:T(8,128)}, u32[]{:S(2)}, u32[]{:S(2)}) collective-permute-start(f32[64,1024]{1,0:T(8,128)} %convolution_multiply_fusion.5), channel_id=1, source_target_pairs={{1,0},{2,1},{3,2},{4,3},{5,4},{6,5},{7,6},{8,7},{9,8},{10,9},{11,1... | collective-permute-start | bytes 786440 | tf_op jit(solution)/shard_map/ppermute | solution.py:86
  139.2 2.1 %convolution_multiply_fusion.1 = f32[64,2048]{1,0:T(8,128)S(1)} fusion(f32[64,256]{1,0:T(8,128)S(1)} %fusion.23, f32[2048,256]{1,0:T(8,128)S(1)} %fusion.3), kind=kOutput, calls=%fused_computation.9 | convolution fusion | flops 402784256 | bytes 2686976 | tf_op jit(solution)/shard_map/dot_general | solution.py:35
  141.3 2.8 %collective-permute-done.4 = f32[64,1024]{1,0:T(8,128)} collective-permute-done((f32[64,1024]{1,0:T(8,128)}, f32[64,1024]{1,0:T(8,128)}, u32[]{:S(2)}, u32[]{:S(2)}) %collective-permute-start.4) | collective-permute-done | bytes 262176 | tf_op jit(solution)/shard_map/ppermute | solution.py:86
  145.2 1.5 %fusion.36 = (f32[64,2048]{1,0:T(8,128)}, f32[64,2048]{1,0:T(8,128)}) fusion(f32[64,1024]{1,0:T(8,128)S(1)} %get-tuple-element.55, f32[64,1024]{1,0:T(8,128)S(1)} %get-tuple-element.54, f32[64,2048]{1,0:T(8,128)S(1)} %copy-done.4, f32[64]{0:T(128)S(1)} %get-tuple-element.47, f32[64]{0:T(128)S(1)} %get-tuple-element.49, f32[64]{0:T(128)S(1)} %get-tuple-element.48, ...), kind=kLoop, calls=%fused_computation.74 | loop fusion | flops 2228224 | bytes 2622720 | tf_op jit(solution)/shard_map/sub | solution.py:189
  (111 shorter events, 31.2 us)
Async XLA Ops:
  3.2 1.9 %copy-start.4 = (f32[64,2048]{1,0:T(8,128)S(1)}, f32[64,2048]{1,0:T(8,128)}, u32[]{:S(2)}) copy-start(f32[64,2048]{1,0:T(8,128)} %param.14) | copy-start | bytes 1572868
  7.2 33.8 %all-to-all-start = ((bf16[8,64,256]{2,1,0:T(8,128)(2,1)}), bf16[8,64,256]{2,1,0:T(8,128)(2,1)}, u32[]{:S(2)}, u32[]{:S(2)}) async-start(bf16[8,64,256]{2,1,0:T(8,128)(2,1)} %broadcast_in_dim.12), calls=%async_computation | async-start | bytes 524288 | tf_op jit(solution)/shard_map/all_to_all | solution.py:57
  15.7 10.0 %copy-start.7 = (bf16[2048,256]{1,0:T(8,128)(2,1)S(1)}, bf16[2048,256]{1,0:T(8,128)(2,1)}, u32[]{:S(2)}) copy-start(bf16[2048,256]{1,0:T(8,128)(2,1)} %param.13) | copy-start | bytes 3145732
  17.7 29.8 %collective-permute-start = (bf16[1024,256]{1,0:T(8,128)(2,1)}, bf16[1024,256]{1,0:T(8,128)(2,1)}, u32[]{:S(2)}, u32[]{:S(2)}) collective-permute-start(bf16[1024,256]{1,0:T(8,128)(2,1)} %slice.169), channel_id=1, source_target_pairs={{0,1},{1,2},{2,3},{3,4},{4,5},{5,6},{6,7},{7,8},{8,9},{9,10},{10,1... | collective-permute-start | bytes 1572872 | tf_op jit(solution)/shard_map/ppermute | solution.py:81
  22.3 50.3 %collective-permute-start.1 = (bf16[64,1024]{1,0:T(8,128)(2,1)}, bf16[64,1024]{1,0:T(8,128)(2,1)}, u32[]{:S(2)}, u32[]{:S(2)}) collective-permute-start(bf16[64,1024]{1,0:T(8,128)(2,1)} %slice.202), channel_id=1, source_target_pairs={{0,1},{1,2},{2,3},{3,4},{4,5},{5,6},{6,7},{7,8},{8,9},{9,10},{10,1... | collective-permute-start | bytes 393224 | tf_op jit(solution)/shard_map/ppermute | solution.py:81
  30.9 2.5 %copy-start.19 = (s32[2]{0:T(128)S(1)}, s32[2]{0:T(128)}, u32[]{:S(2)}) copy-start(s32[2]{0:T(128)} %param.19) | copy-start | bytes 28
  33.3 2.3 %copy-start.14 = (bf16[256,256]{1,0:T(8,128)(2,1)S(1)}, bf16[256,256]{1,0:T(8,128)(2,1)}, u32[]{:S(2)}) copy-start(bf16[256,256]{1,0:T(8,128)(2,1)} %param.16) | copy-start | bytes 393220
  33.3 2.5 %copy-start.13 = (bf16[256,256]{1,0:T(8,128)(2,1)S(1)}, bf16[256,256]{1,0:T(8,128)(2,1)}, u32[]{:S(2)}) copy-start(bf16[256,256]{1,0:T(8,128)(2,1)} %param.15) | copy-start | bytes 393220
  33.3 2.7 %copy-start.15 = (bf16[256,256]{1,0:T(8,128)(2,1)S(1)}, bf16[256,256]{1,0:T(8,128)(2,1)}, u32[]{:S(2)}) copy-start(bf16[256,256]{1,0:T(8,128)(2,1)} %param.17) | copy-start | bytes 393220
  33.3 2.9 %copy-start.18 = (s32[2,2]{1,0:T(2,128)S(1)}, s32[2,2]{1,0:T(2,128)}, u32[]{:S(2)}) copy-start(s32[2,2]{1,0:T(2,128)} %param.18) | copy-start | bytes 52
  33.3 3.5 %copy-start.1 = (bf16[1024,1024]{1,0:T(8,128)(2,1)S(1)}, bf16[1024,1024]{1,0:T(8,128)(2,1)}, u32[]{:S(2)}) copy-start(bf16[1024,1024]{1,0:T(8,128)(2,1)} %exponential_convert_fusion.2) | copy-start | bytes 6291460
  35.6 2.7 %copy-start.5 = (bf16[1024,1024]{1,0:T(8,128)(2,1)S(1)}, bf16[1024,1024]{1,0:T(8,128)(2,1)}, u32[]{:S(2)}) copy-start(bf16[1024,1024]{1,0:T(8,128)(2,1)} %exponential_convert_fusion.3) | copy-start | bytes 6291460
  38.3 1.6 %copy-start.16 = (bf16[256,256]{1,0:T(8,128)(2,1)S(1)}, bf16[256,256]{1,0:T(8,128)(2,1)}, u32[]{:S(2)}) copy-start(bf16[256,256]{1,0:T(8,128)(2,1)} %param.17) | copy-start | bytes 393220
  40.2 29.6 %copy-start.8 = (f32[256,256]{1,0:T(8,128)}, f32[256,256]{1,0:T(8,128)S(1)}, u32[]{:S(2)}) copy-start(f32[256,256]{1,0:T(8,128)S(1)} %fusion.21) | copy-start | bytes 786436
  43.0 12.1 %all-to-all-start.1 = ((bf16[8,64,256]{2,1,0:T(8,128)(2,1)}), bf16[8,64,256]{2,1,0:T(8,128)(2,1)}, u32[]{:S(2)}, u32[]{:S(2)}) async-start(bf16[8,64,256]{2,1,0:T(8,128)(2,1)} %broadcast_in_dim.13), calls=%async_computation.1 | async-start | bytes 524288 | tf_op jit(solution)/shard_map/all_to_all | solution.py:57
  57.0 11.6 %all-to-all-start.2 = ((bf16[4,64,256]{2,1,0:T(8,128)(2,1)}), bf16[4,64,256]{2,1,0:T(8,128)(2,1)}, u32[]{:S(2)}, u32[]{:S(2)}) async-start(bf16[4,64,256]{2,1,0:T(8,128)(2,1)} %broadcast_in_dim.14), calls=%async_computation.2 | async-start | bytes 262144 | tf_op jit(solution)/shard_map/all_to_all | solution.py:57
  65.5 9.4 %collective-permute-start.2 = (f32[64,1024]{1,0:T(8,128)}, f32[64,1024]{1,0:T(8,128)}, u32[]{:S(2)}, u32[]{:S(2)}) collective-permute-start(f32[64,1024]{1,0:T(8,128)} %fusion.13), channel_id=1, source_target_pairs={{1,0},{2,1},{3,2},{4,3},{5,4},{6,5},{7,6},{8,7},{9,8},{10,9},{11,1... | collective-permute-start | bytes 786440 | tf_op jit(solution)/shard_map/ppermute | solution.py:86
  68.6 4.0 %copy-start = (bf16[1024,1024]{1,0:T(8,128)(2,1)S(1)}, bf16[1024,1024]{1,0:T(8,128)(2,1)}, u32[]{:S(2)}) copy-start(bf16[1024,1024]{1,0:T(8,128)(2,1)} %exponential_convert_fusion) | copy-start | bytes 6291460
  68.6 4.0 %copy-start.11 = (f32[64,2048]{1,0:T(8,128)S(1)}, f32[64,2048]{1,0:T(8,128)}, u32[]{:S(2)}) copy-start(f32[64,2048]{1,0:T(8,128)} %maximum_multiply_fusion) | copy-start | bytes 1572868
  75.9 1.6 %copy-start.6 = (bf16[1024,1024]{1,0:T(8,128)(2,1)S(1)}, bf16[1024,1024]{1,0:T(8,128)(2,1)}, u32[]{:S(2)}) copy-start(bf16[1024,1024]{1,0:T(8,128)(2,1)} %exponential_convert_fusion.3) | copy-start | bytes 6291460
  77.1 1.8 %copy-start.3 = (bf16[1024,1024]{1,0:T(8,128)(2,1)S(1)}, bf16[1024,1024]{1,0:T(8,128)(2,1)}, u32[]{:S(2)}) copy-start(bf16[1024,1024]{1,0:T(8,128)(2,1)} %exponential_convert_fusion.1) | copy-start | bytes 6291460
  77.1 7.9 %copy-start.9 = (bf16[64,2048]{1,0:T(8,128)(2,1)}, bf16[64,2048]{1,0:T(8,128)(2,1)S(1)}, u32[]{:S(2)}) copy-start(bf16[64,2048]{1,0:T(8,128)(2,1)S(1)} %fusion.111) | copy-start | bytes 786436
  77.5 6.1 %copy-start.2 = (bf16[1024,1024]{1,0:T(8,128)(2,1)S(1)}, bf16[1024,1024]{1,0:T(8,128)(2,1)}, u32[]{:S(2)}) copy-start(bf16[1024,1024]{1,0:T(8,128)(2,1)} %exponential_convert_fusion.2) | copy-start | bytes 6291460
  79.4 10.8 %collective-permute-start.3 = (bf16[64,1024]{1,0:T(8,128)(2,1)S(1)}, bf16[64,1024]{1,0:T(8,128)(2,1)S(1)}, u32[]{:S(2)}, u32[]{:S(2)}) collective-permute-start(bf16[64,1024]{1,0:T(8,128)(2,1)S(1)} %slice.208), channel_id=1, source_target_pairs={{0,1},{1,2},{2,3},{3,4},{4,5},{5,6},{6,7},{7,8},{8,9},{9,10},{10,1... | collective-permute-start | bytes 393224 | tf_op jit(solution)/shard_map/ppermute | solution.py:81
  121.1 0.6 copy-start.17
  125.6 10.7 %all-to-all-start.5 = ((bf16[4,72,256]{2,1,0:T(8,128)(2,1)}), bf16[4,72,256]{2,1,0:T(8,128)(2,1)}, u32[]{:S(2)}, u32[]{:S(2)}) async-start(bf16[4,72,256]{2,1,0:T(8,128)(2,1)} %broadcast_in_dim.17), calls=%async_computation.5 | async-start | bytes 294912 | tf_op jit(solution)/shard_map/all_to_all | solution.py:57
  134.3 9.8 %collective-permute-start.4 = (f32[64,1024]{1,0:T(8,128)}, f32[64,1024]{1,0:T(8,128)}, u32[]{:S(2)}, u32[]{:S(2)}) collective-permute-start(f32[64,1024]{1,0:T(8,128)} %convolution_multiply_fusion.5), channel_id=1, source_target_pairs={{1,0},{2,1},{3,2},{4,3},{5,4},{6,5},{7,6},{8,7},{9,8},{10,9},{11,1... | collective-permute-start | bytes 786440 | tf_op jit(solution)/shard_map/ppermute | solution.py:86
  136.3 7.9 %copy-start.10 = (f32[64,2048]{1,0:T(8,128)S(1)}, f32[64,2048]{1,0:T(8,128)}, u32[]{:S(2)}) copy-start(f32[64,2048]{1,0:T(8,128)} %get-tuple-element.56) | copy-start | bytes 1572868
  136.3 7.9 %copy-start.12 = (f32[64,1024]{1,0:T(8,128)S(1)}, f32[64,1024]{1,0:T(8,128)}, u32[]{:S(2)}) copy-start(f32[64,1024]{1,0:T(8,128)} %get-tuple-element.67) | copy-start | bytes 786436

commit v2 on v0

v2 whole, which is shorter than its diff:
```python
import math

import jax
import jax.numpy as jnp
from jax import lax
from jax.experimental import pallas as pl
from jax.experimental.pallas import tpu as pltpu
from jax.sharding import PartitionSpec as P

LEAF = 1024
SKEL = 256
RHS = 64
DIM = 256
ROWS = 256
STEPS = LEAF // ROWS
WIDE = 512
ALL = ("group", "sub", "leaf")

ridge_term = 3.0
level_one = 0.5
level_two = 0.25
level_top = 0.3

bf16 = jnp.bfloat16
f32 = jnp.float32
per_unit = 0.25 / DIM * math.log2(math.e)
vmem_bytes = 40 * 1024 * 1024


def shape_of(shape, dtype):
    return jax.ShapeDtypeStruct(shape, dtype)


def cost(flops, moved, exps=0):
    return pl.CostEstimate(flops=flops, bytes_accessed=moved, transcendentals=exps)


params = pltpu.CompilerParams(vmem_limit_bytes=vmem_bytes)


def nn(left, right, precision=None):
    return lax.dot_general(
        left, right, (((1,), (0,)), ((), ())), precision=precision, preferred_element_type=f32
    )


def nt(left, right, precision=None):
    return lax.dot_general(
        left, right, (((1,), (1,)), ((), ())), precision=precision, preferred_element_type=f32
    )


highest = lax.Precision.HIGHEST


def squares(rows):
    wide = rows.astype(f32)
    return wide * wide


def left_column(rows):
    return jnp.sum(squares(rows), axis=1, keepdims=True) * per_unit


def right_row(rows):
    square = squares(rows)
    high = square.astype(bf16)
    low = (square - high.astype(f32)).astype(bf16)
    ones = jnp.ones((8, rows.shape[1]), bf16)
    return (nt(ones, high) + nt(ones, low))[0:1] * per_unit


def gauss(left, column, right, row):
    return jnp.exp2(nt(left, right) * (2.0 * per_unit) - column - row)


def split(value):
    high = value.astype(bf16)
    low = (value - high.astype(f32)).astype(bf16)
    return high, low


def up_dot(field, table_high, table_low):
    high, low = split(field)
    both = nn(jnp.concatenate([high, low], axis=0), table_high)
    return both[:RHS] + both[RHS:] + nn(high, table_low)


def down_dot(weights, table_high, table_low):
    high, low = split(weights)
    both = nt(jnp.concatenate([high, low], axis=0), table_high)
    return both[:RHS] + both[RHS:] + nt(high, table_low)


def start_kernel(
    x_ref, z1_ref, z2_ref, z3_ref, b_ref, sent_ref, gh_ref, gl_ref, t1_ref, t2_ref, halo_ref
):
    z1 = z1_ref[...]
    row = right_row(z1)
    total = jnp.zeros((RHS, SKEL), f32)
    for k in range(0, x_ref.shape[0], WIDE):
        part = x_ref[k : k + WIDE, :]
        table = gauss(part, left_column(part), z1, row)
        high, low = split(table)
        gh_ref[k : k + WIDE, :] = high
        gl_ref[k : k + WIDE, :] = low
        total += up_dot(b_ref[:, k : k + WIDE], high, low)
    value = (total * (1.0 / LEAF)).astype(bf16)
    for k in range(sent_ref.shape[0]):
        sent_ref[k] = value
    halo_ref[0:LEAF, :] = x_ref[LEAF:, :]
    for k in range(STEPS):
        first = LEAF + k * RHS
        halo_ref[first : first + RHS, :] = b_ref[
            :, LEAF + k * ROWS : LEAF + (k + 1) * ROWS
        ].astype(bf16)
    z2, z3 = z2_ref[...], z3_ref[...]
    t1_ref[...] = gauss(z1, left_column(z1), z2, right_row(z2))
    t2_ref[...] = gauss(z2, left_column(z2), z3, right_row(z3))


def start_call(points, z1, z2, z3, field, peers):
    count = points.shape[0]
    return pl.pallas_call(
        start_kernel,
        out_shape=(
            shape_of((peers, RHS, SKEL), bf16),
            shape_of((count, SKEL), bf16),
            shape_of((count, SKEL), bf16),
            shape_of((SKEL, SKEL), f32),
            shape_of((SKEL, SKEL), f32),
            shape_of((LEAF + STEPS * RHS, DIM), bf16),
        ),
        compiler_params=params,
        cost_estimate=cost(600_000_000, 5_000_000, 655_360),
        name="start",
    )(points, z1, z2, z3, field)


def listed(nb_ref, ct_ref, position, target):
    found = 0.0
    for k in range(nb_ref.shape[1]):
        hit = (k < ct_ref[position]) & (nb_ref[position, k] == target)
        found = found + jnp.where(hit, 1.0, 0.0)
    return found


def first_leaf_of():
    return lax.axis_index(ALL) * 2


def chunk(step):
    return pl.ds(pl.multiple_of(step * ROWS, ROWS), ROWS)


def near_own(step, b_a, b_b, b_a_part, b_b_part, t_a, t_b, t_ab, nb_ref, ct_ref, out_ref):
    first = first_leaf_of()
    inner = listed(nb_ref, ct_ref, 0, first + 1)
    inner_back = listed(nb_ref, ct_ref, 1, first)
    add_a = nn(b_a_part, t_a)
    add_b = nn(b_b_part, t_b) + inner_back * nn(b_a_part, t_ab)
    cross = inner * nt(b_b, t_ab)

    @pl.when(step == 0)
    def _():
        out_ref[:, :LEAF] = add_a
        out_ref[:, LEAF:] = add_b

    @pl.when(step > 0)
    def _():
        out_ref[:, :LEAF] += add_a
        out_ref[:, LEAF:] += add_b

    out_ref[:, chunk(step)] += cross


def tables_kernel(
    nb_ref, ct_ref, x_ref, b_ref, after_ref, tabs_ref, out_ref, row_ref
):
    del after_ref
    step = pl.program_id(0)

    @pl.when(step == 0)
    def _():
        row_ref[...] = right_row(x_ref[...])

    x_a, x_b = x_ref[:LEAF, :], x_ref[LEAF:, :]
    rows_a = x_ref[chunk(step), :]
    rows_b = x_ref[pl.ds(pl.multiple_of(LEAF + step * ROWS, ROWS), ROWS), :]
    row_a, row_b = row_ref[:, :LEAF], row_ref[:, LEAF:]
    col_a, col_b = left_column(rows_a), left_column(rows_b)
    t_a = gauss(rows_a, col_a, x_a, row_a).astype(bf16)
    t_b = gauss(rows_b, col_b, x_b, row_b).astype(bf16)
    t_ab = gauss(rows_a, col_a, x_b, row_b).astype(bf16)
    tabs_ref[0] = t_a
    tabs_ref[1] = t_b
    tabs_ref[2] = t_ab
    b_b = b_ref[:, LEAF:].astype(bf16)
    b_a_part = b_ref[:, chunk(step)].astype(bf16)
    b_b_part = b_ref[:, pl.ds(pl.multiple_of(LEAF + step * ROWS, ROWS), ROWS)].astype(bf16)
    near_own(step, None, b_b, b_a_part, b_b_part, t_a, t_b, t_ab, nb_ref, ct_ref, out_ref)


def smem():
    return pl.BlockSpec(memory_space=pltpu.SMEM)


def whole(*shape):
    return pl.BlockSpec(shape, lambda i: (0,) * len(shape))


def anywhere():
    return pl.BlockSpec(memory_space=pl.ANY)


def tables_call(neighbors, counts, points, field, after):
    return pl.pallas_call(
        tables_kernel,
        grid=(STEPS,),
        in_specs=[
            smem(),
            smem(),
            whole(2 * LEAF, DIM),
            whole(RHS, 2 * LEAF),
            anywhere(),
        ],
        out_specs=(
            pl.BlockSpec((3, ROWS, LEAF), lambda i: (0, i, 0)),
            whole(RHS, 2 * LEAF),
        ),
        out_shape=(
            shape_of((3, LEAF, LEAF), bf16),
            shape_of((RHS, 2 * LEAF), f32),
        ),
        scratch_shapes=[pltpu.VMEM((1, 2 * LEAF), f32)],
        compiler_params=params,
        cost_estimate=cost(2_200_000_000, 8_000_000, 3_145_728),
        name="tables",
    )(neighbors, counts, points, field, after)


def before_kernel(nb_ref, ct_ref, hx_ref, hb_ref, x_ref, b_ref, after_ref, tab_ref, out_ref, back_ref, row_ref):
    del after_ref
    step = pl.program_id(0)
    x_a = x_ref[...]

    @pl.when(step == 0)
    def _():
        row_ref[...] = right_row(x_a)

    rows = hx_ref[...]
    table = gauss(rows, left_column(rows), x_a, row_ref[...]).astype(bf16)
    tab_ref[...] = table
    weight = listed(nb_ref, ct_ref, 0, first_leaf_of() - 1)
    add = weight * nn(hb_ref[...], table)

    @pl.when(step == 0)
    def _():
        out_ref[...] = add

    @pl.when(step > 0)
    def _():
        out_ref[...] += add

    back_ref[...] = weight * nt(b_ref[...].astype(bf16), table)


def before_call(neighbors, counts, halo, points, field, after):
    return pl.pallas_call(
        before_kernel,
        grid=(STEPS,),
        in_specs=[
            smem(),
            smem(),
            pl.BlockSpec((ROWS, DIM), lambda i: (i, 0)),
            pl.BlockSpec((RHS, DIM), lambda i: (LEAF // RHS + i, 0)),
            whole(LEAF, DIM),
            whole(RHS, LEAF),
            anywhere(),
        ],
        out_specs=(
            pl.BlockSpec((ROWS, LEAF), lambda i: (i, 0)),
            whole(RHS, LEAF),
            pl.BlockSpec((RHS, ROWS), lambda i: (0, i)),
        ),
        out_shape=(
            shape_of((LEAF, LEAF), bf16),
            shape_of((RHS, LEAF), f32),
            shape_of((RHS, LEAF), f32),
        ),
        scratch_shapes=[pltpu.VMEM((1, LEAF), f32)],
        compiler_params=params,
        cost_estimate=cost(800_000_000, 4_000_000, 1_048_576),
        name="before",
    )(neighbors, counts, halo, halo, points, field, after)


def total_of(got_ref):
    total = got_ref[0].astype(f32)
    for k in range(1, got_ref.shape[0]):
        total += got_ref[k].astype(f32)
    return total


def climb_kernel(got_ref, table_ref, up_ref, sent_ref):
    total = total_of(got_ref)
    up_ref[...] = total
    value = (nn(total, table_ref[...], highest) * (1.0 / SKEL)).astype(bf16)
    for k in range(sent_ref.shape[0]):
        sent_ref[k] = value


def climb_call(got, table, peers):
    return pl.pallas_call(
        climb_kernel,
        out_shape=(shape_of((RHS, SKEL), f32), shape_of((peers, RHS, SKEL), bf16)),
        compiler_params=params,
        cost_estimate=cost(50_000_000, 900_000),
        name="climb",
    )(got, table)


def down_weights(up_one, up_two, up_top, low_table, high_table):
    down_top = level_top * up_top
    down_two = level_two * up_two + nt(down_top, high_table, highest) * (1.0 / SKEL)
    return level_one * up_one + nt(down_two, low_table, highest) * (1.0 / SKEL)


def second_kernel(
    got_ref, p1_ref, p2_ref, t1_ref, t2_ref, gh_ref, gl_ref, own_ref, cross_ref, after_ref,
    u_ref, edge_ref, d1_ref
):
    step = pl.program_id(0)

    @pl.when(step == 0)
    def _():
        d1_ref[...] = down_weights(
            p1_ref[...], p2_ref[...], total_of(got_ref), t1_ref[...], t2_ref[...]
        )

    far = down_dot(d1_ref[...], gh_ref[...], gl_ref[...])
    side = jnp.where(step < 2, cross_ref[...], after_ref[...])
    value = (own_ref[...] + side + far) * (1.0 / LEAF)
    u_ref[...] = value
    edge_ref[...] = value.astype(bf16)


def tail_block(i):
    return (0, jnp.maximum(i - 2, 0))


def head_block(i):
    return (0, jnp.minimum(i, 1))


def second_call(got, p1, p2, t1, t2, gh, gl, own, cross, after):
    small = whole(RHS, SKEL)
    square = whole(SKEL, SKEL)
    return pl.pallas_call(
        second_kernel,
        grid=(4,),
        in_specs=[
            whole(*got.shape),
            small,
            small,
            square,
            square,
            pl.BlockSpec((WIDE, SKEL), lambda i: (i, 0)),
            pl.BlockSpec((WIDE, SKEL), lambda i: (i, 0)),
            pl.BlockSpec((RHS, WIDE), lambda i: (0, i)),
            pl.BlockSpec((RHS, WIDE), head_block),
            pl.BlockSpec((RHS, WIDE), tail_block),
        ],
        out_specs=(
            pl.BlockSpec((RHS, WIDE), lambda i: (0, i)),
            pl.BlockSpec((RHS, WIDE), tail_block),
        ),
        out_shape=(shape_of((RHS, 2 * LEAF), f32), shape_of((RHS, LEAF), bf16)),
        scratch_shapes=[pltpu.VMEM((RHS, SKEL), f32)],
        compiler_params=params,
        cost_estimate=cost(250_000_000, 5_000_000),
        name="second",
    )(got, p1, p2, t1, t2, gh, gl, own, cross, after)


def row_sum(value):
    return jnp.sum(value, axis=1, keepdims=True)


def third_kernel(
    nb_ref, ct_ref, u_ref, b_ref, tabs_ref, gha_ref, gla_ref, ghb_ref, glb_ref,
    out_ref, up_ref, sums_ref
):
    step = pl.program_id(0)
    part_a = chunk(step)
    part_b = pl.ds(pl.multiple_of(LEAF + step * ROWS, ROWS), ROWS)
    u_a, u_b = u_ref[:, part_a], u_ref[:, part_b]
    up = up_dot(u_a, gha_ref[...], gla_ref[...]) + up_dot(u_b, ghb_ref[...], glb_ref[...])

    @pl.when(step == 0)
    def _():
        up_ref[...] = up

    @pl.when(step > 0)
    def _():
        up_ref[...] += up

    near_own(
        step, None, u_ref[:, LEAF:].astype(bf16), u_a.astype(bf16), u_b.astype(bf16),
        tabs_ref[0], tabs_ref[1], tabs_ref[2], nb_ref, ct_ref, out_ref,
    )

    @pl.when(step == STEPS - 1)
    def _():
        b, u = b_ref[...], u_ref[...]
        lane = lax.broadcasted_iota(jnp.int32, (RHS, 128), 1)
        sums = (row_sum(b * b), row_sum(b * u), row_sum(u * u), row_sum(u * out_ref[...]))
        total = jnp.zeros((RHS, 128), f32)
        for k in range(4):
            total = jnp.where(lane == k, sums[k], total)
        sums_ref[...] = total


def third_call(neighbors, counts, u, field, tabs, gh, gl):
    near_rows = pl.BlockSpec((ROWS, SKEL), lambda i: (i, 0))
    far_rows = pl.BlockSpec((ROWS, SKEL), lambda i: (STEPS + i, 0))
    return pl.pallas_call(
        third_kernel,
        grid=(STEPS,),
        in_specs=[
            smem(),
            smem(),
            whole(RHS, 2 * LEAF),
            whole(RHS, 2 * LEAF),
            pl.BlockSpec((3, ROWS, LEAF), lambda i: (0, i, 0)),
            near_rows,
            near_rows,
            far_rows,
            far_rows,
        ],
        out_specs=(whole(RHS, 2 * LEAF), whole(RHS, SKEL), whole(RHS, 128)),
        out_shape=(
            shape_of((RHS, 2 * LEAF), f32),
            shape_of((RHS, SKEL), f32),
            shape_of((RHS, 128), f32),
        ),
        compiler_params=params,
        cost_estimate=cost(700_000_000, 10_000_000),
        name="third",
    )(neighbors, counts, u, field, tabs, gh, gl, gh, gl)


def rows_of(sums):
    high = sums.astype(bf16).astype(f32)
    rest = sums - high
    middle = rest.astype(bf16).astype(f32)
    low = rest - middle
    lane = lax.broadcasted_iota(jnp.int32, (RHS, 128), 1)
    packed = jnp.where(lane < 4, high, 0.0)
    packed += jnp.where((lane >= 4) & (lane < 8), pltpu.roll(middle, 4, 1), 0.0)
    packed += jnp.where((lane >= 8) & (lane < 12), pltpu.roll(low, 8, 1), 0.0)
    turned = packed.T[:16]
    return jnp.concatenate([turned, jnp.zeros((16, SKEL - RHS), f32)], axis=1)


def sums_of(rows):
    turned = jnp.concatenate([rows[:, :RHS], jnp.zeros((112, RHS), f32)], axis=0).T
    total = turned + (pltpu.roll(turned, 124, 1) + pltpu.roll(turned, 120, 1))
    lane = lax.broadcasted_iota(jnp.int32, (RHS, 128), 1)
    return jnp.where(lane < 4, total, 0.0)


def put_all(sent_ref, value, sums):
    message = jnp.concatenate([value, rows_of(sums)], axis=0).astype(bf16)
    for k in range(sent_ref.shape[0]):
        sent_ref[k] = message


def add_last(sums, column):
    lane = lax.broadcasted_iota(jnp.int32, (RHS, 128), 1)
    return sums + jnp.where(lane == 3, column, 0.0)


def finish_kernel(
    nb_ref, ct_ref, edge_ref, tab_ref, u_ref, up_ref, sums_ref, sent_ref, out_ref, back_ref
):
    weight = listed(nb_ref, ct_ref, 0, first_leaf_of() - 1)
    u_a = u_ref[...]
    table = tab_ref[...]
    cross = weight * nn(edge_ref[...], table)
    out_ref[...] = cross
    back_ref[...] = weight * nt(u_a.astype(bf16), table)
    sums = add_last(sums_ref[...], 2.0 * row_sum(u_a * cross))
    lane = lax.broadcasted_iota(jnp.int32, (RHS, 128), 1)
    sums = jnp.where(lane == 3, sums * (1.0 / LEAF), sums)
    put_all(sent_ref, up_ref[...] * (1.0 / LEAF), sums)


def finish_call(neighbors, counts, edge, tab, u, up, sums, peers):
    return pl.pallas_call(
        finish_kernel,
        grid=(1,),
        in_specs=[
            smem(),
            smem(),
            whole(RHS, LEAF),
            whole(LEAF, LEAF),
            whole(RHS, LEAF),
            whole(RHS, SKEL),
            whole(RHS, 128),
        ],
        out_specs=(whole(peers, RHS + 16, SKEL), whole(RHS, LEAF), whole(RHS, LEAF)),
        out_shape=(
            shape_of((peers, RHS + 16, SKEL), bf16),
            shape_of((RHS, LEAF), f32),
            shape_of((RHS, LEAF), f32),
        ),
        compiler_params=params,
        cost_estimate=cost(270_000_000, 4_000_000),
        name="finish",
    )(neighbors, counts, edge, tab, u, up, sums)


def climb_sums_kernel(level, got_ref, table_ref, up_ref, sent_ref):
    total = total_of(got_ref)
    up = total[:RHS]
    up_ref[...] = up
    sums = add_last(sums_of(total[RHS:]), level * row_sum(up * up))
    put_all(sent_ref, nn(up, table_ref[...], highest) * (1.0 / SKEL), sums)


def climb_sums_call(got, table, level, peers):
    return pl.pallas_call(
        lambda *refs: climb_sums_kernel(level, *refs),
        out_shape=(shape_of((RHS, SKEL), f32), shape_of((peers, RHS + 16, SKEL), bf16)),
        compiler_params=params,
        cost_estimate=cost(50_000_000, 900_000),
        name="climb_sums",
    )(got, table)


def last_kernel(
    got_ref, p1_ref, p2_ref, t1_ref, t2_ref, gh_ref, gl_ref, own_ref, cross_ref, after_ref,
    b_ref, u_ref, x_ref, r_ref, d1_ref, coef_ref
):
    step = pl.program_id(0)

    @pl.when(step == 0)
    def _():
        total = total_of(got_ref)
        top = total[:RHS]
        d1_ref[...] = down_weights(p1_ref[...], p2_ref[...], top, t1_ref[...], t2_ref[...])
        sums = add_last(sums_of(total[RHS:]), level_top * row_sum(top * top))
        bb, bu, uu, uv = sums[:, 0:1], sums[:, 1:2], sums[:, 2:3], sums[:, 3:4]
        step_one = bb / (ridge_term * bb + bu)
        ratio = bu / bb
        norm_one = step_one * step_one * (uu - ratio * bu)
        beta = norm_one / bb
        bend_rr = step_one * step_one * (ratio * ratio * bu - 2.0 * ratio * uu + uv)
        bend_rb = step_one * (ratio * bu - uu)
        bending = (
            ridge_term * (norm_one + beta * beta * bb)
            + bend_rr
            + 2.0 * beta * bend_rb
            + beta * beta * bu
        )
        step_two = norm_one / bending
        lane = lax.broadcasted_iota(jnp.int32, (RHS, 128), 1)
        coefs = jnp.where(lane == 0, step_one, jnp.where(lane == 1, ratio, 0.0))
        coef_ref[...] = jnp.where(lane == 2, beta, jnp.where(lane == 3, step_two, coefs))

    coefs = coef_ref[...]
    step_one, ratio, beta, step_two = (coefs[:, k : k + 1] for k in range(4))
    far = down_dot(d1_ref[...], gh_ref[...], gl_ref[...])
    side = jnp.where(step < 2, cross_ref[...], after_ref[...])
    third = (own_ref[...] + side + far) * (1.0 / LEAF)
    first, second = b_ref[...], u_ref[...]
    residual_one = (step_one * ratio) * first - step_one * second
    direction = residual_one + beta * first
    applied = (
        ridge_term * direction + (step_one * ratio + beta) * second - step_one * third
    )
    x_ref[...] = step_one * first + step_two * direction
    r_ref[...] = residual_one - step_two * applied


def last_call(got, p1, p2, t1, t2, gh, gl, own, cross, after, field, u):
    small = whole(RHS, SKEL)
    square = whole(SKEL, SKEL)
    wide = pl.BlockSpec((RHS, WIDE), lambda i: (0, i))
    return pl.pallas_call(
        last_kernel,
        grid=(4,),
        in_specs=[
            whole(*got.shape),
            small,
            small,
            square,
            square,
            pl.BlockSpec((WIDE, SKEL), lambda i: (i, 0)),
            pl.BlockSpec((WIDE, SKEL), lambda i: (i, 0)),
            wide,
            pl.BlockSpec((RHS, WIDE), head_block),
            pl.BlockSpec((RHS, WIDE), tail_block),
            wide,
            wide,
        ],
        out_specs=(wide, wide),
        out_shape=(shape_of((RHS, 2 * LEAF), f32), shape_of((RHS, 2 * LEAF), f32)),
        scratch_shapes=[pltpu.VMEM((RHS, SKEL), f32), pltpu.VMEM((RHS, 128), f32)],
        compiler_params=params,
        cost_estimate=cost(250_000_000, 7_000_000),
        name="last",
    )(got, p1, p2, t1, t2, gh, gl, own, cross, after, field, u)


def exchange(sent, axis):
    return lax.all_to_all(sent, axis, 0, 0)


def shift_up(value):
    count = lax.axis_size(ALL)
    return lax.ppermute(value, ALL, [(i, i + 1) for i in range(count - 1)])


def shift_down(value):
    count = lax.axis_size(ALL)
    return lax.ppermute(value, ALL, [(i + 1, i) for i in range(count - 1)])


def shards(points, right_side, skel_sub, skel_group, skel_top, neighbors, counts):
    leaves, subs, groups = (lax.axis_size(axis) for axis in ("leaf", "sub", "group"))
    sent, gh, gl, t1, t2, halo = start_call(
        points, skel_sub, skel_group, skel_top, right_side, leaves
    )
    got = exchange(sent, "leaf")
    halo = shift_up(halo)
    tabs, own = tables_call(neighbors, counts, points, right_side, sent)
    up_one, sent = climb_call(got, t1, subs)
    got = exchange(sent, "sub")
    tab, cross, back = before_call(neighbors, counts, halo, points, right_side, sent)
    after = shift_down(back)
    up_two, sent = climb_call(got, t2, groups)
    got = exchange(sent, "group")
    second, edge = second_call(got, up_one, up_two, t1, t2, gh, gl, own, cross, after)

    edge = shift_up(edge)
    own, up, sums = third_call(neighbors, counts, second, right_side, tabs, gh, gl)
    sent, cross, back = finish_call(neighbors, counts, edge, tab, second, up, sums, leaves)
    got = exchange(sent, "leaf")
    after = shift_down(back)
    up_one, sent = climb_sums_call(got, t1, level_one, subs)
    got = exchange(sent, "sub")
    up_two, sent = climb_sums_call(got, t2, level_two, groups)
    got = exchange(sent, "group")
    return last_call(
        got, up_one, up_two, t1, t2, gh, gl, own, cross, after, right_side, second
    )


def solution(mesh):
    return jax.shard_map(
        shards,
        mesh=mesh,
        in_specs=(
            P(ALL, None),
            P(None, ALL),
            P(("group", "sub"), None),
            P("group", None),
            P(),
            P(ALL, None),
            P(ALL),
        ),
        out_specs=(P(None, ALL), P(None, ALL)),
        check_vma=False,
    )
```

time: 448 us -> 153 us (0.34)
  blocking collectives: 353 us -> 40.5 us
  matrix products: 37 us -> 0 us
  Pallas kernels: 0 us -> 33.9 us
  local copies, waits for them, and re-layouts: 5.94 us -> 30.9 us
  other arithmetic: 12.5 us -> 0 us
  waiting for transfers between devices: 0.02 us -> 11.3 us
  between operations: 6.19 us -> 0.84 us
    psum x9 -> x0, blocking collectives: 353 us -> none  [the longest x2 149 us: squares(): lax.psum(jnp.sum(residual * residual, axis=1), ('group', 'sub', 'leaf'))]
    all_to_all x0 -> x2, blocking collectives: none -> 40.5 us  [exchange(): return lax.all_to_all(sent, axis, 0, 0)]
    dot_general x33 -> x0, matrix products: 37 us -> none  [the longest x9 12 us: gauss_block(): lax.dot_general(left_rows, right_rows, (((1,), (1,)), ((), ())), preferre...]
    pallas_call x0 -> x11, Pallas kernels: none -> 33.9 us  [the longest x1 6.85 us: tables_call(): pl.pallas_call(tables_kernel, grid=(STEPS,), in_specs=[smem(), smem(), wh...]
    unnamed x42 -> x78, local copies, waits for them, and re-layouts: 3.4 us -> 30.9 us
    all_to_all x0 -> x4, starting transfers between devices: none -> 20.1 us  [exchange(): return lax.all_to_all(sent, axis, 0, 0)]
    ppermute x6 -> x4, starting transfers between devices: 31.1 us -> 13.7 us  [the longest x2 7.97 us: shift_down(): return lax.ppermute(value, ALL, [(i + 1, i) for i in range(count - 1)])]
    all_to_all x0 -> x4, waiting for transfers between devices: none -> 10.4 us  [exchange(): return lax.all_to_all(sent, axis, 0, 0)]
  transfers between devices with their start and end apart: 6 -> 8, of which waited for: 0 -> 3; matrix products, arithmetic and copies ran while one was open for 7% -> 0% of each run, Pallas kernels for 0% -> 14%
where the time goes in v2:
time: 153 us; the launch traced here: 151 us
  blocking collectives  40.5 us (26%)
  Pallas kernels  33.9 us (22%)
  starting transfers between devices  33.8 us (22%)
  local copies, waits for them, and re-layouts  30.9 us (20%)
  waiting for transfers between devices  11.3 us (7%)
    all_to_all x2, blocking collectives, exchange(): return lax.all_to_all(sent, axis, 0, 0)  40.5 us
    unnamed x78, local copies, waits for them, and re-layouts  30.9 us
    all_to_all x4, starting transfers between devices, exchange(): return lax.all_to_all(sent, axis, 0, 0)  20.1 us
    all_to_all x4, waiting for transfers between devices, exchange(): return lax.all_to_all(sent, axis, 0, 0)  10.4 us
    ppermute x2, starting transfers between devices, shift_down(): return lax.ppermute(value, ALL, [(i + 1, i) for i in range(count - 1)])  7.97 us
    pallas_call x1, Pallas kernels, tables_call(): pl.pallas_call(tables_kernel, grid=(STEPS,), in_specs=[smem(), smem(), wh...  6.85 us
    pallas_call x1, Pallas kernels, before_call(): pl.pallas_call(before_kernel, grid=(STEPS,), in_specs=[smem(), smem(), pl...  6.37 us
    ppermute x2, starting transfers between devices, shift_up(): return lax.ppermute(value, ALL, [(i, i + 1) for i in range(count - 1)])  5.73 us
  transfers between devices with their start and end apart: 8, of which 3 were waited for; matrix products, arithmetic and copies ran while one was open for 0% of the time, Pallas kernels for 14%

profile of v2, /device:TPU:2, one launch (start us, length us, event | category | flops | bytes accessed | tf_op | source)
XLA Modules:
  0.0 151.2 jit_solution(2233065199477994531)
XLA Ops:
  0.6 1.0 copy-done.2
  1.7 1.2 copy-done.11
  5.6 2.3 %start.1 = (bf16[8,64,256]{2,1,0:T(8,128)(2,1)S(1)}, bf16[2048,256]{1,0:T(8,128)(2,1)S(1)}, bf16[2048,256]{1,0:T(8,128)(2,1)S(1)}, f32[256,256]{1,0:T(8,128)S(1)...) custom-call(bf16[2048,256]{1,0:T(8,128)(2,1)S(1)} %copy-done.11, bf16[256,256]{1,0:T(8,128)(2,1)S(1)} %copy-done.36, ...), custom_call_target="tpu_custom_call" | custom-call | flops 600000000 | bytes 5000000 | tf_op jit(solution)/shard_map/start/pallas_call | solution.py:124
  7.9 3.8 %collective-permute-start = (bf16[1280,256]{1,0:T(8,128)(2,1)}, bf16[1280,256]{1,0:T(8,128)(2,1)}, u32[]{:S(2)}, u32[]{:S(2)}) collective-permute-start(bf16[1280,256]{1,0:T(8,128)(2,1)} %get-tuple-element.39), channel_id=1, source_target_pairs={{0,1},{1,2},{2,3},{3,4},{4,5},{5,6},{6,7},{7,8},{8,9},{9,10},{10,1... | collective-permute-start | bytes 1966088 | tf_op jit(solution)/shard_map/ppermute | solution.py:623
  11.7 25.0 %all_to_all.30.got_ref = bf16[8,64,256]{2,1,0:T(8,128)(2,1)S(1)} all-to-all(bf16[8,64,256]{2,1,0:T(8,128)(2,1)S(1)} %get-tuple-element.29.after_ref), channel_id=1, replica_groups=mesh['group'=4,'sub'=8,'leaf'=8] {'leaf'}, dimensions={0} | all-to-all | bytes 524288 | tf_op jit(solution)/shard_map/all_to_all | solution.py:618
  36.7 1.0 climb.2
  38.3 4.5 %all-to-all-start.1 = ((bf16[8,64,256]{2,1,0:T(8,128)(2,1)}), bf16[8,64,256]{2,1,0:T(8,128)(2,1)S(1)}, u32[]{:S(2)}, u32[]{:S(2)}) async-start(bf16[8,64,256]{2,1,0:T(8,128)(2,1)} %get-tuple-element.31.after_ref), calls=%async_computation.1 | async-start | bytes 524288 | tf_op jit(solution)/shard_map/all_to_all | solution.py:618
  42.8 1.0 copy-done.3
  43.8 1.2 copy-done.12
  46.4 6.4 %before.1 = (bf16[1024,1024]{1,0:T(8,128)(2,1)S(1)}, f32[64,1024]{1,0:T(8,128)S(1)}, f32[64,1024]{1,0:T(8,128)}) custom-call(s32[2,2]{1,0:T(2,128)S(1)} %copy-done.31, s32[2]{0:T(128)S(1)} %copy-done.33, bf16[1280,256]{1,0:T(8,128)(2,1)} %collective-permute-done.hx_ref.hb_ref, bf16[1280,256]{1,0:T(8,128)(2,1)} %collective-permute-done.hx_ref.hb_ref, ...), custom_call_target="tpu_custom_call" | custom-call | flops 800000000 | bytes 4000000 | tf_op jit(solution)/shard_map/before/pallas_call | solution.py:269
  52.8 1.4 copy-done.9
  54.8 5.2 %collective-permute-start.1 = (f32[64,1024]{1,0:T(8,128)}, f32[64,1024]{1,0:T(8,128)}, u32[]{:S(2)}, u32[]{:S(2)}) collective-permute-start(f32[64,1024]{1,0:T(8,128)} %get-tuple-element.41), channel_id=1, source_target_pairs={{1,0},{2,1},{3,2},{4,3},{5,4},{6,5},{7,6},{8,7},{9,8},{10,9},{11,1... | collective-permute-start | bytes 786440 | tf_op jit(solution)/shard_map/ppermute | solution.py:628
  61.6 4.9 %all-to-all-start.2 = ((bf16[4,64,256]{2,1,0:T(8,128)(2,1)}), bf16[4,64,256]{2,1,0:T(8,128)(2,1)S(1)}, u32[]{:S(2)}, u32[]{:S(2)}) async-start(bf16[4,64,256]{2,1,0:T(8,128)(2,1)} %copy-done.26), calls=%async_computation.2 | async-start | bytes 262144 | tf_op jit(solution)/shard_map/all_to_all | solution.py:618
  66.5 1.2 copy-done.13
  68.7 6.8 %tables.1 = (bf16[3,1024,1024]{2,1,0:T(8,128)(2,1)S(1)}, f32[64,2048]{1,0:T(8,128)S(1)}) custom-call(s32[2,2]{1,0:T(2,128)S(1)} %copy-done.32, s32[2]{0:T(128)S(1)} %copy-done.34, bf16[2048,256]{1,0:T(8,128)(2,1)S(1)} %copy-done.13, f32[64,2048]{1,0:T(8,128)S(1)} %copy-done.4, bf16[8,64,256]{2,1,0:T(8,128)(2,1)S(1)} %copy-done.22), custom_call_target="tpu_custom_call" | custom-call | flops 2200000000 | bytes 8000000 | tf_op jit(solution)/shard_map/tables/pallas_call | solution.py:217
  75.5 2.7 %copy-done = bf16[3,1024,1024]{2,1,0:T(8,128)(2,1)} copy-done((bf16[3,1024,1024]{2,1,0:T(8,128)(2,1)}, bf16[3,1024,1024]{2,1,0:T(8,128)(2,1)S(1)}, u32[]{:S(2)}) %copy-start) | copy-done | bytes 6291480
  80.0 1.0 copy-done.17
  83.6 4.0 %second.1 = (f32[64,2048]{1,0:T(8,128)S(1)}, bf16[64,1024]{1,0:T(8,128)(2,1)S(1)}) custom-call(bf16[4,64,256]{2,1,0:T(8,128)(2,1)S(1)} %all-to-all-done.2.got_ref, f32[64,256]{1,0:T(8,128)S(1)} %copy-done.28, f32[64,256]{1,0:T(8,128)S(1)} %copy-done.30, f32[256,256]{1,0:T(8,128)S(1)} %get-tuple-element.30.table_ref.t1_ref.refs_1_, f32[256,256]{1,0:T(8,128)S(1)} %copy-done.6, ...), custom_call_target="tpu_custom_call" | custom-call | flops 250000000 | bytes 5000000 | tf_op jit(solution)/shard_map/second/pallas_call | solution.py:359
  87.7 1.9 %collective-permute-start.2 = (bf16[64,1024]{1,0:T(8,128)(2,1)S(1)}, bf16[64,1024]{1,0:T(8,128)(2,1)S(1)}, u32[]{:S(2)}, u32[]{:S(2)}) collective-permute-start(bf16[64,1024]{1,0:T(8,128)(2,1)S(1)} %get-tuple-element.42), channel_id=1, source_target_pairs={{0,1},{1,2},{2,3},{3,4},{4,5},{5,6},{6,7},{7,8},{8,9},{9,10},{10,1... | collective-permute-start | bytes 393224 | tf_op jit(solution)/shard_map/ppermute | solution.py:623
  89.6 2.8 %copy-done.1 = bf16[3,1024,1024]{2,1,0:T(8,128)(2,1)S(1)} copy-done((bf16[3,1024,1024]{2,1,0:T(8,128)(2,1)S(1)}, bf16[3,1024,1024]{2,1,0:T(8,128)(2,1)}, u32[]{:S(2)}) %copy-start.1) | copy-done | bytes 6291480
  92.4 4.9 %third.1 = (f32[64,2048]{1,0:T(8,128)S(1)}, f32[64,256]{1,0:T(8,128)S(1)}, f32[64,128]{1,0:T(8,128)S(1)}) custom-call(s32[2,2]{1,0:T(2,128)S(1)} %copy-done.32, s32[2]{0:T(128)S(1)} %copy-done.34, f32[64,2048]{1,0:T(8,128)S(1)} %get-tuple-element.44.u_ref, f32[64,2048]{1,0:T(8,128)S(1)} %copy-done.4, bf16[3,1024,1024]{2,1,0:T(8,128)(2,1)S(1)} %copy-done.1, ...), custom_call_target="tpu_custom_call" | custom-call | flops 700000000 | bytes 10000000 | tf_op jit(solution)/shard_map/third/pallas_call | solution.py:427
  98.2 1.7 %finish.1 = (bf16[8,80,256]{2,1,0:T(8,128)(2,1)S(1)}, f32[64,1024]{1,0:T(8,128)S(1)}, f32[64,1024]{1,0:T(8,128)S(1)}) custom-call(s32[2,2]{1,0:T(2,128)S(1)} %copy-done.32, s32[2]{0:T(128)S(1)} %copy-done.34, bf16[64,1024]{1,0:T(8,128)(2,1)S(1)} %collective-permute-done.2.edge_ref, bf16[1024,1024]{1,0:T(8,128)(2,1)S(1)} %copy-done.10, ...), custom_call_target="tpu_custom_call" | custom-call | flops 270000000 | bytes 4000000 | tf_op jit(solution)/shard_map/finish/pallas_call | solution.py:500
  99.9 15.5 %all_to_all.31.refs_0_ = bf16[8,80,256]{2,1,0:T(8,128)(2,1)S(1)} all-to-all(bf16[8,80,256]{2,1,0:T(8,128)(2,1)S(1)} %get-tuple-element.48), channel_id=1, replica_groups=mesh['group'=4,'sub'=8,'leaf'=8] {'leaf'}, dimensions={0} | all-to-all | bytes 655360 | tf_op jit(solution)/shard_map/all_to_all | solution.py:618
  116.5 6.3 %all-to-all-start.4 = ((bf16[8,80,256]{2,1,0:T(8,128)(2,1)}), bf16[8,80,256]{2,1,0:T(8,128)(2,1)}, u32[]{:S(2)}, u32[]{:S(2)}) async-start(bf16[8,80,256]{2,1,0:T(8,128)(2,1)} %copy-done.18), calls=%async_computation.4 | async-start | bytes 655360 | tf_op jit(solution)/shard_map/all_to_all | solution.py:618
  122.8 2.8 %collective-permute-start.3 = (f32[64,1024]{1,0:T(8,128)}, f32[64,1024]{1,0:T(8,128)}, u32[]{:S(2)}, u32[]{:S(2)}) collective-permute-start(f32[64,1024]{1,0:T(8,128)} %copy-done.35), channel_id=1, source_target_pairs={{1,0},{2,1},{3,2},{4,3},{5,4},{6,5},{7,6},{8,7},{9,8},{10,9},{11,1... | collective-permute-start | bytes 786440 | tf_op jit(solution)/shard_map/ppermute | solution.py:628
  125.6 5.6 %all-to-all-done.4.refs_0_ = bf16[8,80,256]{2,1,0:T(8,128)(2,1)} async-done(((bf16[8,80,256]{2,1,0:T(8,128)(2,1)}), bf16[8,80,256]{2,1,0:T(8,128)(2,1)}, u32[]{:S(2)}, u32[]{:S(2)}) %all-to-all-start.4) | async-done | bytes 327712 | tf_op jit(solution)/shard_map/all_to_all | solution.py:618
  131.2 0.9 copy-done.7
  132.1 1.3 climb_sums.3
  134.1 4.5 %all-to-all-start.5 = ((bf16[4,80,256]{2,1,0:T(8,128)(2,1)}), bf16[4,80,256]{2,1,0:T(8,128)(2,1)}, u32[]{:S(2)}, u32[]{:S(2)}) async-start(bf16[4,80,256]{2,1,0:T(8,128)(2,1)} %copy-done.25), calls=%async_computation.5 | async-start | bytes 327680 | tf_op jit(solution)/shard_map/all_to_all | solution.py:618
  138.6 4.8 %all-to-all-done.5.got_ref = bf16[4,80,256]{2,1,0:T(8,128)(2,1)} async-done(((bf16[4,80,256]{2,1,0:T(8,128)(2,1)}), bf16[4,80,256]{2,1,0:T(8,128)(2,1)}, u32[]{:S(2)}, u32[]{:S(2)}) %all-to-all-start.5) | async-done | bytes 163872 | tf_op jit(solution)/shard_map/all_to_all | solution.py:618
  144.4 1.0 copy-done.15
  146.4 4.9 %last.1 = (f32[64,2048]{1,0:T(8,128)}, f32[64,2048]{1,0:T(8,128)}) custom-call(bf16[4,80,256]{2,1,0:T(8,128)(2,1)} %all-to-all-done.5.got_ref, f32[64,256]{1,0:T(8,128)S(1)} %get-tuple-element.51.p1_ref, f32[64,256]{1,0:T(8,128)S(1)} %get-tuple-element.52.p2_ref, f32[256,256]{1,0:T(8,128)S(1)} %get-tuple-element.30.table_ref.t1_ref.refs_1_, ...), custom_call_target="tpu_custom_call" | custom-call | flops 250000000 | bytes 7000000 | tf_op jit(solution)/shard_map/last/pallas_call | solution.py:591
  (75 shorter events, 16.9 us)
Async XLA Ops:
  0.6 1.0 copy-start.2
  1.7 1.2 copy-start.11
  5.6 60.9 %copy-start.4 = (f32[64,2048]{1,0:T(8,128)S(1)}, f32[64,2048]{1,0:T(8,128)}, u32[]{:S(2)}) copy-start(f32[64,2048]{1,0:T(8,128)} %b_ref.9) | copy-start | bytes 1572868
  5.6 60.9 %copy-start.32 = (s32[2,2]{1,0:T(2,128)S(1)}, s32[2,2]{1,0:T(2,128)}, u32[]{:S(2)}) copy-start(s32[2,2]{1,0:T(2,128)} %nb_ref.7) | copy-start | bytes 52
  5.6 60.9 %copy-start.34 = (s32[2]{0:T(128)S(1)}, s32[2]{0:T(128)}, u32[]{:S(2)}) copy-start(s32[2]{0:T(128)} %ct_ref.7) | copy-start | bytes 28
  7.9 29.8 %copy-start.21 = (bf16[8,64,256]{2,1,0:T(8,128)(2,1)}, bf16[8,64,256]{2,1,0:T(8,128)(2,1)S(1)}, u32[]{:S(2)}) copy-start(bf16[8,64,256]{2,1,0:T(8,128)(2,1)S(1)} %get-tuple-element.29.after_ref) | copy-start | bytes 786436
  7.9 67.6 %copy-start.5 = (f32[256,256]{1,0:T(8,128)}, f32[256,256]{1,0:T(8,128)S(1)}, u32[]{:S(2)}) copy-start(f32[256,256]{1,0:T(8,128)S(1)} %get-tuple-element.32.table_ref.t2_ref.refs_1_) | copy-start | bytes 786436
  7.9 34.9 %collective-permute-start = (bf16[1280,256]{1,0:T(8,128)(2,1)}, bf16[1280,256]{1,0:T(8,128)(2,1)}, u32[]{:S(2)}, u32[]{:S(2)}) collective-permute-start(bf16[1280,256]{1,0:T(8,128)(2,1)} %get-tuple-element.39), channel_id=1, source_target_pairs={{0,1},{1,2},{2,3},{3,4},{4,5},{5,6},{6,7},{7,8},{8,9},{9,10},{10,1... | collective-permute-start | bytes 1966088 | tf_op jit(solution)/shard_map/ppermute | solution.py:623
  38.3 21.7 %all-to-all-start.1 = ((bf16[8,64,256]{2,1,0:T(8,128)(2,1)}), bf16[8,64,256]{2,1,0:T(8,128)(2,1)S(1)}, u32[]{:S(2)}, u32[]{:S(2)}) async-start(bf16[8,64,256]{2,1,0:T(8,128)(2,1)} %get-tuple-element.31.after_ref), calls=%async_computation.1 | async-start | bytes 524288 | tf_op jit(solution)/shard_map/all_to_all | solution.py:618
  42.8 1.0 copy-start.3
  43.8 1.2 copy-start.12
  52.8 1.4 copy-start.9
  54.8 24.2 %collective-permute-start.1 = (f32[64,1024]{1,0:T(8,128)}, f32[64,1024]{1,0:T(8,128)}, u32[]{:S(2)}, u32[]{:S(2)}) collective-permute-start(f32[64,1024]{1,0:T(8,128)} %get-tuple-element.41), channel_id=1, source_target_pairs={{1,0},{2,1},{3,2},{4,3},{5,4},{6,5},{7,6},{8,7},{9,8},{10,9},{11,1... | collective-permute-start | bytes 786440 | tf_op jit(solution)/shard_map/ppermute | solution.py:628
  61.6 17.4 %all-to-all-start.2 = ((bf16[4,64,256]{2,1,0:T(8,128)(2,1)}), bf16[4,64,256]{2,1,0:T(8,128)(2,1)S(1)}, u32[]{:S(2)}, u32[]{:S(2)}) async-start(bf16[4,64,256]{2,1,0:T(8,128)(2,1)} %copy-done.26), calls=%async_computation.2 | async-start | bytes 262144 | tf_op jit(solution)/shard_map/all_to_all | solution.py:618
  66.5 1.2 copy-start.13
  67.7 0.9 copy-start.22
  75.5 2.7 %copy-start = (bf16[3,1024,1024]{2,1,0:T(8,128)(2,1)}, bf16[3,1024,1024]{2,1,0:T(8,128)(2,1)S(1)}, u32[]{:S(2)}) copy-start(bf16[3,1024,1024]{2,1,0:T(8,128)(2,1)S(1)} %get-tuple-element.45.tabs_ref) | copy-start | bytes 18874372
  79.0 1.0 copy-start.6
  80.0 1.0 copy-start.17
  81.0 0.9 copy-start.24
  83.6 14.6 %copy-start.10 = (bf16[1024,1024]{1,0:T(8,128)(2,1)S(1)}, bf16[1024,1024]{1,0:T(8,128)(2,1)}, u32[]{:S(2)}) copy-start(bf16[1024,1024]{1,0:T(8,128)(2,1)} %copy-done.9) | copy-start | bytes 6291460
  87.7 10.5 %collective-permute-start.2 = (bf16[64,1024]{1,0:T(8,128)(2,1)S(1)}, bf16[64,1024]{1,0:T(8,128)(2,1)S(1)}, u32[]{:S(2)}, u32[]{:S(2)}) collective-permute-start(bf16[64,1024]{1,0:T(8,128)(2,1)S(1)} %get-tuple-element.42), channel_id=1, source_target_pairs={{0,1},{1,2},{2,3},{3,4},{4,5},{5,6},{6,7},{7,8},{8,9},{9,10},{10,1... | collective-permute-start | bytes 393224 | tf_op jit(solution)/shard_map/ppermute | solution.py:623
  89.6 2.8 %copy-start.1 = (bf16[3,1024,1024]{2,1,0:T(8,128)(2,1)S(1)}, bf16[3,1024,1024]{2,1,0:T(8,128)(2,1)}, u32[]{:S(2)}) copy-start(bf16[3,1024,1024]{2,1,0:T(8,128)(2,1)} %copy-done) | copy-start | bytes 18874372
  97.3 18.5 %copy-start.14 = (f32[64,2048]{1,0:T(8,128)}, f32[64,2048]{1,0:T(8,128)S(1)}, u32[]{:S(2)}) copy-start(f32[64,2048]{1,0:T(8,128)S(1)} %get-tuple-element.53.own_ref) | copy-start | bytes 1572868
  99.9 15.9 %copy-start.19 = (f32[64,1024]{1,0:T(8,128)}, f32[64,1024]{1,0:T(8,128)S(1)}, u32[]{:S(2)}) copy-start(f32[64,1024]{1,0:T(8,128)S(1)} %get-tuple-element.54.cross_ref) | copy-start | bytes 786436
  99.9 15.9 %copy-start.35 = (f32[64,1024]{1,0:T(8,128)}, f32[64,1024]{1,0:T(8,128)S(1)}, u32[]{:S(2)}) copy-start(f32[64,1024]{1,0:T(8,128)S(1)} %get-tuple-element.55) | copy-start | bytes 786436
  116.5 14.6 %all-to-all-start.4 = ((bf16[8,80,256]{2,1,0:T(8,128)(2,1)}), bf16[8,80,256]{2,1,0:T(8,128)(2,1)}, u32[]{:S(2)}, u32[]{:S(2)}) async-start(bf16[8,80,256]{2,1,0:T(8,128)(2,1)} %copy-done.18), calls=%async_computation.4 | async-start | bytes 655360 | tf_op jit(solution)/shard_map/all_to_all | solution.py:618
  122.8 15.8 %collective-permute-start.3 = (f32[64,1024]{1,0:T(8,128)}, f32[64,1024]{1,0:T(8,128)}, u32[]{:S(2)}, u32[]{:S(2)}) collective-permute-start(f32[64,1024]{1,0:T(8,128)} %copy-done.35), channel_id=1, source_target_pairs={{1,0},{2,1},{3,2},{4,3},{5,4},{6,5},{7,6},{8,7},{9,8},{10,9},{11,1... | collective-permute-start | bytes 786440 | tf_op jit(solution)/shard_map/ppermute | solution.py:628
  131.1 1.0 copy-start.7
  134.1 9.3 %all-to-all-start.5 = ((bf16[4,80,256]{2,1,0:T(8,128)(2,1)}), bf16[4,80,256]{2,1,0:T(8,128)(2,1)}, u32[]{:S(2)}, u32[]{:S(2)}) async-start(bf16[4,80,256]{2,1,0:T(8,128)(2,1)} %copy-done.25), calls=%async_computation.5 | async-start | bytes 327680 | tf_op jit(solution)/shard_map/all_to_all | solution.py:618
  143.4 1.0 copy-start.8
  144.4 1.0 copy-start.15
  (15 other events, 11.5 us)

commit v3 on v0

v3 whole, which is shorter than its diff:
```python
import math

import jax
import jax.numpy as jnp
from jax import lax
from jax.experimental import pallas as pl
from jax.experimental.pallas import tpu as pltpu
from jax.sharding import PartitionSpec as P

LEAF = 1024
SKEL = 256
RHS = 64
DIM = 256
ROWS = 256
STEPS = LEAF // ROWS
WIDE = 512
ALL = ("group", "sub", "leaf")

ridge_term = 3.0
level_one = 0.5
level_two = 0.25
level_top = 0.3

bf16 = jnp.bfloat16
f32 = jnp.float32
per_unit = 0.25 / DIM * math.log2(math.e)
vmem_bytes = 20 * 1024 * 1024


def shape_of(shape, dtype):
    return jax.ShapeDtypeStruct(shape, dtype)


def cost(flops, moved, exps=0):
    return pl.CostEstimate(flops=flops, bytes_accessed=moved, transcendentals=exps)


params = pltpu.CompilerParams(vmem_limit_bytes=vmem_bytes)


def nn(left, right, precision=None):
    return lax.dot_general(
        left, right, (((1,), (0,)), ((), ())), precision=precision, preferred_element_type=f32
    )


def nt(left, right, precision=None):
    return lax.dot_general(
        left, right, (((1,), (1,)), ((), ())), precision=precision, preferred_element_type=f32
    )


highest = lax.Precision.HIGHEST


def squares(rows):
    wide = rows.astype(f32)
    return wide * wide


def left_column(rows):
    return jnp.sum(squares(rows), axis=1, keepdims=True) * per_unit


def right_row(rows):
    square = squares(rows)
    high = square.astype(bf16)
    low = (square - high.astype(f32)).astype(bf16)
    ones = jnp.ones((8, rows.shape[1]), bf16)
    return (nt(ones, high) + nt(ones, low))[0:1] * per_unit


def gauss(left, column, right, row):
    return jnp.exp2(nt(left, right) * (2.0 * per_unit) - column - row)


def split(value):
    high = value.astype(bf16)
    low = (value - high.astype(f32)).astype(bf16)
    return high, low


def up_dot(field, table_high, table_low):
    high, low = split(field)
    both = nn(jnp.concatenate([high, low], axis=0), table_high)
    return both[:RHS] + both[RHS:] + nn(high, table_low)


def down_dot(weights, table_high, table_low):
    high, low = split(weights)
    both = nt(jnp.concatenate([high, low], axis=0), table_high)
    return both[:RHS] + both[RHS:] + nt(high, table_low)


def start_kernel(
    nb_ref, ct_ref, x_ref, z1_ref, z2_ref, z3_ref, b_ref,
    sent_ref, gh_ref, gl_ref, t1_ref, t2_ref, xv_ref, bv_ref, w_ref,
    z_ref, x_sem, b_sem, z_sem
):
    parts = x_ref.shape[0] // WIDE
    loads = []
    for k, source in enumerate((z1_ref, z2_ref, z3_ref)):
        loads.append(pltpu.make_async_copy(source, z_ref.at[k], z_sem.at[k]))
    x_loads, b_loads = [], []
    for k in range(parts):
        rows = pl.ds(k * WIDE, WIDE)
        x_loads.append(pltpu.make_async_copy(x_ref.at[rows, :], xv_ref.at[rows, :], x_sem.at[k]))
        b_loads.append(pltpu.make_async_copy(b_ref.at[:, rows], bv_ref.at[:, rows], b_sem.at[k]))
    loads[0].start()
    for k in range(parts):
        x_loads[k].start()
        b_loads[k].start()
    loads[1].start()
    loads[2].start()

    first = first_leaf_of()
    weights = (
        listed(nb_ref, ct_ref, 0, first - 1),
        listed(nb_ref, ct_ref, 0, first + 1),
        listed(nb_ref, ct_ref, 1, first),
        listed(nb_ref, ct_ref, 1, first + 2),
    )
    place = lax.broadcasted_iota(jnp.int32, (8, 128), 0)
    spread = jnp.zeros((8, 128), f32)
    for k in range(4):
        spread = jnp.where(place == k, weights[k], spread)
    w_ref[...] = spread

    loads[0].wait()
    z1 = z_ref[0]
    row = right_row(z1)
    total = jnp.zeros((RHS, SKEL), f32)
    for k in range(parts):
        rows = slice(k * WIDE, (k + 1) * WIDE)
        x_loads[k].wait()
        part = xv_ref[rows, :]
        high, low = split(gauss(part, left_column(part), z1, row))
        gh_ref[rows, :] = high
        gl_ref[rows, :] = low
        b_loads[k].wait()
        total += up_dot(bv_ref[:, rows], high, low)
    value = (total * (1.0 / LEAF)).astype(bf16)
    for k in range(sent_ref.shape[0]):
        sent_ref[k] = value
    loads[1].wait()
    loads[2].wait()
    z2, z3 = z_ref[1], z_ref[2]
    t1_ref[...] = gauss(z1, left_column(z1), z2, right_row(z2))
    t2_ref[...] = gauss(z2, left_column(z2), z3, right_row(z3))


def start_call(neighbors, counts, points, z1, z2, z3, field, peers):
    count = points.shape[0]
    parts = count // WIDE
    far_off = pl.BlockSpec(memory_space=pltpu.HBM)
    return pl.pallas_call(
        start_kernel,
        in_specs=[smem(), smem()] + [far_off] * 5,
        out_shape=(
            shape_of((peers, RHS, SKEL), bf16),
            shape_of((count, SKEL), bf16),
            shape_of((count, SKEL), bf16),
            shape_of((SKEL, SKEL), f32),
            shape_of((SKEL, SKEL), f32),
            shape_of((count, DIM), bf16),
            shape_of((RHS, count), f32),
            shape_of((8, 128), f32),
        ),
        scratch_shapes=[
            pltpu.VMEM((3, SKEL, DIM), bf16),
            pltpu.SemaphoreType.DMA((parts,)),
            pltpu.SemaphoreType.DMA((parts,)),
            pltpu.SemaphoreType.DMA((3,)),
        ],
        compiler_params=params,
        cost_estimate=cost(600_000_000, 5_000_000, 655_360),
        name="start",
    )(neighbors, counts, points, z1, z2, z3, field)


def smem():
    return pl.BlockSpec(memory_space=pltpu.SMEM)


def anywhere():
    return pl.BlockSpec(memory_space=pl.ANY)


def inside(count):
    return [pl.BlockSpec(memory_space=pltpu.VMEM)] * count


def listed(nb_ref, ct_ref, position, target):
    found = 0.0
    for k in range(nb_ref.shape[1]):
        hit = (k < ct_ref[position]) & (nb_ref[position, k] == target)
        found = found + jnp.where(hit, 1.0, 0.0)
    return found


def first_leaf_of():
    return lax.axis_index(ALL) * 2


def weight_of(w_ref, k):
    return w_ref[k : k + 1, 0:1]


def block(k):
    return slice(k * ROWS, (k + 1) * ROWS)


def make_symmetric(points, row, table_ref):
    for i in range(STEPS):
        rows = points[block(i), :]
        rest = slice(i * ROWS, LEAF)
        table_ref[block(i), rest] = gauss(
            rows, left_column(rows), points[rest, :], row[:, rest]
        ).astype(bf16)


def dot_symmetric(field, table_ref):
    out = [None] * STEPS

    def add(k, value):
        out[k] = value if out[k] is None else out[k] + value

    for i in range(STEPS):
        straight = nn(field[:, block(i)], table_ref[block(i), i * ROWS : LEAF])
        for j in range(i, STEPS):
            add(j, straight[:, block(j - i)])
        if i + 1 < STEPS:
            after = slice((i + 1) * ROWS, LEAF)
            add(i, nt(field[:, after], table_ref[block(i), after]))
    return jnp.concatenate(out, axis=1)


def make_block(left, points, row, table_ref):
    for i in range(STEPS):
        rows = left[block(i), :]
        table_ref[block(i), :] = gauss(rows, left_column(rows), points, row).astype(bf16)


def tables_a_kernel(
    x_ref, b_ref, after_ref, table_ref, own_ref, row_ref, up_ref, down_ref
):
    del after_ref
    for k in range(STEPS):
        place = slice(LEAF + k * RHS, LEAF + (k + 1) * RHS)
        up_ref[place, :] = b_ref[:, LEAF + k * ROWS : LEAF + (k + 1) * ROWS].astype(bf16)
        down_ref[place, :] = b_ref[:, k * ROWS : (k + 1) * ROWS].astype(bf16)
    up_ref[:LEAF, :] = x_ref[LEAF:, :]
    down_ref[:LEAF, :] = x_ref[:LEAF, :]
    row_ref[...] = right_row(x_ref[...])
    make_symmetric(x_ref[:LEAF, :], row_ref[:, :LEAF], table_ref)
    own_ref[...] = dot_symmetric(b_ref[:, :LEAF].astype(bf16), table_ref)


def tables_a_call(points, field, after):
    return pl.pallas_call(
        tables_a_kernel,
        in_specs=inside(2) + [anywhere()],
        out_shape=(
            shape_of((LEAF, LEAF), bf16),
            shape_of((RHS, LEAF), f32),
            shape_of((1, 2 * LEAF), f32),
            shape_of((LEAF + STEPS * RHS, DIM), bf16),
            shape_of((LEAF + STEPS * RHS, DIM), bf16),
        ),
        compiler_params=params,
        cost_estimate=cost(700_000_000, 5_000_000, 700_000),
        name="tables_a",
    )(points, field, after)


def tables_b_kernel(
    w_ref, x_ref, b_ref, row_ref, own_a_ref, after_ref, table_b_ref, table_ab_ref, own_ref
):
    del after_ref
    row_b = row_ref[:, LEAF:]
    make_symmetric(x_ref[LEAF:, :], row_b, table_b_ref)
    make_block(x_ref[:LEAF, :], x_ref[LEAF:, :], row_b, table_ab_ref)
    b_a, b_b = b_ref[:, :LEAF].astype(bf16), b_ref[:, LEAF:].astype(bf16)
    own_ref[:, :LEAF] = own_a_ref[...] + weight_of(w_ref, 1) * nt(b_b, table_ab_ref[...])
    own_ref[:, LEAF:] = dot_symmetric(b_b, table_b_ref) + weight_of(w_ref, 2) * nn(
        b_a, table_ab_ref[...]
    )


def tables_b_call(w, points, field, row, own_a, after):
    return pl.pallas_call(
        tables_b_kernel,
        in_specs=inside(5) + [anywhere()],
        out_shape=(
            shape_of((LEAF, LEAF), bf16),
            shape_of((LEAF, LEAF), bf16),
            shape_of((RHS, 2 * LEAF), f32),
        ),
        compiler_params=params,
        cost_estimate=cost(1_500_000_000, 7_000_000, 1_800_000),
        name="tables_b",
    )(w, points, field, row, own_a, after)


def unfold(halo_ref):
    parts = [halo_ref[LEAF + k * RHS : LEAF + (k + 1) * RHS, :] for k in range(STEPS)]
    return jnp.concatenate(parts, axis=1)


def around_kernel(
    w_ref, below_ref, above_ref, x_ref, row_ref, own_ref, below_table_ref, above_table_ref, out_ref
):
    make_block(below_ref[:LEAF, :], x_ref[:LEAF, :], row_ref[:, :LEAF], below_table_ref)
    out_ref[:, :LEAF] = own_ref[:, :LEAF] + weight_of(w_ref, 0) * nn(
        unfold(below_ref), below_table_ref[...]
    )
    make_block(above_ref[:LEAF, :], x_ref[LEAF:, :], row_ref[:, LEAF:], above_table_ref)
    out_ref[:, LEAF:] = own_ref[:, LEAF:] + weight_of(w_ref, 3) * nn(
        unfold(above_ref), above_table_ref[...]
    )


def around_call(w, below, above, points, row, own):
    return pl.pallas_call(
        around_kernel,
        in_specs=inside(6),
        out_shape=(
            shape_of((LEAF, LEAF), bf16),
            shape_of((LEAF, LEAF), bf16),
            shape_of((RHS, 2 * LEAF), f32),
        ),
        compiler_params=params,
        cost_estimate=cost(1_400_000_000, 7_000_000, 2_097_152),
        name="around",
    )(w, below, above, points, row, own)


def total_of(got_ref):
    total = got_ref[0].astype(f32)
    for k in range(1, got_ref.shape[0]):
        total += got_ref[k].astype(f32)
    return total


def climb_kernel(got_ref, table_ref, after_ref, up_ref, sent_ref):
    del after_ref
    total = total_of(got_ref)
    up_ref[...] = total
    value = (nn(total, table_ref[...], highest) * (1.0 / SKEL)).astype(bf16)
    for k in range(sent_ref.shape[0]):
        sent_ref[k] = value


def climb_call(got, table, peers, after):
    return pl.pallas_call(
        climb_kernel,
        in_specs=inside(2) + [anywhere()],
        out_shape=(shape_of((RHS, SKEL), f32), shape_of((peers, RHS, SKEL), bf16)),
        compiler_params=params,
        cost_estimate=cost(50_000_000, 900_000),
        name="climb",
    )(got, table, after)


def down_weights(up_one, up_two, up_top, low_table, high_table):
    down_top = level_top * up_top
    down_two = level_two * up_two + nt(down_top, high_table, highest) * (1.0 / SKEL)
    return level_one * up_one + nt(down_two, low_table, highest) * (1.0 / SKEL)


def second_kernel(
    got_ref, p1_ref, p2_ref, t1_ref, t2_ref, gh_ref, gl_ref, own_ref, u_ref, up_ref, down_ref
):
    weights = down_weights(p1_ref[...], p2_ref[...], total_of(got_ref), t1_ref[...], t2_ref[...])
    for k in range(2):
        part = slice(k * LEAF, (k + 1) * LEAF)
        far = down_dot(weights, gh_ref[part, :], gl_ref[part, :])
        value = (own_ref[:, part] + far) * (1.0 / LEAF)
        u_ref[:, part] = value
        (down_ref, up_ref)[k][...] = value.astype(bf16)


def second_call(got, p1, p2, t1, t2, gh, gl, own):
    return pl.pallas_call(
        second_kernel,
        in_specs=inside(8),
        out_shape=(
            shape_of((RHS, 2 * LEAF), f32),
            shape_of((RHS, LEAF), bf16),
            shape_of((RHS, LEAF), bf16),
        ),
        compiler_params=params,
        cost_estimate=cost(250_000_000, 5_000_000),
        name="second",
    )(got, p1, p2, t1, t2, gh, gl, own)


def row_sum(value):
    return jnp.sum(value, axis=1, keepdims=True)


def third_kernel(
    w_ref, u_ref, b_ref, u_a_ref, u_b_ref, table_a_ref, table_b_ref, table_ab_ref,
    gh_ref, gl_ref, out_ref, up_ref, sums_ref
):
    up_ref[...] = up_dot(u_ref[...], gh_ref[...], gl_ref[...])
    u_a, u_b = u_a_ref[...], u_b_ref[...]
    out_ref[:, :LEAF] = dot_symmetric(u_a, table_a_ref) + weight_of(w_ref, 1) * nt(
        u_b, table_ab_ref[...]
    )
    out_ref[:, LEAF:] = dot_symmetric(u_b, table_b_ref) + weight_of(w_ref, 2) * nn(
        u_a, table_ab_ref[...]
    )
    b, u = b_ref[...], u_ref[...]
    lane = lax.broadcasted_iota(jnp.int32, (RHS, 128), 1)
    sums = (row_sum(b * b), row_sum(b * u), row_sum(u * u))
    total = jnp.zeros((RHS, 128), f32)
    for k in range(3):
        total = jnp.where(lane == k, sums[k], total)
    sums_ref[...] = total


def third_call(w, u, field, u_a, u_b, table_a, table_b, table_ab, gh, gl):
    return pl.pallas_call(
        third_kernel,
        in_specs=inside(10),
        out_shape=(
            shape_of((RHS, 2 * LEAF), f32),
            shape_of((RHS, SKEL), f32),
            shape_of((RHS, 128), f32),
        ),
        compiler_params=params,
        cost_estimate=cost(700_000_000, 10_000_000),
        name="third",
    )(w, u, field, u_a, u_b, table_a, table_b, table_ab, gh, gl)


def rows_of(sums):
    high = sums.astype(bf16).astype(f32)
    rest = sums - high
    middle = rest.astype(bf16).astype(f32)
    low = rest - middle
    lane = lax.broadcasted_iota(jnp.int32, (RHS, 128), 1)
    packed = jnp.where(lane < 4, high, 0.0)
    packed += jnp.where((lane >= 4) & (lane < 8), pltpu.roll(middle, 4, 1), 0.0)
    packed += jnp.where((lane >= 8) & (lane < 12), pltpu.roll(low, 8, 1), 0.0)
    turned = packed.T[:16]
    return jnp.concatenate([turned, jnp.zeros((16, SKEL - RHS), f32)], axis=1)


def sums_of(rows):
    turned = jnp.concatenate([rows[:, :RHS], jnp.zeros((112, RHS), f32)], axis=0).T
    total = turned + (pltpu.roll(turned, 124, 1) + pltpu.roll(turned, 120, 1))
    lane = lax.broadcasted_iota(jnp.int32, (RHS, 128), 1)
    return jnp.where(lane < 4, total, 0.0)


def put_all(sent_ref, value, sums):
    message = jnp.concatenate([value, rows_of(sums)], axis=0).astype(bf16)
    for k in range(sent_ref.shape[0]):
        sent_ref[k] = message


def add_last(sums, column):
    lane = lax.broadcasted_iota(jnp.int32, (RHS, 128), 1)
    return sums + jnp.where(lane == 3, column, 0.0)


def finish_kernel(
    w_ref, below_ref, above_ref, below_table_ref, above_table_ref, u_ref, own_ref, up_ref,
    sums_ref, sent_ref, out_ref
):
    near_a = own_ref[:, :LEAF] + weight_of(w_ref, 0) * nn(below_ref[...], below_table_ref[...])
    near_b = own_ref[:, LEAF:] + weight_of(w_ref, 3) * nn(above_ref[...], above_table_ref[...])
    out_ref[:, :LEAF] = near_a
    out_ref[:, LEAF:] = near_b
    bend = row_sum(u_ref[:, :LEAF] * near_a) + row_sum(u_ref[:, LEAF:] * near_b)
    put_all(sent_ref, up_ref[...] * (1.0 / LEAF), add_last(sums_ref[...], bend * (1.0 / LEAF)))


def finish_call(w, below, above, below_table, above_table, u, own, up, sums, peers):
    return pl.pallas_call(
        finish_kernel,
        in_specs=inside(9),
        out_shape=(
            shape_of((peers, RHS + 16, SKEL), bf16),
            shape_of((RHS, 2 * LEAF), f32),
        ),
        compiler_params=params,
        cost_estimate=cost(270_000_000, 4_000_000),
        name="finish",
    )(w, below, above, below_table, above_table, u, own, up, sums)


def climb_sums_kernel(level, got_ref, table_ref, up_ref, sent_ref):
    total = total_of(got_ref)
    up = total[:RHS]
    up_ref[...] = up
    sums = add_last(sums_of(total[RHS:]), level * row_sum(up * up))
    put_all(sent_ref, nn(up, table_ref[...], highest) * (1.0 / SKEL), sums)


def climb_sums_call(got, table, level, peers):
    return pl.pallas_call(
        lambda *refs: climb_sums_kernel(level, *refs),
        out_shape=(shape_of((RHS, SKEL), f32), shape_of((peers, RHS + 16, SKEL), bf16)),
        compiler_params=params,
        cost_estimate=cost(50_000_000, 900_000),
        name="climb_sums",
    )(got, table)


def last_kernel(
    got_ref, p1_ref, p2_ref, t1_ref, t2_ref, gh_ref, gl_ref, near_ref, b_ref, u_ref, x_ref, r_ref
):
    total = total_of(got_ref)
    top = total[:RHS]
    weights = down_weights(p1_ref[...], p2_ref[...], top, t1_ref[...], t2_ref[...])
    sums = add_last(sums_of(total[RHS:]), level_top * row_sum(top * top))
    bb, bu, uu, uv = sums[:, 0:1], sums[:, 1:2], sums[:, 2:3], sums[:, 3:4]
    step_one = bb / (ridge_term * bb + bu)
    ratio = bu / bb
    norm_one = step_one * step_one * (uu - ratio * bu)
    beta = norm_one / bb
    bend_rr = step_one * step_one * (ratio * ratio * bu - 2.0 * ratio * uu + uv)
    bend_rb = step_one * (ratio * bu - uu)
    bending = (
        ridge_term * (norm_one + beta * beta * bb)
        + bend_rr
        + 2.0 * beta * bend_rb
        + beta * beta * bu
    )
    step_two = norm_one / bending
    for k in range(2):
        part = slice(k * LEAF, (k + 1) * LEAF)
        far = down_dot(weights, gh_ref[part, :], gl_ref[part, :])
        third = (near_ref[:, part] + far) * (1.0 / LEAF)
        first, second = b_ref[:, part], u_ref[:, part]
        residual_one = (step_one * ratio) * first - step_one * second
        direction = residual_one + beta * first
        applied = (
            ridge_term * direction + (step_one * ratio + beta) * second - step_one * third
        )
        x_ref[:, part] = step_one * first + step_two * direction
        r_ref[:, part] = residual_one - step_two * applied


def last_call(got, p1, p2, t1, t2, gh, gl, near, field, u):
    return pl.pallas_call(
        last_kernel,
        in_specs=inside(10),
        out_shape=(shape_of((RHS, 2 * LEAF), f32), shape_of((RHS, 2 * LEAF), f32)),
        compiler_params=params,
        cost_estimate=cost(250_000_000, 7_000_000),
        name="last",
    )(got, p1, p2, t1, t2, gh, gl, near, field, u)


def exchange(sent, axis):
    return lax.all_to_all(sent, axis, 0, 0)


def shift_up(value):
    count = lax.axis_size(ALL)
    return lax.ppermute(value, ALL, [(i, i + 1) for i in range(count - 1)])


def shift_down(value):
    count = lax.axis_size(ALL)
    return lax.ppermute(value, ALL, [(i + 1, i) for i in range(count - 1)])


def shards(points, right_side, skel_sub, skel_group, skel_top, neighbors, counts):
    leaves, subs, groups = (lax.axis_size(axis) for axis in ("leaf", "sub", "group"))
    sent, gh, gl, t1, t2, x, b, w = start_call(
        neighbors, counts, points, skel_sub, skel_group, skel_top, right_side, leaves
    )
    got = exchange(sent, "leaf")
    table_a, own_a, row, up, down = tables_a_call(x, b, sent)
    below, above = shift_up(up), shift_down(down)
    up_one, sent = climb_call(got, t1, subs, own_a)
    got = exchange(sent, "sub")
    table_b, table_ab, own = tables_b_call(w, x, b, row, own_a, sent)
    up_two, sent = climb_call(got, t2, groups, own)
    got = exchange(sent, "group")
    below_table, above_table, own = around_call(w, below, above, x, row, own)
    u, up, down = second_call(got, up_one, up_two, t1, t2, gh, gl, own)

    below, above = shift_up(up), shift_down(down)
    own, weights, sums = third_call(w, u, b, down, up, table_a, table_b, table_ab, gh, gl)
    sent, near = finish_call(
        w, below, above, below_table, above_table, u, own, weights, sums, leaves
    )
    got = exchange(sent, "leaf")
    up_one, sent = climb_sums_call(got, t1, level_one, subs)
    got = exchange(sent, "sub")
    up_two, sent = climb_sums_call(got, t2, level_two, groups)
    got = exchange(sent, "group")
    return last_call(got, up_one, up_two, t1, t2, gh, gl, near, b, u)


def solution(mesh):
    return jax.shard_map(
        shards,
        mesh=mesh,
        in_specs=(
            P(ALL, None),
            P(None, ALL),
            P(("group", "sub"), None),
            P("group", None),
            P(),
            P(ALL, None),
            P(ALL),
        ),
        out_specs=(P(None, ALL), P(None, ALL)),
        check_vma=False,
    )
```

time: 448 us -> 131 us (0.29)
  blocking collectives: 353 us -> 37.2 us
  matrix products: 37 us -> 0 us
  local copies, waits for them, and re-layouts: 5.94 us -> 31.6 us
  Pallas kernels: 0 us -> 23.8 us
  other arithmetic: 12.5 us -> 0 us
  between operations: 6.19 us -> 0.86 us
  starting transfers between devices: 31.1 us -> 36.4 us
    psum x9 -> x0, blocking collectives: 353 us -> none  [the longest x2 149 us: squares(): lax.psum(jnp.sum(residual * residual, axis=1), ('group', 'sub', 'leaf'))]
    all_to_all x0 -> x3, blocking collectives: none -> 37.2 us  [exchange(): return lax.all_to_all(sent, axis, 0, 0)]
    dot_general x33 -> x0, matrix products: 37 us -> none  [the longest x9 12 us: gauss_block(): lax.dot_general(left_rows, right_rows, (((1,), (1,)), ((), ())), preferre...]
    unnamed x42 -> x66, local copies, waits for them, and re-layouts: 3.4 us -> 31.6 us
    pallas_call x0 -> x12, Pallas kernels: none -> 23.8 us  [the longest x1 4.16 us: start_call(): pl.pallas_call(start_kernel, in_specs=[smem(), smem()] + [far_off] * 5, o...]
    all_to_all x0 -> x3, starting transfers between devices: none -> 16.7 us  [exchange(): return lax.all_to_all(sent, axis, 0, 0)]
    ppermute x6 -> x4, starting transfers between devices: 31.1 us -> 19.7 us  [the longest x2 13.9 us: shift_down(): return lax.ppermute(value, ALL, [(i + 1, i) for i in range(count - 1)])]
    reduce_sum x7 -> x0, other arithmetic: 5.23 us -> none  [the longest x3 3.74 us: gauss_block(): left_sq = jnp.sum(jnp.square(left_rows.astype(jnp.float32)), axis=1)]
  transfers between devices with their start and end apart: 6 -> 7, of which waited for: 0 -> 0; matrix products, arithmetic and copies ran while one was open for 7% -> 0% of each run, Pallas kernels for 0% -> 10%
where the time goes in v3:
time: 131 us; the launch traced here: 130 us
  blocking collectives  37.2 us (28%)
  starting transfers between devices  36.4 us (28%)
  local copies, waits for them, and re-layouts  31.6 us (24%)
  Pallas kernels  23.8 us (18%)
    all_to_all x3, blocking collectives, exchange(): return lax.all_to_all(sent, axis, 0, 0)  37.2 us
    unnamed x66, local copies, waits for them, and re-layouts  31.6 us
    all_to_all x3, starting transfers between devices, exchange(): return lax.all_to_all(sent, axis, 0, 0)  16.7 us
    ppermute x2, starting transfers between devices, shift_down(): return lax.ppermute(value, ALL, [(i + 1, i) for i in range(count - 1)])  13.9 us
    ppermute x2, starting transfers between devices, shift_up(): return lax.ppermute(value, ALL, [(i, i + 1) for i in range(count - 1)])  5.83 us
    pallas_call x1, Pallas kernels, start_call(): pl.pallas_call(start_kernel, in_specs=[smem(), smem()] + [far_off] * 5, o...  4.16 us
    pallas_call x1, Pallas kernels, around_call(): pl.pallas_call(around_kernel, in_specs=inside(6), out_shape=(shape_of((LE...  4.11 us
    pallas_call x1, Pallas kernels, tables_b_call(): pl.pallas_call(tables_b_kernel, in_specs=inside(5) + [anywhere()], out_sh...  3.04 us
  transfers between devices with their start and end apart: 7, of which 0 were waited for; matrix products, arithmetic and copies ran while one was open for 0% of the time, Pallas kernels for 10%

profile of v3, /device:TPU:2, one launch (start us, length us, event | category | flops | bytes accessed | tf_op | source)
XLA Modules:
  0.0 129.9 jit_solution(4483800673208554758)
XLA Ops:
  0.6 1.2 copy-done.22
  1.9 1.0 copy-done.23
  6.9 4.2 %start.1 = (bf16[8,64,256]{2,1,0:T(8,128)(2,1)S(1)}, bf16[2048,256]{1,0:T(8,128)(2,1)S(1)}, bf16[2048,256]{1,0:T(8,128)(2,1)S(1)}, f32[256,256]{1,0:T(8,128)S(1)...) custom-call(s32[2,2]{1,0:T(2,128)S(1)} %copy-done.27, ...), custom_call_target="tpu_custom_call" | custom-call | flops 600000000 | bytes 5000000 | tf_op jit(solution)/shard_map/start/pallas_call | solution.py:156
  12.8 8.5 %all-to-all-start = ((bf16[8,64,256]{2,1,0:T(8,128)(2,1)}), bf16[8,64,256]{2,1,0:T(8,128)(2,1)S(1)}, u32[]{:S(2)}, u32[]{:S(2)}) async-start(bf16[8,64,256]{2,1,0:T(8,128)(2,1)} %copy-done.18), calls=%async_computation | async-start | bytes 524288 | tf_op jit(solution)/shard_map/all_to_all | solution.py:560
  22.2 1.2 copy-done.30
  23.5 2.9 %tables_a.1 = (bf16[1024,1024]{1,0:T(8,128)(2,1)S(1)}, f32[64,1024]{1,0:T(8,128)S(1)}, f32[1,2048]{1,0:T(1,128)S(1)}, bf16[1280,256]{1,0:T(8,128)(2,1)}, bf16[1280,256]{1,0:T(8,128)(2,1)}) custom-call(bf16[2048,256]{1,0:T(8,128)(2,1)S(1)} %copy-done.30, f32[64,2048]{1,0:T(8,128)S(1)} %get-tuple-element.41.b_ref, bf16[8,64,256]{2,1,0:T(8,128)(2,1)S(1)} %copy-done.19), custom_call_target="tpu_custom_call" | custom-call | flops 700000000 | bytes 5000000 | tf_op jit(solution)/shard_map/tables_a/pallas_call | solution.py:260
  26.3 1.3 %copy-done.4 = bf16[1024,1024]{1,0:T(8,128)(2,1)} copy-done((bf16[1024,1024]{1,0:T(8,128)(2,1)}, bf16[1024,1024]{1,0:T(8,128)(2,1)S(1)}, u32[]{:S(2)}) %copy-start.4) | copy-done | bytes 2097176
  28.4 3.9 %collective-permute-start = (bf16[1280,256]{1,0:T(8,128)(2,1)}, bf16[1280,256]{1,0:T(8,128)(2,1)}, u32[]{:S(2)}, u32[]{:S(2)}) collective-permute-start(bf16[1280,256]{1,0:T(8,128)(2,1)} %get-tuple-element.52), channel_id=1, source_target_pairs={{0,1},{1,2},{2,3},{3,4},{4,5},{5,6},{6,7},{7,8},{8,9},{9,10},{10,1... | collective-permute-start | bytes 1966088 | tf_op jit(solution)/shard_map/ppermute | solution.py:565
  32.3 5.9 %collective-permute-start.1 = (bf16[1280,256]{1,0:T(8,128)(2,1)}, bf16[1280,256]{1,0:T(8,128)(2,1)}, u32[]{:S(2)}, u32[]{:S(2)}) collective-permute-start(bf16[1280,256]{1,0:T(8,128)(2,1)} %get-tuple-element.53), channel_id=1, source_target_pairs={{1,0},{2,1},{3,2},{4,3},{5,4},{6,5},{7,6},{8,7},{9,8},{10,9},{11,1... | collective-permute-start | bytes 1966088 | tf_op jit(solution)/shard_map/ppermute | solution.py:570
  40.1 3.4 %all-to-all-start.1 = ((bf16[8,64,256]{2,1,0:T(8,128)(2,1)}), bf16[8,64,256]{2,1,0:T(8,128)(2,1)S(1)}, u32[]{:S(2)}, u32[]{:S(2)}) async-start(bf16[8,64,256]{2,1,0:T(8,128)(2,1)} %copy-done.20), calls=%async_computation.1 | async-start | bytes 524288 | tf_op jit(solution)/shard_map/all_to_all | solution.py:560
  45.4 1.2 copy-done.31
  46.7 3.0 %tables_b.1 = (bf16[1024,1024]{1,0:T(8,128)(2,1)S(1)}, bf16[1024,1024]{1,0:T(8,128)(2,1)S(1)}, f32[64,2048]{1,0:T(8,128)S(1)}) custom-call(f32[8,128]{1,0:T(8,128)S(1)} %get-tuple-element.37.w_ref, bf16[2048,256]{1,0:T(8,128)(2,1)S(1)} %copy-done.31, f32[64,2048]{1,0:T(8,128)S(1)} %get-tuple-element.41.b_ref, f32[1,2048]{1,0:T(1,128)S(1)} %get-tuple-element.45.row_ref, ...), custom_call_target="tpu_custom_call" | custom-call | flops 1500000000 | bytes 7000000 | tf_op jit(solution)/shard_map/tables_b/pallas_call | solution.py:291
  49.7 1.3 %copy-done.6 = bf16[1024,1024]{1,0:T(8,128)(2,1)} copy-done((bf16[1024,1024]{1,0:T(8,128)(2,1)}, bf16[1024,1024]{1,0:T(8,128)(2,1)S(1)}, u32[]{:S(2)}) %copy-start.6) | copy-done | bytes 2097176
  51.1 1.4 %copy-done.8 = bf16[1024,1024]{1,0:T(8,128)(2,1)} copy-done((bf16[1024,1024]{1,0:T(8,128)(2,1)}, bf16[1024,1024]{1,0:T(8,128)(2,1)S(1)}, u32[]{:S(2)}) %copy-start.8) | copy-done | bytes 2097176
  53.2 1.0 copy-done.11
  55.2 4.8 %all-to-all-start.2 = ((bf16[4,64,256]{2,1,0:T(8,128)(2,1)}), bf16[4,64,256]{2,1,0:T(8,128)(2,1)S(1)}, u32[]{:S(2)}, u32[]{:S(2)}) async-start(bf16[4,64,256]{2,1,0:T(8,128)(2,1)} %get-tuple-element.47), calls=%async_computation.2 | async-start | bytes 262144 | tf_op jit(solution)/shard_map/all_to_all | solution.py:560
  61.1 1.2 copy-done.32
  62.3 4.1 %around.1 = (bf16[1024,1024]{1,0:T(8,128)(2,1)S(1)}, bf16[1024,1024]{1,0:T(8,128)(2,1)S(1)}, f32[64,2048]{1,0:T(8,128)S(1)}) custom-call(f32[8,128]{1,0:T(8,128)S(1)} %get-tuple-element.37.w_ref, bf16[1280,256]{1,0:T(8,128)(2,1)} %collective-permute-done.below_ref, bf16[1280,256]{1,0:T(8,128)(2,1)} %collective-permute-done.1.above_ref, ...), custom_call_target="tpu_custom_call" | custom-call | flops 1400000000 | bytes 7000000 | tf_op jit(solution)/shard_map/around/pallas_call | solution.py:324
  66.4 1.4 %copy-done = bf16[1024,1024]{1,0:T(8,128)(2,1)} copy-done((bf16[1024,1024]{1,0:T(8,128)(2,1)}, bf16[1024,1024]{1,0:T(8,128)(2,1)S(1)}, u32[]{:S(2)}) %copy-start) | copy-done | bytes 2097176
  67.8 1.3 %copy-done.2 = bf16[1024,1024]{1,0:T(8,128)(2,1)} copy-done((bf16[1024,1024]{1,0:T(8,128)(2,1)}, bf16[1024,1024]{1,0:T(8,128)(2,1)S(1)}, u32[]{:S(2)}) %copy-start.2) | copy-done | bytes 2097176
  69.9 1.2 copy-done.14
  71.1 1.7 %second.1 = (f32[64,2048]{1,0:T(8,128)S(1)}, bf16[64,1024]{1,0:T(8,128)(2,1)S(1)}, bf16[64,1024]{1,0:T(8,128)(2,1)S(1)}) custom-call(bf16[4,64,256]{2,1,0:T(8,128)(2,1)S(1)} %all-to-all-done.2.got_ref, f32[64,256]{1,0:T(8,128)S(1)} %get-tuple-element.48.p1_ref, f32[64,256]{1,0:T(8,128)S(1)} %get-tuple-element.49.p2_ref, ...), custom_call_target="tpu_custom_call" | custom-call | flops 250000000 | bytes 5000000 | tf_op jit(solution)/shard_map/second/pallas_call | solution.py:384
  72.8 1.9 %collective-permute-start.2 = (bf16[64,1024]{1,0:T(8,128)(2,1)S(1)}, bf16[64,1024]{1,0:T(8,128)(2,1)S(1)}, u32[]{:S(2)}, u32[]{:S(2)}) collective-permute-start(bf16[64,1024]{1,0:T(8,128)(2,1)S(1)} %get-tuple-element.55.u_b_ref), channel_id=1, source_target_pairs={{0,1},{1,2},{2,3},{3,4},{4,5},{5,6},{6,7},{7,8},{8,9},{9,10},{10,1... | collective-permute-start | bytes 393224 | tf_op jit(solution)/shard_map/ppermute | solution.py:565
  74.8 8.0 %collective-permute-start.3 = (bf16[64,1024]{1,0:T(8,128)(2,1)S(1)}, bf16[64,1024]{1,0:T(8,128)(2,1)S(1)}, u32[]{:S(2)}, u32[]{:S(2)}) collective-permute-start(bf16[64,1024]{1,0:T(8,128)(2,1)S(1)} %get-tuple-element.56.u_a_ref), channel_id=1, source_target_pairs={{1,0},{2,1},{3,2},{4,3},{5,4},{6,5},{7,6},{8,7},{9,8},{10,9},{11,1... | collective-permute-start | bytes 393224 | tf_op jit(solution)/shard_map/ppermute | solution.py:570
  82.8 1.6 %copy-done.7 = bf16[1024,1024]{1,0:T(8,128)(2,1)S(1)} copy-done((bf16[1024,1024]{1,0:T(8,128)(2,1)S(1)}, bf16[1024,1024]{1,0:T(8,128)(2,1)}, u32[]{:S(2)}) %copy-start.7) | copy-done | bytes 2097176
  84.4 1.6 %copy-done.9 = bf16[1024,1024]{1,0:T(8,128)(2,1)S(1)} copy-done((bf16[1024,1024]{1,0:T(8,128)(2,1)S(1)}, bf16[1024,1024]{1,0:T(8,128)(2,1)}, u32[]{:S(2)}) %copy-start.9) | copy-done | bytes 2097176
  86.0 2.3 %third.1 = (f32[64,2048]{1,0:T(8,128)S(1)}, f32[64,256]{1,0:T(8,128)S(1)}, f32[64,128]{1,0:T(8,128)S(1)}) custom-call(f32[8,128]{1,0:T(8,128)S(1)} %get-tuple-element.37.w_ref, f32[64,2048]{1,0:T(8,128)S(1)} %get-tuple-element.59.u_ref, f32[64,2048]{1,0:T(8,128)S(1)} %get-tuple-element.41.b_ref, bf16[64,1024]{1,0:T(8,128)(2,1)S(1)} %get-tuple-element.56.u_a_ref, ...), custom_call_target="tpu_custom_call" | custom-call | flops 700000000 | bytes 10000000 | tf_op jit(solution)/shard_map/third/pallas_call | solution.py:424
  88.4 1.1 finish.1
  89.5 15.4 %all_to_all.30.refs_0_ = bf16[8,80,256]{2,1,0:T(8,128)(2,1)S(1)} all-to-all(bf16[8,80,256]{2,1,0:T(8,128)(2,1)S(1)} %get-tuple-element.66), channel_id=1, replica_groups=mesh['group'=4,'sub'=8,'leaf'=8] {'leaf'}, dimensions={0} | all-to-all | bytes 655360 | tf_op jit(solution)/shard_map/all_to_all | solution.py:560
  105.3 12.5 %all_to_all.31.refs_0_ = bf16[8,80,256]{2,1,0:T(8,128)(2,1)S(1)} all-to-all(bf16[8,80,256]{2,1,0:T(8,128)(2,1)S(1)} %get-tuple-element.67), channel_id=1, replica_groups=mesh['group'=4,'sub'=8,'leaf'=8] {'sub'}, dimensions={0} | all-to-all | bytes 655360 | tf_op jit(solution)/shard_map/all_to_all | solution.py:560
  118.1 9.3 %all_to_all.32.got_ref = bf16[4,80,256]{2,1,0:T(8,128)(2,1)S(1)} all-to-all(bf16[4,80,256]{2,1,0:T(8,128)(2,1)S(1)} %get-tuple-element.68), channel_id=1, replica_groups=mesh['group'=4,'sub'=8,'leaf'=8] {'group'}, dimensions={0} | all-to-all | bytes 327680 | tf_op jit(solution)/shard_map/all_to_all | solution.py:560
  127.4 2.6 %last.1 = (f32[64,2048]{1,0:T(8,128)}, f32[64,2048]{1,0:T(8,128)}) custom-call(bf16[4,80,256]{2,1,0:T(8,128)(2,1)S(1)} %all_to_all.32.got_ref, f32[64,256]{1,0:T(8,128)S(1)} %get-tuple-element.69.p1_ref, f32[64,256]{1,0:T(8,128)S(1)} %get-tuple-element.70.p2_ref, f32[256,256]{1,0:T(8,128)S(1)} %get-tuple-element.39.table_ref.t1_ref.refs_1_, ...), custom_call_target="tpu_custom_call" | custom-call | flops 250000000 | bytes 7000000 | tf_op jit(solution)/shard_map/last/pallas_call | solution.py:549
  (63 shorter events, 15.5 us)
Async XLA Ops:
  0.6 1.2 copy-start.22
  1.9 1.0 copy-start.23
  2.9 0.9 copy-start.24
  3.8 0.9 copy-start.25
  11.8 1.0 copy-start.29
  12.8 25.4 %all-to-all-start = ((bf16[8,64,256]{2,1,0:T(8,128)(2,1)}), bf16[8,64,256]{2,1,0:T(8,128)(2,1)S(1)}, u32[]{:S(2)}, u32[]{:S(2)}) async-start(bf16[8,64,256]{2,1,0:T(8,128)(2,1)} %copy-done.18), calls=%async_computation | async-start | bytes 524288 | tf_op jit(solution)/shard_map/all_to_all | solution.py:560
  21.3 1.0 copy-start.19
  22.2 1.2 copy-start.30
  26.3 1.3 %copy-start.4 = (bf16[1024,1024]{1,0:T(8,128)(2,1)}, bf16[1024,1024]{1,0:T(8,128)(2,1)S(1)}, u32[]{:S(2)}) copy-start(bf16[1024,1024]{1,0:T(8,128)(2,1)S(1)} %get-tuple-element.60.table_a_ref) | copy-start | bytes 6291460
  28.4 31.7 %collective-permute-start = (bf16[1280,256]{1,0:T(8,128)(2,1)}, bf16[1280,256]{1,0:T(8,128)(2,1)}, u32[]{:S(2)}, u32[]{:S(2)}) collective-permute-start(bf16[1280,256]{1,0:T(8,128)(2,1)} %get-tuple-element.52), channel_id=1, source_target_pairs={{0,1},{1,2},{2,3},{3,4},{4,5},{5,6},{6,7},{7,8},{8,9},{9,10},{10,1... | collective-permute-start | bytes 1966088 | tf_op jit(solution)/shard_map/ppermute | solution.py:565
  32.3 27.7 %collective-permute-start.1 = (bf16[1280,256]{1,0:T(8,128)(2,1)}, bf16[1280,256]{1,0:T(8,128)(2,1)}, u32[]{:S(2)}, u32[]{:S(2)}) collective-permute-start(bf16[1280,256]{1,0:T(8,128)(2,1)} %get-tuple-element.53), channel_id=1, source_target_pairs={{1,0},{2,1},{3,2},{4,3},{5,4},{6,5},{7,6},{8,7},{9,8},{10,9},{11,1... | collective-permute-start | bytes 1966088 | tf_op jit(solution)/shard_map/ppermute | solution.py:570
  38.2 1.0 copy-start.16
  40.1 13.1 %all-to-all-start.1 = ((bf16[8,64,256]{2,1,0:T(8,128)(2,1)}), bf16[8,64,256]{2,1,0:T(8,128)(2,1)S(1)}, u32[]{:S(2)}, u32[]{:S(2)}) async-start(bf16[8,64,256]{2,1,0:T(8,128)(2,1)} %copy-done.20), calls=%async_computation.1 | async-start | bytes 524288 | tf_op jit(solution)/shard_map/all_to_all | solution.py:560
  43.5 1.0 copy-start.17
  44.5 0.9 copy-start.21
  45.4 1.2 copy-start.31
  49.7 1.4 %copy-start.6 = (bf16[1024,1024]{1,0:T(8,128)(2,1)}, bf16[1024,1024]{1,0:T(8,128)(2,1)S(1)}, u32[]{:S(2)}) copy-start(bf16[1024,1024]{1,0:T(8,128)(2,1)S(1)} %get-tuple-element.61.table_b_ref) | copy-start | bytes 6291460
  51.1 1.4 %copy-start.8 = (bf16[1024,1024]{1,0:T(8,128)(2,1)}, bf16[1024,1024]{1,0:T(8,128)(2,1)S(1)}, u32[]{:S(2)}) copy-start(bf16[1024,1024]{1,0:T(8,128)(2,1)S(1)} %get-tuple-element.62.table_ab_ref) | copy-start | bytes 6291460
  53.2 1.0 copy-start.11
  55.2 14.7 %all-to-all-start.2 = ((bf16[4,64,256]{2,1,0:T(8,128)(2,1)}), bf16[4,64,256]{2,1,0:T(8,128)(2,1)S(1)}, u32[]{:S(2)}, u32[]{:S(2)}) async-start(bf16[4,64,256]{2,1,0:T(8,128)(2,1)} %get-tuple-element.47), calls=%async_computation.2 | async-start | bytes 262144 | tf_op jit(solution)/shard_map/all_to_all | solution.py:560
  60.0 1.0 copy-start.12
  61.1 1.2 copy-start.32
  66.4 1.4 %copy-start = (bf16[1024,1024]{1,0:T(8,128)(2,1)}, bf16[1024,1024]{1,0:T(8,128)(2,1)S(1)}, u32[]{:S(2)}) copy-start(bf16[1024,1024]{1,0:T(8,128)(2,1)S(1)} %get-tuple-element.57.below_table_ref) | copy-start | bytes 6291460
  67.8 1.3 %copy-start.2 = (bf16[1024,1024]{1,0:T(8,128)(2,1)}, bf16[1024,1024]{1,0:T(8,128)(2,1)S(1)}, u32[]{:S(2)}) copy-start(bf16[1024,1024]{1,0:T(8,128)(2,1)S(1)} %get-tuple-element.58.above_table_ref) | copy-start | bytes 6291460
  69.9 12.9 %copy-start.5 = (bf16[1024,1024]{1,0:T(8,128)(2,1)S(1)}, bf16[1024,1024]{1,0:T(8,128)(2,1)}, u32[]{:S(2)}) copy-start(bf16[1024,1024]{1,0:T(8,128)(2,1)} %copy-done.4) | copy-start | bytes 6291460
  69.9 1.2 copy-start.14
  72.8 15.5 %collective-permute-start.2 = (bf16[64,1024]{1,0:T(8,128)(2,1)S(1)}, bf16[64,1024]{1,0:T(8,128)(2,1)S(1)}, u32[]{:S(2)}, u32[]{:S(2)}) collective-permute-start(bf16[64,1024]{1,0:T(8,128)(2,1)S(1)} %get-tuple-element.55.u_b_ref), channel_id=1, source_target_pairs={{0,1},{1,2},{2,3},{3,4},{4,5},{5,6},{6,7},{7,8},{8,9},{9,10},{10,1... | collective-permute-start | bytes 393224 | tf_op jit(solution)/shard_map/ppermute | solution.py:565
  74.8 13.6 %collective-permute-start.3 = (bf16[64,1024]{1,0:T(8,128)(2,1)S(1)}, bf16[64,1024]{1,0:T(8,128)(2,1)S(1)}, u32[]{:S(2)}, u32[]{:S(2)}) collective-permute-start(bf16[64,1024]{1,0:T(8,128)(2,1)S(1)} %get-tuple-element.56.u_a_ref), channel_id=1, source_target_pairs={{1,0},{2,1},{3,2},{4,3},{5,4},{6,5},{7,6},{8,7},{9,8},{10,9},{11,1... | collective-permute-start | bytes 393224 | tf_op jit(solution)/shard_map/ppermute | solution.py:570
  82.8 1.6 %copy-start.7 = (bf16[1024,1024]{1,0:T(8,128)(2,1)S(1)}, bf16[1024,1024]{1,0:T(8,128)(2,1)}, u32[]{:S(2)}) copy-start(bf16[1024,1024]{1,0:T(8,128)(2,1)} %copy-done.6) | copy-start | bytes 6291460
  84.4 1.6 %copy-start.9 = (bf16[1024,1024]{1,0:T(8,128)(2,1)S(1)}, bf16[1024,1024]{1,0:T(8,128)(2,1)}, u32[]{:S(2)}) copy-start(bf16[1024,1024]{1,0:T(8,128)(2,1)} %copy-done.8) | copy-start | bytes 6291460
  86.0 2.4 %copy-start.1 = (bf16[1024,1024]{1,0:T(8,128)(2,1)S(1)}, bf16[1024,1024]{1,0:T(8,128)(2,1)}, u32[]{:S(2)}) copy-start(bf16[1024,1024]{1,0:T(8,128)(2,1)} %copy-done) | copy-start | bytes 6291460
  86.0 2.4 %copy-start.3 = (bf16[1024,1024]{1,0:T(8,128)(2,1)S(1)}, bf16[1024,1024]{1,0:T(8,128)(2,1)}, u32[]{:S(2)}) copy-start(bf16[1024,1024]{1,0:T(8,128)(2,1)} %copy-done.2) | copy-start | bytes 6291460
  (8 other events, 5.9 us)

commit v4 on v3

v4 whole, which is shorter than its diff:
```python
import math

import jax
import jax.numpy as jnp
from jax import lax
from jax.experimental import pallas as pl
from jax.experimental.pallas import tpu as pltpu
from jax.sharding import PartitionSpec as P

LEAF = 1024
SKEL = 256
RHS = 64
DIM = 256
ROWS = 256
STEPS = LEAF // ROWS
WIDE = 512
ALL = ("group", "sub", "leaf")

ridge_term = 3.0
level_one = 0.5
level_two = 0.25
level_top = 0.3

bf16 = jnp.bfloat16
f32 = jnp.float32
per_unit = 0.25 / DIM * math.log2(math.e)
vmem_bytes = 20 * 1024 * 1024


def shape_of(shape, dtype):
    return jax.ShapeDtypeStruct(shape, dtype)


def cost(flops, moved, exps=0):
    return pl.CostEstimate(flops=flops, bytes_accessed=moved, transcendentals=exps)


params = pltpu.CompilerParams(vmem_limit_bytes=vmem_bytes)


def nn(left, right, precision=None):
    return lax.dot_general(
        left, right, (((1,), (0,)), ((), ())), precision=precision, preferred_element_type=f32
    )


def nt(left, right, precision=None):
    return lax.dot_general(
        left, right, (((1,), (1,)), ((), ())), precision=precision, preferred_element_type=f32
    )


highest = lax.Precision.HIGHEST


def squares(rows):
    wide = rows.astype(f32)
    return wide * wide


def left_column(rows):
    return jnp.sum(squares(rows), axis=1, keepdims=True) * per_unit


def right_row(rows):
    square = squares(rows)
    high = square.astype(bf16)
    low = (square - high.astype(f32)).astype(bf16)
    ones = jnp.ones((8, rows.shape[1]), bf16)
    return (nt(ones, high) + nt(ones, low))[0:1] * per_unit


def gauss(left, column, right, row):
    return jnp.exp2(nt(left, right) * (2.0 * per_unit) - column - row)


def split(value):
    high = value.astype(bf16)
    low = (value - high.astype(f32)).astype(bf16)
    return high, low


def up_dot(field, table_high, table_low):
    high, low = split(field)
    both = nn(jnp.concatenate([high, low], axis=0), table_high)
    return both[:RHS] + both[RHS:] + nn(high, table_low)


def down_dot(weights, table_high, table_low):
    high, low = split(weights)
    both = nt(jnp.concatenate([high, low], axis=0), table_high)
    return both[:RHS] + both[RHS:] + nt(high, table_low)


def even_leaf():
    return lax.rem(lax.axis_index("leaf"), 2) == 0


def pack_kernel(x_ref, b_ref, odd_ref, even_ref, xv_ref, bv_ref, x_sem, b_sem):
    loads = []
    for k in range(2):
        part = pl.ds(k * LEAF, LEAF)
        loads.append(
            (
                pltpu.make_async_copy(b_ref.at[:, part], bv_ref.at[:, part], b_sem.at[k]),
                pltpu.make_async_copy(x_ref.at[part, :], xv_ref.at[part, :], x_sem.at[k]),
            )
        )
    for pair_of in loads:
        for load in pair_of:
            load.start()
    for pair_of in loads:
        for load in pair_of:
            load.wait()

    def fill(out_ref, first):
        out_ref[:LEAF, :] = xv_ref[first : first + LEAF, :]
        for k in range(STEPS):
            place = slice(LEAF + k * RHS, LEAF + (k + 1) * RHS)
            out_ref[place, :] = bv_ref[:, first + k * ROWS : first + (k + 1) * ROWS].astype(bf16)

    even = even_leaf()

    @pl.when(even)
    def _():
        fill(odd_ref, 0)
        fill(even_ref, LEAF)

    @pl.when(jnp.logical_not(even))
    def _():
        fill(odd_ref, LEAF)
        fill(even_ref, 0)


def in_hbm(value):
    return pltpu.with_memory_space_constraint(value, pltpu.HBM)


def pack_call(points, field):
    count = points.shape[0]
    return pl.pallas_call(
        pack_kernel,
        in_specs=[pl.BlockSpec(memory_space=pltpu.HBM)] * 2,
        out_shape=(
            shape_of((LEAF + STEPS * RHS, DIM), bf16),
            shape_of((LEAF + STEPS * RHS, DIM), bf16),
        ),
        scratch_shapes=[
            pltpu.VMEM((count, DIM), bf16),
            pltpu.VMEM((RHS, count), f32),
            pltpu.SemaphoreType.DMA((2,)),
            pltpu.SemaphoreType.DMA((2,)),
        ],
        compiler_params=params,
        cost_estimate=cost(1_000_000, 5_000_000),
        name="pack",
    )(in_hbm(points), in_hbm(field))


def start_kernel(
    x_ref, b_ref, z1_ref, z2_ref, z3_ref, sent_ref, gh_ref, gl_ref, t1_ref, t2_ref,
    xv_ref, bv_ref, z_ref, x_sem, b_sem, z_sem
):
    parts = x_ref.shape[0] // WIDE
    z_loads, x_loads, b_loads = [], [], []
    for k, source in enumerate((z1_ref, z2_ref, z3_ref)):
        z_loads.append(pltpu.make_async_copy(source, z_ref.at[k], z_sem.at[k]))
    for k in range(parts):
        rows = pl.ds(k * WIDE, WIDE)
        x_loads.append(pltpu.make_async_copy(x_ref.at[rows, :], xv_ref.at[rows, :], x_sem.at[k]))
        b_loads.append(pltpu.make_async_copy(b_ref.at[:, rows], bv_ref.at[:, rows], b_sem.at[k]))
    z_loads[0].start()
    for k in range(parts):
        x_loads[k].start()
        b_loads[k].start()
    z_loads[1].start()
    z_loads[2].start()
    z_loads[0].wait()
    z1 = z_ref[0]
    row = right_row(z1)
    total = jnp.zeros((RHS, SKEL), f32)
    for k in range(parts):
        rows = slice(k * WIDE, (k + 1) * WIDE)
        x_loads[k].wait()
        part = xv_ref[rows, :]
        high, low = split(gauss(part, left_column(part), z1, row))
        gh_ref[rows, :] = high
        gl_ref[rows, :] = low
        b_loads[k].wait()
        total += up_dot(bv_ref[:, rows], high, low)
    value = (total * (1.0 / LEAF)).astype(bf16)
    for k in range(sent_ref.shape[0]):
        sent_ref[k] = value
    z_loads[1].wait()
    z_loads[2].wait()
    z2, z3 = z_ref[1], z_ref[2]
    t1_ref[...] = gauss(z1, left_column(z1), z2, right_row(z2))
    t2_ref[...] = gauss(z2, left_column(z2), z3, right_row(z3))


def start_call(points, field, z1, z2, z3, peers):
    count = points.shape[0]
    parts = count // WIDE
    return pl.pallas_call(
        start_kernel,
        in_specs=[pl.BlockSpec(memory_space=pltpu.HBM)] * 5,
        out_shape=(
            shape_of((peers, RHS, SKEL), bf16),
            shape_of((count, SKEL), bf16),
            shape_of((count, SKEL), bf16),
            shape_of((SKEL, SKEL), f32),
            shape_of((SKEL, SKEL), f32),
        ),
        scratch_shapes=[
            pltpu.VMEM((count, DIM), bf16),
            pltpu.VMEM((RHS, count), f32),
            pltpu.VMEM((3, SKEL, DIM), bf16),
            pltpu.SemaphoreType.DMA((parts,)),
            pltpu.SemaphoreType.DMA((parts,)),
            pltpu.SemaphoreType.DMA((3,)),
        ],
        compiler_params=params,
        cost_estimate=cost(600_000_000, 5_000_000, 655_360),
        name="start",
    )(*(in_hbm(value) for value in (points, field, z1, z2, z3)))


def smem():
    return pl.BlockSpec(memory_space=pltpu.SMEM)


def anywhere():
    return pl.BlockSpec(memory_space=pl.ANY)


def inside(count):
    return [pl.BlockSpec(memory_space=pltpu.VMEM)] * count


def listed(nb_ref, ct_ref, position, target):
    found = 0.0
    for k in range(nb_ref.shape[1]):
        hit = (k < ct_ref[position]) & (nb_ref[position, k] == target)
        found = found + jnp.where(hit, 1.0, 0.0)
    return found


def first_leaf_of():
    return lax.axis_index(ALL) * 2


def weight_of(w_ref, k):
    return w_ref[k : k + 1, 0:1]


def block(k):
    return slice(k * ROWS, (k + 1) * ROWS)


def make_symmetric(points, row, table_ref):
    for i in range(STEPS):
        rows = points[block(i), :]
        rest = slice(i * ROWS, LEAF)
        table_ref[block(i), rest] = gauss(
            rows, left_column(rows), points[rest, :], row[:, rest]
        ).astype(bf16)


def dot_symmetric(field, table_ref):
    out = [None] * STEPS

    def add(k, value):
        out[k] = value if out[k] is None else out[k] + value

    for i in range(STEPS):
        straight = nn(field[:, block(i)], table_ref[block(i), i * ROWS : LEAF])
        for j in range(i, STEPS):
            add(j, straight[:, block(j - i)])
        if i + 1 < STEPS:
            after = slice((i + 1) * ROWS, LEAF)
            add(i, nt(field[:, after], table_ref[block(i), after]))
    return jnp.concatenate(out, axis=1)


def make_block(left, points, row, table_ref):
    for i in range(STEPS):
        rows = left[block(i), :]
        table_ref[block(i), :] = gauss(rows, left_column(rows), points, row).astype(bf16)


def tables_kernel(
    nb_ref, ct_ref, x_ref, b_ref, after_ref,
    table_a_ref, table_b_ref, table_ab_ref, own_ref, row_ref, w_ref, xv_ref, bv_ref,
    x_sem, b_sem
):
    del after_ref
    x_loads, b_loads = [], []
    for k in range(2):
        part = pl.ds(k * LEAF, LEAF)
        x_loads.append(pltpu.make_async_copy(x_ref.at[part, :], xv_ref.at[part, :], x_sem.at[k]))
        b_loads.append(pltpu.make_async_copy(b_ref.at[:, part], bv_ref.at[:, part], b_sem.at[k]))
    for load in x_loads + b_loads:
        load.start()
    first = first_leaf_of()
    weights = (
        listed(nb_ref, ct_ref, 0, first - 1),
        listed(nb_ref, ct_ref, 0, first + 1),
        listed(nb_ref, ct_ref, 1, first),
        listed(nb_ref, ct_ref, 1, first + 2),
    )
    place = lax.broadcasted_iota(jnp.int32, (8, 128), 0)
    spread = jnp.zeros((8, 128), f32)
    for k in range(4):
        spread = jnp.where(place == k, weights[k], spread)
    w_ref[...] = spread
    x_loads[0].wait()
    x_a = xv_ref[:LEAF, :]
    row_ref[:, :LEAF] = right_row(x_a)
    make_symmetric(x_a, row_ref[:, :LEAF], table_a_ref)
    x_loads[1].wait()
    x_b = xv_ref[LEAF:, :]
    row_ref[:, LEAF:] = right_row(x_b)
    make_symmetric(x_b, row_ref[:, LEAF:], table_b_ref)
    make_block(x_a, x_b, row_ref[:, LEAF:], table_ab_ref)
    b_loads[0].wait()
    b_loads[1].wait()
    b_a, b_b = bv_ref[:, :LEAF].astype(bf16), bv_ref[:, LEAF:].astype(bf16)
    own_ref[:, :LEAF] = dot_symmetric(b_a, table_a_ref) + weights[1] * nt(b_b, table_ab_ref[...])
    own_ref[:, LEAF:] = dot_symmetric(b_b, table_b_ref) + weights[2] * nn(b_a, table_ab_ref[...])


def tables_call(neighbors, counts, points, field, after):
    count = points.shape[0]
    return pl.pallas_call(
        tables_kernel,
        in_specs=[smem(), smem()]
        + [pl.BlockSpec(memory_space=pltpu.HBM)] * 2
        + [anywhere()],
        out_shape=(
            shape_of((LEAF, LEAF), bf16),
            shape_of((LEAF, LEAF), bf16),
            shape_of((LEAF, LEAF), bf16),
            shape_of((RHS, 2 * LEAF), f32),
            shape_of((1, 2 * LEAF), f32),
            shape_of((8, 128), f32),
            shape_of((count, DIM), bf16),
            shape_of((RHS, count), f32),
        ),
        scratch_shapes=[pltpu.SemaphoreType.DMA((2,)), pltpu.SemaphoreType.DMA((2,))],
        compiler_params=params,
        cost_estimate=cost(2_200_000_000, 9_000_000, 2_400_000),
        name="tables",
    )(neighbors, counts, in_hbm(points), in_hbm(field), after)


def unfold(halo):
    parts = [halo[LEAF + k * RHS : LEAF + (k + 1) * RHS, :] for k in range(STEPS)]
    return jnp.concatenate(parts, axis=1)


def in_order(odd_ref, even_ref):
    even = even_leaf()
    odd_got, even_got = odd_ref[...], even_ref[...]
    return jnp.where(even, odd_got, even_got), jnp.where(even, even_got, odd_got)


def around_kernel(
    w_ref, odd_ref, even_ref, x_ref, row_ref, own_ref, after_ref,
    below_table_ref, above_table_ref, out_ref
):
    del after_ref

    def build(below_ref, above_ref):
        make_block(below_ref, x_ref[:LEAF, :], row_ref[:, :LEAF], below_table_ref)
        out_ref[:, :LEAF] = own_ref[:, :LEAF] + weight_of(w_ref, 0) * nn(
            unfold(below_ref), below_table_ref[...]
        )
        make_block(above_ref, x_ref[LEAF:, :], row_ref[:, LEAF:], above_table_ref)
        out_ref[:, LEAF:] = own_ref[:, LEAF:] + weight_of(w_ref, 3) * nn(
            unfold(above_ref), above_table_ref[...]
        )

    even = even_leaf()

    @pl.when(even)
    def _():
        build(odd_ref, even_ref)

    @pl.when(jnp.logical_not(even))
    def _():
        build(even_ref, odd_ref)


def around_call(w, odd, even, points, row, own, after):
    return pl.pallas_call(
        around_kernel,
        in_specs=inside(6) + [anywhere()],
        out_shape=(
            shape_of((LEAF, LEAF), bf16),
            shape_of((LEAF, LEAF), bf16),
            shape_of((RHS, 2 * LEAF), f32),
        ),
        compiler_params=params,
        cost_estimate=cost(1_400_000_000, 7_000_000, 2_097_152),
        name="around",
    )(w, odd, even, points, row, own, after)


def total_of(got_ref):
    total = got_ref[0].astype(f32)
    for k in range(1, got_ref.shape[0]):
        total += got_ref[k].astype(f32)
    return total


def climb_kernel(got_ref, table_ref, after_ref, up_ref, sent_ref):
    del after_ref
    total = total_of(got_ref)
    up_ref[...] = total
    value = (nn(total, table_ref[...], highest) * (1.0 / SKEL)).astype(bf16)
    if len(sent_ref.shape) == 2:
        sent_ref[...] = value
    else:
        for k in range(sent_ref.shape[0]):
            sent_ref[k] = value


def climb_call(got, table, shape, after):
    return pl.pallas_call(
        climb_kernel,
        in_specs=inside(2) + [anywhere()],
        out_shape=(shape_of((RHS, SKEL), f32), shape_of(shape + (RHS, SKEL), bf16)),
        compiler_params=params,
        cost_estimate=cost(50_000_000, 900_000),
        name="climb",
    )(got, table, after)


def sum_of(refs):
    total = refs[0][...].astype(f32)
    for ref in refs[1:]:
        total += ref[...].astype(f32)
    return total


def down_weights(up_one, up_two, up_top, low_table, high_table):
    down_top = level_top * up_top
    down_two = level_two * up_two + nt(down_top, high_table, highest) * (1.0 / SKEL)
    return level_one * up_one + nt(down_two, low_table, highest) * (1.0 / SKEL)


def second_kernel(
    g0_ref, g1_ref, g2_ref, g3_ref, p1_ref, p2_ref, t1_ref, t2_ref, gh_ref, gl_ref, own_ref,
    u_ref, u16_ref, odd_ref, even_ref
):
    top = sum_of((g0_ref, g1_ref, g2_ref, g3_ref))
    weights = down_weights(p1_ref[...], p2_ref[...], top, t1_ref[...], t2_ref[...])
    for k in range(2):
        part = slice(k * LEAF, (k + 1) * LEAF)
        far = down_dot(weights, gh_ref[part, :], gl_ref[part, :])
        value = (own_ref[:, part] + far) * (1.0 / LEAF)
        u_ref[:, part] = value
        u16_ref[:, part] = value.astype(bf16)
    even = even_leaf()

    @pl.when(even)
    def _():
        odd_ref[...] = u16_ref[:, :LEAF]
        even_ref[...] = u16_ref[:, LEAF:]

    @pl.when(jnp.logical_not(even))
    def _():
        odd_ref[...] = u16_ref[:, LEAF:]
        even_ref[...] = u16_ref[:, :LEAF]


def second_call(parts, p1, p2, t1, t2, gh, gl, own):
    return pl.pallas_call(
        second_kernel,
        in_specs=inside(11),
        out_shape=(
            shape_of((RHS, 2 * LEAF), f32),
            shape_of((RHS, 2 * LEAF), bf16),
            shape_of((RHS, LEAF), bf16),
            shape_of((RHS, LEAF), bf16),
        ),
        compiler_params=params,
        cost_estimate=cost(250_000_000, 5_000_000),
        name="second",
    )(*parts, p1, p2, t1, t2, gh, gl, own)


def row_sum(value):
    return jnp.sum(value, axis=1, keepdims=True)


def third_kernel(
    w_ref, u_ref, b_ref, u16_ref, table_a_ref, table_b_ref, table_ab_ref,
    gh_ref, gl_ref, out_ref, up_ref, sums_ref
):
    up_ref[...] = up_dot(u_ref[...], gh_ref[...], gl_ref[...])
    u_a, u_b = u16_ref[:, :LEAF], u16_ref[:, LEAF:]
    out_ref[:, :LEAF] = dot_symmetric(u_a, table_a_ref) + weight_of(w_ref, 1) * nt(
        u_b, table_ab_ref[...]
    )
    out_ref[:, LEAF:] = dot_symmetric(u_b, table_b_ref) + weight_of(w_ref, 2) * nn(
        u_a, table_ab_ref[...]
    )
    b, u = b_ref[...], u_ref[...]
    lane = lax.broadcasted_iota(jnp.int32, (RHS, 128), 1)
    sums = (row_sum(b * b), row_sum(b * u), row_sum(u * u))
    total = jnp.zeros((RHS, 128), f32)
    for k in range(3):
        total = jnp.where(lane == k, sums[k], total)
    sums_ref[...] = total


def third_call(w, u, field, u16, table_a, table_b, table_ab, gh, gl):
    return pl.pallas_call(
        third_kernel,
        in_specs=inside(9),
        out_shape=(
            shape_of((RHS, 2 * LEAF), f32),
            shape_of((RHS, SKEL), f32),
            shape_of((RHS, 128), f32),
        ),
        compiler_params=params,
        cost_estimate=cost(700_000_000, 10_000_000),
        name="third",
    )(w, u, field, u16, table_a, table_b, table_ab, gh, gl)


def rows_of(sums):
    high = sums.astype(bf16).astype(f32)
    rest = sums - high
    middle = rest.astype(bf16).astype(f32)
    low = rest - middle
    lane = lax.broadcasted_iota(jnp.int32, (RHS, 128), 1)
    packed = jnp.where(lane < 4, high, 0.0)
    packed += jnp.where((lane >= 4) & (lane < 8), pltpu.roll(middle, 4, 1), 0.0)
    packed += jnp.where((lane >= 8) & (lane < 12), pltpu.roll(low, 8, 1), 0.0)
    turned = packed.T[:16]
    return jnp.concatenate([turned, jnp.zeros((16, SKEL - RHS), f32)], axis=1)


def sums_of(rows):
    turned = jnp.concatenate([rows[:, :RHS], jnp.zeros((112, RHS), f32)], axis=0).T
    total = turned + (pltpu.roll(turned, 124, 1) + pltpu.roll(turned, 120, 1))
    lane = lax.broadcasted_iota(jnp.int32, (RHS, 128), 1)
    return jnp.where(lane < 4, total, 0.0)


def put_all(sent_ref, value, sums):
    message = jnp.concatenate([value, rows_of(sums)], axis=0).astype(bf16)
    if len(sent_ref.shape) == 2:
        sent_ref[...] = message
    else:
        for k in range(sent_ref.shape[0]):
            sent_ref[k] = message


def add_last(sums, column):
    lane = lax.broadcasted_iota(jnp.int32, (RHS, 128), 1)
    return sums + jnp.where(lane == 3, column, 0.0)


def finish_kernel(
    w_ref, odd_ref, even_ref, below_table_ref, above_table_ref, u_ref, own_ref, up_ref,
    sums_ref, sent_ref, out_ref
):
    below, above = in_order(odd_ref, even_ref)
    near_a = own_ref[:, :LEAF] + weight_of(w_ref, 0) * nn(below, below_table_ref[...])
    near_b = own_ref[:, LEAF:] + weight_of(w_ref, 3) * nn(above, above_table_ref[...])
    out_ref[:, :LEAF] = near_a
    out_ref[:, LEAF:] = near_b
    bend = row_sum(u_ref[:, :LEAF] * near_a) + row_sum(u_ref[:, LEAF:] * near_b)
    put_all(sent_ref, up_ref[...] * (1.0 / LEAF), add_last(sums_ref[...], bend * (1.0 / LEAF)))


def finish_call(w, odd, even, below_table, above_table, u, own, up, sums, peers):
    return pl.pallas_call(
        finish_kernel,
        in_specs=inside(9),
        out_shape=(
            shape_of((peers, RHS + 16, SKEL), bf16),
            shape_of((RHS, 2 * LEAF), f32),
        ),
        compiler_params=params,
        cost_estimate=cost(270_000_000, 4_000_000),
        name="finish",
    )(w, odd, even, below_table, above_table, u, own, up, sums)


def climb_sums_kernel(level, got_ref, table_ref, up_ref, sent_ref):
    total = total_of(got_ref)
    up = total[:RHS]
    up_ref[...] = up
    sums = add_last(sums_of(total[RHS:]), level * row_sum(up * up))
    put_all(sent_ref, nn(up, table_ref[...], highest) * (1.0 / SKEL), sums)


def climb_sums_call(got, table, level, shape):
    return pl.pallas_call(
        lambda *refs: climb_sums_kernel(level, *refs),
        out_shape=(shape_of((RHS, SKEL), f32), shape_of(shape + (RHS + 16, SKEL), bf16)),
        compiler_params=params,
        cost_estimate=cost(50_000_000, 900_000),
        name="climb_sums",
    )(got, table)


def last_kernel(
    g0_ref, g1_ref, g2_ref, g3_ref, p1_ref, p2_ref, t1_ref, t2_ref, gh_ref, gl_ref, near_ref,
    b_ref, u_ref, x_ref, r_ref
):
    total = sum_of((g0_ref, g1_ref, g2_ref, g3_ref))
    top = total[:RHS]
    weights = down_weights(p1_ref[...], p2_ref[...], top, t1_ref[...], t2_ref[...])
    sums = add_last(sums_of(total[RHS:]), level_top * row_sum(top * top))
    bb, bu, uu, uv = sums[:, 0:1], sums[:, 1:2], sums[:, 2:3], sums[:, 3:4]
    step_one = bb / (ridge_term * bb + bu)
    ratio = bu / bb
    norm_one = step_one * step_one * (uu - ratio * bu)
    beta = norm_one / bb
    bend_rr = step_one * step_one * (ratio * ratio * bu - 2.0 * ratio * uu + uv)
    bend_rb = step_one * (ratio * bu - uu)
    bending = (
        ridge_term * (norm_one + beta * beta * bb)
        + bend_rr
        + 2.0 * beta * bend_rb
        + beta * beta * bu
    )
    step_two = norm_one / bending
    for k in range(2):
        part = slice(k * LEAF, (k + 1) * LEAF)
        far = down_dot(weights, gh_ref[part, :], gl_ref[part, :])
        third = (near_ref[:, part] + far) * (1.0 / LEAF)
        first, second = b_ref[:, part], u_ref[:, part]
        residual_one = (step_one * ratio) * first - step_one * second
        direction = residual_one + beta * first
        applied = (
            ridge_term * direction + (step_one * ratio + beta) * second - step_one * third
        )
        x_ref[:, part] = step_one * first + step_two * direction
        r_ref[:, part] = residual_one - step_two * applied


def last_call(parts, p1, p2, t1, t2, gh, gl, near, field, u):
    return pl.pallas_call(
        last_kernel,
        in_specs=inside(13),
        out_shape=(shape_of((RHS, 2 * LEAF), f32), shape_of((RHS, 2 * LEAF), f32)),
        compiler_params=params,
        cost_estimate=cost(250_000_000, 7_000_000),
        name="last",
    )(*parts, p1, p2, t1, t2, gh, gl, near, field, u)


def exchange(sent, axis):
    return lax.all_to_all(sent, axis, 0, 0)


def chain_swap(value, first):
    count = lax.axis_size(ALL)
    pairs = [(i, i + 1) for i in range(first, count - 1, 2)]
    return lax.ppermute(value, ALL, pairs + [(j, i) for i, j in pairs])


def swap_both(odd, even):
    return chain_swap(odd, 1), chain_swap(even, 0)


def turned(value, axis, shift):
    count = lax.axis_size(axis)
    return lax.ppermute(value, axis, [(i, (i + shift) % count) for i in range(count)])


def turns(value, axis):
    return [value] + [turned(value, axis, k) for k in range(1, lax.axis_size(axis))]


def shards(points, right_side, skel_sub, skel_group, skel_top, neighbors, counts):
    leaves, subs = (lax.axis_size(axis) for axis in ("leaf", "sub"))
    odd, even = swap_both(*pack_call(points, right_side))
    sent, gh, gl, t1, t2 = start_call(
        points, right_side, skel_sub, skel_group, skel_top, leaves
    )
    got = exchange(sent, "leaf")
    table_a, table_b, table_ab, own, row, w, x, b = tables_call(
        neighbors, counts, points, right_side, got
    )
    up_one, sent = climb_call(got, t1, (subs,), w)
    up_two, sent = climb_call(exchange(sent, "sub"), t2, (), w)
    parts = turns(sent, "group")
    below_table, above_table, own = around_call(w, odd, even, x, row, own, sent)
    u, u16, odd, even = second_call(parts, up_one, up_two, t1, t2, gh, gl, own)

    odd, even = swap_both(odd, even)
    own, weights, sums = third_call(w, u, b, u16, table_a, table_b, table_ab, gh, gl)
    sent, near = finish_call(
        w, odd, even, below_table, above_table, u, own, weights, sums, leaves
    )
    up_one, sent = climb_sums_call(exchange(sent, "leaf"), t1, level_one, (subs,))
    up_two, sent = climb_sums_call(exchange(sent, "sub"), t2, level_two, ())
    parts = turns(sent, "group")
    return last_call(parts, up_one, up_two, t1, t2, gh, gl, near, b, u)


def solution(mesh):
    return jax.shard_map(
        shards,
        mesh=mesh,
        in_specs=(
            P(ALL, None),
            P(None, ALL),
            P(("group", "sub"), None),
            P("group", None),
            P(),
            P(ALL, None),
            P(ALL),
        ),
        out_specs=(P(None, ALL), P(None, ALL)),
        check_vma=False,
    )
```

time: 131 us -> 103 us (0.79)
  local copies, waits for them, and re-layouts: 31.6 us -> 0.01 us
  waiting for transfers between devices: 0.02 us -> 12.7 us
  starting transfers between devices: 36.4 us -> 26.5 us
  Pallas kernels: 23.8 us -> 26.8 us
    unnamed x66 -> x4, local copies, waits for them, and re-layouts: 31.6 us -> 0.01 us
    ppermute x4 -> x10, waiting for transfers between devices: 0.01 us -> 9.72 us  [the longest x4 5.71 us: chain_swap(): return lax.ppermute(value, ALL, pairs + [(j, i) for i, j in pairs])]
    all_to_all x3 -> x1, starting transfers between devices: 16.7 us -> 8.48 us  [exchange(): return lax.all_to_all(sent, axis, 0, 0)]
    pallas_call x7, Pallas kernels: 20.8 us -> 24.3 us  [the longest x1 6.58 us: tables_call(): pl.pallas_call(tables_kernel, in_specs=[smem(), smem()] + [pl.BlockSpec(m...]
    all_to_all x3 -> x1, waiting for transfers between devices: 0.01 us -> 2.96 us  [exchange(): return lax.all_to_all(sent, axis, 0, 0)]
    ppermute x4 -> x10, starting transfers between devices: 19.7 us -> 18 us  [the longest x6 9.01 us: turned(): lax.ppermute(value, axis, [(i, (i + shift) % count) for i in range(count)])]
  transfers between devices with their start and end apart: 7 -> 11, of which waited for: 0 -> 4; matrix products, arithmetic and copies ran while one was open for 0% -> 0% of each run, Pallas kernels for 10% -> 16%
where the time goes in v4:
time: 103 us
  blocking collectives  36.3 us (35%)
  Pallas kernels  26.8 us (26%)
  starting transfers between devices  26.5 us (26%)
  waiting for transfers between devices  12.7 us (12%)
    all_to_all x3, blocking collectives, exchange(): return lax.all_to_all(sent, axis, 0, 0)  36.3 us
    ppermute x6, starting transfers between devices, turned(): lax.ppermute(value, axis, [(i, (i + shift) % count) for i in range(count)])  9.01 us
    ppermute x4, starting transfers between devices, chain_swap(): return lax.ppermute(value, ALL, pairs + [(j, i) for i, j in pairs])  8.97 us
    all_to_all x1, starting transfers between devices, exchange(): return lax.all_to_all(sent, axis, 0, 0)  8.48 us
    pallas_call x1, Pallas kernels, tables_call(): pl.pallas_call(tables_kernel, in_specs=[smem(), smem()] + [pl.BlockSpec(m...  6.58 us
    ppermute x4, waiting for transfers between devices, chain_swap(): return lax.ppermute(value, ALL, pairs + [(j, i) for i, j in pairs])  5.71 us
    pallas_call x1, Pallas kernels, start_call(): pl.pallas_call(start_kernel, in_specs=[pl.BlockSpec(memory_space=pltpu.HB...  4.54 us
    ppermute x6, waiting for transfers between devices, turned(): lax.ppermute(value, axis, [(i, (i + shift) % count) for i in range(count)])  4.01 us
  transfers between devices with their start and end apart: 11, of which 4 were waited for; matrix products, arithmetic and copies ran while one was open for 0% of the time, Pallas kernels for 16%

profile of v4, /device:TPU:2, one launch (start us, length us, event | category | flops | bytes accessed | tf_op | source)
XLA Modules:
  0.0 103.0 jit_solution(3660469092458855523)
XLA Ops:
  0.7 4.5 %start.1 = (bf16[8,64,256]{2,1,0:T(8,128)(2,1)}, bf16[2048,256]{1,0:T(8,128)(2,1)S(1)}, bf16[2048,256]{1,0:T(8,128)(2,1)S(1)}, f32[256,256]{1,0:T(8,128)S(1)}, f32[256,256]{1,0:T(8,128)S(1)}) custom-call(bf16[2048,256]{1,0:T(8,128)(2,1)} %x_ref.5, f32[64,2048]{1,0:T(8,128)} %b_ref.5, bf16[256,256]{1,0:T(8,128)(2,1)} %z1_ref.1, bf16[256,256]{1,0:T(8,128)(2,1)} %z2_ref.1, ...), custom_call_target="tpu_custom_call" | custom-call | flops 600000000 | bytes 5000000 | tf_op jit(solution)/shard_map/start/pallas_call | solution.py:204
  5.2 8.5 %all-to-all-start = ((bf16[8,64,256]{2,1,0:T(8,128)(2,1)}), bf16[8,64,256]{2,1,0:T(8,128)(2,1)S(1)}, u32[]{:S(2)}, u32[]{:S(2)}) async-start(bf16[8,64,256]{2,1,0:T(8,128)(2,1)} %get-tuple-element.37), calls=%async_computation | async-start | bytes 524288 | tf_op jit(solution)/shard_map/all_to_all | solution.py:660
  13.7 2.6 %pack.1 = (bf16[1280,256]{1,0:T(8,128)(2,1)}, bf16[1280,256]{1,0:T(8,128)(2,1)}) custom-call(bf16[2048,256]{1,0:T(8,128)(2,1)} %x_ref.5, f32[64,2048]{1,0:T(8,128)} %b_ref.5), custom_call_target="tpu_custom_call" | custom-call | flops 1000000 | bytes 5000000 | tf_op jit(solution)/shard_map/pack/pallas_call | solution.py:141
  16.2 6.4 %collective-permute-start.3 = (bf16[1280,256]{1,0:T(8,128)(2,1)}, bf16[1280,256]{1,0:T(8,128)(2,1)S(1)}, u32[]{:S(2)}, u32[]{:S(2)}) collective-permute-start(bf16[1280,256]{1,0:T(8,128)(2,1)} %get-tuple-element.47), channel_id=1, source_target_pairs={{1,2},{3,4},{5,6},{7,8},{9,10},{11,12},{13,14},{15,16},{17,18},{19... | collective-permute-start | bytes 1966088 | tf_op jit(solution)/shard_map/ppermute | solution.py:666
  22.7 0.1 collective-permute-start.4
  22.8 3.0 %all-to-all-done.after_ref.got_ref = bf16[8,64,256]{2,1,0:T(8,128)(2,1)S(1)} async-done(((bf16[8,64,256]{2,1,0:T(8,128)(2,1)}), bf16[8,64,256]{2,1,0:T(8,128)(2,1)S(1)}, u32[]{:S(2)}, u32[]{:S(2)}) %all-to-all-start) | async-done | bytes 262176 | tf_op jit(solution)/shard_map/all_to_all | solution.py:660
  25.8 6.6 %tables.1 = (bf16[1024,1024]{1,0:T(8,128)(2,1)S(1)}, bf16[1024,1024]{1,0:T(8,128)(2,1)S(1)}, bf16[1024,1024]{1,0:T(8,128)(2,1)S(1)}, f32[64,2048]{1,0:T(8,128)S(...) custom-call(s32[2,2]{1,0:T(2,128)S(1)} %copy-done, ...), custom_call_target="tpu_custom_call" | custom-call | flops 2200000000 | bytes 9000000 | tf_op jit(solution)/shard_map/tables/pallas_call | solution.py:334
  32.4 0.3 climb.2
  32.6 11.8 %all_to_all.20.got_ref = bf16[8,64,256]{2,1,0:T(8,128)(2,1)S(1)} all-to-all(bf16[8,64,256]{2,1,0:T(8,128)(2,1)S(1)} %get-tuple-element.40), channel_id=1, replica_groups=mesh['group'=4,'sub'=8,'leaf'=8] {'sub'}, dimensions={0} | all-to-all | bytes 524288 | tf_op jit(solution)/shard_map/all_to_all | solution.py:660
  44.5 0.3 climb.3
  44.7 1.6 %collective-permute-start = (bf16[64,256]{1,0:T(8,128)(2,1)S(1)}, bf16[64,256]{1,0:T(8,128)(2,1)S(1)}, u32[]{:S(2)}, u32[]{:S(2)}) collective-permute-start(bf16[64,256]{1,0:T(8,128)(2,1)S(1)} %get-tuple-element.42.after_ref.g0_ref), channel_id=1, source_target_pairs={{0,64},{64,128},{128,192},{192,0},{1,65},{65,129},{129,193},{193,1... | collective-permute-start | bytes 98312 | tf_op jit(solution)/shard_map/ppermute | solution.py:675
  46.3 1.1 %collective-permute-start.1 = (bf16[64,256]{1,0:T(8,128)(2,1)S(1)}, bf16[64,256]{1,0:T(8,128)(2,1)S(1)}, u32[]{:S(2)}, u32[]{:S(2)}) collective-permute-start(bf16[64,256]{1,0:T(8,128)(2,1)S(1)} %get-tuple-element.42.after_ref.g0_ref), channel_id=1, source_target_pairs={{0,128},{64,192},{128,0},{192,64},{1,129},{65,193},{129,1},{193,65... | collective-permute-start | bytes 98312 | tf_op jit(solution)/shard_map/ppermute | solution.py:675
  47.4 2.2 %collective-permute-start.2 = (bf16[64,256]{1,0:T(8,128)(2,1)S(1)}, bf16[64,256]{1,0:T(8,128)(2,1)S(1)}, u32[]{:S(2)}, u32[]{:S(2)}) collective-permute-start(bf16[64,256]{1,0:T(8,128)(2,1)S(1)} %get-tuple-element.42.after_ref.g0_ref), channel_id=1, source_target_pairs={{0,192},{64,0},{128,64},{192,128},{1,193},{65,1},{129,65},{193,129... | collective-permute-start | bytes 98312 | tf_op jit(solution)/shard_map/ppermute | solution.py:675
  49.6 4.0 %around.1 = (bf16[1024,1024]{1,0:T(8,128)(2,1)S(1)}, bf16[1024,1024]{1,0:T(8,128)(2,1)S(1)}, f32[64,2048]{1,0:T(8,128)S(1)}) custom-call(f32[8,128]{1,0:T(8,128)S(1)} %get-tuple-element.38.after_ref.w_ref, bf16[1280,256]{1,0:T(8,128)(2,1)S(1)} %collective-permute-done.3.odd_ref, bf16[1280,256]{1,0:T(8,128)(2,1)} %collective-permute-done.4.even_ref, ...), custom_call_target="tpu_custom_call" | custom-call | flops 1400000000 | bytes 7000000 | tf_op jit(solution)/shard_map/around/pallas_call | solution.py:395
  53.6 0.0 collective-permute-done.g1_ref
  53.6 0.0 collective-permute-done.2.g3_ref
  53.6 1.7 %second.1 = (f32[64,2048]{1,0:T(8,128)S(1)}, bf16[64,2048]{1,0:T(8,128)(2,1)S(1)}, bf16[64,1024]{1,0:T(8,128)(2,1)S(1)}, bf16[64,1024]{1,0:T(8,128)(2,1)S(1)}) custom-call(bf16[64,256]{1,0:T(8,128)(2,1)S(1)} %get-tuple-element.42.after_ref.g0_ref, bf16[64,256]{1,0:T(8,128)(2,1)S(1)} %collective-permute-done.g1_ref, ...), custom_call_target="tpu_custom_call" | custom-call | flops 250000000 | bytes 5000000 | tf_op jit(solution)/shard_map/second/pallas_call | solution.py:478
  55.4 1.9 %collective-permute-start.5 = (bf16[64,1024]{1,0:T(8,128)(2,1)S(1)}, bf16[64,1024]{1,0:T(8,128)(2,1)S(1)}, u32[]{:S(2)}, u32[]{:S(2)}) collective-permute-start(bf16[64,1024]{1,0:T(8,128)(2,1)S(1)} %get-tuple-element.53), channel_id=1, source_target_pairs={{1,2},{3,4},{5,6},{7,8},{9,10},{11,12},{13,14},{15,16},{17,18},{19... | collective-permute-start | bytes 393224 | tf_op jit(solution)/shard_map/ppermute | solution.py:666
  57.3 0.5 collective-permute-start.6
  57.8 2.3 %third.1 = (f32[64,2048]{1,0:T(8,128)S(1)}, f32[64,256]{1,0:T(8,128)S(1)}, f32[64,128]{1,0:T(8,128)S(1)}) custom-call(f32[8,128]{1,0:T(8,128)S(1)} %get-tuple-element.38.after_ref.w_ref, f32[64,2048]{1,0:T(8,128)S(1)} %get-tuple-element.57.u_ref, f32[64,2048]{1,0:T(8,128)S(1)} %get-tuple-element.58.b_ref, bf16[64,2048]{1,0:T(8,128)(2,1)S(1)} %get-tuple-element.59.u16_ref, ...), custom_call_target="tpu_custom_call" | custom-call | flops 700000000 | bytes 10000000 | tf_op jit(solution)/shard_map/third/pallas_call | solution.py:519
  60.2 5.7 %collective-permute-done.5.odd_ref = bf16[64,1024]{1,0:T(8,128)(2,1)S(1)} collective-permute-done((bf16[64,1024]{1,0:T(8,128)(2,1)S(1)}, bf16[64,1024]{1,0:T(8,128)(2,1)S(1)}, u32[]{:S(2)}, u32[]{:S(2)}) %collective-permute-start.5) | collective-permute-done | bytes 131104 | tf_op jit(solution)/shard_map/ppermute | solution.py:666
  65.9 1.1 %finish.1 = (bf16[8,80,256]{2,1,0:T(8,128)(2,1)S(1)}, f32[64,2048]{1,0:T(8,128)S(1)}) custom-call(f32[8,128]{1,0:T(8,128)S(1)} %get-tuple-element.38.after_ref.w_ref, bf16[64,1024]{1,0:T(8,128)(2,1)S(1)} %collective-permute-done.5.odd_ref, bf16[64,1024]{1,0:T(8,128)(2,1)S(1)} %collective-permute-done.6.even_ref, ...), custom_call_target="tpu_custom_call" | custom-call | flops 270000000 | bytes 4000000 | tf_op jit(solution)/shard_map/finish/pallas_call | solution.py:581
  67.0 13.7 %all_to_all.21.refs_0_ = bf16[8,80,256]{2,1,0:T(8,128)(2,1)S(1)} all-to-all(bf16[8,80,256]{2,1,0:T(8,128)(2,1)S(1)} %get-tuple-element.66), channel_id=1, replica_groups=mesh['group'=4,'sub'=8,'leaf'=8] {'leaf'}, dimensions={0} | all-to-all | bytes 655360 | tf_op jit(solution)/shard_map/all_to_all | solution.py:660
  80.7 0.4 climb_sums.2
  81.0 10.9 %all_to_all.22.refs_0_ = bf16[8,80,256]{2,1,0:T(8,128)(2,1)S(1)} all-to-all(bf16[8,80,256]{2,1,0:T(8,128)(2,1)S(1)} %get-tuple-element.67), channel_id=1, replica_groups=mesh['group'=4,'sub'=8,'leaf'=8] {'sub'}, dimensions={0} | all-to-all | bytes 655360 | tf_op jit(solution)/shard_map/all_to_all | solution.py:660
  91.9 0.3 climb_sums.3
  92.2 0.3 collective-permute-start.7
  92.5 3.9 %collective-permute-start.8 = (bf16[80,256]{1,0:T(8,128)(2,1)S(1)}, bf16[80,256]{1,0:T(8,128)(2,1)S(1)}, u32[]{:S(2)}, u32[]{:S(2)}) collective-permute-start(bf16[80,256]{1,0:T(8,128)(2,1)S(1)} %get-tuple-element.68.g0_ref), channel_id=1, source_target_pairs={{0,128},{64,192},{128,0},{192,64},{1,129},{65,193},{129,1},{193,65... | collective-permute-start | bytes 122888 | tf_op jit(solution)/shard_map/ppermute | solution.py:675
  96.4 0.0 collective-permute-done.7.g1_ref
  96.4 2.0 %collective-permute-done.8.g2_ref = bf16[80,256]{1,0:T(8,128)(2,1)S(1)} collective-permute-done((bf16[80,256]{1,0:T(8,128)(2,1)S(1)}, bf16[80,256]{1,0:T(8,128)(2,1)S(1)}, u32[]{:S(2)}, u32[]{:S(2)}) %collective-permute-start.8) | collective-permute-done | bytes 40992 | tf_op jit(solution)/shard_map/ppermute | solution.py:675
  98.4 2.0 %collective-permute-done.9.g3_ref = bf16[80,256]{1,0:T(8,128)(2,1)S(1)} collective-permute-done((bf16[80,256]{1,0:T(8,128)(2,1)S(1)}, bf16[80,256]{1,0:T(8,128)(2,1)S(1)}, u32[]{:S(2)}, u32[]{:S(2)}) %collective-permute-start.9) | collective-permute-done | bytes 40992 | tf_op jit(solution)/shard_map/ppermute | solution.py:675
  100.4 2.6 %last.1 = (f32[64,2048]{1,0:T(8,128)}, f32[64,2048]{1,0:T(8,128)}) custom-call(bf16[80,256]{1,0:T(8,128)(2,1)S(1)} %get-tuple-element.68.g0_ref, bf16[80,256]{1,0:T(8,128)(2,1)S(1)} %collective-permute-done.7.g1_ref, bf16[80,256]{1,0:T(8,128)(2,1)S(1)} %collective-permute-done.8.g2_ref, bf16[80,256]{1,0:T(8,128)(2,1)S(1)} %collective-permute-done.9.g3_ref, ...), custom_call_target="tpu_custom_call" | custom-call | flops 250000000 | bytes 7000000 | tf_op jit(solution)/shard_map/last/pallas_call | solution.py:649
  (9 shorter events, 0.0 us)
Async XLA Ops:
  0.6 25.1 %copy-start = (s32[2,2]{1,0:T(2,128)S(1)}, s32[2,2]{1,0:T(2,128)}, u32[]{:S(2)}) copy-start(s32[2,2]{1,0:T(2,128)} %nb_ref.1) | copy-start | bytes 52
  0.6 25.1 %copy-start.1 = (s32[2]{0:T(128)S(1)}, s32[2]{0:T(128)}, u32[]{:S(2)}) copy-start(s32[2]{0:T(128)} %ct_ref.1) | copy-start | bytes 28
  5.2 20.6 %all-to-all-start = ((bf16[8,64,256]{2,1,0:T(8,128)(2,1)}), bf16[8,64,256]{2,1,0:T(8,128)(2,1)S(1)}, u32[]{:S(2)}, u32[]{:S(2)}) async-start(bf16[8,64,256]{2,1,0:T(8,128)(2,1)} %get-tuple-element.37), calls=%async_computation | async-start | bytes 524288 | tf_op jit(solution)/shard_map/all_to_all | solution.py:660
  16.2 33.3 %collective-permute-start.3 = (bf16[1280,256]{1,0:T(8,128)(2,1)}, bf16[1280,256]{1,0:T(8,128)(2,1)S(1)}, u32[]{:S(2)}, u32[]{:S(2)}) collective-permute-start(bf16[1280,256]{1,0:T(8,128)(2,1)} %get-tuple-element.47), channel_id=1, source_target_pairs={{1,2},{3,4},{5,6},{7,8},{9,10},{11,12},{13,14},{15,16},{17,18},{19... | collective-permute-start | bytes 1966088 | tf_op jit(solution)/shard_map/ppermute | solution.py:666
  22.7 26.9 %collective-permute-start.4 = (bf16[1280,256]{1,0:T(8,128)(2,1)}, bf16[1280,256]{1,0:T(8,128)(2,1)}, u32[]{:S(2)}, u32[]{:S(2)}) collective-permute-start(bf16[1280,256]{1,0:T(8,128)(2,1)} %get-tuple-element.48), channel_id=1, source_target_pairs={{0,1},{2,3},{4,5},{6,7},{8,9},{10,11},{12,13},{14,15},{16,17},{18,... | collective-permute-start | bytes 1966088 | tf_op jit(solution)/shard_map/ppermute | solution.py:666
  44.7 8.8 %collective-permute-start = (bf16[64,256]{1,0:T(8,128)(2,1)S(1)}, bf16[64,256]{1,0:T(8,128)(2,1)S(1)}, u32[]{:S(2)}, u32[]{:S(2)}) collective-permute-start(bf16[64,256]{1,0:T(8,128)(2,1)S(1)} %get-tuple-element.42.after_ref.g0_ref), channel_id=1, source_target_pairs={{0,64},{64,128},{128,192},{192,0},{1,65},{65,129},{129,193},{193,1... | collective-permute-start | bytes 98312 | tf_op jit(solution)/shard_map/ppermute | solution.py:675
  46.3 7.3 %collective-permute-start.1 = (bf16[64,256]{1,0:T(8,128)(2,1)S(1)}, bf16[64,256]{1,0:T(8,128)(2,1)S(1)}, u32[]{:S(2)}, u32[]{:S(2)}) collective-permute-start(bf16[64,256]{1,0:T(8,128)(2,1)S(1)} %get-tuple-element.42.after_ref.g0_ref), channel_id=1, source_target_pairs={{0,128},{64,192},{128,0},{192,64},{1,129},{65,193},{129,1},{193,65... | collective-permute-start | bytes 98312 | tf_op jit(solution)/shard_map/ppermute | solution.py:675
  47.4 6.2 %collective-permute-start.2 = (bf16[64,256]{1,0:T(8,128)(2,1)S(1)}, bf16[64,256]{1,0:T(8,128)(2,1)S(1)}, u32[]{:S(2)}, u32[]{:S(2)}) collective-permute-start(bf16[64,256]{1,0:T(8,128)(2,1)S(1)} %get-tuple-element.42.after_ref.g0_ref), channel_id=1, source_target_pairs={{0,192},{64,0},{128,64},{192,128},{1,193},{65,1},{129,65},{193,129... | collective-permute-start | bytes 98312 | tf_op jit(solution)/shard_map/ppermute | solution.py:675
  55.4 10.5 %collective-permute-start.5 = (bf16[64,1024]{1,0:T(8,128)(2,1)S(1)}, bf16[64,1024]{1,0:T(8,128)(2,1)S(1)}, u32[]{:S(2)}, u32[]{:S(2)}) collective-permute-start(bf16[64,1024]{1,0:T(8,128)(2,1)S(1)} %get-tuple-element.53), channel_id=1, source_target_pairs={{1,2},{3,4},{5,6},{7,8},{9,10},{11,12},{13,14},{15,16},{17,18},{19... | collective-permute-start | bytes 393224 | tf_op jit(solution)/shard_map/ppermute | solution.py:666
  57.3 8.6 %collective-permute-start.6 = (bf16[64,1024]{1,0:T(8,128)(2,1)S(1)}, bf16[64,1024]{1,0:T(8,128)(2,1)S(1)}, u32[]{:S(2)}, u32[]{:S(2)}) collective-permute-start(bf16[64,1024]{1,0:T(8,128)(2,1)S(1)} %get-tuple-element.54), channel_id=1, source_target_pairs={{0,1},{2,3},{4,5},{6,7},{8,9},{10,11},{12,13},{14,15},{16,17},{18,... | collective-permute-start | bytes 393224 | tf_op jit(solution)/shard_map/ppermute | solution.py:666
  92.2 4.2 %collective-permute-start.7 = (bf16[80,256]{1,0:T(8,128)(2,1)S(1)}, bf16[80,256]{1,0:T(8,128)(2,1)S(1)}, u32[]{:S(2)}, u32[]{:S(2)}) collective-permute-start(bf16[80,256]{1,0:T(8,128)(2,1)S(1)} %get-tuple-element.68.g0_ref), channel_id=1, source_target_pairs={{0,64},{64,128},{128,192},{192,0},{1,65},{65,129},{129,193},{193,1... | collective-permute-start | bytes 122888 | tf_op jit(solution)/shard_map/ppermute | solution.py:675
  92.5 5.9 %collective-permute-start.8 = (bf16[80,256]{1,0:T(8,128)(2,1)S(1)}, bf16[80,256]{1,0:T(8,128)(2,1)S(1)}, u32[]{:S(2)}, u32[]{:S(2)}) collective-permute-start(bf16[80,256]{1,0:T(8,128)(2,1)S(1)} %get-tuple-element.68.g0_ref), channel_id=1, source_target_pairs={{0,128},{64,192},{128,0},{192,64},{1,129},{65,193},{129,1},{193,65... | collective-permute-start | bytes 122888 | tf_op jit(solution)/shard_map/ppermute | solution.py:675
  96.4 4.0 %collective-permute-start.9 = (bf16[80,256]{1,0:T(8,128)(2,1)S(1)}, bf16[80,256]{1,0:T(8,128)(2,1)S(1)}, u32[]{:S(2)}, u32[]{:S(2)}) collective-permute-start(bf16[80,256]{1,0:T(8,128)(2,1)S(1)} %get-tuple-element.68.g0_ref), channel_id=1, source_target_pairs={{0,192},{64,0},{128,64},{192,128},{1,193},{65,1},{129,65},{193,129... | collective-permute-start | bytes 122888 | tf_op jit(solution)/shard_map/ppermute | solution.py:675

commit v5 on v4

--- a/solution.py
+++ b/solution.py
@@ -96,70 +96,18 @@
     return lax.rem(lax.axis_index("leaf"), 2) == 0
 
 
-def pack_kernel(x_ref, b_ref, odd_ref, even_ref, xv_ref, bv_ref, x_sem, b_sem):
-    loads = []
-    for k in range(2):
-        part = pl.ds(k * LEAF, LEAF)
-        loads.append(
-            (
-                pltpu.make_async_copy(b_ref.at[:, part], bv_ref.at[:, part], b_sem.at[k]),
-                pltpu.make_async_copy(x_ref.at[part, :], xv_ref.at[part, :], x_sem.at[k]),
-            )
-        )
-    for pair_of in loads:
-        for load in pair_of:
-            load.start()
-    for pair_of in loads:
-        for load in pair_of:
-            load.wait()
-
-    def fill(out_ref, first):
-        out_ref[:LEAF, :] = xv_ref[first : first + LEAF, :]
-        for k in range(STEPS):
-            place = slice(LEAF + k * RHS, LEAF + (k + 1) * RHS)
-            out_ref[place, :] = bv_ref[:, first + k * ROWS : first + (k + 1) * ROWS].astype(bf16)
-
-    even = even_leaf()
-
-    @pl.when(even)
-    def _():
-        fill(odd_ref, 0)
-        fill(even_ref, LEAF)
-
-    @pl.when(jnp.logical_not(even))
-    def _():
-        fill(odd_ref, LEAF)
-        fill(even_ref, 0)
-
-
 def in_hbm(value):
     return pltpu.with_memory_space_constraint(value, pltpu.HBM)
 
 
-def pack_call(points, field):
-    count = points.shape[0]
-    return pl.pallas_call(
-        pack_kernel,
-        in_specs=[pl.BlockSpec(memory_space=pltpu.HBM)] * 2,
-        out_shape=(
-            shape_of((LEAF + STEPS * RHS, DIM), bf16),
-            shape_of((LEAF + STEPS * RHS, DIM), bf16),
-        ),
-        scratch_shapes=[
-            pltpu.VMEM((count, DIM), bf16),
-            pltpu.VMEM((RHS, count), f32),
-            pltpu.SemaphoreType.DMA((2,)),
-            pltpu.SemaphoreType.DMA((2,)),
-        ],
-        compiler_params=params,
-        cost_estimate=cost(1_000_000, 5_000_000),
-        name="pack",
-    )(in_hbm(points), in_hbm(field))
+def outside(count):
+    return [pl.BlockSpec(memory_space=pltpu.HBM)] * count
 
 
 def start_kernel(
-    x_ref, b_ref, z1_ref, z2_ref, z3_ref, sent_ref, gh_ref, gl_ref, t1_ref, t2_ref,
-    xv_ref, bv_ref, z_ref, x_sem, b_sem, z_sem
+    x_ref, b_ref, z1_ref, z2_ref, z3_ref,
+    sent_ref, gh_ref, gl_ref, t1_ref, t2_ref, odd_ref, even_ref,
+    xv_ref, bv_ref, z_ref, fold_ref, x_sem, b_sem, z_sem, out_sem
 ):
     parts = x_ref.shape[0] // WIDE
     z_loads, x_loads, b_loads = [], [], []
@@ -175,6 +123,16 @@
         b_loads[k].start()
     z_loads[1].start()
     z_loads[2].start()
+    parity = lax.rem(lax.axis_index("leaf"), 2)
+    halves = (parity, 1 - parity)
+    stores = []
+    for k, out_ref in enumerate((odd_ref, even_ref)):
+        rows = pl.ds(pl.multiple_of(halves[k] * LEAF, LEAF), LEAF)
+        stores.append(
+            pltpu.make_async_copy(x_ref.at[rows, :], out_ref.at[pl.ds(0, LEAF), :], out_sem.at[k])
+        )
+    for store in stores:
+        store.start()
     z_loads[0].wait()
     z1 = z_ref[0]
     row = right_row(z1)
@@ -188,6 +146,19 @@
         gl_ref[rows, :] = low
         b_loads[k].wait()
         total += up_dot(bv_ref[:, rows], high, low)
+    for half in range(2):
+        for k in range(STEPS):
+            fold_ref[half, k * RHS : (k + 1) * RHS, :] = bv_ref[
+                :, half * LEAF + k * ROWS : half * LEAF + (k + 1) * ROWS
+            ].astype(bf16)
+    for k, out_ref in enumerate((odd_ref, even_ref)):
+        stores.append(
+            pltpu.make_async_copy(
+                fold_ref.at[halves[k]], out_ref.at[pl.ds(LEAF, STEPS * RHS), :], out_sem.at[2 + k]
+            )
+        )
+    for store in stores[2:]:
+        store.start()
     value = (total * (1.0 / LEAF)).astype(bf16)
     for k in range(sent_ref.shape[0]):
         sent_ref[k] = value
@@ -196,6 +167,8 @@
     z2, z3 = z_ref[1], z_ref[2]
     t1_ref[...] = gauss(z1, left_column(z1), z2, right_row(z2))
     t2_ref[...] = gauss(z2, left_column(z2), z3, right_row(z3))
+    for store in stores:
+        store.wait()
 
 
 def start_call(points, field, z1, z2, z3, peers):
@@ -203,21 +176,26 @@
     parts = count // WIDE
     return pl.pallas_call(
         start_kernel,
-        in_specs=[pl.BlockSpec(memory_space=pltpu.HBM)] * 5,
+        in_specs=outside(5),
+        out_specs=tuple(inside(5) + outside(2)),
         out_shape=(
             shape_of((peers, RHS, SKEL), bf16),
             shape_of((count, SKEL), bf16),
             shape_of((count, SKEL), bf16),
             shape_of((SKEL, SKEL), f32),
             shape_of((SKEL, SKEL), f32),
+            shape_of((LEAF + STEPS * RHS, DIM), bf16),
+            shape_of((LEAF + STEPS * RHS, DIM), bf16),
         ),
         scratch_shapes=[
             pltpu.VMEM((count, DIM), bf16),
             pltpu.VMEM((RHS, count), f32),
             pltpu.VMEM((3, SKEL, DIM), bf16),
+            pltpu.VMEM((2, STEPS * RHS, ROWS), bf16),
             pltpu.SemaphoreType.DMA((parts,)),
             pltpu.SemaphoreType.DMA((parts,)),
             pltpu.SemaphoreType.DMA((3,)),
+            pltpu.SemaphoreType.DMA((4,)),
         ],
         compiler_params=params,
         cost_estimate=cost(600_000_000, 5_000_000, 655_360),
@@ -288,10 +266,9 @@
         table_ref[block(i), :] = gauss(rows, left_column(rows), points, row).astype(bf16)
 
 
-def tables_kernel(
+def tables_a_kernel(
     nb_ref, ct_ref, x_ref, b_ref, after_ref,
-    table_a_ref, table_b_ref, table_ab_ref, own_ref, row_ref, w_ref, xv_ref, bv_ref,
-    x_sem, b_sem
+    table_ref, own_ref, row_ref, w_ref, xv_ref, bv_ref, x_sem, b_sem
 ):
     del after_ref
     x_loads, b_loads = [], []
@@ -299,7 +276,7 @@
         part = pl.ds(k * LEAF, LEAF)
         x_loads.append(pltpu.make_async_copy(x_ref.at[part, :], xv_ref.at[part, :], x_sem.at[k]))
         b_loads.append(pltpu.make_async_copy(b_ref.at[:, part], bv_ref.at[:, part], b_sem.at[k]))
-    for load in x_loads + b_loads:
+    for load in (x_loads[0], b_loads[0], x_loads[1], b_loads[1]):
         load.start()
     first = first_leaf_of()
     weights = (
@@ -316,31 +293,22 @@
     x_loads[0].wait()
     x_a = xv_ref[:LEAF, :]
     row_ref[:, :LEAF] = right_row(x_a)
-    make_symmetric(x_a, row_ref[:, :LEAF], table_a_ref)
+    make_symmetric(x_a, row_ref[:, :LEAF], table_ref)
+    b_loads[0].wait()
+    own_ref[...] = dot_symmetric(bv_ref[:, :LEAF].astype(bf16), table_ref)
     x_loads[1].wait()
-    x_b = xv_ref[LEAF:, :]
-    row_ref[:, LEAF:] = right_row(x_b)
-    make_symmetric(x_b, row_ref[:, LEAF:], table_b_ref)
-    make_block(x_a, x_b, row_ref[:, LEAF:], table_ab_ref)
-    b_loads[0].wait()
+    row_ref[:, LEAF:] = right_row(xv_ref[LEAF:, :])
     b_loads[1].wait()
-    b_a, b_b = bv_ref[:, :LEAF].astype(bf16), bv_ref[:, LEAF:].astype(bf16)
-    own_ref[:, :LEAF] = dot_symmetric(b_a, table_a_ref) + weights[1] * nt(b_b, table_ab_ref[...])
-    own_ref[:, LEAF:] = dot_symmetric(b_b, table_b_ref) + weights[2] * nn(b_a, table_ab_ref[...])
-
-
-def tables_call(neighbors, counts, points, field, after):
+
+
+def tables_a_call(neighbors, counts, points, field, after):
     count = points.shape[0]
     return pl.pallas_call(
-        tables_kernel,
-        in_specs=[smem(), smem()]
-        + [pl.BlockSpec(memory_space=pltpu.HBM)] * 2
-        + [anywhere()],
+        tables_a_kernel,
+        in_specs=[smem(), smem()] + outside(2) + [anywhere()],
         out_shape=(
             shape_of((LEAF, LEAF), bf16),
-            shape_of((LEAF, LEAF), bf16),
-            shape_of((LEAF, LEAF), bf16),
-            shape_of((RHS, 2 * LEAF), f32),
+            shape_of((RHS, LEAF), f32),
             shape_of((1, 2 * LEAF), f32),
             shape_of((8, 128), f32),
             shape_of((count, DIM), bf16),
@@ -348,9 +316,38 @@
         ),
         scratch_shapes=[pltpu.SemaphoreType.DMA((2,)), pltpu.SemaphoreType.DMA((2,))],
         compiler_params=params,
-        cost_estimate=cost(2_200_000_000, 9_000_000, 2_400_000),
-        name="tables",
+        cost_estimate=cost(700_000_000, 5_000_000, 700_000),
+        name="tables_a",
     )(neighbors, counts, in_hbm(points), in_hbm(field), after)
+
+
+def tables_b_kernel(
+    w_ref, x_ref, b_ref, row_ref, own_a_ref, after_ref, table_b_ref, table_ab_ref, own_ref
+):
+    del after_ref
+    x_a, x_b = x_ref[:LEAF, :], x_ref[LEAF:, :]
+    make_symmetric(x_b, row_ref[:, LEAF:], table_b_ref)
+    make_block(x_a, x_b, row_ref[:, LEAF:], table_ab_ref)
+    b_a, b_b = b_ref[:, :LEAF].astype(bf16), b_ref[:, LEAF:].astype(bf16)
+    own_ref[:, :LEAF] = own_a_ref[...] + weight_of(w_ref, 1) * nt(b_b, table_ab_ref[...])
+    own_ref[:, LEAF:] = dot_symmetric(b_b, table_b_ref) + weight_of(w_ref, 2) * nn(
+        b_a, table_ab_ref[...]
+    )
+
+
+def tables_b_call(w, points, field, row, own_a, after):
+    return pl.pallas_call(
+        tables_b_kernel,
+        in_specs=inside(5) + [anywhere()],
+        out_shape=(
+            shape_of((LEAF, LEAF), bf16),
+            shape_of((LEAF, LEAF), bf16),
+            shape_of((RHS, 2 * LEAF), f32),
+        ),
+        compiler_params=params,
+        cost_estimate=cost(1_500_000_000, 7_000_000, 1_800_000),
+        name="tables_b",
+    )(w, points, field, row, own_a, after)
 
 
 def unfold(halo):
@@ -413,27 +410,55 @@
     return total
 
 
-def climb_kernel(got_ref, table_ref, after_ref, up_ref, sent_ref):
-    del after_ref
+def climb_kernel(got_ref, table_ref, up_ref, sent_ref):
     total = total_of(got_ref)
     up_ref[...] = total
-    value = (nn(total, table_ref[...], highest) * (1.0 / SKEL)).astype(bf16)
-    if len(sent_ref.shape) == 2:
-        sent_ref[...] = value
-    else:
-        for k in range(sent_ref.shape[0]):
-            sent_ref[k] = value
-
-
-def climb_call(got, table, shape, after):
+    sent_ref[...] = (nn(total, table_ref[...], highest) * (1.0 / SKEL)).astype(bf16)
+
+
+def climb_call(got, table):
     return pl.pallas_call(
         climb_kernel,
-        in_specs=inside(2) + [anywhere()],
-        out_shape=(shape_of((RHS, SKEL), f32), shape_of(shape + (RHS, SKEL), bf16)),
+        in_specs=inside(2),
+        out_shape=(shape_of((RHS, SKEL), f32), shape_of((RHS, SKEL), bf16)),
         compiler_params=params,
         cost_estimate=cost(50_000_000, 900_000),
         name="climb",
-    )(got, table, after)
+    )(got, table)
+
+
+def join_kernel(left_ref, right_ref, after_ref, out_ref):
+    del after_ref
+    out_ref[...] = (left_ref[...].astype(f32) + right_ref[...].astype(f32)).astype(bf16)
+
+
+def join_call(left, right, after):
+    return pl.pallas_call(
+        join_kernel,
+        in_specs=inside(2) + [anywhere()],
+        out_shape=shape_of((RHS, SKEL), bf16),
+        compiler_params=params,
+        cost_estimate=cost(100_000, 100_000),
+        name="join",
+    )(left, right, after)
+
+
+def climb_four_kernel(g0_ref, g1_ref, g2_ref, g3_ref, table_ref, after_ref, up_ref, sent_ref):
+    del after_ref
+    total = sum_of((g0_ref, g1_ref, g2_ref, g3_ref))
+    up_ref[...] = total
+    sent_ref[...] = (nn(total, table_ref[...], highest) * (1.0 / SKEL)).astype(bf16)
+
+
+def climb_four_call(parts, table, after):
+    return pl.pallas_call(
+        climb_four_kernel,
+        in_specs=inside(5) + [anywhere()],
+        out_shape=(shape_of((RHS, SKEL), f32), shape_of((RHS, SKEL), bf16)),
+        compiler_params=params,
+        cost_estimate=cost(50_000_000, 900_000),
+        name="climb_four",
+    )(*parts, table, after)
 
 
 def sum_of(refs):
@@ -591,27 +616,54 @@
     )(w, odd, even, below_table, above_table, u, own, up, sums)
 
 
-def climb_sums_kernel(level, got_ref, table_ref, up_ref, sent_ref):
-    total = total_of(got_ref)
+def climb_sums(level, total, table_ref, up_ref, sent_ref):
     up = total[:RHS]
     up_ref[...] = up
     sums = add_last(sums_of(total[RHS:]), level * row_sum(up * up))
     put_all(sent_ref, nn(up, table_ref[...], highest) * (1.0 / SKEL), sums)
 
 
-def climb_sums_call(got, table, level, shape):
-    return pl.pallas_call(
-        lambda *refs: climb_sums_kernel(level, *refs),
-        out_shape=(shape_of((RHS, SKEL), f32), shape_of(shape + (RHS + 16, SKEL), bf16)),
+def climb_sums_kernel(level, got_ref, table_ref, up_ref, sent_ref):
+    climb_sums(level, total_of(got_ref), table_ref, up_ref, sent_ref)
+
+
+def climb_sums_four_kernel(level, g0_ref, g1_ref, g2_ref, g3_ref, table_ref, up_ref, sent_ref):
+    climb_sums(level, sum_of((g0_ref, g1_ref, g2_ref, g3_ref)), table_ref, up_ref, sent_ref)
+
+
+def climb_sums_call(got, table, level):
+    several = isinstance(got, list)
+    kernel = climb_sums_four_kernel if several else climb_sums_kernel
+    inputs = got if several else [got]
+    return pl.pallas_call(
+        lambda *refs: kernel(level, *refs),
+        in_specs=inside(len(inputs) + 1),
+        out_shape=(shape_of((RHS, SKEL), f32), shape_of((RHS + 16, SKEL), bf16)),
         compiler_params=params,
         cost_estimate=cost(50_000_000, 900_000),
         name="climb_sums",
-    )(got, table)
+    )(*inputs, table)
+
+
+def join_sums_kernel(left_ref, right_ref, out_ref):
+    total = sum_of((left_ref, right_ref))
+    put_all(out_ref, total[:RHS], sums_of(total[RHS:]))
+
+
+def join_sums_call(left, right):
+    return pl.pallas_call(
+        join_sums_kernel,
+        in_specs=inside(2),
+        out_shape=shape_of((RHS + 16, SKEL), bf16),
+        compiler_params=params,
+        cost_estimate=cost(100_000, 100_000),
+        name="join_sums",
+    )(left, right)
 
 
 def last_kernel(
     g0_ref, g1_ref, g2_ref, g3_ref, p1_ref, p2_ref, t1_ref, t2_ref, gh_ref, gl_ref, near_ref,
-    b_ref, u_ref, x_ref, r_ref
+    b_ref, u_ref, x_ref, r_ref, xv_ref, rv_ref, x_sem, r_sem
 ):
     total = sum_of((g0_ref, g1_ref, g2_ref, g3_ref))
     top = total[:RHS]
@@ -631,8 +683,9 @@
         + beta * beta * bu
     )
     step_two = norm_one / bending
-    for k in range(2):
-        part = slice(k * LEAF, (k + 1) * LEAF)
+    stores = []
+    for k in range(4):
+        part = slice(k * WIDE, (k + 1) * WIDE)
         far = down_dot(weights, gh_ref[part, :], gl_ref[part, :])
         third = (near_ref[:, part] + far) * (1.0 / LEAF)
         first, second = b_ref[:, part], u_ref[:, part]
@@ -641,15 +694,31 @@
         applied = (
             ridge_term * direction + (step_one * ratio + beta) * second - step_one * third
         )
-        x_ref[:, part] = step_one * first + step_two * direction
-        r_ref[:, part] = residual_one - step_two * applied
+        xv_ref[:, part] = step_one * first + step_two * direction
+        rv_ref[:, part] = residual_one - step_two * applied
+        place = pl.ds(k * WIDE, WIDE)
+        for store in (
+            pltpu.make_async_copy(xv_ref.at[:, place], x_ref.at[:, place], x_sem.at[k]),
+            pltpu.make_async_copy(rv_ref.at[:, place], r_ref.at[:, place], r_sem.at[k]),
+        ):
+            store.start()
+            stores.append(store)
+    for store in stores:
+        store.wait()
 
 
 def last_call(parts, p1, p2, t1, t2, gh, gl, near, field, u):
     return pl.pallas_call(
         last_kernel,
         in_specs=inside(13),
+        out_specs=tuple(outside(2)),
         out_shape=(shape_of((RHS, 2 * LEAF), f32), shape_of((RHS, 2 * LEAF), f32)),
+        scratch_shapes=[
+            pltpu.VMEM((RHS, 2 * LEAF), f32),
+            pltpu.VMEM((RHS, 2 * LEAF), f32),
+            pltpu.SemaphoreType.DMA((4,)),
+            pltpu.SemaphoreType.DMA((4,)),
+        ],
         compiler_params=params,
         cost_estimate=cost(250_000_000, 7_000_000),
         name="last",
@@ -675,23 +744,29 @@
     return lax.ppermute(value, axis, [(i, (i + shift) % count) for i in range(count)])
 
 
-def turns(value, axis):
-    return [value] + [turned(value, axis, k) for k in range(1, lax.axis_size(axis))]
+def turns(value, axis, stride):
+    return [value] + [turned(value, axis, k) for k in range(stride, lax.axis_size(axis), stride)]
+
+
+def swapped(value, axis):
+    count = lax.axis_size(axis)
+    return lax.ppermute(value, axis, [(i, i ^ 1) for i in range(count)])
 
 
 def shards(points, right_side, skel_sub, skel_group, skel_top, neighbors, counts):
-    leaves, subs = (lax.axis_size(axis) for axis in ("leaf", "sub"))
-    odd, even = swap_both(*pack_call(points, right_side))
-    sent, gh, gl, t1, t2 = start_call(
+    leaves = lax.axis_size("leaf")
+    sent, gh, gl, t1, t2, odd, even = start_call(
         points, right_side, skel_sub, skel_group, skel_top, leaves
     )
-    got = exchange(sent, "leaf")
-    table_a, table_b, table_ab, own, row, w, x, b = tables_call(
-        neighbors, counts, points, right_side, got
-    )
-    up_one, sent = climb_call(got, t1, (subs,), w)
-    up_two, sent = climb_call(exchange(sent, "sub"), t2, (), w)
-    parts = turns(sent, "group")
+    odd, even = swap_both(odd, even)
+    up_one, sent = climb_call(exchange(sent, "leaf"), t1)
+    other = swapped(sent, "sub")
+    table_a, own_a, row, w, x, b = tables_a_call(neighbors, counts, points, right_side, sent)
+    sent = join_call(sent, other, w)
+    parts = turns(sent, "sub", 2)
+    table_b, table_ab, own = tables_b_call(w, x, b, row, own_a, sent)
+    up_two, sent = climb_four_call(parts, t2, own)
+    parts = turns(sent, "group", 1)
     below_table, above_table, own = around_call(w, odd, even, x, row, own, sent)
     u, u16, odd, even = second_call(parts, up_one, up_two, t1, t2, gh, gl, own)
 
@@ -700,9 +775,10 @@
     sent, near = finish_call(
         w, odd, even, below_table, above_table, u, own, weights, sums, leaves
     )
-    up_one, sent = climb_sums_call(exchange(sent, "leaf"), t1, level_one, (subs,))
-    up_two, sent = climb_sums_call(exchange(sent, "sub"), t2, level_two, ())
-    parts = turns(sent, "group")
+    up_one, sent = climb_sums_call(exchange(sent, "leaf"), t1, level_one)
+    sent = join_sums_call(sent, swapped(sent, "sub"))
+    up_two, sent = climb_sums_call(turns(sent, "sub", 2), t2, level_two)
+    parts = turns(sent, "group", 1)
     return last_call(parts, up_one, up_two, t1, t2, gh, gl, near, b, u)
 
 

time: 103 us -> 98.1 us (0.952)
  blocking collectives: 36.3 us -> 13.5 us
  starting transfers between devices: 26.5 us -> 38.2 us
  waiting for transfers between devices: 12.7 us -> 18.8 us
  Pallas kernels: 26.8 us -> 25.3 us
    all_to_all x3 -> x1, blocking collectives: 36.3 us -> 13.5 us  [exchange(): return lax.all_to_all(sent, axis, 0, 0)]
    ppermute x6 -> x12, starting transfers between devices: 9.01 us -> 19.8 us  [turned(): lax.ppermute(value, axis, [(i, (i + shift) % count) for i in range(count)])]
    all_to_all x1, waiting for transfers between devices: 2.96 us -> 6.11 us  [exchange(): return lax.all_to_all(sent, axis, 0, 0)]
    ppermute x6 -> x12, waiting for transfers between devices: 4.01 us -> 6.1 us  [turned(): lax.ppermute(value, axis, [(i, (i + shift) % count) for i in range(count)])]
    pallas_call x8 -> x10, Pallas kernels: 17.5 us -> 16 us  [the longest x1 5.05 us: start_call(): pl.pallas_call(start_kernel, in_specs=outside(5), out_specs=tuple(inside(...]
    ppermute x0 -> x2, waiting for transfers between devices: none -> 1.21 us  [swapped(): return lax.ppermute(value, axis, [(i, i ^ 1) for i in range(count)])]
  transfers between devices with their start and end apart: 11 -> 19, of which waited for: 4 -> 7; matrix products, arithmetic and copies ran while one was open for 0% -> 0% of each run, Pallas kernels for 16% -> 14%
where the time goes in v5:
time: 98.1 us; the launch traced here: 97.8 us
  starting transfers between devices  38.2 us (39%)
  Pallas kernels  25.3 us (26%)
  waiting for transfers between devices  18.8 us (19%)
  blocking collectives  13.5 us (14%)
  between operations  1.04 us (1%)
    ppermute x12, starting transfers between devices, turned(): lax.ppermute(value, axis, [(i, (i + shift) % count) for i in range(count)])  19.8 us
    all_to_all x1, blocking collectives, exchange(): return lax.all_to_all(sent, axis, 0, 0)  13.5 us
    ppermute x4, starting transfers between devices, chain_swap(): return lax.ppermute(value, ALL, pairs + [(j, i) for i, j in pairs])  9.86 us
    all_to_all x1, starting transfers between devices, exchange(): return lax.all_to_all(sent, axis, 0, 0)  8.46 us
    all_to_all x1, waiting for transfers between devices, exchange(): return lax.all_to_all(sent, axis, 0, 0)  6.11 us
    ppermute x12, waiting for transfers between devices, turned(): lax.ppermute(value, axis, [(i, (i + shift) % count) for i in range(count)])  6.1 us
    ppermute x4, waiting for transfers between devices, chain_swap(): return lax.ppermute(value, ALL, pairs + [(j, i) for i, j in pairs])  5.4 us
    pallas_call x1, Pallas kernels, start_call(): pl.pallas_call(start_kernel, in_specs=outside(5), out_specs=tuple(inside(...  5.05 us
  transfers between devices with their start and end apart: 19, of which 7 were waited for; matrix products, arithmetic and copies ran while one was open for 0% of the time, Pallas kernels for 14%

profile of v5, /device:TPU:2, one launch (start us, length us, event | category | flops | bytes accessed | tf_op | source)
XLA Modules:
  0.0 97.8 jit_solution(13277166479773564360)
XLA Ops:
  0.7 5.1 %start.1 = (bf16[8,64,256]{2,1,0:T(8,128)(2,1)}, bf16[2048,256]{1,0:T(8,128)(2,1)S(1)}, bf16[2048,256]{1,0:T(8,128)(2,1)S(1)}, f32[256,256]{1,0:T(8,128)S(1)}, f...) custom-call(bf16[2048,256]{1,0:T(8,128)(2,1)} %x_ref.3, f32[64,2048]{1,0:T(8,128)} %b_ref.3, ...), custom_call_target="tpu_custom_call" | custom-call | flops 600000000 | bytes 5000000 | tf_op jit(solution)/shard_map/start/pallas_call | solution.py:177
  5.7 0.8 copy-done
  6.5 8.5 %all-to-all-start = ((bf16[8,64,256]{2,1,0:T(8,128)(2,1)}), bf16[8,64,256]{2,1,0:T(8,128)(2,1)S(1)}, u32[]{:S(2)}, u32[]{:S(2)}) async-start(bf16[8,64,256]{2,1,0:T(8,128)(2,1)} %get-tuple-element.38), calls=%async_computation | async-start | bytes 524288 | tf_op jit(solution)/shard_map/all_to_all | solution.py:729
  15.0 6.4 %collective-permute-start.7 = (bf16[1280,256]{1,0:T(8,128)(2,1)}, bf16[1280,256]{1,0:T(8,128)(2,1)}, u32[]{:S(2)}, u32[]{:S(2)}) collective-permute-start(bf16[1280,256]{1,0:T(8,128)(2,1)} %copy-done), channel_id=1, source_target_pairs={{1,2},{3,4},{5,6},{7,8},{9,10},{11,12},{13,14},{15,16},{17,18},{19... | collective-permute-start | bytes 1966088 | tf_op jit(solution)/shard_map/ppermute | solution.py:735
  21.6 6.1 %all-to-all-done.got_ref = bf16[8,64,256]{2,1,0:T(8,128)(2,1)S(1)} async-done(((bf16[8,64,256]{2,1,0:T(8,128)(2,1)}), bf16[8,64,256]{2,1,0:T(8,128)(2,1)S(1)}, u32[]{:S(2)}, u32[]{:S(2)}) %all-to-all-start) | async-done | bytes 262176 | tf_op jit(solution)/shard_map/all_to_all | solution.py:729
  28.1 3.7 %tables_a.1 = (bf16[1024,1024]{1,0:T(8,128)(2,1)S(1)}, f32[64,1024]{1,0:T(8,128)S(1)}, f32[1,2048]{1,0:T(1,128)S(1)}, f32[8,128]{1,0:T(8,128)S(1)}, bf16[2048,25...) custom-call(s32[2,2]{1,0:T(2,128)S(1)} %copy-done.1, s32[2]{0:T(128)S(1)} %copy-done.2, bf16[2048,256]{1,0:T(8,128)(2,1)} %x_ref.3, ...), custom_call_target="tpu_custom_call" | custom-call | flops 700000000 | bytes 5000000 | tf_op jit(solution)/shard_map/tables_a/pallas_call | solution.py:306
  31.8 1.7 %collective-permute-start.1 = (bf16[64,256]{1,0:T(8,128)(2,1)S(1)}, bf16[64,256]{1,0:T(8,128)(2,1)S(1)}, u32[]{:S(2)}, u32[]{:S(2)}) collective-permute-start(bf16[64,256]{1,0:T(8,128)(2,1)S(1)} %join.1.after_ref.g0_ref), channel_id=1, source_target_pairs={{0,16},{8,24},{16,32},{24,40},{32,48},{40,56},{48,0},{56,8},{1,17}... | collective-permute-start | bytes 98312 | tf_op jit(solution)/shard_map/ppermute | solution.py:744
  33.4 2.9 %collective-permute-start.2 = (bf16[64,256]{1,0:T(8,128)(2,1)S(1)}, bf16[64,256]{1,0:T(8,128)(2,1)S(1)}, u32[]{:S(2)}, u32[]{:S(2)}) collective-permute-start(bf16[64,256]{1,0:T(8,128)(2,1)S(1)} %join.1.after_ref.g0_ref), channel_id=1, source_target_pairs={{0,32},{8,40},{16,48},{24,56},{32,0},{40,8},{48,16},{56,24},{1,33}... | collective-permute-start | bytes 98312 | tf_op jit(solution)/shard_map/ppermute | solution.py:744
  36.3 1.3 %collective-permute-start.3 = (bf16[64,256]{1,0:T(8,128)(2,1)S(1)}, bf16[64,256]{1,0:T(8,128)(2,1)S(1)}, u32[]{:S(2)}, u32[]{:S(2)}) collective-permute-start(bf16[64,256]{1,0:T(8,128)(2,1)S(1)} %join.1.after_ref.g0_ref), channel_id=1, source_target_pairs={{0,48},{8,56},{16,0},{24,8},{32,16},{40,24},{48,32},{56,40},{1,49}... | collective-permute-start | bytes 98312 | tf_op jit(solution)/shard_map/ppermute | solution.py:744
  37.7 3.1 %tables_b.1 = (bf16[1024,1024]{1,0:T(8,128)(2,1)S(1)}, bf16[1024,1024]{1,0:T(8,128)(2,1)S(1)}, f32[64,2048]{1,0:T(8,128)S(1)}) custom-call(f32[8,128]{1,0:T(8,128)S(1)} %get-tuple-element.41.after_ref.w_ref, bf16[2048,256]{1,0:T(8,128)(2,1)S(1)} %get-tuple-element.43.x_ref, f32[64,2048]{1,0:T(8,128)S(1)} %get-tuple-element.44.b_ref, ...), custom_call_target="tpu_custom_call" | custom-call | flops 1500000000 | bytes 7000000 | tf_op jit(solution)/shard_map/tables_b/pallas_call | solution.py:339
  41.1 1.6 %collective-permute-start.4 = (bf16[64,256]{1,0:T(8,128)(2,1)S(1)}, bf16[64,256]{1,0:T(8,128)(2,1)S(1)}, u32[]{:S(2)}, u32[]{:S(2)}) collective-permute-start(bf16[64,256]{1,0:T(8,128)(2,1)S(1)} %get-tuple-element.48.after_ref.g0_ref), channel_id=1, source_target_pairs={{0,64},{64,128},{128,192},{192,0},{1,65},{65,129},{129,193},{193,1... | collective-permute-start | bytes 98312 | tf_op jit(solution)/shard_map/ppermute | solution.py:744
  42.7 1.1 %collective-permute-start.5 = (bf16[64,256]{1,0:T(8,128)(2,1)S(1)}, bf16[64,256]{1,0:T(8,128)(2,1)S(1)}, u32[]{:S(2)}, u32[]{:S(2)}) collective-permute-start(bf16[64,256]{1,0:T(8,128)(2,1)S(1)} %get-tuple-element.48.after_ref.g0_ref), channel_id=1, source_target_pairs={{0,128},{64,192},{128,0},{192,64},{1,129},{65,193},{129,1},{193,65... | collective-permute-start | bytes 98312 | tf_op jit(solution)/shard_map/ppermute | solution.py:744
  43.8 2.2 %collective-permute-start.6 = (bf16[64,256]{1,0:T(8,128)(2,1)S(1)}, bf16[64,256]{1,0:T(8,128)(2,1)S(1)}, u32[]{:S(2)}, u32[]{:S(2)}) collective-permute-start(bf16[64,256]{1,0:T(8,128)(2,1)S(1)} %get-tuple-element.48.after_ref.g0_ref), channel_id=1, source_target_pairs={{0,192},{64,0},{128,64},{192,128},{1,193},{65,1},{129,65},{193,129... | collective-permute-start | bytes 98312 | tf_op jit(solution)/shard_map/ppermute | solution.py:744
  46.0 4.2 %around.1 = (bf16[1024,1024]{1,0:T(8,128)(2,1)S(1)}, bf16[1024,1024]{1,0:T(8,128)(2,1)S(1)}, f32[64,2048]{1,0:T(8,128)S(1)}) custom-call(f32[8,128]{1,0:T(8,128)S(1)} %get-tuple-element.41.after_ref.w_ref, bf16[1280,256]{1,0:T(8,128)(2,1)} %collective-permute-done.7.odd_ref, bf16[1280,256]{1,0:T(8,128)(2,1)} %collective-permute-done.8.even_ref, ...), custom_call_target="tpu_custom_call" | custom-call | flops 1400000000 | bytes 7000000 | tf_op jit(solution)/shard_map/around/pallas_call | solution.py:392
  50.1 1.7 %second.1 = (f32[64,2048]{1,0:T(8,128)S(1)}, bf16[64,2048]{1,0:T(8,128)(2,1)S(1)}, bf16[64,1024]{1,0:T(8,128)(2,1)S(1)}, bf16[64,1024]{1,0:T(8,128)(2,1)S(1)}) custom-call(bf16[64,256]{1,0:T(8,128)(2,1)S(1)} %get-tuple-element.48.after_ref.g0_ref, bf16[64,256]{1,0:T(8,128)(2,1)S(1)} %collective-permute-done.4.g1_ref, ...), custom_call_target="tpu_custom_call" | custom-call | flops 250000000 | bytes 5000000 | tf_op jit(solution)/shard_map/second/pallas_call | solution.py:503
  51.9 0.6 collective-permute-start.10
  52.5 2.7 %collective-permute-start.9 = (bf16[64,1024]{1,0:T(8,128)(2,1)S(1)}, bf16[64,1024]{1,0:T(8,128)(2,1)S(1)}, u32[]{:S(2)}, u32[]{:S(2)}) collective-permute-start(bf16[64,1024]{1,0:T(8,128)(2,1)S(1)} %get-tuple-element.56), channel_id=1, source_target_pairs={{1,2},{3,4},{5,6},{7,8},{9,10},{11,12},{13,14},{15,16},{17,18},{19... | collective-permute-start | bytes 393224 | tf_op jit(solution)/shard_map/ppermute | solution.py:735
  55.2 2.4 %third.1 = (f32[64,2048]{1,0:T(8,128)S(1)}, f32[64,256]{1,0:T(8,128)S(1)}, f32[64,128]{1,0:T(8,128)S(1)}) custom-call(f32[8,128]{1,0:T(8,128)S(1)} %get-tuple-element.41.after_ref.w_ref, f32[64,2048]{1,0:T(8,128)S(1)} %get-tuple-element.60.u_ref, f32[64,2048]{1,0:T(8,128)S(1)} %get-tuple-element.44.b_ref, bf16[64,2048]{1,0:T(8,128)(2,1)S(1)} %get-tuple-element.61.u16_ref, ...), custom_call_target="tpu_custom_call" | custom-call | flops 700000000 | bytes 10000000 | tf_op jit(solution)/shard_map/third/pallas_call | solution.py:544
  57.6 5.4 %collective-permute-done.9.odd_ref = bf16[64,1024]{1,0:T(8,128)(2,1)S(1)} collective-permute-done((bf16[64,1024]{1,0:T(8,128)(2,1)S(1)}, bf16[64,1024]{1,0:T(8,128)(2,1)S(1)}, u32[]{:S(2)}, u32[]{:S(2)}) %collective-permute-start.9) | collective-permute-done | bytes 131104 | tf_op jit(solution)/shard_map/ppermute | solution.py:735
  63.0 1.1 %finish.1 = (bf16[8,80,256]{2,1,0:T(8,128)(2,1)S(1)}, f32[64,2048]{1,0:T(8,128)S(1)}) custom-call(f32[8,128]{1,0:T(8,128)S(1)} %get-tuple-element.41.after_ref.w_ref, bf16[64,1024]{1,0:T(8,128)(2,1)S(1)} %collective-permute-done.9.odd_ref, bf16[64,1024]{1,0:T(8,128)(2,1)S(1)} %collective-permute-done.10.even_ref, ...), custom_call_target="tpu_custom_call" | custom-call | flops 270000000 | bytes 4000000 | tf_op jit(solution)/shard_map/finish/pallas_call | solution.py:606
  64.1 13.5 %all_to_all.10.refs_0_ = bf16[8,80,256]{2,1,0:T(8,128)(2,1)S(1)} all-to-all(bf16[8,80,256]{2,1,0:T(8,128)(2,1)S(1)} %get-tuple-element.68), channel_id=1, replica_groups=mesh['group'=4,'sub'=8,'leaf'=8] {'leaf'}, dimensions={0} | all-to-all | bytes 655360 | tf_op jit(solution)/shard_map/all_to_all | solution.py:729
  78.1 1.2 %collective-permute-done.11.right_ref = bf16[80,256]{1,0:T(8,128)(2,1)S(1)} collective-permute-done((bf16[80,256]{1,0:T(8,128)(2,1)S(1)}, bf16[80,256]{1,0:T(8,128)(2,1)S(1)}, u32[]{:S(2)}, u32[]{:S(2)}) %collective-permute-start.11) | collective-permute-done | bytes 40992 | tf_op jit(solution)/shard_map/ppermute | solution.py:753
  79.6 2.5 %collective-permute-start.13 = (bf16[80,256]{1,0:T(8,128)(2,1)S(1)}, bf16[80,256]{1,0:T(8,128)(2,1)S(1)}, u32[]{:S(2)}, u32[]{:S(2)}) collective-permute-start(bf16[80,256]{1,0:T(8,128)(2,1)S(1)} %join_sums.1.refs_0_), channel_id=1, source_target_pairs={{0,32},{8,40},{16,48},{24,56},{32,0},{40,8},{48,16},{56,24},{1,33}... | collective-permute-start | bytes 122888 | tf_op jit(solution)/shard_map/ppermute | solution.py:744
  82.1 1.9 %collective-permute-start.14 = (bf16[80,256]{1,0:T(8,128)(2,1)S(1)}, bf16[80,256]{1,0:T(8,128)(2,1)S(1)}, u32[]{:S(2)}, u32[]{:S(2)}) collective-permute-start(bf16[80,256]{1,0:T(8,128)(2,1)S(1)} %join_sums.1.refs_0_), channel_id=1, source_target_pairs={{0,48},{8,56},{16,0},{24,8},{32,16},{40,24},{48,32},{56,40},{1,49}... | collective-permute-start | bytes 122888 | tf_op jit(solution)/shard_map/ppermute | solution.py:744
  84.0 1.4 %collective-permute-done.12.refs_1_ = bf16[80,256]{1,0:T(8,128)(2,1)S(1)} collective-permute-done((bf16[80,256]{1,0:T(8,128)(2,1)S(1)}, bf16[80,256]{1,0:T(8,128)(2,1)S(1)}, u32[]{:S(2)}, u32[]{:S(2)}) %collective-permute-start.12) | collective-permute-done | bytes 40992 | tf_op jit(solution)/shard_map/ppermute | solution.py:744
  85.4 0.7 collective-permute-done.14.refs_3_
  86.1 0.3 climb_sums.3
  86.5 2.0 %collective-permute-start.15 = (bf16[80,256]{1,0:T(8,128)(2,1)S(1)}, bf16[80,256]{1,0:T(8,128)(2,1)S(1)}, u32[]{:S(2)}, u32[]{:S(2)}) collective-permute-start(bf16[80,256]{1,0:T(8,128)(2,1)S(1)} %get-tuple-element.70.g0_ref), channel_id=1, source_target_pairs={{0,64},{64,128},{128,192},{192,0},{1,65},{65,129},{129,193},{193,1... | collective-permute-start | bytes 122888 | tf_op jit(solution)/shard_map/ppermute | solution.py:744
  88.4 2.6 %collective-permute-start.16 = (bf16[80,256]{1,0:T(8,128)(2,1)S(1)}, bf16[80,256]{1,0:T(8,128)(2,1)S(1)}, u32[]{:S(2)}, u32[]{:S(2)}) collective-permute-start(bf16[80,256]{1,0:T(8,128)(2,1)S(1)} %get-tuple-element.70.g0_ref), channel_id=1, source_target_pairs={{0,128},{64,192},{128,0},{192,64},{1,129},{65,193},{129,1},{193,65... | collective-permute-start | bytes 122888 | tf_op jit(solution)/shard_map/ppermute | solution.py:744
  91.0 2.9 %collective-permute-done.16.g2_ref = bf16[80,256]{1,0:T(8,128)(2,1)S(1)} collective-permute-done((bf16[80,256]{1,0:T(8,128)(2,1)S(1)}, bf16[80,256]{1,0:T(8,128)(2,1)S(1)}, u32[]{:S(2)}, u32[]{:S(2)}) %collective-permute-start.16) | collective-permute-done | bytes 40992 | tf_op jit(solution)/shard_map/ppermute | solution.py:744
  93.9 1.1 %collective-permute-done.17.g3_ref = bf16[80,256]{1,0:T(8,128)(2,1)S(1)} collective-permute-done((bf16[80,256]{1,0:T(8,128)(2,1)S(1)}, bf16[80,256]{1,0:T(8,128)(2,1)S(1)}, u32[]{:S(2)}, u32[]{:S(2)}) %collective-permute-start.17) | collective-permute-done | bytes 40992 | tf_op jit(solution)/shard_map/ppermute | solution.py:744
  95.0 2.6 %last.1 = (f32[64,2048]{1,0:T(8,128)}, f32[64,2048]{1,0:T(8,128)}) custom-call(bf16[80,256]{1,0:T(8,128)(2,1)S(1)} %get-tuple-element.70.g0_ref, bf16[80,256]{1,0:T(8,128)(2,1)S(1)} %collective-permute-done.15.g1_ref, bf16[80,256]{1,0:T(8,128)(2,1)S(1)} %collective-permute-done.16.g2_ref, bf16[80,256]{1,0:T(8,128)(2,1)S(1)} %collective-permute-done.17.g3_ref, ...), custom_call_target="tpu_custom_call" | custom-call | flops 250000000 | bytes 7000000 | tf_op jit(solution)/shard_map/last/pallas_call | solution.py:711
  (27 shorter events, 1.5 us)
Async XLA Ops:
  0.6 27.4 %copy-start.1 = (s32[2,2]{1,0:T(2,128)S(1)}, s32[2,2]{1,0:T(2,128)}, u32[]{:S(2)}) copy-start(s32[2,2]{1,0:T(2,128)} %nb_ref.1) | copy-start | bytes 52
  0.6 27.4 %copy-start.2 = (s32[2]{0:T(128)S(1)}, s32[2]{0:T(128)}, u32[]{:S(2)}) copy-start(s32[2]{0:T(128)} %ct_ref.1) | copy-start | bytes 28
  5.7 0.8 copy-start
  6.5 21.1 %all-to-all-start = ((bf16[8,64,256]{2,1,0:T(8,128)(2,1)}), bf16[8,64,256]{2,1,0:T(8,128)(2,1)S(1)}, u32[]{:S(2)}, u32[]{:S(2)}) async-start(bf16[8,64,256]{2,1,0:T(8,128)(2,1)} %get-tuple-element.38), calls=%async_computation | async-start | bytes 524288 | tf_op jit(solution)/shard_map/all_to_all | solution.py:729
  15.0 30.9 %collective-permute-start.7 = (bf16[1280,256]{1,0:T(8,128)(2,1)}, bf16[1280,256]{1,0:T(8,128)(2,1)}, u32[]{:S(2)}, u32[]{:S(2)}) collective-permute-start(bf16[1280,256]{1,0:T(8,128)(2,1)} %copy-done), channel_id=1, source_target_pairs={{1,2},{3,4},{5,6},{7,8},{9,10},{11,12},{13,14},{15,16},{17,18},{19... | collective-permute-start | bytes 1966088 | tf_op jit(solution)/shard_map/ppermute | solution.py:735
  21.5 24.5 %collective-permute-start.8 = (bf16[1280,256]{1,0:T(8,128)(2,1)S(1)}, bf16[1280,256]{1,0:T(8,128)(2,1)}, u32[]{:S(2)}, u32[]{:S(2)}) collective-permute-start(bf16[1280,256]{1,0:T(8,128)(2,1)S(1)} %get-tuple-element.54), channel_id=1, source_target_pairs={{0,1},{2,3},{4,5},{6,7},{8,9},{10,11},{12,13},{14,15},{16,17},{18,... | collective-permute-start | bytes 1966088 | tf_op jit(solution)/shard_map/ppermute | solution.py:735
  28.0 3.8 %collective-permute-start = (bf16[64,256]{1,0:T(8,128)(2,1)S(1)}, bf16[64,256]{1,0:T(8,128)(2,1)S(1)}, u32[]{:S(2)}, u32[]{:S(2)}) collective-permute-start(bf16[64,256]{1,0:T(8,128)(2,1)S(1)} %get-tuple-element.40.after_ref.left_ref), channel_id=1, source_target_pairs={{0,8},{8,0},{16,24},{24,16},{32,40},{40,32},{48,56},{56,48},{1,9},... | collective-permute-start | bytes 98312 | tf_op jit(solution)/shard_map/ppermute | solution.py:753
  31.8 9.0 %collective-permute-start.1 = (bf16[64,256]{1,0:T(8,128)(2,1)S(1)}, bf16[64,256]{1,0:T(8,128)(2,1)S(1)}, u32[]{:S(2)}, u32[]{:S(2)}) collective-permute-start(bf16[64,256]{1,0:T(8,128)(2,1)S(1)} %join.1.after_ref.g0_ref), channel_id=1, source_target_pairs={{0,16},{8,24},{16,32},{24,40},{32,48},{40,56},{48,0},{56,8},{1,17}... | collective-permute-start | bytes 98312 | tf_op jit(solution)/shard_map/ppermute | solution.py:744
  33.4 7.4 %collective-permute-start.2 = (bf16[64,256]{1,0:T(8,128)(2,1)S(1)}, bf16[64,256]{1,0:T(8,128)(2,1)S(1)}, u32[]{:S(2)}, u32[]{:S(2)}) collective-permute-start(bf16[64,256]{1,0:T(8,128)(2,1)S(1)} %join.1.after_ref.g0_ref), channel_id=1, source_target_pairs={{0,32},{8,40},{16,48},{24,56},{32,0},{40,8},{48,16},{56,24},{1,33}... | collective-permute-start | bytes 98312 | tf_op jit(solution)/shard_map/ppermute | solution.py:744
  36.3 4.5 %collective-permute-start.3 = (bf16[64,256]{1,0:T(8,128)(2,1)S(1)}, bf16[64,256]{1,0:T(8,128)(2,1)S(1)}, u32[]{:S(2)}, u32[]{:S(2)}) collective-permute-start(bf16[64,256]{1,0:T(8,128)(2,1)S(1)} %join.1.after_ref.g0_ref), channel_id=1, source_target_pairs={{0,48},{8,56},{16,0},{24,8},{32,16},{40,24},{48,32},{56,40},{1,49}... | collective-permute-start | bytes 98312 | tf_op jit(solution)/shard_map/ppermute | solution.py:744
  41.1 9.0 %collective-permute-start.4 = (bf16[64,256]{1,0:T(8,128)(2,1)S(1)}, bf16[64,256]{1,0:T(8,128)(2,1)S(1)}, u32[]{:S(2)}, u32[]{:S(2)}) collective-permute-start(bf16[64,256]{1,0:T(8,128)(2,1)S(1)} %get-tuple-element.48.after_ref.g0_ref), channel_id=1, source_target_pairs={{0,64},{64,128},{128,192},{192,0},{1,65},{65,129},{129,193},{193,1... | collective-permute-start | bytes 98312 | tf_op jit(solution)/shard_map/ppermute | solution.py:744
  42.7 7.5 %collective-permute-start.5 = (bf16[64,256]{1,0:T(8,128)(2,1)S(1)}, bf16[64,256]{1,0:T(8,128)(2,1)S(1)}, u32[]{:S(2)}, u32[]{:S(2)}) collective-permute-start(bf16[64,256]{1,0:T(8,128)(2,1)S(1)} %get-tuple-element.48.after_ref.g0_ref), channel_id=1, source_target_pairs={{0,128},{64,192},{128,0},{192,64},{1,129},{65,193},{129,1},{193,65... | collective-permute-start | bytes 98312 | tf_op jit(solution)/shard_map/ppermute | solution.py:744
  43.8 6.3 %collective-permute-start.6 = (bf16[64,256]{1,0:T(8,128)(2,1)S(1)}, bf16[64,256]{1,0:T(8,128)(2,1)S(1)}, u32[]{:S(2)}, u32[]{:S(2)}) collective-permute-start(bf16[64,256]{1,0:T(8,128)(2,1)S(1)} %get-tuple-element.48.after_ref.g0_ref), channel_id=1, source_target_pairs={{0,192},{64,0},{128,64},{192,128},{1,193},{65,1},{129,65},{193,129... | collective-permute-start | bytes 98312 | tf_op jit(solution)/shard_map/ppermute | solution.py:744
  51.9 5.7 %collective-permute-start.10 = (bf16[64,1024]{1,0:T(8,128)(2,1)S(1)}, bf16[64,1024]{1,0:T(8,128)(2,1)S(1)}, u32[]{:S(2)}, u32[]{:S(2)}) collective-permute-start(bf16[64,1024]{1,0:T(8,128)(2,1)S(1)} %get-tuple-element.57), channel_id=1, source_target_pairs={{0,1},{2,3},{4,5},{6,7},{8,9},{10,11},{12,13},{14,15},{16,17},{18,... | collective-permute-start | bytes 393224 | tf_op jit(solution)/shard_map/ppermute | solution.py:735
  52.5 10.5 %collective-permute-start.9 = (bf16[64,1024]{1,0:T(8,128)(2,1)S(1)}, bf16[64,1024]{1,0:T(8,128)(2,1)S(1)}, u32[]{:S(2)}, u32[]{:S(2)}) collective-permute-start(bf16[64,1024]{1,0:T(8,128)(2,1)S(1)} %get-tuple-element.56), channel_id=1, source_target_pairs={{1,2},{3,4},{5,6},{7,8},{9,10},{11,12},{13,14},{15,16},{17,18},{19... | collective-permute-start | bytes 393224 | tf_op jit(solution)/shard_map/ppermute | solution.py:735
  78.0 1.3 %collective-permute-start.11 = (bf16[80,256]{1,0:T(8,128)(2,1)S(1)}, bf16[80,256]{1,0:T(8,128)(2,1)S(1)}, u32[]{:S(2)}, u32[]{:S(2)}) collective-permute-start(bf16[80,256]{1,0:T(8,128)(2,1)S(1)} %get-tuple-element.69.left_ref), channel_id=1, source_target_pairs={{0,8},{8,0},{16,24},{24,16},{32,40},{40,32},{48,56},{56,48},{1,9},... | collective-permute-start | bytes 122888 | tf_op jit(solution)/shard_map/ppermute | solution.py:753
  79.6 5.8 %collective-permute-start.12 = (bf16[80,256]{1,0:T(8,128)(2,1)S(1)}, bf16[80,256]{1,0:T(8,128)(2,1)S(1)}, u32[]{:S(2)}, u32[]{:S(2)}) collective-permute-start(bf16[80,256]{1,0:T(8,128)(2,1)S(1)} %join_sums.1.refs_0_), channel_id=1, source_target_pairs={{0,16},{8,24},{16,32},{24,40},{32,48},{40,56},{48,0},{56,8},{1,17}... | collective-permute-start | bytes 122888 | tf_op jit(solution)/shard_map/ppermute | solution.py:744
  79.6 5.8 %collective-permute-start.13 = (bf16[80,256]{1,0:T(8,128)(2,1)S(1)}, bf16[80,256]{1,0:T(8,128)(2,1)S(1)}, u32[]{:S(2)}, u32[]{:S(2)}) collective-permute-start(bf16[80,256]{1,0:T(8,128)(2,1)S(1)} %join_sums.1.refs_0_), channel_id=1, source_target_pairs={{0,32},{8,40},{16,48},{24,56},{32,0},{40,8},{48,16},{56,24},{1,33}... | collective-permute-start | bytes 122888 | tf_op jit(solution)/shard_map/ppermute | solution.py:744
  82.1 4.0 %collective-permute-start.14 = (bf16[80,256]{1,0:T(8,128)(2,1)S(1)}, bf16[80,256]{1,0:T(8,128)(2,1)S(1)}, u32[]{:S(2)}, u32[]{:S(2)}) collective-permute-start(bf16[80,256]{1,0:T(8,128)(2,1)S(1)} %join_sums.1.refs_0_), channel_id=1, source_target_pairs={{0,48},{8,56},{16,0},{24,8},{32,16},{40,24},{48,32},{56,40},{1,49}... | collective-permute-start | bytes 122888 | tf_op jit(solution)/shard_map/ppermute | solution.py:744
  86.5 4.6 %collective-permute-start.15 = (bf16[80,256]{1,0:T(8,128)(2,1)S(1)}, bf16[80,256]{1,0:T(8,128)(2,1)S(1)}, u32[]{:S(2)}, u32[]{:S(2)}) collective-permute-start(bf16[80,256]{1,0:T(8,128)(2,1)S(1)} %get-tuple-element.70.g0_ref), channel_id=1, source_target_pairs={{0,64},{64,128},{128,192},{192,0},{1,65},{65,129},{129,193},{193,1... | collective-permute-start | bytes 122888 | tf_op jit(solution)/shard_map/ppermute | solution.py:744
  88.4 5.5 %collective-permute-start.16 = (bf16[80,256]{1,0:T(8,128)(2,1)S(1)}, bf16[80,256]{1,0:T(8,128)(2,1)S(1)}, u32[]{:S(2)}, u32[]{:S(2)}) collective-permute-start(bf16[80,256]{1,0:T(8,128)(2,1)S(1)} %get-tuple-element.70.g0_ref), channel_id=1, source_target_pairs={{0,128},{64,192},{128,0},{192,64},{1,129},{65,193},{129,1},{193,65... | collective-permute-start | bytes 122888 | tf_op jit(solution)/shard_map/ppermute | solution.py:744
  91.0 4.0 %collective-permute-start.17 = (bf16[80,256]{1,0:T(8,128)(2,1)S(1)}, bf16[80,256]{1,0:T(8,128)(2,1)S(1)}, u32[]{:S(2)}, u32[]{:S(2)}) collective-permute-start(bf16[80,256]{1,0:T(8,128)(2,1)S(1)} %get-tuple-element.70.g0_ref), channel_id=1, source_target_pairs={{0,192},{64,0},{128,64},{192,128},{1,193},{65,1},{129,65},{193,129... | collective-permute-start | bytes 122888 | tf_op jit(solution)/shard_map/ppermute | solution.py:744

commit v6 on v5

--- a/solution.py
+++ b/solution.py
@@ -80,16 +80,14 @@
     return high, low
 
 
-def up_dot(field, table_high, table_low):
-    high, low = split(field)
-    both = nn(jnp.concatenate([high, low], axis=0), table_high)
-    return both[:RHS] + both[RHS:] + nn(high, table_low)
-
-
-def down_dot(weights, table_high, table_low):
-    high, low = split(weights)
-    both = nt(jnp.concatenate([high, low], axis=0), table_high)
-    return both[:RHS] + both[RHS:] + nt(high, table_low)
+def up_dot(field, table):
+    both = nn(jnp.concatenate(split(field), axis=0), table)
+    return both[:RHS] + both[RHS:]
+
+
+def down_dot(weights, table):
+    both = nt(jnp.concatenate(split(weights), axis=0), table)
+    return both[:RHS] + both[RHS:]
 
 
 def even_leaf():
@@ -105,13 +103,12 @@
 
 
 def start_kernel(
-    x_ref, b_ref, z1_ref, z2_ref, z3_ref,
-    sent_ref, gh_ref, gl_ref, t1_ref, t2_ref, odd_ref, even_ref,
-    xv_ref, bv_ref, z_ref, fold_ref, x_sem, b_sem, z_sem, out_sem
+    x_ref, b_ref, z1_ref, z2_ref,
+    sent_ref, g_ref, t1_ref, xv_ref, bv_ref, gv_ref, z_ref, x_sem, b_sem, z_sem, g_sem
 ):
     parts = x_ref.shape[0] // WIDE
     z_loads, x_loads, b_loads = [], [], []
-    for k, source in enumerate((z1_ref, z2_ref, z3_ref)):
+    for k, source in enumerate((z1_ref, z2_ref)):
         z_loads.append(pltpu.make_async_copy(source, z_ref.at[k], z_sem.at[k]))
     for k in range(parts):
         rows = pl.ds(k * WIDE, WIDE)
@@ -122,7 +119,62 @@
         x_loads[k].start()
         b_loads[k].start()
     z_loads[1].start()
-    z_loads[2].start()
+    stores = []
+    z_loads[0].wait()
+    z1 = z_ref[0]
+    row = right_row(z1)
+    total = jnp.zeros((RHS, SKEL), f32)
+    for k in range(parts):
+        rows = slice(k * WIDE, (k + 1) * WIDE)
+        x_loads[k].wait()
+        part = xv_ref[rows, :]
+        table = gauss(part, left_column(part), z1, row).astype(bf16)
+        gv_ref[rows, :] = table
+        place = pl.ds(k * WIDE, WIDE)
+        store = pltpu.make_async_copy(gv_ref.at[place, :], g_ref.at[place, :], g_sem.at[k])
+        store.start()
+        stores.append(store)
+        b_loads[k].wait()
+        total += up_dot(bv_ref[:, rows], table)
+    value = (total * (1.0 / LEAF)).astype(bf16)
+    for k in range(sent_ref.shape[0]):
+        sent_ref[k] = value
+    z_loads[1].wait()
+    z2 = z_ref[1]
+    t1_ref[...] = gauss(z1, left_column(z1), z2, right_row(z2))
+    for store in stores:
+        store.wait()
+
+
+def start_call(points, field, z1, z2, peers):
+    count = points.shape[0]
+    parts = count // WIDE
+    return pl.pallas_call(
+        start_kernel,
+        in_specs=outside(4),
+        out_specs=tuple(inside(1) + outside(1) + inside(3)),
+        out_shape=(
+            shape_of((peers, RHS, SKEL), bf16),
+            pltpu.HBM((count, SKEL), bf16),
+            shape_of((SKEL, SKEL), f32),
+            shape_of((count, DIM), bf16),
+            shape_of((RHS, count), f32),
+        ),
+        scratch_shapes=[
+            pltpu.VMEM((count, SKEL), bf16),
+            pltpu.VMEM((2, SKEL, DIM), bf16),
+            pltpu.SemaphoreType.DMA((parts,)),
+            pltpu.SemaphoreType.DMA((parts,)),
+            pltpu.SemaphoreType.DMA((2,)),
+            pltpu.SemaphoreType.DMA((parts,)),
+        ],
+        compiler_params=params,
+        cost_estimate=cost(600_000_000, 5_000_000, 655_360),
+        name="start",
+    )(*(in_hbm(value) for value in (points, field, z1, z2)))
+
+
+def pack_kernel(x_ref, b_ref, odd_ref, even_ref, fold_ref, out_sem):
     parity = lax.rem(lax.axis_index("leaf"), 2)
     halves = (parity, 1 - parity)
     stores = []
@@ -133,22 +185,9 @@
         )
     for store in stores:
         store.start()
-    z_loads[0].wait()
-    z1 = z_ref[0]
-    row = right_row(z1)
-    total = jnp.zeros((RHS, SKEL), f32)
-    for k in range(parts):
-        rows = slice(k * WIDE, (k + 1) * WIDE)
-        x_loads[k].wait()
-        part = xv_ref[rows, :]
-        high, low = split(gauss(part, left_column(part), z1, row))
-        gh_ref[rows, :] = high
-        gl_ref[rows, :] = low
-        b_loads[k].wait()
-        total += up_dot(bv_ref[:, rows], high, low)
     for half in range(2):
         for k in range(STEPS):
-            fold_ref[half, k * RHS : (k + 1) * RHS, :] = bv_ref[
+            fold_ref[half, k * RHS : (k + 1) * RHS, :] = b_ref[
                 :, half * LEAF + k * ROWS : half * LEAF + (k + 1) * ROWS
             ].astype(bf16)
     for k, out_ref in enumerate((odd_ref, even_ref)):
@@ -159,48 +198,27 @@
         )
     for store in stores[2:]:
         store.start()
-    value = (total * (1.0 / LEAF)).astype(bf16)
-    for k in range(sent_ref.shape[0]):
-        sent_ref[k] = value
-    z_loads[1].wait()
-    z_loads[2].wait()
-    z2, z3 = z_ref[1], z_ref[2]
-    t1_ref[...] = gauss(z1, left_column(z1), z2, right_row(z2))
-    t2_ref[...] = gauss(z2, left_column(z2), z3, right_row(z3))
     for store in stores:
         store.wait()
 
 
-def start_call(points, field, z1, z2, z3, peers):
-    count = points.shape[0]
-    parts = count // WIDE
-    return pl.pallas_call(
-        start_kernel,
-        in_specs=outside(5),
-        out_specs=tuple(inside(5) + outside(2)),
+def pack_call(points, field):
+    return pl.pallas_call(
+        pack_kernel,
+        in_specs=inside(2),
+        out_specs=tuple(outside(2)),
         out_shape=(
-            shape_of((peers, RHS, SKEL), bf16),
-            shape_of((count, SKEL), bf16),
-            shape_of((count, SKEL), bf16),
-            shape_of((SKEL, SKEL), f32),
-            shape_of((SKEL, SKEL), f32),
-            shape_of((LEAF + STEPS * RHS, DIM), bf16),
-            shape_of((LEAF + STEPS * RHS, DIM), bf16),
+            pltpu.HBM((LEAF + STEPS * RHS, DIM), bf16),
+            pltpu.HBM((LEAF + STEPS * RHS, DIM), bf16),
         ),
         scratch_shapes=[
-            pltpu.VMEM((count, DIM), bf16),
-            pltpu.VMEM((RHS, count), f32),
-            pltpu.VMEM((3, SKEL, DIM), bf16),
             pltpu.VMEM((2, STEPS * RHS, ROWS), bf16),
-            pltpu.SemaphoreType.DMA((parts,)),
-            pltpu.SemaphoreType.DMA((parts,)),
-            pltpu.SemaphoreType.DMA((3,)),
             pltpu.SemaphoreType.DMA((4,)),
         ],
         compiler_params=params,
-        cost_estimate=cost(600_000_000, 5_000_000, 655_360),
-        name="start",
-    )(*(in_hbm(value) for value in (points, field, z1, z2, z3)))
+        cost_estimate=cost(1_000_000, 5_000_000),
+        name="pack",
+    )(points, field)
 
 
 def smem():
@@ -266,18 +284,14 @@
         table_ref[block(i), :] = gauss(rows, left_column(rows), points, row).astype(bf16)
 
 
-def tables_a_kernel(
-    nb_ref, ct_ref, x_ref, b_ref, after_ref,
-    table_ref, own_ref, row_ref, w_ref, xv_ref, bv_ref, x_sem, b_sem
+def prepare_kernel(
+    nb_ref, ct_ref, x_ref, z2_ref, z3_ref, after_ref, row_ref, w_ref, t2_ref, z_ref, z_sem
 ):
     del after_ref
-    x_loads, b_loads = [], []
-    for k in range(2):
-        part = pl.ds(k * LEAF, LEAF)
-        x_loads.append(pltpu.make_async_copy(x_ref.at[part, :], xv_ref.at[part, :], x_sem.at[k]))
-        b_loads.append(pltpu.make_async_copy(b_ref.at[:, part], bv_ref.at[:, part], b_sem.at[k]))
-    for load in (x_loads[0], b_loads[0], x_loads[1], b_loads[1]):
-        load.start()
+    loads = []
+    for k, source in enumerate((z2_ref, z3_ref)):
+        loads.append(pltpu.make_async_copy(source, z_ref.at[k], z_sem.at[k]))
+        loads[k].start()
     first = first_leaf_of()
     weights = (
         listed(nb_ref, ct_ref, 0, first - 1),
@@ -290,64 +304,50 @@
     for k in range(4):
         spread = jnp.where(place == k, weights[k], spread)
     w_ref[...] = spread
-    x_loads[0].wait()
-    x_a = xv_ref[:LEAF, :]
-    row_ref[:, :LEAF] = right_row(x_a)
-    make_symmetric(x_a, row_ref[:, :LEAF], table_ref)
-    b_loads[0].wait()
-    own_ref[...] = dot_symmetric(bv_ref[:, :LEAF].astype(bf16), table_ref)
-    x_loads[1].wait()
-    row_ref[:, LEAF:] = right_row(xv_ref[LEAF:, :])
-    b_loads[1].wait()
-
-
-def tables_a_call(neighbors, counts, points, field, after):
-    count = points.shape[0]
-    return pl.pallas_call(
-        tables_a_kernel,
-        in_specs=[smem(), smem()] + outside(2) + [anywhere()],
+    row_ref[...] = right_row(x_ref[...])
+    for load in loads:
+        load.wait()
+    z2, z3 = z_ref[0], z_ref[1]
+    t2_ref[...] = gauss(z2, left_column(z2), z3, right_row(z3))
+
+
+def prepare_call(neighbors, counts, points, z2, z3, after):
+    return pl.pallas_call(
+        prepare_kernel,
+        in_specs=[smem(), smem()] + inside(1) + outside(2) + [anywhere()],
         out_shape=(
-            shape_of((LEAF, LEAF), bf16),
-            shape_of((RHS, LEAF), f32),
             shape_of((1, 2 * LEAF), f32),
             shape_of((8, 128), f32),
-            shape_of((count, DIM), bf16),
-            shape_of((RHS, count), f32),
+            shape_of((SKEL, SKEL), f32),
         ),
-        scratch_shapes=[pltpu.SemaphoreType.DMA((2,)), pltpu.SemaphoreType.DMA((2,))],
-        compiler_params=params,
-        cost_estimate=cost(700_000_000, 5_000_000, 700_000),
-        name="tables_a",
-    )(neighbors, counts, in_hbm(points), in_hbm(field), after)
-
-
-def tables_b_kernel(
-    w_ref, x_ref, b_ref, row_ref, own_a_ref, after_ref, table_b_ref, table_ab_ref, own_ref
-):
+        scratch_shapes=[pltpu.VMEM((2, SKEL, DIM), bf16), pltpu.SemaphoreType.DMA((2,))],
+        compiler_params=params,
+        cost_estimate=cost(50_000_000, 2_000_000, 65_536),
+        name="prepare",
+    )(neighbors, counts, points, in_hbm(z2), in_hbm(z3), after)
+
+
+def tables_kernel(x_ref, b_ref, row_ref, after_ref, table_a_ref, table_b_ref, own_ref):
     del after_ref
-    x_a, x_b = x_ref[:LEAF, :], x_ref[LEAF:, :]
-    make_symmetric(x_b, row_ref[:, LEAF:], table_b_ref)
-    make_block(x_a, x_b, row_ref[:, LEAF:], table_ab_ref)
-    b_a, b_b = b_ref[:, :LEAF].astype(bf16), b_ref[:, LEAF:].astype(bf16)
-    own_ref[:, :LEAF] = own_a_ref[...] + weight_of(w_ref, 1) * nt(b_b, table_ab_ref[...])
-    own_ref[:, LEAF:] = dot_symmetric(b_b, table_b_ref) + weight_of(w_ref, 2) * nn(
-        b_a, table_ab_ref[...]
-    )
-
-
-def tables_b_call(w, points, field, row, own_a, after):
-    return pl.pallas_call(
-        tables_b_kernel,
-        in_specs=inside(5) + [anywhere()],
+    make_symmetric(x_ref[:LEAF, :], row_ref[:, :LEAF], table_a_ref)
+    make_symmetric(x_ref[LEAF:, :], row_ref[:, LEAF:], table_b_ref)
+    own_ref[:, :LEAF] = dot_symmetric(b_ref[:, :LEAF].astype(bf16), table_a_ref)
+    own_ref[:, LEAF:] = dot_symmetric(b_ref[:, LEAF:].astype(bf16), table_b_ref)
+
+
+def tables_call(points, field, row, after):
+    return pl.pallas_call(
+        tables_kernel,
+        in_specs=inside(3) + [anywhere()],
         out_shape=(
             shape_of((LEAF, LEAF), bf16),
             shape_of((LEAF, LEAF), bf16),
             shape_of((RHS, 2 * LEAF), f32),
         ),
         compiler_params=params,
-        cost_estimate=cost(1_500_000_000, 7_000_000, 1_800_000),
-        name="tables_b",
-    )(w, points, field, row, own_a, after)
+        cost_estimate=cost(2_200_000_000, 9_000_000, 2_400_000),
+        name="tables",
+    )(points, field, row, after)
 
 
 def unfold(halo):
@@ -362,18 +362,24 @@
 
 
 def around_kernel(
-    w_ref, odd_ref, even_ref, x_ref, row_ref, own_ref, after_ref,
-    below_table_ref, above_table_ref, out_ref
+    w_ref, odd_ref, even_ref, x_ref, b_ref, row_ref, own_ref, after_ref,
+    table_ab_ref, below_table_ref, above_table_ref, out_ref
 ):
     del after_ref
+    x_a, x_b = x_ref[:LEAF, :], x_ref[LEAF:, :]
+    row_a, row_b = row_ref[:, :LEAF], row_ref[:, LEAF:]
+    b_a, b_b = b_ref[:, :LEAF].astype(bf16), b_ref[:, LEAF:].astype(bf16)
+    make_block(x_a, x_b, row_b, table_ab_ref)
+    near_a = own_ref[:, :LEAF] + weight_of(w_ref, 1) * nt(b_b, table_ab_ref[...])
+    near_b = own_ref[:, LEAF:] + weight_of(w_ref, 2) * nn(b_a, table_ab_ref[...])
 
     def build(below_ref, above_ref):
-        make_block(below_ref, x_ref[:LEAF, :], row_ref[:, :LEAF], below_table_ref)
-        out_ref[:, :LEAF] = own_ref[:, :LEAF] + weight_of(w_ref, 0) * nn(
+        make_block(below_ref, x_a, row_a, below_table_ref)
+        out_ref[:, :LEAF] = near_a + weight_of(w_ref, 0) * nn(
             unfold(below_ref), below_table_ref[...]
         )
-        make_block(above_ref, x_ref[LEAF:, :], row_ref[:, LEAF:], above_table_ref)
-        out_ref[:, LEAF:] = own_ref[:, LEAF:] + weight_of(w_ref, 3) * nn(
+        make_block(above_ref, x_b, row_b, above_table_ref)
+        out_ref[:, LEAF:] = near_b + weight_of(w_ref, 3) * nn(
             unfold(above_ref), above_table_ref[...]
         )
 
@@ -388,19 +394,20 @@
         build(even_ref, odd_ref)
 
 
-def around_call(w, odd, even, points, row, own, after):
+def around_call(w, odd, even, points, field, row, own, after):
     return pl.pallas_call(
         around_kernel,
-        in_specs=inside(6) + [anywhere()],
+        in_specs=inside(7) + [anywhere()],
         out_shape=(
+            shape_of((LEAF, LEAF), bf16),
             shape_of((LEAF, LEAF), bf16),
             shape_of((LEAF, LEAF), bf16),
             shape_of((RHS, 2 * LEAF), f32),
         ),
         compiler_params=params,
-        cost_estimate=cost(1_400_000_000, 7_000_000, 2_097_152),
+        cost_estimate=cost(2_200_000_000, 9_000_000, 3_145_728),
         name="around",
-    )(w, odd, even, points, row, own, after)
+    )(w, odd, even, points, field, row, own, after)
 
 
 def total_of(got_ref):
@@ -475,14 +482,14 @@
 
 
 def second_kernel(
-    g0_ref, g1_ref, g2_ref, g3_ref, p1_ref, p2_ref, t1_ref, t2_ref, gh_ref, gl_ref, own_ref,
+    g0_ref, g1_ref, g2_ref, g3_ref, p1_ref, p2_ref, t1_ref, t2_ref, g_ref, own_ref,
     u_ref, u16_ref, odd_ref, even_ref
 ):
     top = sum_of((g0_ref, g1_ref, g2_ref, g3_ref))
     weights = down_weights(p1_ref[...], p2_ref[...], top, t1_ref[...], t2_ref[...])
     for k in range(2):
         part = slice(k * LEAF, (k + 1) * LEAF)
-        far = down_dot(weights, gh_ref[part, :], gl_ref[part, :])
+        far = down_dot(weights, g_ref[part, :])
         value = (own_ref[:, part] + far) * (1.0 / LEAF)
         u_ref[:, part] = value
         u16_ref[:, part] = value.astype(bf16)
@@ -499,10 +506,10 @@
         even_ref[...] = u16_ref[:, :LEAF]
 
 
-def second_call(parts, p1, p2, t1, t2, gh, gl, own):
+def second_call(parts, p1, p2, t1, t2, table, own):
     return pl.pallas_call(
         second_kernel,
-        in_specs=inside(11),
+        in_specs=inside(10),
         out_shape=(
             shape_of((RHS, 2 * LEAF), f32),
             shape_of((RHS, 2 * LEAF), bf16),
@@ -512,7 +519,7 @@
         compiler_params=params,
         cost_estimate=cost(250_000_000, 5_000_000),
         name="second",
-    )(*parts, p1, p2, t1, t2, gh, gl, own)
+    )(*parts, p1, p2, t1, t2, table, own)
 
 
 def row_sum(value):
@@ -521,9 +528,9 @@
 
 def third_kernel(
     w_ref, u_ref, b_ref, u16_ref, table_a_ref, table_b_ref, table_ab_ref,
-    gh_ref, gl_ref, out_ref, up_ref, sums_ref
+    g_ref, out_ref, up_ref, sums_ref
 ):
-    up_ref[...] = up_dot(u_ref[...], gh_ref[...], gl_ref[...])
+    up_ref[...] = up_dot(u_ref[...], g_ref[...])
     u_a, u_b = u16_ref[:, :LEAF], u16_ref[:, LEAF:]
     out_ref[:, :LEAF] = dot_symmetric(u_a, table_a_ref) + weight_of(w_ref, 1) * nt(
         u_b, table_ab_ref[...]
@@ -540,10 +547,10 @@
     sums_ref[...] = total
 
 
-def third_call(w, u, field, u16, table_a, table_b, table_ab, gh, gl):
+def third_call(w, u, field, u16, table_a, table_b, table_ab, table):
     return pl.pallas_call(
         third_kernel,
-        in_specs=inside(9),
+        in_specs=inside(8),
         out_shape=(
             shape_of((RHS, 2 * LEAF), f32),
             shape_of((RHS, SKEL), f32),
@@ -552,7 +559,7 @@
         compiler_params=params,
         cost_estimate=cost(700_000_000, 10_000_000),
         name="third",
-    )(w, u, field, u16, table_a, table_b, table_ab, gh, gl)
+    )(w, u, field, u16, table_a, table_b, table_ab, table)
 
 
 def rows_of(sums):
@@ -565,14 +572,15 @@
     packed += jnp.where((lane >= 4) & (lane < 8), pltpu.roll(middle, 4, 1), 0.0)
     packed += jnp.where((lane >= 8) & (lane < 12), pltpu.roll(low, 8, 1), 0.0)
     turned = packed.T[:16]
-    return jnp.concatenate([turned, jnp.zeros((16, SKEL - RHS), f32)], axis=1)
+    pieces = [turned[4 * k : 4 * k + 4] for k in range(4)]
+    row = jnp.concatenate(pieces, axis=1)
+    return jnp.concatenate([row, jnp.zeros((4, SKEL), f32)], axis=0)
 
 
 def sums_of(rows):
-    turned = jnp.concatenate([rows[:, :RHS], jnp.zeros((112, RHS), f32)], axis=0).T
-    total = turned + (pltpu.roll(turned, 124, 1) + pltpu.roll(turned, 120, 1))
-    lane = lax.broadcasted_iota(jnp.int32, (RHS, 128), 1)
-    return jnp.where(lane < 4, total, 0.0)
+    high, middle, low = (rows[:4, k * RHS : (k + 1) * RHS] for k in range(3))
+    total = high + (middle + low)
+    return jnp.concatenate([total, jnp.zeros((124, RHS), f32)], axis=0).T
 
 
 def put_all(sent_ref, value, sums):
@@ -607,7 +615,7 @@
         finish_kernel,
         in_specs=inside(9),
         out_shape=(
-            shape_of((peers, RHS + 16, SKEL), bf16),
+            shape_of((peers, RHS + 8, SKEL), bf16),
             shape_of((RHS, 2 * LEAF), f32),
         ),
         compiler_params=params,
@@ -638,7 +646,7 @@
     return pl.pallas_call(
         lambda *refs: kernel(level, *refs),
         in_specs=inside(len(inputs) + 1),
-        out_shape=(shape_of((RHS, SKEL), f32), shape_of((RHS + 16, SKEL), bf16)),
+        out_shape=(shape_of((RHS, SKEL), f32), shape_of((RHS + 8, SKEL), bf16)),
         compiler_params=params,
         cost_estimate=cost(50_000_000, 900_000),
         name="climb_sums",
@@ -654,7 +662,7 @@
     return pl.pallas_call(
         join_sums_kernel,
         in_specs=inside(2),
-        out_shape=shape_of((RHS + 16, SKEL), bf16),
+        out_shape=shape_of((RHS + 8, SKEL), bf16),
         compiler_params=params,
         cost_estimate=cost(100_000, 100_000),
         name="join_sums",
@@ -662,7 +670,7 @@
 
 
 def last_kernel(
-    g0_ref, g1_ref, g2_ref, g3_ref, p1_ref, p2_ref, t1_ref, t2_ref, gh_ref, gl_ref, near_ref,
+    g0_ref, g1_ref, g2_ref, g3_ref, p1_ref, p2_ref, t1_ref, t2_ref, g_ref, near_ref,
     b_ref, u_ref, x_ref, r_ref, xv_ref, rv_ref, x_sem, r_sem
 ):
     total = sum_of((g0_ref, g1_ref, g2_ref, g3_ref))
@@ -686,7 +694,7 @@
     stores = []
     for k in range(4):
         part = slice(k * WIDE, (k + 1) * WIDE)
-        far = down_dot(weights, gh_ref[part, :], gl_ref[part, :])
+        far = down_dot(weights, g_ref[part, :])
         third = (near_ref[:, part] + far) * (1.0 / LEAF)
         first, second = b_ref[:, part], u_ref[:, part]
         residual_one = (step_one * ratio) * first - step_one * second
@@ -707,10 +715,10 @@
         store.wait()
 
 
-def last_call(parts, p1, p2, t1, t2, gh, gl, near, field, u):
+def last_call(parts, p1, p2, t1, t2, table, near, field, u):
     return pl.pallas_call(
         last_kernel,
-        in_specs=inside(13),
+        in_specs=inside(12),
         out_specs=tuple(outside(2)),
         out_shape=(shape_of((RHS, 2 * LEAF), f32), shape_of((RHS, 2 * LEAF), f32)),
         scratch_shapes=[
@@ -722,7 +730,7 @@
         compiler_params=params,
         cost_estimate=cost(250_000_000, 7_000_000),
         name="last",
-    )(*parts, p1, p2, t1, t2, gh, gl, near, field, u)
+    )(*parts, p1, p2, t1, t2, table, near, field, u)
 
 
 def exchange(sent, axis):
@@ -755,23 +763,23 @@
 
 def shards(points, right_side, skel_sub, skel_group, skel_top, neighbors, counts):
     leaves = lax.axis_size("leaf")
-    sent, gh, gl, t1, t2, odd, even = start_call(
-        points, right_side, skel_sub, skel_group, skel_top, leaves
-    )
-    odd, even = swap_both(odd, even)
+    sent, g, t1, x, b = start_call(points, right_side, skel_sub, skel_group, leaves)
+    odd, even = swap_both(*pack_call(x, b))
     up_one, sent = climb_call(exchange(sent, "leaf"), t1)
     other = swapped(sent, "sub")
-    table_a, own_a, row, w, x, b = tables_a_call(neighbors, counts, points, right_side, sent)
+    row, w, t2 = prepare_call(neighbors, counts, x, skel_group, skel_top, sent)
     sent = join_call(sent, other, w)
     parts = turns(sent, "sub", 2)
-    table_b, table_ab, own = tables_b_call(w, x, b, row, own_a, sent)
+    table_a, table_b, own = tables_call(x, b, row, sent)
     up_two, sent = climb_four_call(parts, t2, own)
     parts = turns(sent, "group", 1)
-    below_table, above_table, own = around_call(w, odd, even, x, row, own, sent)
-    u, u16, odd, even = second_call(parts, up_one, up_two, t1, t2, gh, gl, own)
+    table_ab, below_table, above_table, own = around_call(
+        w, odd, even, x, b, row, own, sent
+    )
+    u, u16, odd, even = second_call(parts, up_one, up_two, t1, t2, g, own)
 
     odd, even = swap_both(odd, even)
-    own, weights, sums = third_call(w, u, b, u16, table_a, table_b, table_ab, gh, gl)
+    own, weights, sums = third_call(w, u, b, u16, table_a, table_b, table_ab, g)
     sent, near = finish_call(
         w, odd, even, below_table, above_table, u, own, weights, sums, leaves
     )
@@ -779,7 +787,7 @@
     sent = join_sums_call(sent, swapped(sent, "sub"))
     up_two, sent = climb_sums_call(turns(sent, "sub", 2), t2, level_two)
     parts = turns(sent, "group", 1)
-    return last_call(parts, up_one, up_two, t1, t2, gh, gl, near, b, u)
+    return last_call(parts, up_one, up_two, t1, t2, g, near, b, u)
 
 
 def solution(mesh):

time: 98.1 us -> 94.3 us (0.961)
  starting transfers between devices: 38.2 us -> 37 us
  Pallas kernels: 25.3 us -> 24.1 us
    pallas_call x7 -> x8, Pallas kernels: 22.7 us -> 21.1 us  [the longest x1 5.15 us: around_call(): pl.pallas_call(around_kernel, in_specs=inside(7) + [anywhere()], out_shap...]
    all_to_all x1, waiting for transfers between devices: 6.11 us -> 4.98 us  [exchange(): return lax.all_to_all(sent, axis, 0, 0)]
    ppermute x4, starting transfers between devices: 9.86 us -> 8.77 us  [chain_swap(): return lax.ppermute(value, ALL, pairs + [(j, i) for i, j in pairs])]
    ppermute x4, waiting for transfers between devices: 5.4 us -> 6.45 us  [chain_swap(): return lax.ppermute(value, ALL, pairs + [(j, i) for i, j in pairs])]
  transfers between devices with their start and end apart: 19 -> 19, of which waited for: 7 -> 11; matrix products, arithmetic and copies ran while one was open for 0% -> 0% of each run, Pallas kernels for 14% -> 14%
where the time goes in v6:
time: 94.3 us; the launch traced here: 93.9 us
  starting transfers between devices  37 us (39%)
  Pallas kernels  24.1 us (26%)
  waiting for transfers between devices  18.6 us (20%)
  blocking collectives  13.2 us (14%)
  between operations  1.01 us (1%)
    ppermute x12, starting transfers between devices, turned(): lax.ppermute(value, axis, [(i, (i + shift) % count) for i in range(count)])  19.6 us
    all_to_all x1, blocking collectives, exchange(): return lax.all_to_all(sent, axis, 0, 0)  13.2 us
    ppermute x4, starting transfers between devices, chain_swap(): return lax.ppermute(value, ALL, pairs + [(j, i) for i, j in pairs])  8.77 us
    all_to_all x1, starting transfers between devices, exchange(): return lax.all_to_all(sent, axis, 0, 0)  8.48 us
    ppermute x4, waiting for transfers between devices, chain_swap(): return lax.ppermute(value, ALL, pairs + [(j, i) for i, j in pairs])  6.45 us
    ppermute x12, waiting for transfers between devices, turned(): lax.ppermute(value, axis, [(i, (i + shift) % count) for i in range(count)])  5.96 us
    pallas_call x1, Pallas kernels, around_call(): pl.pallas_call(around_kernel, in_specs=inside(7) + [anywhere()], out_shap...  5.15 us
    all_to_all x1, waiting for transfers between devices, exchange(): return lax.all_to_all(sent, axis, 0, 0)  4.98 us
  transfers between devices with their start and end apart: 19, of which 11 were waited for; matrix products, arithmetic and copies ran while one was open for 0% of the time, Pallas kernels for 14%

profile of v6, /device:TPU:2, one launch (start us, length us, event | category | flops | bytes accessed | tf_op | source)
XLA Modules:
  0.0 93.9 jit_solution(11812368158199490577)
XLA Ops:
  0.7 4.6 %start.1 = (bf16[8,64,256]{2,1,0:T(8,128)(2,1)}, bf16[2048,256]{1,0:T(8,128)(2,1)}, f32[256,256]{1,0:T(8,128)S(1)}, bf16[2048,256]{1,0:T(8,128)(2,1)S(1)}, f32[64,2048]{1,0:T(8,128)S(1)}) custom-call(bf16[2048,256]{1,0:T(8,128)(2,1)} %x_ref.1, f32[64,2048]{1,0:T(8,128)} %b_ref.1, bf16[256,256]{1,0:T(8,128)(2,1)} %z1_ref.1, bf16[256,256]{1,0:T(8,128)(2,1)} %z2_ref.3), custom_call_target="tpu_custom_call" | custom-call | flops 600000000 | bytes 5000000 | tf_op jit(solution)/shard_map/start/pallas_call | solution.py:152
  5.2 8.5 %all-to-all-start = ((bf16[8,64,256]{2,1,0:T(8,128)(2,1)}), bf16[8,64,256]{2,1,0:T(8,128)(2,1)S(1)}, u32[]{:S(2)}, u32[]{:S(2)}) async-start(bf16[8,64,256]{2,1,0:T(8,128)(2,1)} %get-tuple-element.37), calls=%async_computation | async-start | bytes 524288 | tf_op jit(solution)/shard_map/all_to_all | solution.py:737
  13.7 1.1 %pack.1 = (bf16[1280,256]{1,0:T(8,128)(2,1)}, bf16[1280,256]{1,0:T(8,128)(2,1)}) custom-call(bf16[2048,256]{1,0:T(8,128)(2,1)S(1)} %get-tuple-element.36.x_ref, f32[64,2048]{1,0:T(8,128)S(1)} %get-tuple-element.42.b_ref), custom_call_target="tpu_custom_call" | custom-call | flops 1000000 | bytes 5000000 | tf_op jit(solution)/shard_map/pack/pallas_call | solution.py:206
  14.8 6.4 %collective-permute-start.7 = (bf16[1280,256]{1,0:T(8,128)(2,1)}, bf16[1280,256]{1,0:T(8,128)(2,1)S(1)}, u32[]{:S(2)}, u32[]{:S(2)}) collective-permute-start(bf16[1280,256]{1,0:T(8,128)(2,1)} %get-tuple-element.49), channel_id=1, source_target_pairs={{1,2},{3,4},{5,6},{7,8},{9,10},{11,12},{13,14},{15,16},{17,18},{19... | collective-permute-start | bytes 1966088 | tf_op jit(solution)/shard_map/ppermute | solution.py:743
  21.4 5.0 %all-to-all-done.got_ref = bf16[8,64,256]{2,1,0:T(8,128)(2,1)S(1)} async-done(((bf16[8,64,256]{2,1,0:T(8,128)(2,1)}), bf16[8,64,256]{2,1,0:T(8,128)(2,1)S(1)}, u32[]{:S(2)}, u32[]{:S(2)}) %all-to-all-start) | async-done | bytes 262176 | tf_op jit(solution)/shard_map/all_to_all | solution.py:737
  26.8 2.2 %prepare.1 = (f32[1,2048]{1,0:T(1,128)S(1)}, f32[8,128]{1,0:T(8,128)S(1)}, f32[256,256]{1,0:T(8,128)S(1)}) custom-call(s32[2,2]{1,0:T(2,128)S(1)} %copy-done.1, s32[2]{0:T(128)S(1)} %copy-done.2, bf16[2048,256]{1,0:T(8,128)(2,1)S(1)} %get-tuple-element.36.x_ref, bf16[256,256]{1,0:T(8,128)(2,1)} %z2_ref.3, bf16[256,256]{1,0:T(8,128)(2,1)} %z3_ref.1, ...), custom_call_target="tpu_custom_call" | custom-call | flops 50000000 | bytes 2000000 | tf_op jit(solution)/shard_map/prepare/pallas_call | solution.py:315
  29.0 1.7 %collective-permute-start.1 = (bf16[64,256]{1,0:T(8,128)(2,1)S(1)}, bf16[64,256]{1,0:T(8,128)(2,1)S(1)}, u32[]{:S(2)}, u32[]{:S(2)}) collective-permute-start(bf16[64,256]{1,0:T(8,128)(2,1)S(1)} %join.1.after_ref.g0_ref), channel_id=1, source_target_pairs={{0,16},{8,24},{16,32},{24,40},{32,48},{40,56},{48,0},{56,8},{1,17}... | collective-permute-start | bytes 98312 | tf_op jit(solution)/shard_map/ppermute | solution.py:752
  30.7 2.9 %collective-permute-start.2 = (bf16[64,256]{1,0:T(8,128)(2,1)S(1)}, bf16[64,256]{1,0:T(8,128)(2,1)S(1)}, u32[]{:S(2)}, u32[]{:S(2)}) collective-permute-start(bf16[64,256]{1,0:T(8,128)(2,1)S(1)} %join.1.after_ref.g0_ref), channel_id=1, source_target_pairs={{0,32},{8,40},{16,48},{24,56},{32,0},{40,8},{48,16},{56,24},{1,33}... | collective-permute-start | bytes 98312 | tf_op jit(solution)/shard_map/ppermute | solution.py:752
  33.6 1.3 %collective-permute-start.3 = (bf16[64,256]{1,0:T(8,128)(2,1)S(1)}, bf16[64,256]{1,0:T(8,128)(2,1)S(1)}, u32[]{:S(2)}, u32[]{:S(2)}) collective-permute-start(bf16[64,256]{1,0:T(8,128)(2,1)S(1)} %join.1.after_ref.g0_ref), channel_id=1, source_target_pairs={{0,48},{8,56},{16,0},{24,8},{32,16},{40,24},{48,32},{56,40},{1,49}... | collective-permute-start | bytes 98312 | tf_op jit(solution)/shard_map/ppermute | solution.py:752
  34.9 2.2 %tables.1 = (bf16[1024,1024]{1,0:T(8,128)(2,1)S(1)}, bf16[1024,1024]{1,0:T(8,128)(2,1)S(1)}, f32[64,2048]{1,0:T(8,128)S(1)}) custom-call(bf16[2048,256]{1,0:T(8,128)(2,1)S(1)} %get-tuple-element.36.x_ref, f32[64,2048]{1,0:T(8,128)S(1)} %get-tuple-element.42.b_ref, f32[1,2048]{1,0:T(1,128)S(1)} %get-tuple-element.43.row_ref, ...), custom_call_target="tpu_custom_call" | custom-call | flops 2200000000 | bytes 9000000 | tf_op jit(solution)/shard_map/tables/pallas_call | solution.py:339
  37.8 1.6 %collective-permute-start.4 = (bf16[64,256]{1,0:T(8,128)(2,1)S(1)}, bf16[64,256]{1,0:T(8,128)(2,1)S(1)}, u32[]{:S(2)}, u32[]{:S(2)}) collective-permute-start(bf16[64,256]{1,0:T(8,128)(2,1)S(1)} %get-tuple-element.45.after_ref.g0_ref), channel_id=1, source_target_pairs={{0,64},{64,128},{128,192},{192,0},{1,65},{65,129},{129,193},{193,1... | collective-permute-start | bytes 98312 | tf_op jit(solution)/shard_map/ppermute | solution.py:752
  39.3 1.1 %collective-permute-start.5 = (bf16[64,256]{1,0:T(8,128)(2,1)S(1)}, bf16[64,256]{1,0:T(8,128)(2,1)S(1)}, u32[]{:S(2)}, u32[]{:S(2)}) collective-permute-start(bf16[64,256]{1,0:T(8,128)(2,1)S(1)} %get-tuple-element.45.after_ref.g0_ref), channel_id=1, source_target_pairs={{0,128},{64,192},{128,0},{192,64},{1,129},{65,193},{129,1},{193,65... | collective-permute-start | bytes 98312 | tf_op jit(solution)/shard_map/ppermute | solution.py:752
  40.4 2.2 %collective-permute-start.6 = (bf16[64,256]{1,0:T(8,128)(2,1)S(1)}, bf16[64,256]{1,0:T(8,128)(2,1)S(1)}, u32[]{:S(2)}, u32[]{:S(2)}) collective-permute-start(bf16[64,256]{1,0:T(8,128)(2,1)S(1)} %get-tuple-element.45.after_ref.g0_ref), channel_id=1, source_target_pairs={{0,192},{64,0},{128,64},{192,128},{1,193},{65,1},{129,65},{193,129... | collective-permute-start | bytes 98312 | tf_op jit(solution)/shard_map/ppermute | solution.py:752
  42.6 5.1 %around.1 = (bf16[1024,1024]{1,0:T(8,128)(2,1)S(1)}, bf16[1024,1024]{1,0:T(8,128)(2,1)S(1)}, bf16[1024,1024]{1,0:T(8,128)(2,1)S(1)}, f32[64,2048]{1,0:T(8,128)S(1)}) custom-call(f32[8,128]{1,0:T(8,128)S(1)} %get-tuple-element.40.after_ref.w_ref, bf16[1280,256]{1,0:T(8,128)(2,1)S(1)} %collective-permute-done.7.odd_ref, ...), custom_call_target="tpu_custom_call" | custom-call | flops 2200000000 | bytes 9000000 | tf_op jit(solution)/shard_map/around/pallas_call | solution.py:398
  47.8 1.4 %second.1 = (f32[64,2048]{1,0:T(8,128)S(1)}, bf16[64,2048]{1,0:T(8,128)(2,1)S(1)}, bf16[64,1024]{1,0:T(8,128)(2,1)S(1)}, bf16[64,1024]{1,0:T(8,128)(2,1)S(1)}) custom-call(bf16[64,256]{1,0:T(8,128)(2,1)S(1)} %get-tuple-element.45.after_ref.g0_ref, bf16[64,256]{1,0:T(8,128)(2,1)S(1)} %collective-permute-done.4.g1_ref, ...), custom_call_target="tpu_custom_call" | custom-call | flops 250000000 | bytes 5000000 | tf_op jit(solution)/shard_map/second/pallas_call | solution.py:510
  49.6 1.9 %collective-permute-start.9 = (bf16[64,1024]{1,0:T(8,128)(2,1)S(1)}, bf16[64,1024]{1,0:T(8,128)(2,1)S(1)}, u32[]{:S(2)}, u32[]{:S(2)}) collective-permute-start(bf16[64,1024]{1,0:T(8,128)(2,1)S(1)} %get-tuple-element.52), channel_id=1, source_target_pairs={{1,2},{3,4},{5,6},{7,8},{9,10},{11,12},{13,14},{15,16},{17,18},{19... | collective-permute-start | bytes 393224 | tf_op jit(solution)/shard_map/ppermute | solution.py:743
  51.5 2.1 %third.1 = (f32[64,2048]{1,0:T(8,128)S(1)}, f32[64,256]{1,0:T(8,128)S(1)}, f32[64,128]{1,0:T(8,128)S(1)}) custom-call(f32[8,128]{1,0:T(8,128)S(1)} %get-tuple-element.40.after_ref.w_ref, f32[64,2048]{1,0:T(8,128)S(1)} %get-tuple-element.56.u_ref, f32[64,2048]{1,0:T(8,128)S(1)} %get-tuple-element.42.b_ref, bf16[64,2048]{1,0:T(8,128)(2,1)S(1)} %get-tuple-element.57.u16_ref, ...), custom_call_target="tpu_custom_call" | custom-call | flops 700000000 | bytes 10000000 | tf_op jit(solution)/shard_map/third/pallas_call | solution.py:551
  53.6 0.7 collective-permute-done.10.even_ref
  54.3 5.8 %collective-permute-done.9.odd_ref = bf16[64,1024]{1,0:T(8,128)(2,1)S(1)} collective-permute-done((bf16[64,1024]{1,0:T(8,128)(2,1)S(1)}, bf16[64,1024]{1,0:T(8,128)(2,1)S(1)}, u32[]{:S(2)}, u32[]{:S(2)}) %collective-permute-start.9) | collective-permute-done | bytes 131104 | tf_op jit(solution)/shard_map/ppermute | solution.py:743
  60.1 1.2 %finish.1 = (bf16[8,72,256]{2,1,0:T(8,128)(2,1)S(1)}, f32[64,2048]{1,0:T(8,128)S(1)}) custom-call(f32[8,128]{1,0:T(8,128)S(1)} %get-tuple-element.40.after_ref.w_ref, bf16[64,1024]{1,0:T(8,128)(2,1)S(1)} %collective-permute-done.9.odd_ref, bf16[64,1024]{1,0:T(8,128)(2,1)S(1)} %collective-permute-done.10.even_ref, ...), custom_call_target="tpu_custom_call" | custom-call | flops 270000000 | bytes 4000000 | tf_op jit(solution)/shard_map/finish/pallas_call | solution.py:614
  61.2 13.2 %all_to_all.10.refs_0_ = bf16[8,72,256]{2,1,0:T(8,128)(2,1)S(1)} all-to-all(bf16[8,72,256]{2,1,0:T(8,128)(2,1)S(1)} %get-tuple-element.64), channel_id=1, replica_groups=mesh['group'=4,'sub'=8,'leaf'=8] {'leaf'}, dimensions={0} | all-to-all | bytes 589824 | tf_op jit(solution)/shard_map/all_to_all | solution.py:737
  74.4 0.4 climb_sums.2
  74.9 1.2 %collective-permute-done.11.right_ref = bf16[72,256]{1,0:T(8,128)(2,1)S(1)} collective-permute-done((bf16[72,256]{1,0:T(8,128)(2,1)S(1)}, bf16[72,256]{1,0:T(8,128)(2,1)S(1)}, u32[]{:S(2)}, u32[]{:S(2)}) %collective-permute-start.11) | collective-permute-done | bytes 36896 | tf_op jit(solution)/shard_map/ppermute | solution.py:761
  76.5 2.2 %collective-permute-start.13 = (bf16[72,256]{1,0:T(8,128)(2,1)S(1)}, bf16[72,256]{1,0:T(8,128)(2,1)S(1)}, u32[]{:S(2)}, u32[]{:S(2)}) collective-permute-start(bf16[72,256]{1,0:T(8,128)(2,1)S(1)} %join_sums.1.refs_0_), channel_id=1, source_target_pairs={{0,32},{8,40},{16,48},{24,56},{32,0},{40,8},{48,16},{56,24},{1,33}... | collective-permute-start | bytes 110600 | tf_op jit(solution)/shard_map/ppermute | solution.py:752
  78.8 2.6 %collective-permute-start.14 = (bf16[72,256]{1,0:T(8,128)(2,1)S(1)}, bf16[72,256]{1,0:T(8,128)(2,1)S(1)}, u32[]{:S(2)}, u32[]{:S(2)}) collective-permute-start(bf16[72,256]{1,0:T(8,128)(2,1)S(1)} %join_sums.1.refs_0_), channel_id=1, source_target_pairs={{0,48},{8,56},{16,0},{24,8},{32,16},{40,24},{48,32},{56,40},{1,49}... | collective-permute-start | bytes 110600 | tf_op jit(solution)/shard_map/ppermute | solution.py:752
  81.3 0.7 collective-permute-done.12.refs_1_
  82.1 0.9 collective-permute-done.14.refs_3_
  83.4 1.0 %collective-permute-start.15 = (bf16[72,256]{1,0:T(8,128)(2,1)S(1)}, bf16[72,256]{1,0:T(8,128)(2,1)S(1)}, u32[]{:S(2)}, u32[]{:S(2)}) collective-permute-start(bf16[72,256]{1,0:T(8,128)(2,1)S(1)} %get-tuple-element.66.g0_ref), channel_id=1, source_target_pairs={{0,64},{64,128},{128,192},{192,0},{1,65},{65,129},{129,193},{193,1... | collective-permute-start | bytes 110600 | tf_op jit(solution)/shard_map/ppermute | solution.py:752
  84.4 3.1 %collective-permute-start.16 = (bf16[72,256]{1,0:T(8,128)(2,1)S(1)}, bf16[72,256]{1,0:T(8,128)(2,1)S(1)}, u32[]{:S(2)}, u32[]{:S(2)}) collective-permute-start(bf16[72,256]{1,0:T(8,128)(2,1)S(1)} %get-tuple-element.66.g0_ref), channel_id=1, source_target_pairs={{0,128},{64,192},{128,0},{192,64},{1,129},{65,193},{129,1},{193,65... | collective-permute-start | bytes 110600 | tf_op jit(solution)/shard_map/ppermute | solution.py:752
  87.6 2.3 %collective-permute-done.16.g2_ref = bf16[72,256]{1,0:T(8,128)(2,1)S(1)} collective-permute-done((bf16[72,256]{1,0:T(8,128)(2,1)S(1)}, bf16[72,256]{1,0:T(8,128)(2,1)S(1)}, u32[]{:S(2)}, u32[]{:S(2)}) %collective-permute-start.16) | collective-permute-done | bytes 36896 | tf_op jit(solution)/shard_map/ppermute | solution.py:752
  89.9 1.5 %collective-permute-done.17.g3_ref = bf16[72,256]{1,0:T(8,128)(2,1)S(1)} collective-permute-done((bf16[72,256]{1,0:T(8,128)(2,1)S(1)}, bf16[72,256]{1,0:T(8,128)(2,1)S(1)}, u32[]{:S(2)}, u32[]{:S(2)}) %collective-permute-start.17) | collective-permute-done | bytes 36896 | tf_op jit(solution)/shard_map/ppermute | solution.py:752
  91.4 2.3 %last.1 = (f32[64,2048]{1,0:T(8,128)}, f32[64,2048]{1,0:T(8,128)}) custom-call(bf16[72,256]{1,0:T(8,128)(2,1)S(1)} %get-tuple-element.66.g0_ref, bf16[72,256]{1,0:T(8,128)(2,1)S(1)} %collective-permute-done.15.g1_ref, bf16[72,256]{1,0:T(8,128)(2,1)S(1)} %collective-permute-done.16.g2_ref, bf16[72,256]{1,0:T(8,128)(2,1)S(1)} %collective-permute-done.17.g3_ref, ...), custom_call_target="tpu_custom_call" | custom-call | flops 250000000 | bytes 7000000 | tf_op jit(solution)/shard_map/last/pallas_call | solution.py:719
  (28 shorter events, 2.5 us)
Async XLA Ops:
  0.6 26.1 %copy-start.1 = (s32[2,2]{1,0:T(2,128)S(1)}, s32[2,2]{1,0:T(2,128)}, u32[]{:S(2)}) copy-start(s32[2,2]{1,0:T(2,128)} %nb_ref.1) | copy-start | bytes 52
  0.6 26.1 %copy-start.2 = (s32[2]{0:T(128)S(1)}, s32[2]{0:T(128)}, u32[]{:S(2)}) copy-start(s32[2]{0:T(128)} %ct_ref.1) | copy-start | bytes 28
  5.2 21.1 %all-to-all-start = ((bf16[8,64,256]{2,1,0:T(8,128)(2,1)}), bf16[8,64,256]{2,1,0:T(8,128)(2,1)S(1)}, u32[]{:S(2)}, u32[]{:S(2)}) async-start(bf16[8,64,256]{2,1,0:T(8,128)(2,1)} %get-tuple-element.37), calls=%async_computation | async-start | bytes 524288 | tf_op jit(solution)/shard_map/all_to_all | solution.py:737
  14.8 27.8 %collective-permute-start.7 = (bf16[1280,256]{1,0:T(8,128)(2,1)}, bf16[1280,256]{1,0:T(8,128)(2,1)S(1)}, u32[]{:S(2)}, u32[]{:S(2)}) collective-permute-start(bf16[1280,256]{1,0:T(8,128)(2,1)} %get-tuple-element.49), channel_id=1, source_target_pairs={{1,2},{3,4},{5,6},{7,8},{9,10},{11,12},{13,14},{15,16},{17,18},{19... | collective-permute-start | bytes 1966088 | tf_op jit(solution)/shard_map/ppermute | solution.py:743
  21.3 21.3 %collective-permute-start.8 = (bf16[1280,256]{1,0:T(8,128)(2,1)}, bf16[1280,256]{1,0:T(8,128)(2,1)S(1)}, u32[]{:S(2)}, u32[]{:S(2)}) collective-permute-start(bf16[1280,256]{1,0:T(8,128)(2,1)} %get-tuple-element.50), channel_id=1, source_target_pairs={{0,1},{2,3},{4,5},{6,7},{8,9},{10,11},{12,13},{14,15},{16,17},{18,... | collective-permute-start | bytes 1966088 | tf_op jit(solution)/shard_map/ppermute | solution.py:743
  26.7 2.3 %collective-permute-start = (bf16[64,256]{1,0:T(8,128)(2,1)S(1)}, bf16[64,256]{1,0:T(8,128)(2,1)S(1)}, u32[]{:S(2)}, u32[]{:S(2)}) collective-permute-start(bf16[64,256]{1,0:T(8,128)(2,1)S(1)} %get-tuple-element.39.after_ref.left_ref), channel_id=1, source_target_pairs={{0,8},{8,0},{16,24},{24,16},{32,40},{40,32},{48,56},{56,48},{1,9},... | collective-permute-start | bytes 98312 | tf_op jit(solution)/shard_map/ppermute | solution.py:761
  29.0 8.1 %collective-permute-start.1 = (bf16[64,256]{1,0:T(8,128)(2,1)S(1)}, bf16[64,256]{1,0:T(8,128)(2,1)S(1)}, u32[]{:S(2)}, u32[]{:S(2)}) collective-permute-start(bf16[64,256]{1,0:T(8,128)(2,1)S(1)} %join.1.after_ref.g0_ref), channel_id=1, source_target_pairs={{0,16},{8,24},{16,32},{24,40},{32,48},{40,56},{48,0},{56,8},{1,17}... | collective-permute-start | bytes 98312 | tf_op jit(solution)/shard_map/ppermute | solution.py:752
  30.7 6.8 %collective-permute-start.2 = (bf16[64,256]{1,0:T(8,128)(2,1)S(1)}, bf16[64,256]{1,0:T(8,128)(2,1)S(1)}, u32[]{:S(2)}, u32[]{:S(2)}) collective-permute-start(bf16[64,256]{1,0:T(8,128)(2,1)S(1)} %join.1.after_ref.g0_ref), channel_id=1, source_target_pairs={{0,32},{8,40},{16,48},{24,56},{32,0},{40,8},{48,16},{56,24},{1,33}... | collective-permute-start | bytes 98312 | tf_op jit(solution)/shard_map/ppermute | solution.py:752
  33.6 3.9 %collective-permute-start.3 = (bf16[64,256]{1,0:T(8,128)(2,1)S(1)}, bf16[64,256]{1,0:T(8,128)(2,1)S(1)}, u32[]{:S(2)}, u32[]{:S(2)}) collective-permute-start(bf16[64,256]{1,0:T(8,128)(2,1)S(1)} %join.1.after_ref.g0_ref), channel_id=1, source_target_pairs={{0,48},{8,56},{16,0},{24,8},{32,16},{40,24},{48,32},{56,40},{1,49}... | collective-permute-start | bytes 98312 | tf_op jit(solution)/shard_map/ppermute | solution.py:752
  37.8 10.0 %copy-start = (bf16[2048,256]{1,0:T(8,128)(2,1)S(1)}, bf16[2048,256]{1,0:T(8,128)(2,1)}, u32[]{:S(2)}) copy-start(bf16[2048,256]{1,0:T(8,128)(2,1)} %get-tuple-element.48.g_ref) | copy-start | bytes 3145732
  37.8 10.0 %collective-permute-start.4 = (bf16[64,256]{1,0:T(8,128)(2,1)S(1)}, bf16[64,256]{1,0:T(8,128)(2,1)S(1)}, u32[]{:S(2)}, u32[]{:S(2)}) collective-permute-start(bf16[64,256]{1,0:T(8,128)(2,1)S(1)} %get-tuple-element.45.after_ref.g0_ref), channel_id=1, source_target_pairs={{0,64},{64,128},{128,192},{192,0},{1,65},{65,129},{129,193},{193,1... | collective-permute-start | bytes 98312 | tf_op jit(solution)/shard_map/ppermute | solution.py:752
  39.3 8.4 %collective-permute-start.5 = (bf16[64,256]{1,0:T(8,128)(2,1)S(1)}, bf16[64,256]{1,0:T(8,128)(2,1)S(1)}, u32[]{:S(2)}, u32[]{:S(2)}) collective-permute-start(bf16[64,256]{1,0:T(8,128)(2,1)S(1)} %get-tuple-element.45.after_ref.g0_ref), channel_id=1, source_target_pairs={{0,128},{64,192},{128,0},{192,64},{1,129},{65,193},{129,1},{193,65... | collective-permute-start | bytes 98312 | tf_op jit(solution)/shard_map/ppermute | solution.py:752
  40.4 7.3 %collective-permute-start.6 = (bf16[64,256]{1,0:T(8,128)(2,1)S(1)}, bf16[64,256]{1,0:T(8,128)(2,1)S(1)}, u32[]{:S(2)}, u32[]{:S(2)}) collective-permute-start(bf16[64,256]{1,0:T(8,128)(2,1)S(1)} %get-tuple-element.45.after_ref.g0_ref), channel_id=1, source_target_pairs={{0,192},{64,0},{128,64},{192,128},{1,193},{65,1},{129,65},{193,129... | collective-permute-start | bytes 98312 | tf_op jit(solution)/shard_map/ppermute | solution.py:752
  49.2 5.1 %collective-permute-start.10 = (bf16[64,1024]{1,0:T(8,128)(2,1)S(1)}, bf16[64,1024]{1,0:T(8,128)(2,1)S(1)}, u32[]{:S(2)}, u32[]{:S(2)}) collective-permute-start(bf16[64,1024]{1,0:T(8,128)(2,1)S(1)} %get-tuple-element.53), channel_id=1, source_target_pairs={{0,1},{2,3},{4,5},{6,7},{8,9},{10,11},{12,13},{14,15},{16,17},{18,... | collective-permute-start | bytes 393224 | tf_op jit(solution)/shard_map/ppermute | solution.py:743
  49.6 10.5 %collective-permute-start.9 = (bf16[64,1024]{1,0:T(8,128)(2,1)S(1)}, bf16[64,1024]{1,0:T(8,128)(2,1)S(1)}, u32[]{:S(2)}, u32[]{:S(2)}) collective-permute-start(bf16[64,1024]{1,0:T(8,128)(2,1)S(1)} %get-tuple-element.52), channel_id=1, source_target_pairs={{1,2},{3,4},{5,6},{7,8},{9,10},{11,12},{13,14},{15,16},{17,18},{19... | collective-permute-start | bytes 393224 | tf_op jit(solution)/shard_map/ppermute | solution.py:743
  74.9 1.2 %collective-permute-start.11 = (bf16[72,256]{1,0:T(8,128)(2,1)S(1)}, bf16[72,256]{1,0:T(8,128)(2,1)S(1)}, u32[]{:S(2)}, u32[]{:S(2)}) collective-permute-start(bf16[72,256]{1,0:T(8,128)(2,1)S(1)} %get-tuple-element.65.left_ref), channel_id=1, source_target_pairs={{0,8},{8,0},{16,24},{24,16},{32,40},{40,32},{48,56},{56,48},{1,9},... | collective-permute-start | bytes 110600 | tf_op jit(solution)/shard_map/ppermute | solution.py:761
  76.5 5.5 %collective-permute-start.12 = (bf16[72,256]{1,0:T(8,128)(2,1)S(1)}, bf16[72,256]{1,0:T(8,128)(2,1)S(1)}, u32[]{:S(2)}, u32[]{:S(2)}) collective-permute-start(bf16[72,256]{1,0:T(8,128)(2,1)S(1)} %join_sums.1.refs_0_), channel_id=1, source_target_pairs={{0,16},{8,24},{16,32},{24,40},{32,48},{40,56},{48,0},{56,8},{1,17}... | collective-permute-start | bytes 110600 | tf_op jit(solution)/shard_map/ppermute | solution.py:752
  76.5 5.6 %collective-permute-start.13 = (bf16[72,256]{1,0:T(8,128)(2,1)S(1)}, bf16[72,256]{1,0:T(8,128)(2,1)S(1)}, u32[]{:S(2)}, u32[]{:S(2)}) collective-permute-start(bf16[72,256]{1,0:T(8,128)(2,1)S(1)} %join_sums.1.refs_0_), channel_id=1, source_target_pairs={{0,32},{8,40},{16,48},{24,56},{32,0},{40,8},{48,16},{56,24},{1,33}... | collective-permute-start | bytes 110600 | tf_op jit(solution)/shard_map/ppermute | solution.py:752
  78.8 4.2 %collective-permute-start.14 = (bf16[72,256]{1,0:T(8,128)(2,1)S(1)}, bf16[72,256]{1,0:T(8,128)(2,1)S(1)}, u32[]{:S(2)}, u32[]{:S(2)}) collective-permute-start(bf16[72,256]{1,0:T(8,128)(2,1)S(1)} %join_sums.1.refs_0_), channel_id=1, source_target_pairs={{0,48},{8,56},{16,0},{24,8},{32,16},{40,24},{48,32},{56,40},{1,49}... | collective-permute-start | bytes 110600 | tf_op jit(solution)/shard_map/ppermute | solution.py:752
  83.4 4.1 %collective-permute-start.15 = (bf16[72,256]{1,0:T(8,128)(2,1)S(1)}, bf16[72,256]{1,0:T(8,128)(2,1)S(1)}, u32[]{:S(2)}, u32[]{:S(2)}) collective-permute-start(bf16[72,256]{1,0:T(8,128)(2,1)S(1)} %get-tuple-element.66.g0_ref), channel_id=1, source_target_pairs={{0,64},{64,128},{128,192},{192,0},{1,65},{65,129},{129,193},{193,1... | collective-permute-start | bytes 110600 | tf_op jit(solution)/shard_map/ppermute | solution.py:752
  84.4 5.5 %collective-permute-start.16 = (bf16[72,256]{1,0:T(8,128)(2,1)S(1)}, bf16[72,256]{1,0:T(8,128)(2,1)S(1)}, u32[]{:S(2)}, u32[]{:S(2)}) collective-permute-start(bf16[72,256]{1,0:T(8,128)(2,1)S(1)} %get-tuple-element.66.g0_ref), channel_id=1, source_target_pairs={{0,128},{64,192},{128,0},{192,64},{1,129},{65,193},{129,1},{193,65... | collective-permute-start | bytes 110600 | tf_op jit(solution)/shard_map/ppermute | solution.py:752
  87.5 4.0 %collective-permute-start.17 = (bf16[72,256]{1,0:T(8,128)(2,1)S(1)}, bf16[72,256]{1,0:T(8,128)(2,1)S(1)}, u32[]{:S(2)}, u32[]{:S(2)}) collective-permute-start(bf16[72,256]{1,0:T(8,128)(2,1)S(1)} %get-tuple-element.66.g0_ref), channel_id=1, source_target_pairs={{0,192},{64,0},{128,64},{192,128},{1,193},{65,1},{129,65},{193,129... | collective-permute-start | bytes 110600 | tf_op jit(solution)/shard_map/ppermute | solution.py:752

commit v7 on v6

--- a/solution.py
+++ b/solution.py
@@ -327,6 +327,37 @@
     )(neighbors, counts, points, in_hbm(z2), in_hbm(z3), after)
 
 
+def inner_kernel(x_ref, b_ref, after_ref, table_ref, out_ref, tv_ref, sem):
+    del after_ref
+    x_a, x_b = x_ref[:LEAF, :], x_ref[LEAF:, :]
+    row_b = right_row(x_b)
+    stores = []
+    for i in range(STEPS):
+        rows = x_a[block(i), :]
+        tv_ref[block(i), :] = gauss(rows, left_column(rows), x_b, row_b).astype(bf16)
+        place = pl.ds(i * ROWS, ROWS)
+        store = pltpu.make_async_copy(tv_ref.at[place, :], table_ref.at[place, :], sem.at[i])
+        store.start()
+        stores.append(store)
+    out_ref[:, :LEAF] = nt(b_ref[:, LEAF:].astype(bf16), tv_ref[...])
+    out_ref[:, LEAF:] = nn(b_ref[:, :LEAF].astype(bf16), tv_ref[...])
+    for store in stores:
+        store.wait()
+
+
+def inner_call(points, field, after):
+    return pl.pallas_call(
+        inner_kernel,
+        in_specs=inside(2) + [anywhere()],
+        out_specs=tuple(outside(1) + inside(1)),
+        out_shape=(pltpu.HBM((LEAF, LEAF), bf16), shape_of((RHS, 2 * LEAF), f32)),
+        scratch_shapes=[pltpu.VMEM((LEAF, LEAF), bf16), pltpu.SemaphoreType.DMA((STEPS,))],
+        compiler_params=params,
+        cost_estimate=cost(100_000_000, 1_000_000, 100_000),
+        name="inner",
+    )(points, field, after)
+
+
 def tables_kernel(x_ref, b_ref, row_ref, after_ref, table_a_ref, table_b_ref, own_ref):
     del after_ref
     make_symmetric(x_ref[:LEAF, :], row_ref[:, :LEAF], table_a_ref)
@@ -345,7 +376,7 @@
             shape_of((RHS, 2 * LEAF), f32),
         ),
         compiler_params=params,
-        cost_estimate=cost(2_200_000_000, 9_000_000, 2_400_000),
+        cost_estimate=cost(3_000_000_000, 9_000_000, 2_400_000),
         name="tables",
     )(points, field, row, after)
 
@@ -362,16 +393,14 @@
 
 
 def around_kernel(
-    w_ref, odd_ref, even_ref, x_ref, b_ref, row_ref, own_ref, after_ref,
-    table_ab_ref, below_table_ref, above_table_ref, out_ref
+    w_ref, odd_ref, even_ref, x_ref, inner_ref, row_ref, own_ref, after_ref,
+    below_table_ref, above_table_ref, out_ref
 ):
     del after_ref
     x_a, x_b = x_ref[:LEAF, :], x_ref[LEAF:, :]
     row_a, row_b = row_ref[:, :LEAF], row_ref[:, LEAF:]
-    b_a, b_b = b_ref[:, :LEAF].astype(bf16), b_ref[:, LEAF:].astype(bf16)
-    make_block(x_a, x_b, row_b, table_ab_ref)
-    near_a = own_ref[:, :LEAF] + weight_of(w_ref, 1) * nt(b_b, table_ab_ref[...])
-    near_b = own_ref[:, LEAF:] + weight_of(w_ref, 2) * nn(b_a, table_ab_ref[...])
+    near_a = own_ref[:, :LEAF] + weight_of(w_ref, 1) * inner_ref[:, :LEAF]
+    near_b = own_ref[:, LEAF:] + weight_of(w_ref, 2) * inner_ref[:, LEAF:]
 
     def build(below_ref, above_ref):
         make_block(below_ref, x_a, row_a, below_table_ref)
@@ -394,20 +423,19 @@
         build(even_ref, odd_ref)
 
 
-def around_call(w, odd, even, points, field, row, own, after):
+def around_call(w, odd, even, points, inner, row, own, after):
     return pl.pallas_call(
         around_kernel,
         in_specs=inside(7) + [anywhere()],
         out_shape=(
             shape_of((LEAF, LEAF), bf16),
             shape_of((LEAF, LEAF), bf16),
-            shape_of((LEAF, LEAF), bf16),
             shape_of((RHS, 2 * LEAF), f32),
         ),
         compiler_params=params,
         cost_estimate=cost(2_200_000_000, 9_000_000, 3_145_728),
         name="around",
-    )(w, odd, even, points, field, row, own, after)
+    )(w, odd, even, points, inner, row, own, after)
 
 
 def total_of(got_ref):
@@ -417,21 +445,22 @@
     return total
 
 
-def climb_kernel(got_ref, table_ref, up_ref, sent_ref):
+def climb_kernel(got_ref, table_ref, after_ref, up_ref, sent_ref):
+    del after_ref
     total = total_of(got_ref)
     up_ref[...] = total
     sent_ref[...] = (nn(total, table_ref[...], highest) * (1.0 / SKEL)).astype(bf16)
 
 
-def climb_call(got, table):
+def climb_call(got, table, after):
     return pl.pallas_call(
         climb_kernel,
-        in_specs=inside(2),
+        in_specs=inside(2) + [anywhere()],
         out_shape=(shape_of((RHS, SKEL), f32), shape_of((RHS, SKEL), bf16)),
         compiler_params=params,
         cost_estimate=cost(50_000_000, 900_000),
         name="climb",
-    )(got, table)
+    )(got, table, after)
 
 
 def join_kernel(left_ref, right_ref, after_ref, out_ref):
@@ -765,7 +794,8 @@
     leaves = lax.axis_size("leaf")
     sent, g, t1, x, b = start_call(points, right_side, skel_sub, skel_group, leaves)
     odd, even = swap_both(*pack_call(x, b))
-    up_one, sent = climb_call(exchange(sent, "leaf"), t1)
+    table_ab, inner = inner_call(x, b, sent)
+    up_one, sent = climb_call(exchange(sent, "leaf"), t1, inner)
     other = swapped(sent, "sub")
     row, w, t2 = prepare_call(neighbors, counts, x, skel_group, skel_top, sent)
     sent = join_call(sent, other, w)
@@ -773,9 +803,7 @@
     table_a, table_b, own = tables_call(x, b, row, sent)
     up_two, sent = climb_four_call(parts, t2, own)
     parts = turns(sent, "group", 1)
-    table_ab, below_table, above_table, own = around_call(
-        w, odd, even, x, b, row, own, sent
-    )
+    below_table, above_table, own = around_call(w, odd, even, x, inner, row, own, sent)
     u, u16, odd, even = second_call(parts, up_one, up_two, t1, t2, g, own)
 
     odd, even = swap_both(odd, even)

time: 94.3 us -> 93.5 us (level)
  waiting for transfers between devices: 18.6 us -> 16.2 us
  Pallas kernels: 24.1 us -> 25.5 us
    all_to_all x1, waiting for transfers between devices: 4.98 us -> 2.56 us  [exchange(): return lax.all_to_all(sent, axis, 0, 0)]
    pallas_call x1 -> x2, Pallas kernels: 0.29 us -> 2.7 us  [the longest x1 2.41 us: inner_call(): pl.pallas_call(inner_kernel, in_specs=inside(2) + [anywhere()], out_specs...]
    pallas_call x1, Pallas kernels: 5.15 us -> 4.14 us  [around_call(): pl.pallas_call(around_kernel, in_specs=inside(7) + [anywhere()], out_shap...]
  transfers between devices with their start and end apart: 19 -> 19, of which waited for: 11 -> 11; matrix products, arithmetic and copies ran while one was open for 0% -> 0% of each run, Pallas kernels for 14% -> 16%
where the time goes in v7:
time: 93.5 us; the launch traced here: 92.8 us
  starting transfers between devices  36.9 us (39%)
  Pallas kernels  25.5 us (27%)
  waiting for transfers between devices  16.2 us (17%)
  blocking collectives  13.2 us (14%)
  between operations  1.03 us (1%)
    ppermute x12, starting transfers between devices, turned(): lax.ppermute(value, axis, [(i, (i + shift) % count) for i in range(count)])  19.6 us
    all_to_all x1, blocking collectives, exchange(): return lax.all_to_all(sent, axis, 0, 0)  13.2 us
    ppermute x4, starting transfers between devices, chain_swap(): return lax.ppermute(value, ALL, pairs + [(j, i) for i, j in pairs])  8.76 us
    all_to_all x1, starting transfers between devices, exchange(): return lax.all_to_all(sent, axis, 0, 0)  8.47 us
    ppermute x4, waiting for transfers between devices, chain_swap(): return lax.ppermute(value, ALL, pairs + [(j, i) for i, j in pairs])  6.46 us
    ppermute x12, waiting for transfers between devices, turned(): lax.ppermute(value, axis, [(i, (i + shift) % count) for i in range(count)])  5.95 us
    pallas_call x1, Pallas kernels, start_call(): pl.pallas_call(start_kernel, in_specs=outside(4), out_specs=tuple(inside(...  4.56 us
    pallas_call x1, Pallas kernels, around_call(): pl.pallas_call(around_kernel, in_specs=inside(7) + [anywhere()], out_shap...  4.14 us
  transfers between devices with their start and end apart: 19, of which 11 were waited for; matrix products, arithmetic and copies ran while one was open for 0% of the time, Pallas kernels for 16%

profile of v7, /device:TPU:2, one launch (start us, length us, event | category | flops | bytes accessed | tf_op | source)
XLA Modules:
  0.0 92.8 jit_solution(1064318371401104968)
XLA Ops:
  0.6 4.6 %start.1 = (bf16[8,64,256]{2,1,0:T(8,128)(2,1)}, bf16[2048,256]{1,0:T(8,128)(2,1)}, f32[256,256]{1,0:T(8,128)S(1)}, bf16[2048,256]{1,0:T(8,128)(2,1)S(1)}, f32[64,2048]{1,0:T(8,128)S(1)}) custom-call(bf16[2048,256]{1,0:T(8,128)(2,1)} %x_ref.1, f32[64,2048]{1,0:T(8,128)} %b_ref.1, bf16[256,256]{1,0:T(8,128)(2,1)} %z1_ref.1, bf16[256,256]{1,0:T(8,128)(2,1)} %z2_ref.3), custom_call_target="tpu_custom_call" | custom-call | flops 600000000 | bytes 5000000 | tf_op jit(solution)/shard_map/start/pallas_call | solution.py:152
  5.2 8.5 %all-to-all-start = ((bf16[8,64,256]{2,1,0:T(8,128)(2,1)}), bf16[8,64,256]{2,1,0:T(8,128)(2,1)S(1)}, u32[]{:S(2)}, u32[]{:S(2)}) async-start(bf16[8,64,256]{2,1,0:T(8,128)(2,1)} %get-tuple-element.38.after_ref), calls=%async_computation | async-start | bytes 524288 | tf_op jit(solution)/shard_map/all_to_all | solution.py:766
  13.7 1.1 %pack.1 = (bf16[1280,256]{1,0:T(8,128)(2,1)}, bf16[1280,256]{1,0:T(8,128)(2,1)}) custom-call(bf16[2048,256]{1,0:T(8,128)(2,1)S(1)} %get-tuple-element.37.x_ref, f32[64,2048]{1,0:T(8,128)S(1)} %get-tuple-element.40.b_ref), custom_call_target="tpu_custom_call" | custom-call | flops 1000000 | bytes 5000000 | tf_op jit(solution)/shard_map/pack/pallas_call | solution.py:206
  14.8 6.4 %collective-permute-start.7 = (bf16[1280,256]{1,0:T(8,128)(2,1)}, bf16[1280,256]{1,0:T(8,128)(2,1)S(1)}, u32[]{:S(2)}, u32[]{:S(2)}) collective-permute-start(bf16[1280,256]{1,0:T(8,128)(2,1)} %get-tuple-element.51), channel_id=1, source_target_pairs={{1,2},{3,4},{5,6},{7,8},{9,10},{11,12},{13,14},{15,16},{17,18},{19... | collective-permute-start | bytes 1966088 | tf_op jit(solution)/shard_map/ppermute | solution.py:772
  21.4 2.4 %inner.1 = (bf16[1024,1024]{1,0:T(8,128)(2,1)}, f32[64,2048]{1,0:T(8,128)S(1)}) custom-call(bf16[2048,256]{1,0:T(8,128)(2,1)S(1)} %get-tuple-element.37.x_ref, f32[64,2048]{1,0:T(8,128)S(1)} %get-tuple-element.40.b_ref, bf16[8,64,256]{2,1,0:T(8,128)(2,1)} %get-tuple-element.38.after_ref), custom_call_target="tpu_custom_call" | custom-call | flops 100000000 | bytes 1000000 | tf_op jit(solution)/shard_map/inner/pallas_call | solution.py:349
  23.8 2.6 %all-to-all-done.got_ref = bf16[8,64,256]{2,1,0:T(8,128)(2,1)S(1)} async-done(((bf16[8,64,256]{2,1,0:T(8,128)(2,1)}), bf16[8,64,256]{2,1,0:T(8,128)(2,1)S(1)}, u32[]{:S(2)}, u32[]{:S(2)}) %all-to-all-start) | async-done | bytes 262176 | tf_op jit(solution)/shard_map/all_to_all | solution.py:766
  26.7 2.2 %prepare.1 = (f32[1,2048]{1,0:T(1,128)S(1)}, f32[8,128]{1,0:T(8,128)S(1)}, f32[256,256]{1,0:T(8,128)S(1)}) custom-call(s32[2,2]{1,0:T(2,128)S(1)} %copy-done.2, s32[2]{0:T(128)S(1)} %copy-done.3, bf16[2048,256]{1,0:T(8,128)(2,1)S(1)} %get-tuple-element.37.x_ref, bf16[256,256]{1,0:T(8,128)(2,1)} %z2_ref.3, bf16[256,256]{1,0:T(8,128)(2,1)} %z3_ref.1, ...), custom_call_target="tpu_custom_call" | custom-call | flops 50000000 | bytes 2000000 | tf_op jit(solution)/shard_map/prepare/pallas_call | solution.py:315
  29.0 1.7 %collective-permute-start.1 = (bf16[64,256]{1,0:T(8,128)(2,1)S(1)}, bf16[64,256]{1,0:T(8,128)(2,1)S(1)}, u32[]{:S(2)}, u32[]{:S(2)}) collective-permute-start(bf16[64,256]{1,0:T(8,128)(2,1)S(1)} %join.1.after_ref.g0_ref), channel_id=1, source_target_pairs={{0,16},{8,24},{16,32},{24,40},{32,48},{40,56},{48,0},{56,8},{1,17}... | collective-permute-start | bytes 98312 | tf_op jit(solution)/shard_map/ppermute | solution.py:781
  30.6 2.9 %collective-permute-start.2 = (bf16[64,256]{1,0:T(8,128)(2,1)S(1)}, bf16[64,256]{1,0:T(8,128)(2,1)S(1)}, u32[]{:S(2)}, u32[]{:S(2)}) collective-permute-start(bf16[64,256]{1,0:T(8,128)(2,1)S(1)} %join.1.after_ref.g0_ref), channel_id=1, source_target_pairs={{0,32},{8,40},{16,48},{24,56},{32,0},{40,8},{48,16},{56,24},{1,33}... | collective-permute-start | bytes 98312 | tf_op jit(solution)/shard_map/ppermute | solution.py:781
  33.5 1.3 %collective-permute-start.3 = (bf16[64,256]{1,0:T(8,128)(2,1)S(1)}, bf16[64,256]{1,0:T(8,128)(2,1)S(1)}, u32[]{:S(2)}, u32[]{:S(2)}) collective-permute-start(bf16[64,256]{1,0:T(8,128)(2,1)S(1)} %join.1.after_ref.g0_ref), channel_id=1, source_target_pairs={{0,48},{8,56},{16,0},{24,8},{32,16},{40,24},{48,32},{56,40},{1,49}... | collective-permute-start | bytes 98312 | tf_op jit(solution)/shard_map/ppermute | solution.py:781
  34.9 2.2 %tables.1 = (bf16[1024,1024]{1,0:T(8,128)(2,1)S(1)}, bf16[1024,1024]{1,0:T(8,128)(2,1)S(1)}, f32[64,2048]{1,0:T(8,128)S(1)}) custom-call(bf16[2048,256]{1,0:T(8,128)(2,1)S(1)} %get-tuple-element.37.x_ref, f32[64,2048]{1,0:T(8,128)S(1)} %get-tuple-element.40.b_ref, f32[1,2048]{1,0:T(1,128)S(1)} %get-tuple-element.45.row_ref, ...), custom_call_target="tpu_custom_call" | custom-call | flops 3000000000 | bytes 9000000 | tf_op jit(solution)/shard_map/tables/pallas_call | solution.py:370
  37.7 1.6 %collective-permute-start.4 = (bf16[64,256]{1,0:T(8,128)(2,1)S(1)}, bf16[64,256]{1,0:T(8,128)(2,1)S(1)}, u32[]{:S(2)}, u32[]{:S(2)}) collective-permute-start(bf16[64,256]{1,0:T(8,128)(2,1)S(1)} %get-tuple-element.47.after_ref.g0_ref), channel_id=1, source_target_pairs={{0,64},{64,128},{128,192},{192,0},{1,65},{65,129},{129,193},{193,1... | collective-permute-start | bytes 98312 | tf_op jit(solution)/shard_map/ppermute | solution.py:781
  39.3 1.1 %collective-permute-start.5 = (bf16[64,256]{1,0:T(8,128)(2,1)S(1)}, bf16[64,256]{1,0:T(8,128)(2,1)S(1)}, u32[]{:S(2)}, u32[]{:S(2)}) collective-permute-start(bf16[64,256]{1,0:T(8,128)(2,1)S(1)} %get-tuple-element.47.after_ref.g0_ref), channel_id=1, source_target_pairs={{0,128},{64,192},{128,0},{192,64},{1,129},{65,193},{129,1},{193,65... | collective-permute-start | bytes 98312 | tf_op jit(solution)/shard_map/ppermute | solution.py:781
  40.4 2.2 %collective-permute-start.6 = (bf16[64,256]{1,0:T(8,128)(2,1)S(1)}, bf16[64,256]{1,0:T(8,128)(2,1)S(1)}, u32[]{:S(2)}, u32[]{:S(2)}) collective-permute-start(bf16[64,256]{1,0:T(8,128)(2,1)S(1)} %get-tuple-element.47.after_ref.g0_ref), channel_id=1, source_target_pairs={{0,192},{64,0},{128,64},{192,128},{1,193},{65,1},{129,65},{193,129... | collective-permute-start | bytes 98312 | tf_op jit(solution)/shard_map/ppermute | solution.py:781
  42.6 4.1 %around.1 = (bf16[1024,1024]{1,0:T(8,128)(2,1)S(1)}, bf16[1024,1024]{1,0:T(8,128)(2,1)S(1)}, f32[64,2048]{1,0:T(8,128)S(1)}) custom-call(f32[8,128]{1,0:T(8,128)S(1)} %get-tuple-element.43.after_ref.w_ref, bf16[1280,256]{1,0:T(8,128)(2,1)S(1)} %collective-permute-done.7.odd_ref, bf16[1280,256]{1,0:T(8,128)(2,1)} %collective-permute-done.8.even_ref, ...), custom_call_target="tpu_custom_call" | custom-call | flops 2200000000 | bytes 9000000 | tf_op jit(solution)/shard_map/around/pallas_call | solution.py:427
  46.8 1.4 %second.1 = (f32[64,2048]{1,0:T(8,128)S(1)}, bf16[64,2048]{1,0:T(8,128)(2,1)S(1)}, bf16[64,1024]{1,0:T(8,128)(2,1)S(1)}, bf16[64,1024]{1,0:T(8,128)(2,1)S(1)}) custom-call(bf16[64,256]{1,0:T(8,128)(2,1)S(1)} %get-tuple-element.47.after_ref.g0_ref, bf16[64,256]{1,0:T(8,128)(2,1)S(1)} %collective-permute-done.4.g1_ref, ...), custom_call_target="tpu_custom_call" | custom-call | flops 250000000 | bytes 5000000 | tf_op jit(solution)/shard_map/second/pallas_call | solution.py:539
  48.5 1.9 %collective-permute-start.9 = (bf16[64,1024]{1,0:T(8,128)(2,1)S(1)}, bf16[64,1024]{1,0:T(8,128)(2,1)S(1)}, u32[]{:S(2)}, u32[]{:S(2)}) collective-permute-start(bf16[64,1024]{1,0:T(8,128)(2,1)S(1)} %get-tuple-element.54), channel_id=1, source_target_pairs={{1,2},{3,4},{5,6},{7,8},{9,10},{11,12},{13,14},{15,16},{17,18},{19... | collective-permute-start | bytes 393224 | tf_op jit(solution)/shard_map/ppermute | solution.py:772
  50.5 2.1 %third.1 = (f32[64,2048]{1,0:T(8,128)S(1)}, f32[64,256]{1,0:T(8,128)S(1)}, f32[64,128]{1,0:T(8,128)S(1)}) custom-call(f32[8,128]{1,0:T(8,128)S(1)} %get-tuple-element.43.after_ref.w_ref, f32[64,2048]{1,0:T(8,128)S(1)} %get-tuple-element.58.u_ref, f32[64,2048]{1,0:T(8,128)S(1)} %get-tuple-element.40.b_ref, bf16[64,2048]{1,0:T(8,128)(2,1)S(1)} %get-tuple-element.59.u16_ref, ...), custom_call_target="tpu_custom_call" | custom-call | flops 700000000 | bytes 10000000 | tf_op jit(solution)/shard_map/third/pallas_call | solution.py:580
  52.6 0.7 collective-permute-done.10.even_ref
  53.3 5.8 %collective-permute-done.9.odd_ref = bf16[64,1024]{1,0:T(8,128)(2,1)S(1)} collective-permute-done((bf16[64,1024]{1,0:T(8,128)(2,1)S(1)}, bf16[64,1024]{1,0:T(8,128)(2,1)S(1)}, u32[]{:S(2)}, u32[]{:S(2)}) %collective-permute-start.9) | collective-permute-done | bytes 131104 | tf_op jit(solution)/shard_map/ppermute | solution.py:772
  59.0 1.2 %finish.1 = (bf16[8,72,256]{2,1,0:T(8,128)(2,1)S(1)}, f32[64,2048]{1,0:T(8,128)S(1)}) custom-call(f32[8,128]{1,0:T(8,128)S(1)} %get-tuple-element.43.after_ref.w_ref, bf16[64,1024]{1,0:T(8,128)(2,1)S(1)} %collective-permute-done.9.odd_ref, bf16[64,1024]{1,0:T(8,128)(2,1)S(1)} %collective-permute-done.10.even_ref, ...), custom_call_target="tpu_custom_call" | custom-call | flops 270000000 | bytes 4000000 | tf_op jit(solution)/shard_map/finish/pallas_call | solution.py:643
  60.2 13.2 %all_to_all.10.refs_0_ = bf16[8,72,256]{2,1,0:T(8,128)(2,1)S(1)} all-to-all(bf16[8,72,256]{2,1,0:T(8,128)(2,1)S(1)} %get-tuple-element.66), channel_id=1, replica_groups=mesh['group'=4,'sub'=8,'leaf'=8] {'leaf'}, dimensions={0} | all-to-all | bytes 589824 | tf_op jit(solution)/shard_map/all_to_all | solution.py:766
  73.8 1.2 %collective-permute-done.11.right_ref = bf16[72,256]{1,0:T(8,128)(2,1)S(1)} collective-permute-done((bf16[72,256]{1,0:T(8,128)(2,1)S(1)}, bf16[72,256]{1,0:T(8,128)(2,1)S(1)}, u32[]{:S(2)}, u32[]{:S(2)}) %collective-permute-start.11) | collective-permute-done | bytes 36896 | tf_op jit(solution)/shard_map/ppermute | solution.py:790
  75.5 2.2 %collective-permute-start.13 = (bf16[72,256]{1,0:T(8,128)(2,1)S(1)}, bf16[72,256]{1,0:T(8,128)(2,1)S(1)}, u32[]{:S(2)}, u32[]{:S(2)}) collective-permute-start(bf16[72,256]{1,0:T(8,128)(2,1)S(1)} %join_sums.1.refs_0_), channel_id=1, source_target_pairs={{0,32},{8,40},{16,48},{24,56},{32,0},{40,8},{48,16},{56,24},{1,33}... | collective-permute-start | bytes 110600 | tf_op jit(solution)/shard_map/ppermute | solution.py:781
  77.7 2.6 %collective-permute-start.14 = (bf16[72,256]{1,0:T(8,128)(2,1)S(1)}, bf16[72,256]{1,0:T(8,128)(2,1)S(1)}, u32[]{:S(2)}, u32[]{:S(2)}) collective-permute-start(bf16[72,256]{1,0:T(8,128)(2,1)S(1)} %join_sums.1.refs_0_), channel_id=1, source_target_pairs={{0,48},{8,56},{16,0},{24,8},{32,16},{40,24},{48,32},{56,40},{1,49}... | collective-permute-start | bytes 110600 | tf_op jit(solution)/shard_map/ppermute | solution.py:781
  80.3 0.7 collective-permute-done.12.refs_1_
  81.1 0.9 collective-permute-done.14.refs_3_
  82.4 1.7 %collective-permute-start.15 = (bf16[72,256]{1,0:T(8,128)(2,1)S(1)}, bf16[72,256]{1,0:T(8,128)(2,1)S(1)}, u32[]{:S(2)}, u32[]{:S(2)}) collective-permute-start(bf16[72,256]{1,0:T(8,128)(2,1)S(1)} %get-tuple-element.68.g0_ref), channel_id=1, source_target_pairs={{0,64},{64,128},{128,192},{192,0},{1,65},{65,129},{129,193},{193,1... | collective-permute-start | bytes 110600 | tf_op jit(solution)/shard_map/ppermute | solution.py:781
  84.1 2.3 %collective-permute-start.16 = (bf16[72,256]{1,0:T(8,128)(2,1)S(1)}, bf16[72,256]{1,0:T(8,128)(2,1)S(1)}, u32[]{:S(2)}, u32[]{:S(2)}) collective-permute-start(bf16[72,256]{1,0:T(8,128)(2,1)S(1)} %get-tuple-element.68.g0_ref), channel_id=1, source_target_pairs={{0,128},{64,192},{128,0},{192,64},{1,129},{65,193},{129,1},{193,65... | collective-permute-start | bytes 110600 | tf_op jit(solution)/shard_map/ppermute | solution.py:781
  86.5 3.1 %collective-permute-done.16.g2_ref = bf16[72,256]{1,0:T(8,128)(2,1)S(1)} collective-permute-done((bf16[72,256]{1,0:T(8,128)(2,1)S(1)}, bf16[72,256]{1,0:T(8,128)(2,1)S(1)}, u32[]{:S(2)}, u32[]{:S(2)}) %collective-permute-start.16) | collective-permute-done | bytes 36896 | tf_op jit(solution)/shard_map/ppermute | solution.py:781
  89.6 0.8 collective-permute-done.17.g3_ref
  90.4 2.3 %last.1 = (f32[64,2048]{1,0:T(8,128)}, f32[64,2048]{1,0:T(8,128)}) custom-call(bf16[72,256]{1,0:T(8,128)(2,1)S(1)} %get-tuple-element.68.g0_ref, bf16[72,256]{1,0:T(8,128)(2,1)S(1)} %collective-permute-done.15.g1_ref, bf16[72,256]{1,0:T(8,128)(2,1)S(1)} %collective-permute-done.16.g2_ref, bf16[72,256]{1,0:T(8,128)(2,1)S(1)} %collective-permute-done.17.g3_ref, ...), custom_call_target="tpu_custom_call" | custom-call | flops 250000000 | bytes 7000000 | tf_op jit(solution)/shard_map/last/pallas_call | solution.py:748
  (31 shorter events, 2.9 us)
Async XLA Ops:
  5.2 21.1 %all-to-all-start = ((bf16[8,64,256]{2,1,0:T(8,128)(2,1)}), bf16[8,64,256]{2,1,0:T(8,128)(2,1)S(1)}, u32[]{:S(2)}, u32[]{:S(2)}) async-start(bf16[8,64,256]{2,1,0:T(8,128)(2,1)} %get-tuple-element.38.after_ref), calls=%async_computation | async-start | bytes 524288 | tf_op jit(solution)/shard_map/all_to_all | solution.py:766
  13.7 13.1 %copy-start.2 = (s32[2,2]{1,0:T(2,128)S(1)}, s32[2,2]{1,0:T(2,128)}, u32[]{:S(2)}) copy-start(s32[2,2]{1,0:T(2,128)} %nb_ref.1) | copy-start | bytes 52
  13.7 13.1 %copy-start.3 = (s32[2]{0:T(128)S(1)}, s32[2]{0:T(128)}, u32[]{:S(2)}) copy-start(s32[2]{0:T(128)} %ct_ref.1) | copy-start | bytes 28
  14.8 27.8 %collective-permute-start.7 = (bf16[1280,256]{1,0:T(8,128)(2,1)}, bf16[1280,256]{1,0:T(8,128)(2,1)S(1)}, u32[]{:S(2)}, u32[]{:S(2)}) collective-permute-start(bf16[1280,256]{1,0:T(8,128)(2,1)} %get-tuple-element.51), channel_id=1, source_target_pairs={{1,2},{3,4},{5,6},{7,8},{9,10},{11,12},{13,14},{15,16},{17,18},{19... | collective-permute-start | bytes 1966088 | tf_op jit(solution)/shard_map/ppermute | solution.py:772
  21.3 21.3 %collective-permute-start.8 = (bf16[1280,256]{1,0:T(8,128)(2,1)}, bf16[1280,256]{1,0:T(8,128)(2,1)}, u32[]{:S(2)}, u32[]{:S(2)}) collective-permute-start(bf16[1280,256]{1,0:T(8,128)(2,1)} %get-tuple-element.52), channel_id=1, source_target_pairs={{0,1},{2,3},{4,5},{6,7},{8,9},{10,11},{12,13},{14,15},{16,17},{18,... | collective-permute-start | bytes 1966088 | tf_op jit(solution)/shard_map/ppermute | solution.py:772
  26.6 2.3 %collective-permute-start = (bf16[64,256]{1,0:T(8,128)(2,1)S(1)}, bf16[64,256]{1,0:T(8,128)(2,1)S(1)}, u32[]{:S(2)}, u32[]{:S(2)}) collective-permute-start(bf16[64,256]{1,0:T(8,128)(2,1)S(1)} %get-tuple-element.42.after_ref.left_ref), channel_id=1, source_target_pairs={{0,8},{8,0},{16,24},{24,16},{32,40},{40,32},{48,56},{56,48},{1,9},... | collective-permute-start | bytes 98312 | tf_op jit(solution)/shard_map/ppermute | solution.py:790
  29.0 8.1 %collective-permute-start.1 = (bf16[64,256]{1,0:T(8,128)(2,1)S(1)}, bf16[64,256]{1,0:T(8,128)(2,1)S(1)}, u32[]{:S(2)}, u32[]{:S(2)}) collective-permute-start(bf16[64,256]{1,0:T(8,128)(2,1)S(1)} %join.1.after_ref.g0_ref), channel_id=1, source_target_pairs={{0,16},{8,24},{16,32},{24,40},{32,48},{40,56},{48,0},{56,8},{1,17}... | collective-permute-start | bytes 98312 | tf_op jit(solution)/shard_map/ppermute | solution.py:781
  30.6 6.7 %collective-permute-start.2 = (bf16[64,256]{1,0:T(8,128)(2,1)S(1)}, bf16[64,256]{1,0:T(8,128)(2,1)S(1)}, u32[]{:S(2)}, u32[]{:S(2)}) collective-permute-start(bf16[64,256]{1,0:T(8,128)(2,1)S(1)} %join.1.after_ref.g0_ref), channel_id=1, source_target_pairs={{0,32},{8,40},{16,48},{24,56},{32,0},{40,8},{48,16},{56,24},{1,33}... | collective-permute-start | bytes 98312 | tf_op jit(solution)/shard_map/ppermute | solution.py:781
  33.5 3.9 %collective-permute-start.3 = (bf16[64,256]{1,0:T(8,128)(2,1)S(1)}, bf16[64,256]{1,0:T(8,128)(2,1)S(1)}, u32[]{:S(2)}, u32[]{:S(2)}) collective-permute-start(bf16[64,256]{1,0:T(8,128)(2,1)S(1)} %join.1.after_ref.g0_ref), channel_id=1, source_target_pairs={{0,48},{8,56},{16,0},{24,8},{32,16},{40,24},{48,32},{56,40},{1,49}... | collective-permute-start | bytes 98312 | tf_op jit(solution)/shard_map/ppermute | solution.py:781
  37.7 9.1 %copy-start = (bf16[2048,256]{1,0:T(8,128)(2,1)S(1)}, bf16[2048,256]{1,0:T(8,128)(2,1)}, u32[]{:S(2)}) copy-start(bf16[2048,256]{1,0:T(8,128)(2,1)} %get-tuple-element.50.g_ref) | copy-start | bytes 3145732
  37.7 9.0 %collective-permute-start.4 = (bf16[64,256]{1,0:T(8,128)(2,1)S(1)}, bf16[64,256]{1,0:T(8,128)(2,1)S(1)}, u32[]{:S(2)}, u32[]{:S(2)}) collective-permute-start(bf16[64,256]{1,0:T(8,128)(2,1)S(1)} %get-tuple-element.47.after_ref.g0_ref), channel_id=1, source_target_pairs={{0,64},{64,128},{128,192},{192,0},{1,65},{65,129},{129,193},{193,1... | collective-permute-start | bytes 98312 | tf_op jit(solution)/shard_map/ppermute | solution.py:781
  39.3 7.5 %collective-permute-start.5 = (bf16[64,256]{1,0:T(8,128)(2,1)S(1)}, bf16[64,256]{1,0:T(8,128)(2,1)S(1)}, u32[]{:S(2)}, u32[]{:S(2)}) collective-permute-start(bf16[64,256]{1,0:T(8,128)(2,1)S(1)} %get-tuple-element.47.after_ref.g0_ref), channel_id=1, source_target_pairs={{0,128},{64,192},{128,0},{192,64},{1,129},{65,193},{129,1},{193,65... | collective-permute-start | bytes 98312 | tf_op jit(solution)/shard_map/ppermute | solution.py:781
  40.4 6.4 %collective-permute-start.6 = (bf16[64,256]{1,0:T(8,128)(2,1)S(1)}, bf16[64,256]{1,0:T(8,128)(2,1)S(1)}, u32[]{:S(2)}, u32[]{:S(2)}) collective-permute-start(bf16[64,256]{1,0:T(8,128)(2,1)S(1)} %get-tuple-element.47.after_ref.g0_ref), channel_id=1, source_target_pairs={{0,192},{64,0},{128,64},{192,128},{1,193},{65,1},{129,65},{193,129... | collective-permute-start | bytes 98312 | tf_op jit(solution)/shard_map/ppermute | solution.py:781
  46.7 3.7 %copy-start.1 = (bf16[1024,1024]{1,0:T(8,128)(2,1)S(1)}, bf16[1024,1024]{1,0:T(8,128)(2,1)}, u32[]{:S(2)}) copy-start(bf16[1024,1024]{1,0:T(8,128)(2,1)} %get-tuple-element.62.table_ab_ref) | copy-start | bytes 6291460
  48.2 5.1 %collective-permute-start.10 = (bf16[64,1024]{1,0:T(8,128)(2,1)S(1)}, bf16[64,1024]{1,0:T(8,128)(2,1)S(1)}, u32[]{:S(2)}, u32[]{:S(2)}) collective-permute-start(bf16[64,1024]{1,0:T(8,128)(2,1)S(1)} %get-tuple-element.55), channel_id=1, source_target_pairs={{0,1},{2,3},{4,5},{6,7},{8,9},{10,11},{12,13},{14,15},{16,17},{18,... | collective-permute-start | bytes 393224 | tf_op jit(solution)/shard_map/ppermute | solution.py:772
  48.5 10.5 %collective-permute-start.9 = (bf16[64,1024]{1,0:T(8,128)(2,1)S(1)}, bf16[64,1024]{1,0:T(8,128)(2,1)S(1)}, u32[]{:S(2)}, u32[]{:S(2)}) collective-permute-start(bf16[64,1024]{1,0:T(8,128)(2,1)S(1)} %get-tuple-element.54), channel_id=1, source_target_pairs={{1,2},{3,4},{5,6},{7,8},{9,10},{11,12},{13,14},{15,16},{17,18},{19... | collective-permute-start | bytes 393224 | tf_op jit(solution)/shard_map/ppermute | solution.py:772
  73.8 1.2 %collective-permute-start.11 = (bf16[72,256]{1,0:T(8,128)(2,1)S(1)}, bf16[72,256]{1,0:T(8,128)(2,1)S(1)}, u32[]{:S(2)}, u32[]{:S(2)}) collective-permute-start(bf16[72,256]{1,0:T(8,128)(2,1)S(1)} %get-tuple-element.67.left_ref), channel_id=1, source_target_pairs={{0,8},{8,0},{16,24},{24,16},{32,40},{40,32},{48,56},{56,48},{1,9},... | collective-permute-start | bytes 110600 | tf_op jit(solution)/shard_map/ppermute | solution.py:790
  75.5 5.5 %collective-permute-start.12 = (bf16[72,256]{1,0:T(8,128)(2,1)S(1)}, bf16[72,256]{1,0:T(8,128)(2,1)S(1)}, u32[]{:S(2)}, u32[]{:S(2)}) collective-permute-start(bf16[72,256]{1,0:T(8,128)(2,1)S(1)} %join_sums.1.refs_0_), channel_id=1, source_target_pairs={{0,16},{8,24},{16,32},{24,40},{32,48},{40,56},{48,0},{56,8},{1,17}... | collective-permute-start | bytes 110600 | tf_op jit(solution)/shard_map/ppermute | solution.py:781
  75.5 5.6 %collective-permute-start.13 = (bf16[72,256]{1,0:T(8,128)(2,1)S(1)}, bf16[72,256]{1,0:T(8,128)(2,1)S(1)}, u32[]{:S(2)}, u32[]{:S(2)}) collective-permute-start(bf16[72,256]{1,0:T(8,128)(2,1)S(1)} %join_sums.1.refs_0_), channel_id=1, source_target_pairs={{0,32},{8,40},{16,48},{24,56},{32,0},{40,8},{48,16},{56,24},{1,33}... | collective-permute-start | bytes 110600 | tf_op jit(solution)/shard_map/ppermute | solution.py:781
  77.7 4.2 %collective-permute-start.14 = (bf16[72,256]{1,0:T(8,128)(2,1)S(1)}, bf16[72,256]{1,0:T(8,128)(2,1)S(1)}, u32[]{:S(2)}, u32[]{:S(2)}) collective-permute-start(bf16[72,256]{1,0:T(8,128)(2,1)S(1)} %join_sums.1.refs_0_), channel_id=1, source_target_pairs={{0,48},{8,56},{16,0},{24,8},{32,16},{40,24},{48,32},{56,40},{1,49}... | collective-permute-start | bytes 110600 | tf_op jit(solution)/shard_map/ppermute | solution.py:781
  82.4 4.1 %collective-permute-start.15 = (bf16[72,256]{1,0:T(8,128)(2,1)S(1)}, bf16[72,256]{1,0:T(8,128)(2,1)S(1)}, u32[]{:S(2)}, u32[]{:S(2)}) collective-permute-start(bf16[72,256]{1,0:T(8,128)(2,1)S(1)} %get-tuple-element.68.g0_ref), channel_id=1, source_target_pairs={{0,64},{64,128},{128,192},{192,0},{1,65},{65,129},{129,193},{193,1... | collective-permute-start | bytes 110600 | tf_op jit(solution)/shard_map/ppermute | solution.py:781
  84.1 5.5 %collective-permute-start.16 = (bf16[72,256]{1,0:T(8,128)(2,1)S(1)}, bf16[72,256]{1,0:T(8,128)(2,1)S(1)}, u32[]{:S(2)}, u32[]{:S(2)}) collective-permute-start(bf16[72,256]{1,0:T(8,128)(2,1)S(1)} %get-tuple-element.68.g0_ref), channel_id=1, source_target_pairs={{0,128},{64,192},{128,0},{192,64},{1,129},{65,193},{129,1},{193,65... | collective-permute-start | bytes 110600 | tf_op jit(solution)/shard_map/ppermute | solution.py:781
  86.4 4.0 %collective-permute-start.17 = (bf16[72,256]{1,0:T(8,128)(2,1)S(1)}, bf16[72,256]{1,0:T(8,128)(2,1)S(1)}, u32[]{:S(2)}, u32[]{:S(2)}) collective-permute-start(bf16[72,256]{1,0:T(8,128)(2,1)S(1)} %get-tuple-element.68.g0_ref), channel_id=1, source_target_pairs={{0,192},{64,0},{128,64},{192,128},{1,193},{65,1},{129,65},{193,129... | collective-permute-start | bytes 110600 | tf_op jit(solution)/shard_map/ppermute | solution.py:781

commit v8 on v7

--- a/solution.py
+++ b/solution.py
@@ -284,14 +284,8 @@
         table_ref[block(i), :] = gauss(rows, left_column(rows), points, row).astype(bf16)
 
 
-def prepare_kernel(
-    nb_ref, ct_ref, x_ref, z2_ref, z3_ref, after_ref, row_ref, w_ref, t2_ref, z_ref, z_sem
-):
+def prepare_kernel(nb_ref, ct_ref, after_ref, w_ref):
     del after_ref
-    loads = []
-    for k, source in enumerate((z2_ref, z3_ref)):
-        loads.append(pltpu.make_async_copy(source, z_ref.at[k], z_sem.at[k]))
-        loads[k].start()
     first = first_leaf_of()
     weights = (
         listed(nb_ref, ct_ref, 0, first - 1),
@@ -304,27 +298,17 @@
     for k in range(4):
         spread = jnp.where(place == k, weights[k], spread)
     w_ref[...] = spread
-    row_ref[...] = right_row(x_ref[...])
-    for load in loads:
-        load.wait()
-    z2, z3 = z_ref[0], z_ref[1]
-    t2_ref[...] = gauss(z2, left_column(z2), z3, right_row(z3))
-
-
-def prepare_call(neighbors, counts, points, z2, z3, after):
+
+
+def prepare_call(neighbors, counts, after):
     return pl.pallas_call(
         prepare_kernel,
-        in_specs=[smem(), smem()] + inside(1) + outside(2) + [anywhere()],
-        out_shape=(
-            shape_of((1, 2 * LEAF), f32),
-            shape_of((8, 128), f32),
-            shape_of((SKEL, SKEL), f32),
-        ),
-        scratch_shapes=[pltpu.VMEM((2, SKEL, DIM), bf16), pltpu.SemaphoreType.DMA((2,))],
+        in_specs=[smem(), smem(), anywhere()],
+        out_shape=shape_of((8, 128), f32),
         compiler_params=params,
         cost_estimate=cost(50_000_000, 2_000_000, 65_536),
         name="prepare",
-    )(neighbors, counts, points, in_hbm(z2), in_hbm(z3), after)
+    )(neighbors, counts, after)
 
 
 def inner_kernel(x_ref, b_ref, after_ref, table_ref, out_ref, tv_ref, sem):
@@ -358,84 +342,100 @@
     )(points, field, after)
 
 
-def tables_kernel(x_ref, b_ref, row_ref, after_ref, table_a_ref, table_b_ref, own_ref):
+def tables_kernel(
+    x_ref, b_ref, z2_ref, z3_ref, after_ref, table_ref, own_ref, row_ref, t2_ref, z_ref, z_sem
+):
     del after_ref
-    make_symmetric(x_ref[:LEAF, :], row_ref[:, :LEAF], table_a_ref)
-    make_symmetric(x_ref[LEAF:, :], row_ref[:, LEAF:], table_b_ref)
-    own_ref[:, :LEAF] = dot_symmetric(b_ref[:, :LEAF].astype(bf16), table_a_ref)
-    own_ref[:, LEAF:] = dot_symmetric(b_ref[:, LEAF:].astype(bf16), table_b_ref)
-
-
-def tables_call(points, field, row, after):
+    loads = []
+    for k, source in enumerate((z2_ref, z3_ref)):
+        loads.append(pltpu.make_async_copy(source, z_ref.at[k], z_sem.at[k]))
+        loads[k].start()
+    row_ref[...] = right_row(x_ref[...])
+    make_symmetric(x_ref[:LEAF, :], row_ref[:, :LEAF], table_ref)
+    own_ref[...] = dot_symmetric(b_ref[:, :LEAF].astype(bf16), table_ref)
+    for load in loads:
+        load.wait()
+    z2, z3 = z_ref[0], z_ref[1]
+    t2_ref[...] = gauss(z2, left_column(z2), z3, right_row(z3))
+
+
+def tables_call(points, field, z2, z3, after):
     return pl.pallas_call(
         tables_kernel,
-        in_specs=inside(3) + [anywhere()],
+        in_specs=inside(2) + outside(2) + [anywhere()],
         out_shape=(
+            shape_of((LEAF, LEAF), bf16),
+            shape_of((RHS, LEAF), f32),
+            shape_of((1, 2 * LEAF), f32),
+            shape_of((SKEL, SKEL), f32),
+        ),
+        scratch_shapes=[pltpu.VMEM((2, SKEL, DIM), bf16), pltpu.SemaphoreType.DMA((2,))],
+        compiler_params=params,
+        cost_estimate=cost(3_000_000_000, 9_000_000, 2_400_000),
+        name="tables",
+    )(points, field, in_hbm(z2), in_hbm(z3), after)
+
+
+def unfold(halo):
+    parts = [halo[LEAF + k * RHS : LEAF + (k + 1) * RHS, :] for k in range(STEPS)]
+    return jnp.concatenate(parts, axis=1)
+
+
+def in_order(odd_ref, even_ref):
+    even = even_leaf()
+    odd_got, even_got = odd_ref[...], even_ref[...]
+    return jnp.where(even, odd_got, even_got), jnp.where(even, even_got, odd_got)
+
+
+def around_kernel(
+    w_ref, odd_ref, even_ref, x_ref, b_ref, inner_ref, row_ref, own_ref, after_ref,
+    table_b_ref, below_table_ref, above_table_ref, out_ref, halo_ref, sem
+):
+    del after_ref
+    parity = lax.rem(lax.axis_index("leaf"), 2)
+    loads = []
+    for k, source in enumerate((odd_ref, even_ref)):
+        slot = parity if k == 0 else 1 - parity
+        loads.append(pltpu.make_async_copy(source, halo_ref.at[slot], sem.at[k]))
+    for load in loads:
+        load.start()
+    x_a, x_b = x_ref[:LEAF, :], x_ref[LEAF:, :]
+    row_a, row_b = row_ref[:, :LEAF], row_ref[:, LEAF:]
+    make_symmetric(x_b, row_b, table_b_ref)
+    own_b = dot_symmetric(b_ref[:, LEAF:].astype(bf16), table_b_ref)
+    near_a = own_ref[...] + weight_of(w_ref, 1) * inner_ref[:, :LEAF]
+    near_b = own_b + weight_of(w_ref, 2) * inner_ref[:, LEAF:]
+    for load in loads:
+        load.wait()
+    below_ref, above_ref = halo_ref.at[0], halo_ref.at[1]
+    make_block(below_ref, x_a, row_a, below_table_ref)
+    out_ref[:, :LEAF] = near_a + weight_of(w_ref, 0) * nn(
+        unfold(below_ref), below_table_ref[...]
+    )
+    make_block(above_ref, x_b, row_b, above_table_ref)
+    out_ref[:, LEAF:] = near_b + weight_of(w_ref, 3) * nn(
+        unfold(above_ref), above_table_ref[...]
+    )
+
+
+def around_call(w, odd, even, points, field, inner, row, own, after):
+    return pl.pallas_call(
+        around_kernel,
+        in_specs=inside(1) + [anywhere()] * 2 + inside(5) + [anywhere()],
+        out_shape=(
+            shape_of((LEAF, LEAF), bf16),
             shape_of((LEAF, LEAF), bf16),
             shape_of((LEAF, LEAF), bf16),
             shape_of((RHS, 2 * LEAF), f32),
         ),
-        compiler_params=params,
-        cost_estimate=cost(3_000_000_000, 9_000_000, 2_400_000),
-        name="tables",
-    )(points, field, row, after)
-
-
-def unfold(halo):
-    parts = [halo[LEAF + k * RHS : LEAF + (k + 1) * RHS, :] for k in range(STEPS)]
-    return jnp.concatenate(parts, axis=1)
-
-
-def in_order(odd_ref, even_ref):
-    even = even_leaf()
-    odd_got, even_got = odd_ref[...], even_ref[...]
-    return jnp.where(even, odd_got, even_got), jnp.where(even, even_got, odd_got)
-
-
-def around_kernel(
-    w_ref, odd_ref, even_ref, x_ref, inner_ref, row_ref, own_ref, after_ref,
-    below_table_ref, above_table_ref, out_ref
-):
-    del after_ref
-    x_a, x_b = x_ref[:LEAF, :], x_ref[LEAF:, :]
-    row_a, row_b = row_ref[:, :LEAF], row_ref[:, LEAF:]
-    near_a = own_ref[:, :LEAF] + weight_of(w_ref, 1) * inner_ref[:, :LEAF]
-    near_b = own_ref[:, LEAF:] + weight_of(w_ref, 2) * inner_ref[:, LEAF:]
-
-    def build(below_ref, above_ref):
-        make_block(below_ref, x_a, row_a, below_table_ref)
-        out_ref[:, :LEAF] = near_a + weight_of(w_ref, 0) * nn(
-            unfold(below_ref), below_table_ref[...]
-        )
-        make_block(above_ref, x_b, row_b, above_table_ref)
-        out_ref[:, LEAF:] = near_b + weight_of(w_ref, 3) * nn(
-            unfold(above_ref), above_table_ref[...]
-        )
-
-    even = even_leaf()
-
-    @pl.when(even)
-    def _():
-        build(odd_ref, even_ref)
-
-    @pl.when(jnp.logical_not(even))
-    def _():
-        build(even_ref, odd_ref)
-
-
-def around_call(w, odd, even, points, inner, row, own, after):
-    return pl.pallas_call(
-        around_kernel,
-        in_specs=inside(7) + [anywhere()],
-        out_shape=(
-            shape_of((LEAF, LEAF), bf16),
-            shape_of((LEAF, LEAF), bf16),
-            shape_of((RHS, 2 * LEAF), f32),
-        ),
+        scratch_shapes=[
+            pltpu.VMEM((2, LEAF + STEPS * RHS, DIM), bf16),
+            pltpu.SemaphoreType.DMA((2,)),
+        ],
         compiler_params=params,
         cost_estimate=cost(2_200_000_000, 9_000_000, 3_145_728),
         name="around",
-    )(w, odd, even, points, inner, row, own, after)
+    )(w, odd, even, points, field, inner, row, own, after)
 
 
 def total_of(got_ref):
@@ -797,13 +797,15 @@
     table_ab, inner = inner_call(x, b, sent)
     up_one, sent = climb_call(exchange(sent, "leaf"), t1, inner)
     other = swapped(sent, "sub")
-    row, w, t2 = prepare_call(neighbors, counts, x, skel_group, skel_top, sent)
+    w = prepare_call(neighbors, counts, sent)
     sent = join_call(sent, other, w)
     parts = turns(sent, "sub", 2)
-    table_a, table_b, own = tables_call(x, b, row, sent)
+    table_a, own, row, t2 = tables_call(x, b, skel_group, skel_top, sent)
     up_two, sent = climb_four_call(parts, t2, own)
     parts = turns(sent, "group", 1)
-    below_table, above_table, own = around_call(w, odd, even, x, inner, row, own, sent)
+    table_b, below_table, above_table, own = around_call(
+        w, odd, even, x, b, inner, row, own, sent
+    )
     u, u16, odd, even = second_call(parts, up_one, up_two, t1, t2, g, own)
 
     odd, even = swap_both(odd, even)

time: 93.5 us -> 93.6 us (level)
  transfers between devices with their start and end apart: 19 -> 19, of which waited for: 11 -> 12; matrix products, arithmetic and copies ran while one was open for 0% -> 0% of each run, Pallas kernels for 16% -> 15%
where the time goes in v8:
time: 93.6 us; the launch traced here: 92.7 us
  starting transfers between devices  36.5 us (39%)
  Pallas kernels  24.9 us (27%)
  waiting for transfers between devices  17.1 us (18%)
  blocking collectives  13.2 us (14%)
  between operations  1 us (1%)
    ppermute x12, starting transfers between devices, turned(): lax.ppermute(value, axis, [(i, (i + shift) % count) for i in range(count)])  19.2 us
    all_to_all x1, blocking collectives, exchange(): return lax.all_to_all(sent, axis, 0, 0)  13.2 us
    ppermute x4, starting transfers between devices, chain_swap(): return lax.ppermute(value, ALL, pairs + [(j, i) for i, j in pairs])  8.79 us
    all_to_all x1, starting transfers between devices, exchange(): return lax.all_to_all(sent, axis, 0, 0)  8.47 us
    ppermute x4, waiting for transfers between devices, chain_swap(): return lax.ppermute(value, ALL, pairs + [(j, i) for i, j in pairs])  6.45 us
    ppermute x12, waiting for transfers between devices, turned(): lax.ppermute(value, axis, [(i, (i + shift) % count) for i in range(count)])  6.31 us
    pallas_call x1, Pallas kernels, around_call(): pl.pallas_call(around_kernel, in_specs=inside(1) + [anywhere()] * 2 + ins...  5.23 us
    pallas_call x1, Pallas kernels, start_call(): pl.pallas_call(start_kernel, in_specs=outside(4), out_specs=tuple(inside(...  4.57 us
  transfers between devices with their start and end apart: 19, of which 12 were waited for; matrix products, arithmetic and copies ran while one was open for 0% of the time, Pallas kernels for 15%

profile of v8, /device:TPU:2, one launch (start us, length us, event | category | flops | bytes accessed | tf_op | source)
XLA Modules:
  0.0 92.7 jit_solution(8936510222520908007)
XLA Ops:
  0.6 4.6 %start.1 = (bf16[8,64,256]{2,1,0:T(8,128)(2,1)}, bf16[2048,256]{1,0:T(8,128)(2,1)}, f32[256,256]{1,0:T(8,128)S(1)}, bf16[2048,256]{1,0:T(8,128)(2,1)S(1)}, f32[64,2048]{1,0:T(8,128)S(1)}) custom-call(bf16[2048,256]{1,0:T(8,128)(2,1)} %x_ref.1, f32[64,2048]{1,0:T(8,128)} %b_ref.1, bf16[256,256]{1,0:T(8,128)(2,1)} %z1_ref.1, bf16[256,256]{1,0:T(8,128)(2,1)} %z2_ref.3), custom_call_target="tpu_custom_call" | custom-call | flops 600000000 | bytes 5000000 | tf_op jit(solution)/shard_map/start/pallas_call | solution.py:152
  5.2 8.5 %all-to-all-start = ((bf16[8,64,256]{2,1,0:T(8,128)(2,1)}), bf16[8,64,256]{2,1,0:T(8,128)(2,1)S(1)}, u32[]{:S(2)}, u32[]{:S(2)}) async-start(bf16[8,64,256]{2,1,0:T(8,128)(2,1)} %get-tuple-element.36.after_ref), calls=%async_computation | async-start | bytes 524288 | tf_op jit(solution)/shard_map/all_to_all | solution.py:766
  13.7 1.1 %pack.1 = (bf16[1280,256]{1,0:T(8,128)(2,1)}, bf16[1280,256]{1,0:T(8,128)(2,1)}) custom-call(bf16[2048,256]{1,0:T(8,128)(2,1)S(1)} %get-tuple-element.38.x_ref, f32[64,2048]{1,0:T(8,128)S(1)} %get-tuple-element.39.b_ref), custom_call_target="tpu_custom_call" | custom-call | flops 1000000 | bytes 5000000 | tf_op jit(solution)/shard_map/pack/pallas_call | solution.py:206
  14.8 6.4 %collective-permute-start.7 = (bf16[1280,256]{1,0:T(8,128)(2,1)}, bf16[1280,256]{1,0:T(8,128)(2,1)S(1)}, u32[]{:S(2)}, u32[]{:S(2)}) collective-permute-start(bf16[1280,256]{1,0:T(8,128)(2,1)} %get-tuple-element.48), channel_id=1, source_target_pairs={{1,2},{3,4},{5,6},{7,8},{9,10},{11,12},{13,14},{15,16},{17,18},{19... | collective-permute-start | bytes 1966088 | tf_op jit(solution)/shard_map/ppermute | solution.py:772
  21.4 2.4 %inner.1 = (bf16[1024,1024]{1,0:T(8,128)(2,1)}, f32[64,2048]{1,0:T(8,128)S(1)}) custom-call(bf16[2048,256]{1,0:T(8,128)(2,1)S(1)} %get-tuple-element.38.x_ref, f32[64,2048]{1,0:T(8,128)S(1)} %get-tuple-element.39.b_ref, bf16[8,64,256]{2,1,0:T(8,128)(2,1)} %get-tuple-element.36.after_ref), custom_call_target="tpu_custom_call" | custom-call | flops 100000000 | bytes 1000000 | tf_op jit(solution)/shard_map/inner/pallas_call | solution.py:333
  23.8 2.6 %all-to-all-done.got_ref = bf16[8,64,256]{2,1,0:T(8,128)(2,1)S(1)} async-done(((bf16[8,64,256]{2,1,0:T(8,128)(2,1)}), bf16[8,64,256]{2,1,0:T(8,128)(2,1)S(1)}, u32[]{:S(2)}, u32[]{:S(2)}) %all-to-all-start) | async-done | bytes 262176 | tf_op jit(solution)/shard_map/all_to_all | solution.py:766
  26.7 0.6 prepare.1.after_ref.w_ref
  27.3 0.6 collective-permute-done.right_ref
  27.9 1.7 %collective-permute-start.1 = (bf16[64,256]{1,0:T(8,128)(2,1)S(1)}, bf16[64,256]{1,0:T(8,128)(2,1)S(1)}, u32[]{:S(2)}, u32[]{:S(2)}) collective-permute-start(bf16[64,256]{1,0:T(8,128)(2,1)S(1)} %join.1.after_ref.g0_ref), channel_id=1, source_target_pairs={{0,16},{8,24},{16,32},{24,40},{32,48},{40,56},{48,0},{56,8},{1,17}... | collective-permute-start | bytes 98312 | tf_op jit(solution)/shard_map/ppermute | solution.py:781
  29.6 2.9 %collective-permute-start.2 = (bf16[64,256]{1,0:T(8,128)(2,1)S(1)}, bf16[64,256]{1,0:T(8,128)(2,1)S(1)}, u32[]{:S(2)}, u32[]{:S(2)}) collective-permute-start(bf16[64,256]{1,0:T(8,128)(2,1)S(1)} %join.1.after_ref.g0_ref), channel_id=1, source_target_pairs={{0,32},{8,40},{16,48},{24,56},{32,0},{40,8},{48,16},{56,24},{1,33}... | collective-permute-start | bytes 98312 | tf_op jit(solution)/shard_map/ppermute | solution.py:781
  32.5 1.3 %collective-permute-start.3 = (bf16[64,256]{1,0:T(8,128)(2,1)S(1)}, bf16[64,256]{1,0:T(8,128)(2,1)S(1)}, u32[]{:S(2)}, u32[]{:S(2)}) collective-permute-start(bf16[64,256]{1,0:T(8,128)(2,1)S(1)} %join.1.after_ref.g0_ref), channel_id=1, source_target_pairs={{0,48},{8,56},{16,0},{24,8},{32,16},{40,24},{48,32},{56,40},{1,49}... | collective-permute-start | bytes 98312 | tf_op jit(solution)/shard_map/ppermute | solution.py:781
  33.8 2.1 %tables.1 = (bf16[1024,1024]{1,0:T(8,128)(2,1)S(1)}, f32[64,1024]{1,0:T(8,128)S(1)}, f32[1,2048]{1,0:T(1,128)S(1)}, f32[256,256]{1,0:T(8,128)S(1)}) custom-call(bf16[2048,256]{1,0:T(8,128)(2,1)S(1)} %get-tuple-element.38.x_ref, f32[64,2048]{1,0:T(8,128)S(1)} %get-tuple-element.39.b_ref, bf16[256,256]{1,0:T(8,128)(2,1)} %z2_ref.3, bf16[256,256]{1,0:T(8,128)(2,1)} %z3_ref.1, ...), custom_call_target="tpu_custom_call" | custom-call | flops 3000000000 | bytes 9000000 | tf_op jit(solution)/shard_map/tables/pallas_call | solution.py:363
  36.7 1.6 %collective-permute-start.4 = (bf16[64,256]{1,0:T(8,128)(2,1)S(1)}, bf16[64,256]{1,0:T(8,128)(2,1)S(1)}, u32[]{:S(2)}, u32[]{:S(2)}) collective-permute-start(bf16[64,256]{1,0:T(8,128)(2,1)S(1)} %get-tuple-element.44.after_ref.g0_ref), channel_id=1, source_target_pairs={{0,64},{64,128},{128,192},{192,0},{1,65},{65,129},{129,193},{193,1... | collective-permute-start | bytes 98312 | tf_op jit(solution)/shard_map/ppermute | solution.py:781
  38.2 1.1 %collective-permute-start.5 = (bf16[64,256]{1,0:T(8,128)(2,1)S(1)}, bf16[64,256]{1,0:T(8,128)(2,1)S(1)}, u32[]{:S(2)}, u32[]{:S(2)}) collective-permute-start(bf16[64,256]{1,0:T(8,128)(2,1)S(1)} %get-tuple-element.44.after_ref.g0_ref), channel_id=1, source_target_pairs={{0,128},{64,192},{128,0},{192,64},{1,129},{65,193},{129,1},{193,65... | collective-permute-start | bytes 98312 | tf_op jit(solution)/shard_map/ppermute | solution.py:781
  39.3 2.2 %collective-permute-start.6 = (bf16[64,256]{1,0:T(8,128)(2,1)S(1)}, bf16[64,256]{1,0:T(8,128)(2,1)S(1)}, u32[]{:S(2)}, u32[]{:S(2)}) collective-permute-start(bf16[64,256]{1,0:T(8,128)(2,1)S(1)} %get-tuple-element.44.after_ref.g0_ref), channel_id=1, source_target_pairs={{0,192},{64,0},{128,64},{192,128},{1,193},{65,1},{129,65},{193,129... | collective-permute-start | bytes 98312 | tf_op jit(solution)/shard_map/ppermute | solution.py:781
  41.5 5.2 %around.1 = (bf16[1024,1024]{1,0:T(8,128)(2,1)S(1)}, bf16[1024,1024]{1,0:T(8,128)(2,1)S(1)}, bf16[1024,1024]{1,0:T(8,128)(2,1)S(1)}, f32[64,2048]{1,0:T(8,128)S(1)}) custom-call(f32[8,128]{1,0:T(8,128)S(1)} %prepare.1.after_ref.w_ref, bf16[1280,256]{1,0:T(8,128)(2,1)S(1)} %collective-permute-done.7.odd_ref, ...), custom_call_target="tpu_custom_call" | custom-call | flops 2200000000 | bytes 9000000 | tf_op jit(solution)/shard_map/around/pallas_call | solution.py:422
  46.8 1.4 %second.1 = (f32[64,2048]{1,0:T(8,128)S(1)}, bf16[64,2048]{1,0:T(8,128)(2,1)S(1)}, bf16[64,1024]{1,0:T(8,128)(2,1)S(1)}, bf16[64,1024]{1,0:T(8,128)(2,1)S(1)}) custom-call(bf16[64,256]{1,0:T(8,128)(2,1)S(1)} %get-tuple-element.44.after_ref.g0_ref, bf16[64,256]{1,0:T(8,128)(2,1)S(1)} %collective-permute-done.4.g1_ref, ...), custom_call_target="tpu_custom_call" | custom-call | flops 250000000 | bytes 5000000 | tf_op jit(solution)/shard_map/second/pallas_call | solution.py:539
  48.6 1.9 %collective-permute-start.9 = (bf16[64,1024]{1,0:T(8,128)(2,1)S(1)}, bf16[64,1024]{1,0:T(8,128)(2,1)S(1)}, u32[]{:S(2)}, u32[]{:S(2)}) collective-permute-start(bf16[64,1024]{1,0:T(8,128)(2,1)S(1)} %get-tuple-element.52), channel_id=1, source_target_pairs={{1,2},{3,4},{5,6},{7,8},{9,10},{11,12},{13,14},{15,16},{17,18},{19... | collective-permute-start | bytes 393224 | tf_op jit(solution)/shard_map/ppermute | solution.py:772
  50.5 2.1 %third.1 = (f32[64,2048]{1,0:T(8,128)S(1)}, f32[64,256]{1,0:T(8,128)S(1)}, f32[64,128]{1,0:T(8,128)S(1)}) custom-call(f32[8,128]{1,0:T(8,128)S(1)} %prepare.1.after_ref.w_ref, f32[64,2048]{1,0:T(8,128)S(1)} %get-tuple-element.56.u_ref, f32[64,2048]{1,0:T(8,128)S(1)} %get-tuple-element.39.b_ref, bf16[64,2048]{1,0:T(8,128)(2,1)S(1)} %get-tuple-element.57.u16_ref, ...), custom_call_target="tpu_custom_call" | custom-call | flops 700000000 | bytes 10000000 | tf_op jit(solution)/shard_map/third/pallas_call | solution.py:580
  52.7 0.7 collective-permute-done.10.even_ref
  53.3 5.8 %collective-permute-done.9.odd_ref = bf16[64,1024]{1,0:T(8,128)(2,1)S(1)} collective-permute-done((bf16[64,1024]{1,0:T(8,128)(2,1)S(1)}, bf16[64,1024]{1,0:T(8,128)(2,1)S(1)}, u32[]{:S(2)}, u32[]{:S(2)}) %collective-permute-start.9) | collective-permute-done | bytes 131104 | tf_op jit(solution)/shard_map/ppermute | solution.py:772
  59.1 1.2 %finish.1 = (bf16[8,72,256]{2,1,0:T(8,128)(2,1)S(1)}, f32[64,2048]{1,0:T(8,128)S(1)}) custom-call(f32[8,128]{1,0:T(8,128)S(1)} %prepare.1.after_ref.w_ref, bf16[64,1024]{1,0:T(8,128)(2,1)S(1)} %collective-permute-done.9.odd_ref, bf16[64,1024]{1,0:T(8,128)(2,1)S(1)} %collective-permute-done.10.even_ref, ...), custom_call_target="tpu_custom_call" | custom-call | flops 270000000 | bytes 4000000 | tf_op jit(solution)/shard_map/finish/pallas_call | solution.py:643
  60.3 13.2 %all_to_all.10.refs_0_ = bf16[8,72,256]{2,1,0:T(8,128)(2,1)S(1)} all-to-all(bf16[8,72,256]{2,1,0:T(8,128)(2,1)S(1)} %get-tuple-element.64), channel_id=1, replica_groups=mesh['group'=4,'sub'=8,'leaf'=8] {'leaf'}, dimensions={0} | all-to-all | bytes 589824 | tf_op jit(solution)/shard_map/all_to_all | solution.py:766
  73.9 1.2 %collective-permute-done.11.right_ref = bf16[72,256]{1,0:T(8,128)(2,1)S(1)} collective-permute-done((bf16[72,256]{1,0:T(8,128)(2,1)S(1)}, bf16[72,256]{1,0:T(8,128)(2,1)S(1)}, u32[]{:S(2)}, u32[]{:S(2)}) %collective-permute-start.11) | collective-permute-done | bytes 36896 | tf_op jit(solution)/shard_map/ppermute | solution.py:790
  75.6 2.9 %collective-permute-start.13 = (bf16[72,256]{1,0:T(8,128)(2,1)S(1)}, bf16[72,256]{1,0:T(8,128)(2,1)S(1)}, u32[]{:S(2)}, u32[]{:S(2)}) collective-permute-start(bf16[72,256]{1,0:T(8,128)(2,1)S(1)} %join_sums.1.refs_0_), channel_id=1, source_target_pairs={{0,32},{8,40},{16,48},{24,56},{32,0},{40,8},{48,16},{56,24},{1,33}... | collective-permute-start | bytes 110600 | tf_op jit(solution)/shard_map/ppermute | solution.py:781
  78.4 1.9 %collective-permute-start.14 = (bf16[72,256]{1,0:T(8,128)(2,1)S(1)}, bf16[72,256]{1,0:T(8,128)(2,1)S(1)}, u32[]{:S(2)}, u32[]{:S(2)}) collective-permute-start(bf16[72,256]{1,0:T(8,128)(2,1)S(1)} %join_sums.1.refs_0_), channel_id=1, source_target_pairs={{0,48},{8,56},{16,0},{24,8},{32,16},{40,24},{48,32},{56,40},{1,49}... | collective-permute-start | bytes 110600 | tf_op jit(solution)/shard_map/ppermute | solution.py:781
  80.3 0.9 collective-permute-done.12.refs_1_
  81.3 1.1 %collective-permute-done.14.refs_3_ = bf16[72,256]{1,0:T(8,128)(2,1)S(1)} collective-permute-done((bf16[72,256]{1,0:T(8,128)(2,1)S(1)}, bf16[72,256]{1,0:T(8,128)(2,1)S(1)}, u32[]{:S(2)}, u32[]{:S(2)}) %collective-permute-start.14) | collective-permute-done | bytes 36896 | tf_op jit(solution)/shard_map/ppermute | solution.py:781
  82.8 1.5 %collective-permute-start.15 = (bf16[72,256]{1,0:T(8,128)(2,1)S(1)}, bf16[72,256]{1,0:T(8,128)(2,1)S(1)}, u32[]{:S(2)}, u32[]{:S(2)}) collective-permute-start(bf16[72,256]{1,0:T(8,128)(2,1)S(1)} %get-tuple-element.66.g0_ref), channel_id=1, source_target_pairs={{0,64},{64,128},{128,192},{192,0},{1,65},{65,129},{129,193},{193,1... | collective-permute-start | bytes 110600 | tf_op jit(solution)/shard_map/ppermute | solution.py:781
  84.3 2.0 %collective-permute-start.16 = (bf16[72,256]{1,0:T(8,128)(2,1)S(1)}, bf16[72,256]{1,0:T(8,128)(2,1)S(1)}, u32[]{:S(2)}, u32[]{:S(2)}) collective-permute-start(bf16[72,256]{1,0:T(8,128)(2,1)S(1)} %get-tuple-element.66.g0_ref), channel_id=1, source_target_pairs={{0,128},{64,192},{128,0},{192,64},{1,129},{65,193},{129,1},{193,65... | collective-permute-start | bytes 110600 | tf_op jit(solution)/shard_map/ppermute | solution.py:781
  86.8 3.0 %collective-permute-done.16.g2_ref = bf16[72,256]{1,0:T(8,128)(2,1)S(1)} collective-permute-done((bf16[72,256]{1,0:T(8,128)(2,1)S(1)}, bf16[72,256]{1,0:T(8,128)(2,1)S(1)}, u32[]{:S(2)}, u32[]{:S(2)}) %collective-permute-start.16) | collective-permute-done | bytes 36896 | tf_op jit(solution)/shard_map/ppermute | solution.py:781
  90.3 2.3 %last.1 = (f32[64,2048]{1,0:T(8,128)}, f32[64,2048]{1,0:T(8,128)}) custom-call(bf16[72,256]{1,0:T(8,128)(2,1)S(1)} %get-tuple-element.66.g0_ref, bf16[72,256]{1,0:T(8,128)(2,1)S(1)} %collective-permute-done.15.g1_ref, bf16[72,256]{1,0:T(8,128)(2,1)S(1)} %collective-permute-done.16.g2_ref, bf16[72,256]{1,0:T(8,128)(2,1)S(1)} %collective-permute-done.17.g3_ref, ...), custom_call_target="tpu_custom_call" | custom-call | flops 250000000 | bytes 7000000 | tf_op jit(solution)/shard_map/last/pallas_call | solution.py:748
  (31 shorter events, 3.8 us)
Async XLA Ops:
  5.2 21.1 %all-to-all-start = ((bf16[8,64,256]{2,1,0:T(8,128)(2,1)}), bf16[8,64,256]{2,1,0:T(8,128)(2,1)S(1)}, u32[]{:S(2)}, u32[]{:S(2)}) async-start(bf16[8,64,256]{2,1,0:T(8,128)(2,1)} %get-tuple-element.36.after_ref), calls=%async_computation | async-start | bytes 524288 | tf_op jit(solution)/shard_map/all_to_all | solution.py:766
  13.7 13.0 %copy-start.2 = (s32[2,2]{1,0:T(2,128)S(1)}, s32[2,2]{1,0:T(2,128)}, u32[]{:S(2)}) copy-start(s32[2,2]{1,0:T(2,128)} %nb_ref.1) | copy-start | bytes 52
  13.7 13.0 %copy-start.3 = (s32[2]{0:T(128)S(1)}, s32[2]{0:T(128)}, u32[]{:S(2)}) copy-start(s32[2]{0:T(128)} %ct_ref.1) | copy-start | bytes 28
  14.8 26.7 %collective-permute-start.7 = (bf16[1280,256]{1,0:T(8,128)(2,1)}, bf16[1280,256]{1,0:T(8,128)(2,1)S(1)}, u32[]{:S(2)}, u32[]{:S(2)}) collective-permute-start(bf16[1280,256]{1,0:T(8,128)(2,1)} %get-tuple-element.48), channel_id=1, source_target_pairs={{1,2},{3,4},{5,6},{7,8},{9,10},{11,12},{13,14},{15,16},{17,18},{19... | collective-permute-start | bytes 1966088 | tf_op jit(solution)/shard_map/ppermute | solution.py:772
  21.3 20.3 %collective-permute-start.8 = (bf16[1280,256]{1,0:T(8,128)(2,1)}, bf16[1280,256]{1,0:T(8,128)(2,1)}, u32[]{:S(2)}, u32[]{:S(2)}) collective-permute-start(bf16[1280,256]{1,0:T(8,128)(2,1)} %get-tuple-element.49), channel_id=1, source_target_pairs={{0,1},{2,3},{4,5},{6,7},{8,9},{10,11},{12,13},{14,15},{16,17},{18,... | collective-permute-start | bytes 1966088 | tf_op jit(solution)/shard_map/ppermute | solution.py:772
  26.6 1.3 %collective-permute-start = (bf16[64,256]{1,0:T(8,128)(2,1)S(1)}, bf16[64,256]{1,0:T(8,128)(2,1)S(1)}, u32[]{:S(2)}, u32[]{:S(2)}) collective-permute-start(bf16[64,256]{1,0:T(8,128)(2,1)S(1)} %get-tuple-element.41.after_ref.left_ref), channel_id=1, source_target_pairs={{0,8},{8,0},{16,24},{24,16},{32,40},{40,32},{48,56},{56,48},{1,9},... | collective-permute-start | bytes 98312 | tf_op jit(solution)/shard_map/ppermute | solution.py:790
  27.9 8.0 %collective-permute-start.1 = (bf16[64,256]{1,0:T(8,128)(2,1)S(1)}, bf16[64,256]{1,0:T(8,128)(2,1)S(1)}, u32[]{:S(2)}, u32[]{:S(2)}) collective-permute-start(bf16[64,256]{1,0:T(8,128)(2,1)S(1)} %join.1.after_ref.g0_ref), channel_id=1, source_target_pairs={{0,16},{8,24},{16,32},{24,40},{32,48},{40,56},{48,0},{56,8},{1,17}... | collective-permute-start | bytes 98312 | tf_op jit(solution)/shard_map/ppermute | solution.py:781
  29.6 6.4 %collective-permute-start.2 = (bf16[64,256]{1,0:T(8,128)(2,1)S(1)}, bf16[64,256]{1,0:T(8,128)(2,1)S(1)}, u32[]{:S(2)}, u32[]{:S(2)}) collective-permute-start(bf16[64,256]{1,0:T(8,128)(2,1)S(1)} %join.1.after_ref.g0_ref), channel_id=1, source_target_pairs={{0,32},{8,40},{16,48},{24,56},{32,0},{40,8},{48,16},{56,24},{1,33}... | collective-permute-start | bytes 98312 | tf_op jit(solution)/shard_map/ppermute | solution.py:781
  32.5 3.9 %collective-permute-start.3 = (bf16[64,256]{1,0:T(8,128)(2,1)S(1)}, bf16[64,256]{1,0:T(8,128)(2,1)S(1)}, u32[]{:S(2)}, u32[]{:S(2)}) collective-permute-start(bf16[64,256]{1,0:T(8,128)(2,1)S(1)} %join.1.after_ref.g0_ref), channel_id=1, source_target_pairs={{0,48},{8,56},{16,0},{24,8},{32,16},{40,24},{48,32},{56,40},{1,49}... | collective-permute-start | bytes 98312 | tf_op jit(solution)/shard_map/ppermute | solution.py:781
  36.7 10.1 %collective-permute-start.4 = (bf16[64,256]{1,0:T(8,128)(2,1)S(1)}, bf16[64,256]{1,0:T(8,128)(2,1)S(1)}, u32[]{:S(2)}, u32[]{:S(2)}) collective-permute-start(bf16[64,256]{1,0:T(8,128)(2,1)S(1)} %get-tuple-element.44.after_ref.g0_ref), channel_id=1, source_target_pairs={{0,64},{64,128},{128,192},{192,0},{1,65},{65,129},{129,193},{193,1... | collective-permute-start | bytes 98312 | tf_op jit(solution)/shard_map/ppermute | solution.py:781
  38.2 8.6 %collective-permute-start.5 = (bf16[64,256]{1,0:T(8,128)(2,1)S(1)}, bf16[64,256]{1,0:T(8,128)(2,1)S(1)}, u32[]{:S(2)}, u32[]{:S(2)}) collective-permute-start(bf16[64,256]{1,0:T(8,128)(2,1)S(1)} %get-tuple-element.44.after_ref.g0_ref), channel_id=1, source_target_pairs={{0,128},{64,192},{128,0},{192,64},{1,129},{65,193},{129,1},{193,65... | collective-permute-start | bytes 98312 | tf_op jit(solution)/shard_map/ppermute | solution.py:781
  39.3 7.4 %collective-permute-start.6 = (bf16[64,256]{1,0:T(8,128)(2,1)S(1)}, bf16[64,256]{1,0:T(8,128)(2,1)S(1)}, u32[]{:S(2)}, u32[]{:S(2)}) collective-permute-start(bf16[64,256]{1,0:T(8,128)(2,1)S(1)} %get-tuple-element.44.after_ref.g0_ref), channel_id=1, source_target_pairs={{0,192},{64,0},{128,64},{192,128},{1,193},{65,1},{129,65},{193,129... | collective-permute-start | bytes 98312 | tf_op jit(solution)/shard_map/ppermute | solution.py:781
  41.5 5.3 %copy-start = (bf16[2048,256]{1,0:T(8,128)(2,1)S(1)}, bf16[2048,256]{1,0:T(8,128)(2,1)}, u32[]{:S(2)}) copy-start(bf16[2048,256]{1,0:T(8,128)(2,1)} %get-tuple-element.47.g_ref) | copy-start | bytes 3145732
  46.8 3.8 %copy-start.1 = (bf16[1024,1024]{1,0:T(8,128)(2,1)S(1)}, bf16[1024,1024]{1,0:T(8,128)(2,1)}, u32[]{:S(2)}) copy-start(bf16[1024,1024]{1,0:T(8,128)(2,1)} %get-tuple-element.60.table_ab_ref) | copy-start | bytes 6291460
  48.3 5.1 %collective-permute-start.10 = (bf16[64,1024]{1,0:T(8,128)(2,1)S(1)}, bf16[64,1024]{1,0:T(8,128)(2,1)S(1)}, u32[]{:S(2)}, u32[]{:S(2)}) collective-permute-start(bf16[64,1024]{1,0:T(8,128)(2,1)S(1)} %get-tuple-element.53), channel_id=1, source_target_pairs={{0,1},{2,3},{4,5},{6,7},{8,9},{10,11},{12,13},{14,15},{16,17},{18,... | collective-permute-start | bytes 393224 | tf_op jit(solution)/shard_map/ppermute | solution.py:772
  48.6 10.5 %collective-permute-start.9 = (bf16[64,1024]{1,0:T(8,128)(2,1)S(1)}, bf16[64,1024]{1,0:T(8,128)(2,1)S(1)}, u32[]{:S(2)}, u32[]{:S(2)}) collective-permute-start(bf16[64,1024]{1,0:T(8,128)(2,1)S(1)} %get-tuple-element.52), channel_id=1, source_target_pairs={{1,2},{3,4},{5,6},{7,8},{9,10},{11,12},{13,14},{15,16},{17,18},{19... | collective-permute-start | bytes 393224 | tf_op jit(solution)/shard_map/ppermute | solution.py:772
  73.9 1.2 %collective-permute-start.11 = (bf16[72,256]{1,0:T(8,128)(2,1)S(1)}, bf16[72,256]{1,0:T(8,128)(2,1)S(1)}, u32[]{:S(2)}, u32[]{:S(2)}) collective-permute-start(bf16[72,256]{1,0:T(8,128)(2,1)S(1)} %get-tuple-element.65.left_ref), channel_id=1, source_target_pairs={{0,8},{8,0},{16,24},{24,16},{32,40},{40,32},{48,56},{56,48},{1,9},... | collective-permute-start | bytes 110600 | tf_op jit(solution)/shard_map/ppermute | solution.py:790
  75.6 5.7 %collective-permute-start.12 = (bf16[72,256]{1,0:T(8,128)(2,1)S(1)}, bf16[72,256]{1,0:T(8,128)(2,1)S(1)}, u32[]{:S(2)}, u32[]{:S(2)}) collective-permute-start(bf16[72,256]{1,0:T(8,128)(2,1)S(1)} %join_sums.1.refs_0_), channel_id=1, source_target_pairs={{0,16},{8,24},{16,32},{24,40},{32,48},{40,56},{48,0},{56,8},{1,17}... | collective-permute-start | bytes 110600 | tf_op jit(solution)/shard_map/ppermute | solution.py:781
  75.6 5.7 %collective-permute-start.13 = (bf16[72,256]{1,0:T(8,128)(2,1)S(1)}, bf16[72,256]{1,0:T(8,128)(2,1)S(1)}, u32[]{:S(2)}, u32[]{:S(2)}) collective-permute-start(bf16[72,256]{1,0:T(8,128)(2,1)S(1)} %join_sums.1.refs_0_), channel_id=1, source_target_pairs={{0,32},{8,40},{16,48},{24,56},{32,0},{40,8},{48,16},{56,24},{1,33}... | collective-permute-start | bytes 110600 | tf_op jit(solution)/shard_map/ppermute | solution.py:781
  78.4 4.0 %collective-permute-start.14 = (bf16[72,256]{1,0:T(8,128)(2,1)S(1)}, bf16[72,256]{1,0:T(8,128)(2,1)S(1)}, u32[]{:S(2)}, u32[]{:S(2)}) collective-permute-start(bf16[72,256]{1,0:T(8,128)(2,1)S(1)} %join_sums.1.refs_0_), channel_id=1, source_target_pairs={{0,48},{8,56},{16,0},{24,8},{32,16},{40,24},{48,32},{56,40},{1,49}... | collective-permute-start | bytes 110600 | tf_op jit(solution)/shard_map/ppermute | solution.py:781
  82.8 4.0 %collective-permute-start.15 = (bf16[72,256]{1,0:T(8,128)(2,1)S(1)}, bf16[72,256]{1,0:T(8,128)(2,1)S(1)}, u32[]{:S(2)}, u32[]{:S(2)}) collective-permute-start(bf16[72,256]{1,0:T(8,128)(2,1)S(1)} %get-tuple-element.66.g0_ref), channel_id=1, source_target_pairs={{0,64},{64,128},{128,192},{192,0},{1,65},{65,129},{129,193},{193,1... | collective-permute-start | bytes 110600 | tf_op jit(solution)/shard_map/ppermute | solution.py:781
  84.3 5.5 %collective-permute-start.16 = (bf16[72,256]{1,0:T(8,128)(2,1)S(1)}, bf16[72,256]{1,0:T(8,128)(2,1)S(1)}, u32[]{:S(2)}, u32[]{:S(2)}) collective-permute-start(bf16[72,256]{1,0:T(8,128)(2,1)S(1)} %get-tuple-element.66.g0_ref), channel_id=1, source_target_pairs={{0,128},{64,192},{128,0},{192,64},{1,129},{65,193},{129,1},{193,65... | collective-permute-start | bytes 110600 | tf_op jit(solution)/shard_map/ppermute | solution.py:781
  86.3 4.0 %collective-permute-start.17 = (bf16[72,256]{1,0:T(8,128)(2,1)S(1)}, bf16[72,256]{1,0:T(8,128)(2,1)S(1)}, u32[]{:S(2)}, u32[]{:S(2)}) collective-permute-start(bf16[72,256]{1,0:T(8,128)(2,1)S(1)} %get-tuple-element.66.g0_ref), channel_id=1, source_target_pairs={{0,192},{64,0},{128,64},{192,128},{1,193},{65,1},{129,65},{193,129... | collective-permute-start | bytes 110600 | tf_op jit(solution)/shard_map/ppermute | solution.py:781
